TPU v7x, 32 devices: a whole 2x2x4 slice. The times are simulated.
32 devices in a mesh: blk: 8 (over z, y), grp: 4 (over x, core).
Axes of the slice: x: 2, y: 2, z: 4, core: 2. Of those that a mesh axis runs over, the one named last changes fastest.
Arguments:
- features: bfloat16 [4096, 602], P(('blk', 'grp')), may hold values from -6 to 6
- adjacency: bfloat16 [4096, 4096], P(('blk', 'grp')), may hold values from -0.125 to 0.125
- tile_mask: int32 [32, 32], P(('blk', 'grp')), may hold values from 0 to 1, as said below
- labels: int32 [4096], P(('blk', 'grp')), may hold values from 0 to 40
- train_mask: int32 [4096], P(('blk', 'grp')), may hold values from 0 to 1
- w_first: float32 [602, 256], replicated, may hold values from -0.25 to 0.25
- w_second: float32 [256, 256], replicated, may hold values from -0.375 to 0.375
- w_head: float32 [256, 41], replicated, may hold values from -0.375 to 0.375
- norm_params: float32 [4, 256], replicated, may hold values from 0.5 to 1.5
- head_bias: float32 [41], replicated, may hold values from -3 to 3
- m_first: float32 [602, 256], replicated, may hold values from -0.001953125 to 0.001953125
- m_second: float32 [256, 256], replicated, may hold values from -0.001953125 to 0.001953125
- m_head: float32 [256, 41], replicated, may hold values from -0.001953125 to 0.001953125
- m_norms: float32 [4, 256], replicated, may hold values from -0.00390625 to 0.00390625
- m_bias: float32 [41], replicated, may hold values from -0.00390625 to 0.00390625
- v_first: float32 [602, 256], replicated, may hold values from 9.765625e-09 to 3.90625e-08
- v_second: float32 [256, 256], replicated, may hold values from 9.765625e-09 to 3.90625e-08
- v_head: float32 [256, 41], replicated, may hold values from 9.765625e-09 to 3.90625e-08
- v_norms: float32 [4, 256], replicated, may hold values from 3.90625e-08 to 1.5625e-07
- v_bias: float32 [41], replicated, may hold values from 3.90625e-08 to 1.5625e-07
Outputs:
- loss_sum: float32 [], replicated
- train_count: float32 [], replicated
- new_first: float32 [602, 256], replicated
- new_second: float32 [256, 256], replicated
- new_head: float32 [256, 41], replicated
- new_norms: float32 [4, 256], replicated
- new_bias: float32 [41], replicated
- first_m_first: float32 [602, 256], replicated
- first_m_second: float32 [256, 256], replicated
- first_m_head: float32 [256, 41], replicated
- first_m_norms: float32 [4, 256], replicated
- first_m_bias: float32 [41], replicated
- second_v_first: float32 [602, 256], replicated
- second_v_second: float32 [256, 256], replicated
- second_v_head: float32 [256, 41], replicated
- second_v_norms: float32 [4, 256], replicated
- second_v_bias: float32 [41], replicated
Inputs may be any that keep to these rules, and one draw needn't show every extreme that they name: `tile_mask`: every diagonal tile is set.
All inputs are finite; a program needn't handle non-finite values.
Results may differ from a plain program's by a relative error of at most 0.0083.
Values may be sent and summed in bfloat16 or wider, within the bound.
No kernel may reach another device: no remote copies, remote signals or barrier semaphores. Data moves between devices by JAX's collectives and lax.ppermute only.
A program may use at most 128 MiB of HBM per device.

v0:
```python
import jax
import jax.numpy as jnp
from jax import lax
from jax.sharding import PartitionSpec as P

TILE = 128
STEP = 10


EPS_NORM = 1e-05
EPS_ADAM = 1e-08
BETA_ONE = 0.9
BETA_TWO = 0.999
DECAY = 0.01
RATE_MATRIX = 0.03
RATE_SMALL = 0.3


def adamw(weight, gradient, first, second, rate):
    first_new = BETA_ONE * first + (1.0 - BETA_ONE) * gradient
    second_new = BETA_TWO * second + (1.0 - BETA_TWO) * gradient * gradient
    scaled = (
        first_new
        / (1.0 - BETA_ONE**STEP)
        / (jnp.sqrt(second_new / (1.0 - BETA_TWO**STEP)) + EPS_ADAM)
    )
    return (weight - rate * (scaled + DECAY * weight), first_new, second_new)


def aggregate(adjacent, block):
    return jnp.dot(
        adjacent,
        lax.all_gather(block, ("blk", "grp"), axis=0, tiled=True),
        preferred_element_type=jnp.float32,
    )


def spread_back(adjacent, gradient):
    return lax.psum_scatter(
        lax.dot_general(
            adjacent, gradient, (((0,), (0,)), ((), ())), preferred_element_type=jnp.float32
        ),
        ("blk", "grp"),
        scatter_dimension=0,
        tiled=True,
    )


def layer_forward(adjacent, inputs, matrix, gain_row, shift_row, node_total):
    projected = jnp.dot(
        inputs, matrix.astype(jnp.bfloat16), preferred_element_type=jnp.float32
    ).astype(jnp.bfloat16)
    summed = aggregate(adjacent, projected)
    mean_value = lax.psum(jnp.sum(summed, axis=0), ("blk", "grp")) / node_total
    centred = summed - mean_value
    variance = lax.psum(jnp.sum(centred * centred, axis=0), ("blk", "grp")) / node_total
    inverse = lax.rsqrt(variance + EPS_NORM)
    normed = centred * inverse
    pre_act = gain_row * normed + shift_row
    return (jax.nn.gelu(pre_act).astype(jnp.bfloat16), (inputs, normed, inverse, pre_act))


def layer_backward(adjacent, saved, d_hidden, matrix, gain_row, node_total, need_input):
    inputs, normed, inverse, pre_act = saved
    unused, gelu_pull = jax.vjp(jax.nn.gelu, pre_act)
    d_pre = gelu_pull(d_hidden)[0]
    shift_grad, gain_grad = lax.psum(
        (jnp.sum(d_pre, axis=0), jnp.sum(d_pre * normed, axis=0)), ("blk", "grp")
    )
    d_summed = (
        gain_row * inverse * (d_pre - (shift_grad + normed * gain_grad) / node_total)
    ).astype(jnp.bfloat16)
    d_projected = spread_back(adjacent, d_summed).astype(jnp.bfloat16)
    weight_grad = lax.dot_general(
        inputs, d_projected, (((0,), (0,)), ((), ())), preferred_element_type=jnp.float32
    )
    d_inputs = None
    if need_input:
        d_inputs = lax.dot_general(
            d_projected,
            matrix.astype(jnp.bfloat16),
            (((1,), (1,)), ((), ())),
            preferred_element_type=jnp.float32,
        )
    return (weight_grad, gain_grad, shift_grad, d_inputs)


def per_device(
    features,
    adjacency,
    tile_mask,
    labels,
    train_mask,
    w_first,
    w_second,
    w_head,
    norm_params,
    head_bias,
    m_first,
    m_second,
    m_head,
    m_norms,
    m_bias,
    v_first,
    v_second,
    v_head,
    v_norms,
    v_bias,
):
    node_total = features.shape[0] * lax.axis_size(("blk", "grp"))
    rows = adjacency.shape[0]
    width = adjacency.shape[1]
    tiled = adjacency.reshape(rows // TILE, TILE, width // TILE, TILE)
    adjacent = (tiled * tile_mask.astype(jnp.bfloat16)[:, None, :, None]).reshape(rows, width)
    matrices = (w_first, w_second)
    hidden_bf = features
    saved_list = []
    for layer in range(2):
        hidden_bf, saved = layer_forward(
            adjacent,
            hidden_bf,
            matrices[layer],
            norm_params[2 * layer],
            norm_params[2 * layer + 1],
            node_total,
        )
        saved_list.append(saved)
    gathered = aggregate(adjacent, hidden_bf).astype(jnp.bfloat16)
    head_low = w_head.astype(jnp.bfloat16)
    logits = jnp.dot(gathered, head_low, preferred_element_type=jnp.float32) + head_bias
    log_probs = jax.nn.log_softmax(logits, axis=1)
    onehot = (labels[:, None] == jnp.arange(logits.shape[1], dtype=jnp.int32)[None, :]).astype(
        jnp.float32
    )
    weights_mask = train_mask.astype(jnp.float32)
    losses = -jnp.sum(onehot * log_probs, axis=1)
    total_loss, count_total = lax.psum(
        (jnp.sum(losses * weights_mask), jnp.sum(weights_mask)), ("blk", "grp")
    )
    d_logits = (jnp.exp(log_probs) - onehot) * (weights_mask / count_total)[:, None]
    bias_grad = jnp.sum(d_logits, axis=0)
    d_low = d_logits.astype(jnp.bfloat16)
    head_grad = lax.dot_general(
        gathered, d_low, (((0,), (0,)), ((), ())), preferred_element_type=jnp.float32
    )
    d_gathered = lax.dot_general(
        d_low, head_low, (((1,), (1,)), ((), ())), preferred_element_type=jnp.float32
    ).astype(jnp.bfloat16)
    d_hidden = spread_back(adjacent, d_gathered)
    second_grad, gain_two, shift_two, d_hidden = layer_backward(
        adjacent, saved_list[1], d_hidden, w_second, norm_params[2], node_total, True
    )
    first_grad, gain_one, shift_one, unused = layer_backward(
        adjacent, saved_list[0], d_hidden, w_first, norm_params[0], node_total, False
    )
    first_grad, second_grad, head_grad, bias_grad = lax.psum(
        (first_grad, second_grad, head_grad, bias_grad), ("blk", "grp")
    )
    norm_grad = jnp.stack([gain_one, shift_one, gain_two, shift_two])
    params = (w_first, w_second, w_head, norm_params, head_bias)
    grads = (first_grad, second_grad, head_grad, norm_grad, bias_grad)
    firsts = (m_first, m_second, m_head, m_norms, m_bias)
    seconds = (v_first, v_second, v_head, v_norms, v_bias)
    rates = (RATE_MATRIX, RATE_MATRIX, RATE_MATRIX, RATE_SMALL, RATE_SMALL)
    updated = [adamw(params[i], grads[i], firsts[i], seconds[i], rates[i]) for i in range(5)]
    return (
        total_loss,
        count_total,
        updated[0][0],
        updated[1][0],
        updated[2][0],
        updated[3][0],
        updated[4][0],
        updated[0][1],
        updated[1][1],
        updated[2][1],
        updated[3][1],
        updated[4][1],
        updated[0][2],
        updated[1][2],
        updated[2][2],
        updated[3][2],
        updated[4][2],
    )


def solution(mesh):
    return jax.shard_map(
        per_device,
        mesh=mesh,
        in_specs=(
            P(("blk", "grp"), None),
            P(("blk", "grp"), None),
            P(("blk", "grp"), None),
            P(("blk", "grp")),
            P(("blk", "grp")),
            P(),
            P(),
            P(),
            P(),
            P(),
            P(),
            P(),
            P(),
            P(),
            P(),
            P(),
            P(),
            P(),
            P(),
            P(),
        ),
        out_specs=(
            P(),
            P(),
            P(),
            P(),
            P(),
            P(),
            P(),
            P(),
            P(),
            P(),
            P(),
            P(),
            P(),
            P(),
            P(),
            P(),
            P(),
        ),
        check_vma=False,
    )
```

profile of v0, /device:TPU:0, one launch (start us, length us, event | category | flops | bytes accessed | tf_op | source)
XLA Modules:
  0.0 999.9 jit_solution(2090493636923601598)
XLA Ops:
  7.3 0.8 copy-done
  8.1 2.0 convolution_convert_fusion.2
  10.1 0.0 all-gather.6.cloned.1.call-start
  10.1 0.7 convert_bitcast_fusion
  10.9 0.8 fusion.65
  11.7 0.1 broadcast_bitcast_fusion
  11.8 58.8 %all-gather.4.cloned.1.call-done = bf16[4096,256]{1,0:T(8,128)(2,1)} async-done(((bf16[128,256]{1,0:T(8,128)(2,1)}), bf16[4096,256]{1,0:T(8,128)(2,1)}) %all-gather.4.cloned.1.call-update) | async-done | bytes 2097168 | tf_op jit(solution)/shard_map/all_gather | solution.py:33
  70.6 2.4 fusion.66
  73.0 38.6 %psum.98 = f32[256]{0:T(256)S(1)} all-reduce(f32[256]{0:T(256)S(1)} %get-tuple-element.58), channel_id=1, replica_groups=mesh['blk'=8,'grp'=4] {'blk','grp'}, use_global_device_ids=true, to_apply=%region_1.0 | all-reduce | flops 256 | bytes 2048 | tf_op jit(solution)/shard_map/psum | solution.py:54
  111.6 40.7 %psum.99 = f32[256]{0:T(256)S(1)} all-reduce(f32[256]{0:T(256)S(1)} %multiply_reduce_fusion.3), channel_id=1, replica_groups=mesh['blk'=8,'grp'=4] {'blk','grp'}, use_global_device_ids=true, to_apply=%region_3.0 | all-reduce | flops 256 | bytes 2048 | tf_op jit(solution)/shard_map/psum | solution.py:56
  152.3 0.8 convolution_convert_fusion.3
  153.1 0.0 all-gather.8.cloned.1.call-start
  153.2 0.6 convert_reduce_fusion
  153.8 55.5 %all-gather.6.cloned.1.call-done = bf16[4096,256]{1,0:T(8,128)(2,1)} async-done(((bf16[128,256]{1,0:T(8,128)(2,1)}), bf16[4096,256]{1,0:T(8,128)(2,1)}) %all-gather.6.cloned.1.call-update) | async-done | bytes 2097168 | tf_op jit(solution)/shard_map/all_gather | solution.py:33
  209.3 2.1 fusion.67
  211.4 38.6 %psum.100 = f32[256]{0:T(256)S(1)} all-reduce(f32[256]{0:T(256)S(1)} %get-tuple-element.60), channel_id=1, replica_groups=mesh['blk'=8,'grp'=4] {'blk','grp'}, use_global_device_ids=true, to_apply=%region_5.0 | all-reduce | flops 256 | bytes 2048 | tf_op jit(solution)/shard_map/psum | solution.py:54
  250.0 40.9 %all-reduce.2 = (f32[256]{0:T(256)S(1)}, f32[]{:T(128)}) all-reduce(f32[256]{0:T(256)S(1)} %multiply_reduce_fusion.2, f32[]{:T(128)} %convert_reduce_fusion), channel_id=1, replica_groups=mesh['blk'=8,'grp'=4] {'blk','grp'}, use_global_device_ids=true, to_apply=%region_7.0 | all-reduce | flops 257 | bytes 2056 | tf_op jit(solution)/shard_map/psum | solution.py:56
  291.0 0.7 multiply_convert_fusion.2
  291.7 0.0 reduce-scatter.4.cloned.1.call-start
  291.7 0.7 convert_divide_fusion
  292.4 55.7 %all-gather.8.cloned.1.call-done = bf16[4096,256]{1,0:T(8,128)(2,1)} async-done(((bf16[128,256]{1,0:T(8,128)(2,1)}), bf16[4096,256]{1,0:T(8,128)(2,1)}) %all-gather.8.cloned.1.call-update) | async-done | bytes 2097168 | tf_op jit(solution)/shard_map/all_gather | solution.py:33
  348.1 2.1 convolution_convert_fusion
  350.2 0.2 fusion.68
  350.4 2.8 fusion
  353.3 0.0 reduce-scatter.6.cloned.1.call-start
  353.3 139.9 %reduce-scatter.4.cloned.1.call-done = f32[128,256]{1,0:T(8,128)} async-done(((f32[4096,256]{1,0:T(8,128)}), f32[128,256]{1,0:T(8,128)}) %reduce-scatter.4.cloned.1.call-update) | async-done | bytes 131088 | tf_op jit(solution)/shard_map/reduce_scatter | solution.py:39
  493.2 1.0 fusion.58
  494.2 36.9 %all-reduce.1 = (f32[256]{0:T(256)S(1)}, f32[256]{0:T(256)S(1)}) all-reduce(f32[256]{0:T(256)S(1)} %get-tuple-element.20, f32[256]{0:T(256)S(1)} %get-tuple-element.19), channel_id=1, replica_groups=mesh['blk'=8,'grp'=4] {'blk','grp'}, use_global_device_ids=true, to_apply=%region_19.20 | all-reduce | flops 512 | bytes 4096 | tf_op jit(solution)/shard_map/psum | solution.py:67
  531.1 2.7 fusion.3
  533.8 0.0 reduce-scatter.8.cloned.1.call-start
  533.9 0.1 fusion.42
  534.0 0.6 multiply_reduce_fusion.4
  534.6 0.1 fusion.53
  534.7 140.7 %reduce-scatter.6.cloned.1.call-done = f32[128,256]{1,0:T(8,128)} async-done(((f32[4096,256]{1,0:T(8,128)}), f32[128,256]{1,0:T(8,128)}) %reduce-scatter.6.cloned.1.call-update) | async-done | bytes 131088 | tf_op jit(solution)/shard_map/reduce_scatter | solution.py:39
  675.4 1.2 fusion.57
  676.6 37.5 %all-reduce = (f32[]{:T(128)}, f32[256]{0:T(256)S(1)}, f32[256]{0:T(256)S(1)}, f32[256,41]{0,1:T(8,128)S(1)}, f32[41]{0:T(128)S(1)}) all-reduce(f32[]{:T(128)} %multiply_reduce_fusion.4, f32[256]{0:T(256)S(1)} %get-tuple-element.18, f32[256]{0:T(256)S(1)} %get-tuple-element.17, ...), channel_id=1, replica_groups=mesh['blk'=8,'grp'=4] {'blk','grp'}, use_global_device_ids=true, to_apply=%region_12.13 | all-reduce | flops 11050 | bytes 88400 | tf_op jit(solution)/shard_map/psum | solution.py:137
  714.1 2.7 fusion.2
  716.9 0.0 all-reduce.6.cloned.1.call-start
  716.9 0.5 copy-done.13
  717.5 0.6 multiply_subtract_fusion.3
  718.1 1.0 fusion.39
  719.1 139.4 %reduce-scatter.8.cloned.1.call-done = f32[128,256]{1,0:T(8,128)} async-done(((f32[4096,256]{1,0:T(8,128)}), f32[128,256]{1,0:T(8,128)}) %reduce-scatter.8.cloned.1.call-update) | async-done | bytes 131088 | tf_op jit(solution)/shard_map/reduce_scatter | solution.py:39
  858.5 2.0 convolution_bitcast_fusion
  860.5 0.5 multiply_subtract_fusion.4
  861.0 0.7 multiply_subtract_fusion.2
  861.7 127.6 %all-reduce.6.cloned.1.call-done = (f32[602,256]{1,0:T(8,128)}, f32[256,256]{1,0:T(8,128)}) async-done(((f32[602,256]{1,0:T(8,128)}, f32[256,256]{1,0:T(8,128)}), (f32[602,256]{1,0:T(8,128)}, f32[256,256]{1,0:T(8,128)})) %all-reduce.6.cloned.1.call-update) | async-done | bytes 878608 | tf_op jit(solution)/shard_map/psum | solution.py:156
  989.4 2.7 multiply_subtract_fusion
  992.1 1.0 multiply_subtract_fusion.1
  (56 shorter events, 0.4 us)
Async XLA Ops:
  7.2 0.9 copy-start
  7.2 145.1 %copy-start.6 = (f32[256,256]{1,0:T(8,128)S(1)}, f32[256,256]{1,0:T(8,128)}, u32[]{:S(2)}) copy-start(f32[256,256]{1,0:T(8,128)} %param.26) | copy-start | bytes 786436
  7.2 63.4 %all-gather.4.cloned.1.call-start = ((), (), s32[]{:S(2)}) async-start(), calls=%async_computation.3 | async-start | bytes 2162688 | tf_op jit(solution)/shard_map/all_gather | solution.py:33
  10.1 143.1 %copy-start.20 = (s32[128]{0:T(128)S(1)}, s32[128]{0:T(128)}, u32[]{:S(2)}) copy-start(s32[128]{0:T(128)} %param.24) | copy-start | bytes 1540
  10.1 199.2 %copy-start.1 = (bf16[128,4096]{1,0:T(8,128)(2,1)S(1)}, bf16[128,4096]{1,0:T(8,128)(2,1)}, u32[]{:S(2)}) copy-start(bf16[128,4096]{1,0:T(8,128)(2,1)} %param.21) | copy-start | bytes 3145732
  10.1 199.2 %all-gather.6.cloned.1.call-start = ((), (), s32[]{:S(2)}) async-start(), calls=%async_computation.4 | async-start | bytes 2162688 | tf_op jit(solution)/shard_map/all_gather | solution.py:33
  153.1 194.9 %all-gather.8.cloned.1.call-start = ((), (), s32[]{:S(2)}) async-start(), calls=%async_computation.5 | async-start | bytes 2162688 | tf_op jit(solution)/shard_map/all_gather | solution.py:33
  211.4 138.8 %copy-start.5 = (f32[256,41]{0,1:T(8,128)S(1)}, f32[256,41]{0,1:T(8,128)}, u32[]{:S(2)}) copy-start(f32[256,41]{0,1:T(8,128)} %param.27) | copy-start | bytes 125956
  211.4 138.8 %copy-start.17 = (f32[41]{0:T(128)S(1)}, f32[41]{0:T(128)}, u32[]{:S(2)}) copy-start(f32[41]{0:T(128)} %param.29) | copy-start | bytes 496
  211.4 139.0 %copy-start.14 = (s32[128]{0:T(128)S(1)}, s32[128]{0:T(128)}, u32[]{:S(2)}) copy-start(s32[128]{0:T(128)} %param.23) | copy-start | bytes 1540
  291.7 201.5 %reduce-scatter.4.cloned.1.call-start = ((), (), s32[]{:S(2)}) async-start(), calls=%async_computation.6 | async-start | bytes 4325376 | tf_op jit(solution)/shard_map/reduce_scatter | solution.py:39
  353.3 322.2 %reduce-scatter.6.cloned.1.call-start = ((), (), s32[]{:S(2)}) async-start(), calls=%async_computation.7 | async-start | bytes 4325376 | tf_op jit(solution)/shard_map/reduce_scatter | solution.py:39
  533.8 324.7 %reduce-scatter.8.cloned.1.call-start = ((), (), s32[]{:S(2)}) async-start(), calls=%async_computation.8 | async-start | bytes 4325376 | tf_op jit(solution)/shard_map/reduce_scatter | solution.py:39
  716.8 0.7 copy-start.13
  716.8 0.7 copy-start.15
  716.8 0.7 copy-start.16
  716.8 1.3 copy-start.10
  716.8 143.6 %copy-start.18 = (f32[41]{0:T(128)S(1)}, f32[41]{0:T(128)}, u32[]{:S(2)}) copy-start(f32[41]{0:T(128)} %param.34) | copy-start | bytes 496
  716.8 143.6 %copy-start.19 = (f32[41]{0:T(128)S(1)}, f32[41]{0:T(128)}, u32[]{:S(2)}) copy-start(f32[41]{0:T(128)} %param.39) | copy-start | bytes 496
  716.8 144.2 %copy-start.11 = (f32[256,41]{0,1:T(8,128)S(1)}, f32[256,41]{0,1:T(8,128)}, u32[]{:S(2)}) copy-start(f32[256,41]{0,1:T(8,128)} %param.32) | copy-start | bytes 125956
  716.8 144.2 %copy-start.12 = (f32[256,41]{0,1:T(8,128)S(1)}, f32[256,41]{0,1:T(8,128)}, u32[]{:S(2)}) copy-start(f32[256,41]{0,1:T(8,128)} %param.37) | copy-start | bytes 125956
  716.8 272.5 %copy-start.2 = (f32[602,256]{1,0:T(8,128)S(1)}, f32[602,256]{1,0:T(8,128)}, u32[]{:S(2)}) copy-start(f32[602,256]{1,0:T(8,128)} %param.25) | copy-start | bytes 1849348
  716.9 272.5 %copy-start.3 = (f32[602,256]{1,0:T(8,128)S(1)}, f32[602,256]{1,0:T(8,128)}, u32[]{:S(2)}) copy-start(f32[602,256]{1,0:T(8,128)} %param.30) | copy-start | bytes 1849348
  716.9 272.5 %copy-start.4 = (f32[602,256]{1,0:T(8,128)S(1)}, f32[602,256]{1,0:T(8,128)}, u32[]{:S(2)}) copy-start(f32[602,256]{1,0:T(8,128)} %param.35) | copy-start | bytes 1849348
  716.9 272.4 %all-reduce.6.cloned.1.call-start = ((), (), s32[]{:S(2)}) async-start(), calls=%async_computation.9 | async-start | bytes 1769472 | tf_op jit(solution)/shard_map/psum | solution.py:156
  989.3 2.7 copy-start.7
  989.3 2.7 copy-start.8
  989.3 2.7 copy-start.9
Sparse Core Ops, SparseCore 0:
  11.5 59.0 all-gather.3
  153.2 56.0 all-gather.5
  291.8 56.1 all-gather.7
  353.4 139.7 reduce-scatter.3
  533.9 141.4 reduce-scatter.5
  716.9 141.4 reduce-scatter.7
  864.3 124.9 all-reduce.5
where the time goes:
time: 1000 us
  waiting for transfers between devices  718 us (72%)
  blocking collectives  233 us (23%)
  matrix products  21.9 us (2%)
  between operations  14.4 us (1%)
  other arithmetic  10.1 us (1%)
    reduce_scatter x3, waiting for transfers between devices, spread_back(): lax.psum_scatter(lax.dot_general(adjacent, gradient, (((0,), (0,)), ((),...  420 us
    all_gather x3, waiting for transfers between devices, aggregate(): lax.all_gather(block, ('blk', 'grp'), axis=0, tiled=True)  170 us
    psum x1, waiting for transfers between devices, per_device(): lax.psum((first_grad, second_grad, head_grad, bias_grad), ('blk', 'grp'))  128 us
    psum x2, blocking collectives, layer_forward(): lax.psum(jnp.sum(centred * centred, axis=0), ('blk', 'grp')) / node_total  81.6 us
    psum x2, blocking collectives, layer_forward(): mean_value = lax.psum(jnp.sum(summed, axis=0), ('blk', 'grp')) / node_total  77.1 us
    psum x1, blocking collectives, per_device(): lax.psum((jnp.sum(losses * weights_mask), jnp.sum(weights_mask)), ('blk',...  37.5 us
    psum x1, blocking collectives, layer_backward(): lax.psum((jnp.sum(d_pre, axis=0), jnp.sum(d_pre * normed, axis=0)), ('blk...  36.9 us
  transfers between devices with their start and end apart: 7, of which 7 were waited for; matrix products, arithmetic and copies ran while one was open for 1% of the time, Pallas kernels for 0%

commit v1 on v0

v1 whole, which is shorter than its diff:
```python
import functools
import math

import jax
import jax.numpy as jnp
from jax import lax
from jax.experimental import pallas as pl
from jax.experimental.pallas import tpu as pltpu
from jax.sharding import Mesh
from jax.sharding import PartitionSpec as P

TILE = 128
STEP = 10
EPS_NORM = 1e-05
EPS_ADAM = 1e-08
BETA_ONE = 0.9
BETA_TWO = 0.999
DECAY = 0.01
RATE_MATRIX = 0.03
RATE_SMALL = 0.3

BF = jnp.bfloat16
F32 = jnp.float32
PLANE = ("y", "x", "c")
EVERY = ("z", "y", "x", "c")
LANES = 128
HEAD_ROWS = 48
EXTRA = 16
ROOT = math.sqrt(2.0 / math.pi)
BEND = 0.044715


def adamw(weight, gradient, first, second, rate):
    first_new = BETA_ONE * first + (1.0 - BETA_ONE) * gradient
    second_new = BETA_TWO * second + (1.0 - BETA_TWO) * gradient * gradient
    scaled = (
        first_new
        / (1.0 - BETA_ONE**STEP)
        / (jnp.sqrt(second_new / (1.0 - BETA_TWO**STEP)) + EPS_ADAM)
    )
    return (weight - rate * (scaled + DECAY * weight), first_new, second_new)


def dot(left, right):
    return jnp.dot(left, right, preferred_element_type=F32)


def dot_turned(left, right):
    return lax.dot_general(left, right, (((1,), (1,)), ((), ())), preferred_element_type=F32)


def shape(dims, kind=F32):
    return jax.ShapeDtypeStruct(dims, kind)


def run(body, outs, ins, scratch=(), flops=0, scalars=0):
    held = sum(math.prod(a.shape[:-1]) * max(a.shape[-1], LANES) * a.dtype.itemsize for a in (*ins, *outs))
    limit = min(60 << 20, 2 * held + (8 << 20))
    return pl.pallas_call(
        body,
        out_shape=tuple(outs),
        in_specs=[pl.BlockSpec(memory_space=pltpu.SMEM)] * scalars
        + [pl.BlockSpec(memory_space=pltpu.VMEM)] * (len(ins) - scalars),
        out_specs=tuple(pl.BlockSpec(memory_space=pltpu.VMEM) for unused in outs),
        scratch_shapes=list(scratch),
        compiler_params=pltpu.CompilerParams(vmem_limit_bytes=limit),
        cost_estimate=pl.CostEstimate(flops=flops, bytes_accessed=held, transcendentals=0),
    )(*ins)


def swap(block, mask):
    return lax.ppermute(block, PLANE, [(i, i ^ mask) for i in range(8)])


def pass_line(block, mask):
    return lax.ppermute(block, "z", [(i, i ^ mask) for i in range(4)])


def short_line():
    return lax.axis_size("z") == 4


def gather_all(block):
    if short_line():
        line = jnp.stack([block] + [pass_line(block, k) for k in range(1, 4)])
    else:
        line = lax.all_gather(block, "z", axis=0)
    half = jnp.concatenate([line] + [swap(line, 2 * k) for k in range(1, 4)])
    return half, swap(half, 1)


def arrange_kernel(mask_ref, values_ref, near_ref, far_ref):
    half = near_ref.shape[1] // TILE
    lines = half // 4
    here = 4 * lax.axis_index("y") + 2 * lax.axis_index("x") + lax.axis_index("c")
    level = lax.axis_index("z") if short_line() else 0

    for core, out_ref in ((0, near_ref), (1, far_ref)):

        def one(step, carry, core=core, out_ref=out_ref):
            place, height = step // lines, jnp.bitwise_xor(step % lines, level)
            source = height * 8 + jnp.bitwise_xor(place * 2 + core, here)
            keep = mask_ref[0, source].astype(F32).astype(BF)
            out_ref[:, pl.ds(pl.multiple_of(step * TILE, TILE), TILE)] = (
                values_ref[:, pl.ds(pl.multiple_of(source * TILE, TILE), TILE)] * keep
            )
            return carry

        lax.fori_loop(0, half, one, 0)


def centre_into(out_ref, summed):
    rows = summed.shape[0]
    centre = (jnp.sum(summed, axis=0, keepdims=True) / rows).astype(BF).astype(F32)
    out_ref[:rows, :] = (summed - centre).astype(BF)
    out_ref[rows:, :] = jnp.broadcast_to(centre, (EXTRA, summed.shape[1])).astype(BF)


def moments(refs, node_total):
    count, tall, width = refs[0].shape
    rows = tall - EXTRA
    pivot = refs[0][0, rows:, :].astype(F32)[:1]
    zero = jnp.zeros((8, width), F32)
    sums = (zero, zero)
    for ref in refs:

        def one(i, carry, ref=ref):
            total, square = carry
            value = ref[i, :rows, :].astype(F32).reshape(rows // 8, 8, width)
            part = jnp.sum(value, axis=0)
            away = ref[i, rows:, :].astype(F32)[:1] - pivot
            each = away * (rows // 8)
            return (
                total + part + each,
                square + jnp.sum(value * value, axis=0) + away * (2.0 * part + each),
            )

        sums = lax.fori_loop(0, count, one, sums)
    shift = jnp.sum(sums[0], axis=0, keepdims=True) / node_total
    variance = jnp.sum(sums[1], axis=0, keepdims=True) / node_total - shift * shift
    return pivot + shift, lax.rsqrt(jnp.maximum(variance, 0.0) + EPS_NORM)


def gelu_half(value):
    square = value * value
    bend = jnp.tanh(value * (ROOT + (ROOT * BEND) * square))
    return 0.5 + 0.5 * bend, bend, square


def gelu_slope(value, half, bend, square):
    return half + (0.5 * value) * (1.0 - bend * bend) * (ROOT + (3 * ROOT * BEND) * square)


def blocks_of(ref, i, pair, rows):
    parts = [
        (ref[i * pair + j, :rows, :].astype(F32), ref[i * pair + j, rows:, :].astype(F32)[:1])
        for j in range(pair)
    ]
    return parts


def columns(ref, i, width):
    return ref[:, pl.ds(pl.multiple_of(i * width, width), width)]


def split_sums(total):
    high = total.astype(BF).astype(F32)
    low = (total - high).astype(BF).astype(F32)
    return jnp.concatenate([high, low])


def joined(parts):
    parts = parts.astype(F32)
    return parts[: EXTRA // 2] + parts[EXTRA // 2 :]


def put_sums(out_ref, width, parts):
    out_ref[width:, :LANES] = parts.astype(BF)
    if out_ref.shape[1] > LANES:
        out_ref[width:, LANES:] = jnp.zeros((EXTRA, out_ref.shape[1] - LANES), BF)


def spread_into(send_ref, turned, far_ref):
    width = turned.shape[0]
    step = min(512, far_ref.shape[1])
    for i in range(far_ref.shape[1] // step):
        send_ref[:width, i * step : (i + 1) * step] = dot(
            turned, far_ref[:, i * step : (i + 1) * step]
        ).astype(BF)


def fold_core_kernel(summing, turned_ref, near_ref, got_ref, *refs):
    if summing:
        parts_ref, kept_ref, *piece_refs, out_parts_ref = refs
    else:
        kept_ref, *piece_refs = refs
    width = turned_ref.shape[0]
    piece = kept_ref.shape[1]
    step = min(512, piece)
    for k in range(4):
        for i in range(piece // step):
            at = k * piece + i * step
            value = dot(turned_ref[...], near_ref[:, at : at + step])
            value = value + got_ref[:width, at : at + step].astype(F32)
            if k == 0:
                kept_ref[:, i * step : (i + 1) * step] = value
            else:
                piece_refs[k - 1][:width, i * step : (i + 1) * step] = value.astype(BF)
    if summing:
        parts = split_sums(joined(parts_ref[...]) + joined(got_ref[width:, :LANES]))
        out_parts_ref[...] = parts
        for piece_ref in piece_refs:
            put_sums(piece_ref, width, parts)


def sum_four(own, got_refs, width, cols=slice(None)):
    got = [ref[:width, cols].astype(F32) for ref in got_refs]
    return (own + got[0]) + (got[1] + got[2])


def sum_parts(parts, got_refs, width):
    got = [joined(ref[width:, :LANES]) for ref in got_refs]
    return (joined(parts) + got[0]) + (got[1] + got[2])


def fold_plane_kernel(summing, short, own_ref, *refs):
    got_refs, refs = refs[:3], refs[3:]
    width = own_ref.shape[0]
    if summing:
        parts = split_sums(sum_parts(refs[0][...], got_refs, width))
        refs = refs[1:]
    if not short:
        refs[0][...] = sum_four(own_ref[...], got_refs, width)
        if summing:
            refs[1][...] = parts
        return
    kept_ref, *piece_refs = refs[:4]
    for k in range(4):
        cols = slice(k * LANES, (k + 1) * LANES)
        value = sum_four(own_ref[:, cols], got_refs, width, cols)
        if k == 0:
            kept_ref[...] = value
        else:
            piece_refs[k - 1][:width, :] = value.astype(BF)
            if summing:
                put_sums(piece_refs[k - 1], width, parts)
    if summing:
        refs[4][...] = parts


def spread_back(turned, send, near, parts):
    width = turned.shape[0]
    tall = send.shape[0]
    piece = near.shape[1] // 4
    summing = parts is not None
    got = swap(send, 1)
    outs = [shape((width, piece))] + [shape((tall, piece), BF)] * 3
    ins = [turned, near, got] + [parts] * summing
    outs += [shape((EXTRA, LANES))] * summing
    own, *rest = run(
        functools.partial(fold_core_kernel, summing), outs, ins, flops=2 * width * LANES * piece * 4
    )
    pieces, parts = rest[:3], rest[3:]
    got = [swap(pieces[k - 1], 2 * k) for k in range(1, 4)]
    short = short_line()
    if short:
        outs = [shape((width, LANES))] + [shape((tall, LANES), BF)] * 3
    else:
        outs = [shape((width, piece))]
    outs += [shape((EXTRA, LANES))] * summing
    folded = run(functools.partial(fold_plane_kernel, summing, short), outs, [own, *got, *parts])
    if short:
        own, *rest = folded
        got = [pass_line(rest[k - 1], k) for k in range(1, 4)]
        return own, got, rest[3:]
    total = lax.psum_scatter(folded[0], "z", scatter_dimension=1, tiled=True)
    if not summing:
        return total, [], []
    return total, [], [lax.psum(folded[1][: EXTRA // 2] + folded[1][EXTRA // 2 :], "z")]


def line_sum(own_ref, got_refs, parts_refs):
    width = own_ref.shape[0]
    if got_refs:
        total = sum_four(own_ref[...], got_refs, width)
        sums = sum_parts(parts_refs[0][...], got_refs, width) if parts_refs else None
        return total, sums
    return own_ref[...], parts_refs[0][...] if parts_refs else None


def wide(sums, row):
    return jnp.concatenate([sums[row : row + 1], sums[row + 1 : row + 2]], axis=1)


def put_wide(ref, row, value):
    ref[row : row + 1, :] = value[:, :LANES]
    ref[row + 1 : row + 2, :] = value[:, LANES:]


def layer_kernel(node_total, layer, near_ref, far_ref, low_ref, norm_ref, half_ref, other_ref, out_ref, stats_ref):
    refs = (half_ref, other_ref)
    count, tall, width = half_ref.shape
    rows = tall - EXTRA
    mean_value, inverse = moments(refs, node_total)
    stats_ref[0:1, :] = mean_value
    stats_ref[1:2, :] = inverse
    scale = norm_ref[2 * layer : 2 * layer + 1, :] * inverse
    start = norm_ref[2 * layer + 1 : 2 * layer + 2, :] - mean_value * scale
    total = jnp.zeros((rows, low_ref.shape[1]), F32)
    for ref, adjacent_ref in ((half_ref, near_ref), (other_ref, far_ref)):

        def one(i, total, ref=ref, adjacent_ref=adjacent_ref):
            hidden = []
            for value, centre in blocks_of(ref, i, 2, rows):
                value = value * scale + (start + centre * scale)
                hidden.append((value * gelu_half(value)[0]).astype(BF))
            projected = dot(jnp.concatenate(hidden), low_ref[...]).astype(BF)
            return total + dot(columns(adjacent_ref, i, 2 * rows), projected)

        total = lax.fori_loop(0, count // 2, one, total, unroll=2)
    centre_into(out_ref, total)


def slopes_kernel(layer, near_ref, far_ref, norm_ref, half_ref, other_ref, stats_ref, out_ref):
    count, tall, width = half_ref.shape
    rows = tall - EXTRA
    mean_value, inverse = stats_ref[0:1, :], stats_ref[1:2, :]
    gain = norm_ref[2 * layer : 2 * layer + 1, :]
    offset = norm_ref[2 * layer + 1 : 2 * layer + 2, :]
    out_ref[...] = jnp.zeros(out_ref.shape, F32)
    for ref, adjacent_ref in ((half_ref, near_ref), (other_ref, far_ref)):

        def one(i, carry, ref=ref, adjacent_ref=adjacent_ref):
            slopes = []
            for value, centre in blocks_of(ref, i, 2, rows):
                normed = value * inverse + (centre - mean_value) * inverse
                value = gain * normed + offset
                slope = gelu_slope(value, *gelu_half(value))
                slopes.append(jnp.concatenate([slope.astype(BF), (slope * normed).astype(BF)], axis=1))
            out_ref[...] += dot(columns(adjacent_ref, i, 2 * rows), jnp.concatenate(slopes))
            return carry

        lax.fori_loop(0, count // 2, one, 0, unroll=2)


def head_kernel(
    node_total,
    classes,
    near_ref,
    far_ref,
    low_ref,
    norm_ref,
    bias_ref,
    label_ref,
    mask_ref,
    half_ref,
    other_ref,
    send_ref,
    turned_ref,
    parts_ref,
    stats_ref,
    total_ref,
    sums_ref,
):
    refs = (half_ref, other_ref)
    count, tall, width = half_ref.shape
    rows = tall - EXTRA
    mean_value, inverse = moments(refs, node_total)
    stats_ref[0:1, :] = mean_value
    stats_ref[1:2, :] = inverse
    gain, offset = norm_ref[2:3, :], norm_ref[3:4, :]
    total_ref[...] = jnp.zeros(total_ref.shape, F32)
    for ref, adjacent_ref in ((half_ref, near_ref), (other_ref, far_ref)):

        def one(i, carry, ref=ref, adjacent_ref=adjacent_ref):
            hidden, slopes = [], []
            for value, centre in blocks_of(ref, i, 2, rows):
                normed = value * inverse + (centre - mean_value) * inverse
                value = gain * normed + offset
                half, bend, square = gelu_half(value)
                slope = gelu_slope(value, half, bend, square)
                hidden.append((value * half).astype(BF))
                slopes.append(jnp.concatenate([slope.astype(BF), (slope * normed).astype(BF)], axis=1))
            headed = dot(jnp.concatenate(hidden), low_ref[...]).astype(BF)
            both = jnp.concatenate([headed, jnp.concatenate(slopes)], axis=1)
            total_ref[...] += dot(columns(adjacent_ref, i, 2 * rows), both)
            return carry

        lax.fori_loop(0, count // 2, one, 0, unroll=2)

    lane = lax.broadcasted_iota(jnp.int32, (rows, LANES), 1)
    logits = jnp.where(lane < classes, total_ref[:, :LANES] + bias_ref[...], -1e30)
    logits = logits - jnp.max(logits, axis=1, keepdims=True)
    raised = jnp.exp(logits)
    whole = jnp.sum(raised, axis=1, keepdims=True)
    onehot = jnp.where(lane == label_ref[...], 1.0, 0.0)
    weight = mask_ref[...].astype(F32)
    losses = jnp.log(whole) - jnp.sum(onehot * logits, axis=1, keepdims=True)
    d_logits = (raised / whole - onehot) * weight
    d_low = d_logits.astype(BF)
    d_wide = dot_turned(d_low, low_ref[...])
    put_wide(sums_ref, 0, jnp.sum(d_wide * total_ref[:, LANES : LANES + width], axis=0, keepdims=True))
    put_wide(sums_ref, 2, jnp.sum(d_wide * total_ref[:, LANES + width :], axis=0, keepdims=True))
    sums_ref[4:5, :] = jnp.sum(d_logits, axis=0, keepdims=True)
    first = lax.broadcasted_iota(jnp.int32, (rows, LANES), 1) == 0
    sums_ref[5:6, :] = jnp.sum(jnp.where(first, losses * weight, weight), axis=0, keepdims=True)
    sums_ref[6:8, :] = jnp.zeros((2, LANES), F32)
    parts = split_sums(sums_ref[...])
    parts_ref[...] = parts
    turned = d_logits.T[:HEAD_ROWS].astype(BF)
    turned_ref[...] = turned
    spread_into(send_ref, turned, far_ref)
    put_sums(send_ref, HEAD_ROWS, parts)


def backward_norm(d_hidden, own_ref, stats_ref, norm_ref, layer, shift_grad, gain_grad, node_total):
    rows = own_ref.shape[0] - EXTRA
    mean_value, inverse = stats_ref[0:1, :], stats_ref[1:2, :]
    gain = norm_ref[2 * layer : 2 * layer + 1, :]
    centre = own_ref[rows:, :].astype(F32)[:1]
    normed = own_ref[:rows, :].astype(F32) * inverse + (centre - mean_value) * inverse
    value = gain * normed + norm_ref[2 * layer + 1 : 2 * layer + 2, :]
    half, bend, square = gelu_half(value)
    d_pre = d_hidden * gelu_slope(value, half, bend, square)
    d_summed = (gain * inverse) * (d_pre - (shift_grad + normed * gain_grad) / node_total)
    return d_summed, value * half


def second_kernel(node_total, n_got, *refs):
    own_ref, got_refs, refs = refs[0], refs[1 : 1 + n_got], refs[1 + n_got :]
    (in_parts_ref, far_ref, head_ref, low_ref, norm_ref, summed_ref, stats_ref, slopes_ref) = refs[:8]
    send_ref, turned_ref, parts_ref, grad_ref, out_ref, sums_ref = refs[8:]
    headed, sums = line_sum(own_ref, got_refs, [in_parts_ref])
    rows = headed.shape[1]
    each = 1.0 / sums[5:6, 1:2]
    headed = headed * each
    put_row = lax.broadcasted_iota(jnp.int32, sums.shape, 0)
    out_ref[...] = jnp.where(put_row == 5, sums, sums * each)
    turned_back = jnp.concatenate([headed, jnp.zeros((LANES - HEAD_ROWS, rows), F32)]).T
    d_hidden = dot_turned(turned_back.astype(BF), head_ref[...])
    d_summed, hidden = backward_norm(
        d_hidden, summed_ref, stats_ref, norm_ref, 1, wide(sums, 0) * each, wide(sums, 2) * each, node_total
    )
    grad_ref[...] = dot(headed.astype(BF), hidden.astype(BF))
    d_low = d_summed.astype(BF)
    d_wide = dot_turned(d_low, low_ref[...])
    width = d_wide.shape[1]
    put_wide(sums_ref, 0, jnp.sum(d_wide * slopes_ref[:, :width], axis=0, keepdims=True))
    put_wide(sums_ref, 2, jnp.sum(d_wide * slopes_ref[:, width:], axis=0, keepdims=True))
    sums_ref[4:8, :] = jnp.zeros((4, LANES), F32)
    parts = split_sums(sums_ref[...])
    parts_ref[...] = parts
    turned = d_summed.T.astype(BF)
    turned_ref[...] = turned
    spread_into(send_ref, turned, far_ref)
    put_sums(send_ref, width, parts)


def first_kernel(node_total, n_got, *refs):
    own_ref, got_refs, refs = refs[0], refs[1 : 1 + n_got], refs[1 + n_got :]
    in_parts_ref, far_ref, low_ref, norm_ref, summed_ref, stats_ref = refs[:6]
    send_ref, turned_ref, grad_ref, out_ref = refs[6:]
    d_projected, sums = line_sum(own_ref, got_refs, [in_parts_ref])
    out_ref[...] = sums
    d_projected = d_projected.T.astype(BF)
    d_hidden = dot_turned(d_projected, low_ref[...])
    d_summed, hidden = backward_norm(
        d_hidden, summed_ref, stats_ref, norm_ref, 0, wide(sums, 0), wide(sums, 2), node_total
    )
    turned = d_summed.T.astype(BF)
    turned_ref[...] = turned
    spread_into(send_ref, turned, far_ref)
    grad_ref[...] = dot(hidden.T.astype(BF), d_projected)


def pile_kernel(n_got, *refs):
    own_ref, got_refs, refs = refs[0], refs[1 : 1 + n_got], refs[1 + n_got :]
    inputs_ref, second_ref, head_ref, away_ref, kept_ref, pile_ref = refs
    d_projected = line_sum(own_ref, got_refs, [])[0].T.astype(BF)
    at = inputs_ref.shape[0]
    pile_ref[:at, :] = dot(inputs_ref[...], d_projected)
    pile_ref[at : at + second_ref.shape[0], :] = second_ref[...]
    at += second_ref.shape[0]
    pile_ref[at : at + HEAD_ROWS, :] = head_ref[...]
    at += HEAD_ROWS
    pile_ref[at:, :] = jnp.zeros((pile_ref.shape[0] - at, pile_ref.shape[1]), F32)
    half = away_ref.shape[0]
    core = lax.axis_index("c")
    away_ref[...] = pile_ref[pl.ds(pl.multiple_of((1 - core) * half, half), half), :].astype(BF)
    kept_ref[...] = pile_ref[pl.ds(pl.multiple_of(core * half, half), half), :]


def pile_core_kernel(kept_ref, got_ref, own_ref, *piece_refs):
    size = own_ref.shape[0]
    here = 2 * lax.axis_index("y") + lax.axis_index("x")
    for k in range(4):
        at = pl.ds(pl.multiple_of(jnp.bitwise_xor(here, k) * size, size), size)
        value = kept_ref[at, :] + got_ref[at, :].astype(F32)
        if k == 0:
            own_ref[...] = value
        else:
            piece_refs[k - 1][...] = value.astype(BF)


def pile_sum_kernel(own_ref, *refs):
    refs[3][...] = sum_four(own_ref[...].astype(F32), refs[:3], own_ref.shape[0]).astype(refs[3].dtype)


def pile_place_kernel(half_ref, other_ref, out_ref):
    unused, size, unused = half_ref.shape
    here = 2 * lax.axis_index("y") + lax.axis_index("x")
    core = lax.axis_index("c")
    for c, ref in ((0, half_ref), (1, other_ref)):
        for k in range(4):
            at = (jnp.bitwise_xor(core, c) * 4 + jnp.bitwise_xor(here, k)) * size
            out_ref[pl.ds(pl.multiple_of(at, size), size), :] = ref[k].astype(F32)


def sum_pile(away, kept):
    size = away.shape[0] // 4
    width = away.shape[1]
    got = swap(away, 1)
    own, *pieces = run(
        pile_core_kernel, [shape((size, width))] + [shape((size, width), BF)] * 3, [kept, got]
    )
    got = [swap(pieces[k - 1], 2 * k) for k in range(1, 4)]
    if short_line():
        (shard,) = run(pile_sum_kernel, [shape((size, width), BF)], [own, *got])
        got = [pass_line(shard, k) for k in range(1, 4)]
        (shard,) = run(pile_sum_kernel, [shape((size, width), BF)], [shard, *got])
    else:
        (shard,) = run(pile_sum_kernel, [shape((size, width))], [own, *got])
        shard = lax.psum(shard, "z").astype(BF)
    half = jnp.stack([shard] + [swap(shard, 2 * k) for k in range(1, 4)])
    return run(pile_place_kernel, [shape((8 * size, width))], [half, swap(half, 1)])[0]


def center_kernel(near_ref, far_ref, half_ref, other_ref, out_ref):
    count, rows, width = half_ref.shape
    total = dot(near_ref[...], half_ref[...].reshape(count * rows, width))
    total = total + dot(far_ref[...], other_ref[...].reshape(count * rows, width))
    centre_into(out_ref, total)


def per_device(
    features,
    adjacency,
    tile_mask,
    labels,
    train_mask,
    w_first,
    w_second,
    w_head,
    norm_params,
    head_bias,
    m_first,
    m_second,
    m_head,
    m_norms,
    m_bias,
    v_first,
    v_second,
    v_head,
    v_norms,
    v_bias,
):
    rows, node_total = adjacency.shape
    inputs, hidden = w_first.shape
    classes = w_head.shape[1]
    half = node_total // 2
    tall = rows + EXTRA
    second_low = w_second.astype(BF)
    head_low = jnp.pad(w_head, ((0, 0), (0, LANES - classes))).astype(BF)
    bias_row = jnp.pad(head_bias, (0, LANES - classes))[None]
    norm_rows = jnp.pad(norm_params, ((0, 4), (0, 0)))
    inputs_tall = -(-inputs // EXTRA) * EXTRA
    features_turned = jnp.pad(features.T, ((0, inputs_tall - inputs), (0, 0)))
    work = 2 * rows * node_total * hidden

    near, far = run(
        arrange_kernel, [shape((rows, half), BF)] * 2, [tile_mask, adjacency], scalars=1
    )

    projected = dot(features, w_first.astype(BF)).astype(BF)
    (summed_one,) = run(
        center_kernel, [shape((tall, hidden), BF)], [near, far, *gather_all(projected)], flops=work
    )
    around = gather_all(summed_one)
    summed_two, stats_one = run(
        functools.partial(layer_kernel, node_total, 0),
        [shape((tall, hidden), BF), shape((8, hidden))],
        [near, far, second_low, norm_rows, *around],
        flops=3 * work,
    )
    (slopes_one,) = run(
        functools.partial(slopes_kernel, 0),
        [shape((rows, 2 * hidden))],
        [near, far, norm_rows, *around, stats_one],
        flops=3 * work,
    )
    send, turned, parts, stats_two = run(
        functools.partial(head_kernel, node_total, classes),
        [
            shape((HEAD_ROWS + EXTRA, half), BF),
            shape((HEAD_ROWS, rows), BF),
            shape((EXTRA, LANES)),
            shape((8, hidden)),
        ],
        [
            near,
            far,
            head_low,
            norm_rows,
            bias_row,
            labels[:, None],
            train_mask[:, None],
            *gather_all(summed_two),
        ],
        scratch=[pltpu.VMEM((rows, LANES + 2 * hidden), F32), pltpu.VMEM((8, LANES), F32)],
        flops=4 * work,
    )

    own, got, sums = spread_back(turned, send, near, parts)
    send, turned, parts, head_grad, sums_two = run(
        functools.partial(second_kernel, node_total, len(got)),
        [
            shape((hidden + EXTRA, half), BF),
            shape((hidden, rows), BF),
            shape((EXTRA, LANES)),
            shape((HEAD_ROWS, hidden)),
            shape((8, LANES)),
        ],
        [own, *got, *sums, far, head_low, second_low, norm_rows, summed_two, stats_two, slopes_one],
        scratch=[pltpu.VMEM((8, LANES), F32)],
        flops=work // 2,
    )
    own, got, sums = spread_back(turned, send, near, parts)
    send, turned, second_grad, sums_one = run(
        functools.partial(first_kernel, node_total, len(got)),
        [
            shape((hidden, half), BF),
            shape((hidden, rows), BF),
            shape((hidden, hidden)),
            shape((8, LANES)),
        ],
        [own, *got, *sums, far, second_low, norm_rows, summed_one, stats_one],
        flops=work // 2,
    )
    own, got, sums = spread_back(turned, send, near, None)
    length = inputs_tall + hidden + HEAD_ROWS
    size = -(-length // (8 * EXTRA)) * EXTRA
    away, kept = run(
        functools.partial(pile_kernel, len(got)),
        [shape((4 * size, hidden), BF), shape((4 * size, hidden))],
        [own, *got, features_turned, second_grad, head_grad],
        scratch=[pltpu.VMEM((8 * size, hidden), F32)],
    )
    pile = sum_pile(away, kept)
    first_grad = pile[:inputs]
    second_grad = pile[inputs_tall : inputs_tall + hidden]
    head_grad = pile[inputs_tall + hidden : inputs_tall + hidden + classes].T

    def pair(sums):
        return sums[2:4].reshape(1, hidden), sums[0:2].reshape(1, hidden)

    norm_grad = jnp.concatenate([*pair(sums_one), *pair(sums_two)])
    bias_grad = sums_two[4, :classes]
    params = (w_first, w_second, w_head, norm_params, head_bias)
    grads = (first_grad, second_grad, head_grad, norm_grad, bias_grad)
    firsts = (m_first, m_second, m_head, m_norms, m_bias)
    seconds = (v_first, v_second, v_head, v_norms, v_bias)
    rates = (RATE_MATRIX, RATE_MATRIX, RATE_MATRIX, RATE_SMALL, RATE_SMALL)
    updated = [adamw(params[i], grads[i], firsts[i], seconds[i], rates[i]) for i in range(5)]
    return (
        sums_two[5, 0],
        sums_two[5, 1],
        *(updated[i][0] for i in range(5)),
        *(updated[i][1] for i in range(5)),
        *(updated[i][2] for i in range(5)),
    )


def solution(mesh):
    wide_mesh = Mesh(mesh.devices.reshape(-1, 2, 2, 2), EVERY)
    split = (P(EVERY, None),) * 3 + (P(EVERY),) * 2
    return jax.shard_map(
        per_device,
        mesh=wide_mesh,
        in_specs=split + (P(),) * 15,
        out_specs=(P(),) * 17,
        check_vma=False,
    )
```

time: 1000 us -> 211 us (0.21)
  waiting for transfers between devices: 718 us -> 104 us
  blocking collectives: 233 us -> 0 us
  starting transfers between devices: 0.29 us -> 63 us
  Pallas kernels: 0 us -> 23.2 us
  matrix products: 21.9 us -> 1.41 us
  between operations: 14.4 us -> 1.25 us
  local copies, waits for them, and re-layouts: 2.42 us -> 13.1 us
    reduce_scatter x3 -> x0, waiting for transfers between devices: 420 us -> none  [spread_back(): lax.psum_scatter(lax.dot_general(adjacent, gradient, (((0,), (0,)), ((),...]
    psum x6 -> x0, blocking collectives: 233 us -> none  [the longest x2 81.6 us: layer_forward(): lax.psum(jnp.sum(centred * centred, axis=0), ('blk', 'grp')) / node_total]
    all_gather x3 -> x0, waiting for transfers between devices: 170 us -> none  [aggregate(): lax.all_gather(block, ('blk', 'grp'), axis=0, tiled=True)]
    psum x1 -> x0, waiting for transfers between devices: 128 us -> none  [per_device(): lax.psum((first_grad, second_grad, head_grad, bias_grad), ('blk', 'grp'))]
    ppermute x0 -> x53, waiting for transfers between devices: none -> 104 us  [the longest x32 74.5 us: swap(): return lax.ppermute(block, PLANE, [(i, i ^ mask) for i in range(8)])]
    ppermute x0 -> x53, starting transfers between devices: none -> 63 us  [the longest x21 33.6 us: pass_line(): return lax.ppermute(block, 'z', [(i, i ^ mask) for i in range(4)])]
    pallas_call x0 -> x18, Pallas kernels: none -> 23.2 us  [run(): pl.pallas_call(body, out_shape=tuple(outs), in_specs=[pl.BlockSpec(memory...]
    dot_general x13 -> x1, matrix products: 21.9 us -> 1.41 us  [dot(): return jnp.dot(left, right, preferred_element_type=F32)]
  transfers between devices with their start and end apart: 7 -> 53, of which waited for: 7 -> 42; matrix products, arithmetic and copies ran while one was open for 1% -> 6% of each run, Pallas kernels for 0% -> 3%
where the time goes in v1:
time: 211 us
  waiting for transfers between devices  104 us (49%)
  starting transfers between devices  63 us (30%)
  Pallas kernels  23.2 us (11%)
  local copies, waits for them, and re-layouts  13.1 us (6%)
  other arithmetic  5.15 us (2%)
    ppermute x32, waiting for transfers between devices, swap(): return lax.ppermute(block, PLANE, [(i, i ^ mask) for i in range(8)])  74.5 us
    ppermute x21, starting transfers between devices, pass_line(): return lax.ppermute(block, 'z', [(i, i ^ mask) for i in range(4)])  33.6 us
    ppermute x21, waiting for transfers between devices, pass_line(): return lax.ppermute(block, 'z', [(i, i ^ mask) for i in range(4)])  29.5 us
    ppermute x32, starting transfers between devices, swap(): return lax.ppermute(block, PLANE, [(i, i ^ mask) for i in range(8)])  29.4 us
    pallas_call x18, Pallas kernels, run(): pl.pallas_call(body, out_shape=tuple(outs), in_specs=[pl.BlockSpec(memory...  23.2 us
    unnamed x71, local copies, waits for them, and re-layouts  5.92 us
    sub x5, other arithmetic, adamw(): return (weight - rate * (scaled + DECAY * weight), first_new, second_new)  4.38 us
  transfers between devices with their start and end apart: 53, of which 42 were waited for; matrix products, arithmetic and copies ran while one was open for 6% of the time, Pallas kernels for 3%

profile of v1, /device:TPU:0, one launch (start us, length us, event | category | flops | bytes accessed | tf_op | source)
XLA Modules:
  0.0 211.1 jit_solution(14837567706227473846)
XLA Ops:
  2.1 3.1 %collective-permute-start = (bf16[128,256]{1,0:T(8,128)(2,1)S(1)}, bf16[128,256]{1,0:T(8,128)(2,1)S(1)}, u32[]{:S(2)}, u32[]{:S(2)}) collective-permute-start(bf16[128,256]{1,0:T(8,128)(2,1)S(1)} %get-tuple-element.141), channel_id=1, source_target_pairs={{0,8},{8,0},{16,24},{24,16},{1,9},{9,1},{17,25},{25,17},{2,10},{10... | collective-permute-start | bytes 196616 | tf_op jit(solution)/shard_map/ppermute | solution.py:76
  5.2 2.6 %collective-permute-start.1 = (bf16[128,256]{1,0:T(8,128)(2,1)S(1)}, bf16[128,256]{1,0:T(8,128)(2,1)S(1)}, u32[]{:S(2)}, u32[]{:S(2)}) collective-permute-start(bf16[128,256]{1,0:T(8,128)(2,1)S(1)} %get-tuple-element.141), channel_id=1, source_target_pairs={{0,16},{8,24},{16,0},{24,8},{1,17},{9,25},{17,1},{25,9},{2,18},{10... | collective-permute-start | bytes 196616 | tf_op jit(solution)/shard_map/ppermute | solution.py:76
  7.8 4.7 %collective-permute-done.1 = bf16[128,256]{1,0:T(8,128)(2,1)S(1)} collective-permute-done((bf16[128,256]{1,0:T(8,128)(2,1)S(1)}, bf16[128,256]{1,0:T(8,128)(2,1)S(1)}, u32[]{:S(2)}, u32[]{:S(2)}) %collective-permute-start.1) | collective-permute-done | bytes 65568 | tf_op jit(solution)/shard_map/ppermute | solution.py:76
  13.9 1.6 collective-permute-start.3
  15.4 1.5 collective-permute-start.4
  17.5 5.7 %collective-permute-done.3 = bf16[4,128,256]{2,1,0:T(8,128)(2,1)S(1)} collective-permute-done((bf16[4,128,256]{2,1,0:T(8,128)(2,1)S(1)}, bf16[4,128,256]{2,1,0:T(8,128)(2,1)S(1)}, u32[]{:S(2)}, u32[]{:S(2)}) %collective-permute-start.3) | collective-permute-done | bytes 262176 | tf_op jit(solution)/shard_map/ppermute | solution.py:72
  23.2 4.0 %collective-permute-done.4 = bf16[4,128,256]{2,1,0:T(8,128)(2,1)S(1)} collective-permute-done((bf16[4,128,256]{2,1,0:T(8,128)(2,1)S(1)}, bf16[4,128,256]{2,1,0:T(8,128)(2,1)S(1)}, u32[]{:S(2)}, u32[]{:S(2)}) %collective-permute-start.4) | collective-permute-done | bytes 262176 | tf_op jit(solution)/shard_map/ppermute | solution.py:72
  31.5 1.6 collective-permute-start.7
  33.1 1.8 collective-permute-start.8
  34.9 2.6 %collective-permute-done.9 = bf16[144,256]{1,0:T(8,128)(2,1)S(1)} collective-permute-done((bf16[144,256]{1,0:T(8,128)(2,1)S(1)}, bf16[144,256]{1,0:T(8,128)(2,1)S(1)}, u32[]{:S(2)}, u32[]{:S(2)}) %collective-permute-start.9) | collective-permute-done | bytes 73760 | tf_op jit(solution)/shard_map/ppermute | solution.py:76
  43.6 6.4 %collective-permute-done.10 = bf16[4,144,256]{2,1,0:T(8,128)(2,1)S(1)} collective-permute-done((bf16[4,144,256]{2,1,0:T(8,128)(2,1)S(1)}, bf16[4,144,256]{2,1,0:T(8,128)(2,1)S(1)}, u32[]{:S(2)}, u32[]{:S(2)}) %collective-permute-start.10) | collective-permute-done | bytes 294944 | tf_op jit(solution)/shard_map/ppermute | solution.py:72
  50.1 2.6 %collective-permute-done.11 = bf16[4,144,256]{2,1,0:T(8,128)(2,1)S(1)} collective-permute-done((bf16[4,144,256]{2,1,0:T(8,128)(2,1)S(1)}, bf16[4,144,256]{2,1,0:T(8,128)(2,1)S(1)}, u32[]{:S(2)}, u32[]{:S(2)}) %collective-permute-start.11) | collective-permute-done | bytes 294944 | tf_op jit(solution)/shard_map/ppermute | solution.py:72
  52.7 1.6 collective-permute-done.12
  54.5 2.8 %collective-permute-done.13.other_ref = bf16[16,144,256]{2,1,0:T(8,128)(2,1)S(1)} collective-permute-done((bf16[16,144,256]{2,1,0:T(8,128)(2,1)S(1)}, bf16[16,144,256]{2,1,0:T(8,128)(2,1)S(1)}, u32[]{:S(2)}, u32[]{:S(2)}) %collective-permute-start.13) | collective-permute-done | bytes 1179680 | tf_op jit(solution)/shard_map/ppermute | solution.py:72
  57.3 4.9 %shard_map.325 = (bf16[144,256]{1,0:T(8,128)(2,1)S(1)}, f32[8,256]{1,0:T(8,128)S(1)}) custom-call(bf16[128,2048]{1,0:T(8,128)(2,1)S(1)} %get-tuple-element.68.near_ref, bf16[128,2048]{1,0:T(8,128)(2,1)S(1)} %get-tuple-element.69.far_ref.refs_5_, bf16[256,256]{1,0:T(8,128)(2,1)S(1)} %convert_element_type.18.low_ref.refs_7_.refs_6_, ...), custom_call_target="tpu_custom_call" | custom-call | flops 805306368 | bytes 3629056 | tf_op jit(solution)/shard_map/pallas_call | solution.py:59
  62.2 1.6 collective-permute-start.14
  63.8 3.4 %collective-permute-start.15 = (bf16[144,256]{1,0:T(8,128)(2,1)S(1)}, bf16[144,256]{1,0:T(8,128)(2,1)S(1)}, u32[]{:S(2)}, u32[]{:S(2)}) collective-permute-start(bf16[144,256]{1,0:T(8,128)(2,1)S(1)} %get-tuple-element.70.refs_9_), channel_id=1, source_target_pairs={{0,16},{8,24},{16,0},{24,8},{1,17},{9,25},{17,1},{25,9},{2,18},{10... | collective-permute-start | bytes 221192 | tf_op jit(solution)/shard_map/ppermute | solution.py:76
  67.9 4.6 %collective-permute-done.15 = bf16[144,256]{1,0:T(8,128)(2,1)S(1)} collective-permute-done((bf16[144,256]{1,0:T(8,128)(2,1)S(1)}, bf16[144,256]{1,0:T(8,128)(2,1)S(1)}, u32[]{:S(2)}, u32[]{:S(2)}) %collective-permute-start.15) | collective-permute-done | bytes 73760 | tf_op jit(solution)/shard_map/ppermute | solution.py:76
  74.4 1.5 collective-permute-start.18
  79.0 4.6 %collective-permute-done.17 = bf16[4,144,256]{2,1,0:T(8,128)(2,1)S(1)} collective-permute-done((bf16[4,144,256]{2,1,0:T(8,128)(2,1)S(1)}, bf16[4,144,256]{2,1,0:T(8,128)(2,1)S(1)}, u32[]{:S(2)}, u32[]{:S(2)}) %collective-permute-start.17) | collective-permute-done | bytes 294944 | tf_op jit(solution)/shard_map/ppermute | solution.py:72
  84.3 3.4 %collective-permute-done.18 = bf16[4,144,256]{2,1,0:T(8,128)(2,1)S(1)} collective-permute-done((bf16[4,144,256]{2,1,0:T(8,128)(2,1)S(1)}, bf16[4,144,256]{2,1,0:T(8,128)(2,1)S(1)}, u32[]{:S(2)}, u32[]{:S(2)}) %collective-permute-start.18) | collective-permute-done | bytes 294944 | tf_op jit(solution)/shard_map/ppermute | solution.py:72
  97.3 8.2 %shard_map.326 = (bf16[64,2048]{1,0:T(8,128)(2,1)S(1)}, bf16[48,128]{1,0:T(8,128)(2,1)S(1)}, f32[16,128]{1,0:T(8,128)S(1)}, f32[8,256]{1,0:T(8,128)S(1)}) custom-call(bf16[128,2048]{1,0:T(8,128)(2,1)S(1)} %get-tuple-element.68.near_ref, bf16[128,2048]{1,0:T(8,128)(2,1)S(1)} %get-tuple-element.69.far_ref.refs_5_, bf16[256,128]{1,0:T(8,128)(2,1)S(1)} %pad.17.low_ref.refs_6_, ...), custom_call_target="tpu_custom_call" | custom-call | flops 1073741824 | bytes 3904000 | tf_op jit(solution)/shard_map/pallas_call | solution.py:59
  108.0 1.5 collective-permute-start.23
  112.3 2.4 %collective-permute-done.24.refs_2_ = bf16[64,512]{1,0:T(8,128)(2,1)S(1)} collective-permute-done((bf16[64,512]{1,0:T(8,128)(2,1)S(1)}, bf16[64,512]{1,0:T(8,128)(2,1)S(1)}, u32[]{:S(2)}, u32[]{:S(2)}) %collective-permute-start.24) | collective-permute-done | bytes 65568 | tf_op jit(solution)/shard_map/ppermute | solution.py:72
  114.8 2.6 %collective-permute-start.25 = (bf16[64,128]{1,0:T(8,128)(2,1)S(1)}, bf16[64,128]{1,0:T(8,128)(2,1)S(1)}, u32[]{:S(2)}, u32[]{:S(2)}) collective-permute-start(bf16[64,128]{1,0:T(8,128)(2,1)S(1)} %get-tuple-element.80), channel_id=1, source_target_pairs={{0,8},{8,0},{16,24},{24,16},{1,9},{9,1},{17,25},{25,17},{2,10},{10... | collective-permute-start | bytes 49160 | tf_op jit(solution)/shard_map/ppermute | solution.py:76
  117.9 1.9 collective-permute-start.27
  119.9 4.7 %shard_map.329.refs_11_ = f32[128,512]{1,0:T(8,128)S(1)} custom-call(bf16[128,2048]{1,0:T(8,128)(2,1)S(1)} %get-tuple-element.68.near_ref, bf16[128,2048]{1,0:T(8,128)(2,1)S(1)} %get-tuple-element.69.far_ref.refs_5_, f32[8,256]{1,0:T(8,128)S(1)} %pad.18.norm_ref.refs_8_.refs_7_, bf16[16,144,256]{2,1,0:T(8,128)(2,1)S(1)} %constant_dynamic-update-slice_fusion.7.half_ref, ...), custom_call_target="tpu_custom_call" | custom-call | flops 805306368 | bytes 3686400 | tf_op jit(solution)/shard_map/pallas_call | solution.py:59
  125.5 2.7 %collective-permute-done.28.got_ref = bf16[272,2048]{1,0:T(8,128)(2,1)S(1)} collective-permute-done((bf16[272,2048]{1,0:T(8,128)(2,1)S(1)}, bf16[272,2048]{1,0:T(8,128)(2,1)S(1)}, u32[]{:S(2)}, u32[]{:S(2)}) %collective-permute-start.28) | collective-permute-done | bytes 1114144 | tf_op jit(solution)/shard_map/ppermute | solution.py:72
  128.6 1.6 collective-permute-start.29
  130.7 1.5 collective-permute-start.31
  132.2 6.0 %collective-permute-done.29.refs_0_ = bf16[272,512]{1,0:T(8,128)(2,1)S(1)} collective-permute-done((bf16[272,512]{1,0:T(8,128)(2,1)S(1)}, bf16[272,512]{1,0:T(8,128)(2,1)S(1)}, u32[]{:S(2)}, u32[]{:S(2)}) %collective-permute-start.29) | collective-permute-done | bytes 278560 | tf_op jit(solution)/shard_map/ppermute | solution.py:72
  138.2 6.4 %collective-permute-done.30.refs_1_ = bf16[272,512]{1,0:T(8,128)(2,1)S(1)} collective-permute-done((bf16[272,512]{1,0:T(8,128)(2,1)S(1)}, bf16[272,512]{1,0:T(8,128)(2,1)S(1)}, u32[]{:S(2)}, u32[]{:S(2)}) %collective-permute-start.30) | collective-permute-done | bytes 278560 | tf_op jit(solution)/shard_map/ppermute | solution.py:72
  147.3 1.9 collective-permute-start.34
  149.3 3.2 %collective-permute-done.33.refs_2_ = bf16[272,128]{1,0:T(8,128)(2,1)S(1)} collective-permute-done((bf16[272,128]{1,0:T(8,128)(2,1)S(1)}, bf16[272,128]{1,0:T(8,128)(2,1)S(1)}, u32[]{:S(2)}, u32[]{:S(2)}) %collective-permute-start.33) | collective-permute-done | bytes 69664 | tf_op jit(solution)/shard_map/ppermute | solution.py:76
  154.3 2.6 %collective-permute-done.35.got_ref = bf16[256,2048]{1,0:T(8,128)(2,1)S(1)} collective-permute-done((bf16[256,2048]{1,0:T(8,128)(2,1)S(1)}, bf16[256,2048]{1,0:T(8,128)(2,1)S(1)}, u32[]{:S(2)}, u32[]{:S(2)}) %collective-permute-start.35) | collective-permute-done | bytes 1048608 | tf_op jit(solution)/shard_map/ppermute | solution.py:72
  159.3 1.6 collective-permute-start.38
  160.9 5.7 %collective-permute-done.36.refs_0_ = bf16[256,512]{1,0:T(8,128)(2,1)S(1)} collective-permute-done((bf16[256,512]{1,0:T(8,128)(2,1)S(1)}, bf16[256,512]{1,0:T(8,128)(2,1)S(1)}, u32[]{:S(2)}, u32[]{:S(2)}) %collective-permute-start.36) | collective-permute-done | bytes 262176 | tf_op jit(solution)/shard_map/ppermute | solution.py:72
  166.6 5.1 %collective-permute-done.37.refs_1_ = bf16[256,512]{1,0:T(8,128)(2,1)S(1)} collective-permute-done((bf16[256,512]{1,0:T(8,128)(2,1)S(1)}, bf16[256,512]{1,0:T(8,128)(2,1)S(1)}, u32[]{:S(2)}, u32[]{:S(2)}) %collective-permute-start.37) | collective-permute-done | bytes 262176 | tf_op jit(solution)/shard_map/ppermute | solution.py:72
  174.4 1.9 collective-permute-start.41
  176.4 3.2 %collective-permute-done.40.refs_2_ = bf16[256,128]{1,0:T(8,128)(2,1)S(1)} collective-permute-done((bf16[256,128]{1,0:T(8,128)(2,1)S(1)}, bf16[256,128]{1,0:T(8,128)(2,1)S(1)}, u32[]{:S(2)}, u32[]{:S(2)}) %collective-permute-start.40) | collective-permute-done | bytes 65568 | tf_op jit(solution)/shard_map/ppermute | solution.py:76
  181.2 1.5 collective-permute-done.42.got_ref
  182.7 1.5 collective-permute-start.43
  184.8 1.5 collective-permute-start.45
  187.1 2.2 %collective-permute-done.44.refs_1_ = bf16[128,256]{1,0:T(8,128)(2,1)S(1)} collective-permute-done((bf16[128,256]{1,0:T(8,128)(2,1)S(1)}, bf16[128,256]{1,0:T(8,128)(2,1)S(1)}, u32[]{:S(2)}, u32[]{:S(2)}) %collective-permute-start.44) | collective-permute-done | bytes 65568 | tf_op jit(solution)/shard_map/ppermute | solution.py:72
  192.5 1.9 collective-permute-start.48
  194.5 2.8 %collective-permute-done.47.refs_1_ = bf16[128,256]{1,0:T(8,128)(2,1)S(1)} collective-permute-done((bf16[128,256]{1,0:T(8,128)(2,1)S(1)}, bf16[128,256]{1,0:T(8,128)(2,1)S(1)}, u32[]{:S(2)}, u32[]{:S(2)}) %collective-permute-start.47) | collective-permute-done | bytes 65568 | tf_op jit(solution)/shard_map/ppermute | solution.py:76
  204.4 1.6 collective-permute-done.51
  207.8 1.5 multiply_subtract_fusion
  (172 shorter events, 63.8 us)
Async XLA Ops:
  2.1 5.7 %collective-permute-start = (bf16[128,256]{1,0:T(8,128)(2,1)S(1)}, bf16[128,256]{1,0:T(8,128)(2,1)S(1)}, u32[]{:S(2)}, u32[]{:S(2)}) collective-permute-start(bf16[128,256]{1,0:T(8,128)(2,1)S(1)} %get-tuple-element.141), channel_id=1, source_target_pairs={{0,8},{8,0},{16,24},{24,16},{1,9},{9,1},{17,25},{25,17},{2,10},{10... | collective-permute-start | bytes 196616 | tf_op jit(solution)/shard_map/ppermute | solution.py:76
  5.2 7.3 %collective-permute-start.1 = (bf16[128,256]{1,0:T(8,128)(2,1)S(1)}, bf16[128,256]{1,0:T(8,128)(2,1)S(1)}, u32[]{:S(2)}, u32[]{:S(2)}) collective-permute-start(bf16[128,256]{1,0:T(8,128)(2,1)S(1)} %get-tuple-element.141), channel_id=1, source_target_pairs={{0,16},{8,24},{16,0},{24,8},{1,17},{9,25},{17,1},{25,9},{2,18},{10... | collective-permute-start | bytes 196616 | tf_op jit(solution)/shard_map/ppermute | solution.py:76
  7.8 6.1 %collective-permute-start.2 = (bf16[128,256]{1,0:T(8,128)(2,1)S(1)}, bf16[128,256]{1,0:T(8,128)(2,1)S(1)}, u32[]{:S(2)}, u32[]{:S(2)}) collective-permute-start(bf16[128,256]{1,0:T(8,128)(2,1)S(1)} %get-tuple-element.141), channel_id=1, source_target_pairs={{0,24},{8,16},{16,8},{24,0},{1,25},{9,17},{17,9},{25,1},{2,26},{10... | collective-permute-start | bytes 196616 | tf_op jit(solution)/shard_map/ppermute | solution.py:76
  13.9 9.3 %collective-permute-start.3 = (bf16[4,128,256]{2,1,0:T(8,128)(2,1)S(1)}, bf16[4,128,256]{2,1,0:T(8,128)(2,1)S(1)}, u32[]{:S(2)}, u32[]{:S(2)}) collective-permute-start(bf16[4,128,256]{2,1,0:T(8,128)(2,1)S(1)} %pad_maximum_fusion.2), channel_id=1, source_target_pairs={{0,2},{1,3},{2,0},{3,1},{4,6},{5,7},{6,4},{7,5},{8,10},{9,11},{10,... | collective-permute-start | bytes 786440 | tf_op jit(solution)/shard_map/ppermute | solution.py:72
  15.4 11.8 %collective-permute-start.4 = (bf16[4,128,256]{2,1,0:T(8,128)(2,1)S(1)}, bf16[4,128,256]{2,1,0:T(8,128)(2,1)S(1)}, u32[]{:S(2)}, u32[]{:S(2)}) collective-permute-start(bf16[4,128,256]{2,1,0:T(8,128)(2,1)S(1)} %pad_maximum_fusion.2), channel_id=1, source_target_pairs={{0,4},{1,5},{2,6},{3,7},{4,0},{5,1},{6,2},{7,3},{8,12},{9,13},{10,... | collective-permute-start | bytes 786440 | tf_op jit(solution)/shard_map/ppermute | solution.py:72
  16.9 10.3 %collective-permute-start.5 = (bf16[4,128,256]{2,1,0:T(8,128)(2,1)S(1)}, bf16[4,128,256]{2,1,0:T(8,128)(2,1)S(1)}, u32[]{:S(2)}, u32[]{:S(2)}) collective-permute-start(bf16[4,128,256]{2,1,0:T(8,128)(2,1)S(1)} %pad_maximum_fusion.2), channel_id=1, source_target_pairs={{0,6},{1,7},{2,4},{3,5},{4,2},{5,3},{6,0},{7,1},{8,14},{9,15},{10,... | collective-permute-start | bytes 786440 | tf_op jit(solution)/shard_map/ppermute | solution.py:72
  30.5 7.0 %collective-permute-start.9 = (bf16[144,256]{1,0:T(8,128)(2,1)S(1)}, bf16[144,256]{1,0:T(8,128)(2,1)S(1)}, u32[]{:S(2)}, u32[]{:S(2)}) collective-permute-start(bf16[144,256]{1,0:T(8,128)(2,1)S(1)} %shard_map.324.refs_8_), channel_id=1, source_target_pairs={{0,24},{8,16},{16,8},{24,0},{1,25},{9,17},{17,9},{25,1},{2,26},{10... | collective-permute-start | bytes 221192 | tf_op jit(solution)/shard_map/ppermute | solution.py:76
  31.5 7.1 %collective-permute-start.7 = (bf16[144,256]{1,0:T(8,128)(2,1)S(1)}, bf16[144,256]{1,0:T(8,128)(2,1)S(1)}, u32[]{:S(2)}, u32[]{:S(2)}) collective-permute-start(bf16[144,256]{1,0:T(8,128)(2,1)S(1)} %shard_map.324.refs_8_), channel_id=1, source_target_pairs={{0,8},{8,0},{16,24},{24,16},{1,9},{9,1},{17,25},{25,17},{2,10},{10... | collective-permute-start | bytes 221192 | tf_op jit(solution)/shard_map/ppermute | solution.py:76
  33.1 6.9 %collective-permute-start.8 = (bf16[144,256]{1,0:T(8,128)(2,1)S(1)}, bf16[144,256]{1,0:T(8,128)(2,1)S(1)}, u32[]{:S(2)}, u32[]{:S(2)}) collective-permute-start(bf16[144,256]{1,0:T(8,128)(2,1)S(1)} %shard_map.324.refs_8_), channel_id=1, source_target_pairs={{0,16},{8,24},{16,0},{24,8},{1,17},{9,25},{17,1},{25,9},{2,18},{10... | collective-permute-start | bytes 221192 | tf_op jit(solution)/shard_map/ppermute | solution.py:76
  40.0 10.0 %collective-permute-start.10 = (bf16[4,144,256]{2,1,0:T(8,128)(2,1)S(1)}, bf16[4,144,256]{2,1,0:T(8,128)(2,1)S(1)}, u32[]{:S(2)}, u32[]{:S(2)}) collective-permute-start(bf16[4,144,256]{2,1,0:T(8,128)(2,1)S(1)} %pad_maximum_fusion), channel_id=1, source_target_pairs={{0,2},{1,3},{2,0},{3,1},{4,6},{5,7},{6,4},{7,5},{8,10},{9,11},{10,... | collective-permute-start | bytes 884744 | tf_op jit(solution)/shard_map/ppermute | solution.py:72
  41.3 11.4 %collective-permute-start.11 = (bf16[4,144,256]{2,1,0:T(8,128)(2,1)S(1)}, bf16[4,144,256]{2,1,0:T(8,128)(2,1)S(1)}, u32[]{:S(2)}, u32[]{:S(2)}) collective-permute-start(bf16[4,144,256]{2,1,0:T(8,128)(2,1)S(1)} %pad_maximum_fusion), channel_id=1, source_target_pairs={{0,4},{1,5},{2,6},{3,7},{4,0},{5,1},{6,2},{7,3},{8,12},{9,13},{10,... | collective-permute-start | bytes 884744 | tf_op jit(solution)/shard_map/ppermute | solution.py:72
  42.2 12.2 %collective-permute-start.12 = (bf16[4,144,256]{2,1,0:T(8,128)(2,1)S(1)}, bf16[4,144,256]{2,1,0:T(8,128)(2,1)S(1)}, u32[]{:S(2)}, u32[]{:S(2)}) collective-permute-start(bf16[4,144,256]{2,1,0:T(8,128)(2,1)S(1)} %pad_maximum_fusion), channel_id=1, source_target_pairs={{0,6},{1,7},{2,4},{3,5},{4,2},{5,3},{6,0},{7,1},{8,14},{9,15},{10,... | collective-permute-start | bytes 884744 | tf_op jit(solution)/shard_map/ppermute | solution.py:72
  54.4 2.9 %collective-permute-start.13 = (bf16[16,144,256]{2,1,0:T(8,128)(2,1)S(1)}, bf16[16,144,256]{2,1,0:T(8,128)(2,1)S(1)}, u32[]{:S(2)}, u32[]{:S(2)}) collective-permute-start(bf16[16,144,256]{2,1,0:T(8,128)(2,1)S(1)} %constant_dynamic-update-slice_fusion.7.half_ref), channel_id=1, source_target_pairs={{0,1},{1,0},{2,3},{3,2},{4,5},{5,4},{6,7},{7,6},{8,9},{9,8},{10,11... | collective-permute-start | bytes 3538952 | tf_op jit(solution)/shard_map/ppermute | solution.py:72
  62.2 5.6 %collective-permute-start.14 = (bf16[144,256]{1,0:T(8,128)(2,1)S(1)}, bf16[144,256]{1,0:T(8,128)(2,1)S(1)}, u32[]{:S(2)}, u32[]{:S(2)}) collective-permute-start(bf16[144,256]{1,0:T(8,128)(2,1)S(1)} %get-tuple-element.70.refs_9_), channel_id=1, source_target_pairs={{0,8},{8,0},{16,24},{24,16},{1,9},{9,1},{17,25},{25,17},{2,10},{10... | collective-permute-start | bytes 221192 | tf_op jit(solution)/shard_map/ppermute | solution.py:76
  63.8 8.6 %collective-permute-start.15 = (bf16[144,256]{1,0:T(8,128)(2,1)S(1)}, bf16[144,256]{1,0:T(8,128)(2,1)S(1)}, u32[]{:S(2)}, u32[]{:S(2)}) collective-permute-start(bf16[144,256]{1,0:T(8,128)(2,1)S(1)} %get-tuple-element.70.refs_9_), channel_id=1, source_target_pairs={{0,16},{8,24},{16,0},{24,8},{1,17},{9,25},{17,1},{25,9},{2,18},{10... | collective-permute-start | bytes 221192 | tf_op jit(solution)/shard_map/ppermute | solution.py:76
  67.2 6.3 %collective-permute-start.16 = (bf16[144,256]{1,0:T(8,128)(2,1)S(1)}, bf16[144,256]{1,0:T(8,128)(2,1)S(1)}, u32[]{:S(2)}, u32[]{:S(2)}) collective-permute-start(bf16[144,256]{1,0:T(8,128)(2,1)S(1)} %get-tuple-element.70.refs_9_), channel_id=1, source_target_pairs={{0,24},{8,16},{16,8},{24,0},{1,25},{9,17},{17,9},{25,1},{2,26},{10... | collective-permute-start | bytes 221192 | tf_op jit(solution)/shard_map/ppermute | solution.py:76
  73.5 10.0 %collective-permute-start.17 = (bf16[4,144,256]{2,1,0:T(8,128)(2,1)S(1)}, bf16[4,144,256]{2,1,0:T(8,128)(2,1)S(1)}, u32[]{:S(2)}, u32[]{:S(2)}) collective-permute-start(bf16[4,144,256]{2,1,0:T(8,128)(2,1)S(1)} %pad_maximum_fusion.1), channel_id=1, source_target_pairs={{0,2},{1,3},{2,0},{3,1},{4,6},{5,7},{6,4},{7,5},{8,10},{9,11},{10,... | collective-permute-start | bytes 884744 | tf_op jit(solution)/shard_map/ppermute | solution.py:72
  74.4 13.3 %collective-permute-start.18 = (bf16[4,144,256]{2,1,0:T(8,128)(2,1)S(1)}, bf16[4,144,256]{2,1,0:T(8,128)(2,1)S(1)}, u32[]{:S(2)}, u32[]{:S(2)}) collective-permute-start(bf16[4,144,256]{2,1,0:T(8,128)(2,1)S(1)} %pad_maximum_fusion.1), channel_id=1, source_target_pairs={{0,4},{1,5},{2,6},{3,7},{4,0},{5,1},{6,2},{7,3},{8,12},{9,13},{10,... | collective-permute-start | bytes 884744 | tf_op jit(solution)/shard_map/ppermute | solution.py:72
  76.0 12.5 %collective-permute-start.19 = (bf16[4,144,256]{2,1,0:T(8,128)(2,1)S(1)}, bf16[4,144,256]{2,1,0:T(8,128)(2,1)S(1)}, u32[]{:S(2)}, u32[]{:S(2)}) collective-permute-start(bf16[4,144,256]{2,1,0:T(8,128)(2,1)S(1)} %pad_maximum_fusion.1), channel_id=1, source_target_pairs={{0,6},{1,7},{2,4},{3,5},{4,2},{5,3},{6,0},{7,1},{8,14},{9,15},{10,... | collective-permute-start | bytes 884744 | tf_op jit(solution)/shard_map/ppermute | solution.py:72
  89.2 6.4 %collective-permute-start.20 = (bf16[16,144,256]{2,1,0:T(8,128)(2,1)}, bf16[16,144,256]{2,1,0:T(8,128)(2,1)}, u32[]{:S(2)}, u32[]{:S(2)}) collective-permute-start(bf16[16,144,256]{2,1,0:T(8,128)(2,1)} %constant_dynamic-update-slice_fusion.14.half_ref), channel_id=1, source_target_pairs={{0,1},{1,0},{2,3},{3,2},{4,5},{5,4},{6,7},{7,6},{8,9},{9,8},{10,11... | collective-permute-start | bytes 3538952 | tf_op jit(solution)/shard_map/ppermute | solution.py:72
  107.4 4.4 %collective-permute-start.22 = (bf16[64,512]{1,0:T(8,128)(2,1)S(1)}, bf16[64,512]{1,0:T(8,128)(2,1)S(1)}, u32[]{:S(2)}, u32[]{:S(2)}) collective-permute-start(bf16[64,512]{1,0:T(8,128)(2,1)S(1)} %get-tuple-element.75), channel_id=1, source_target_pairs={{0,2},{1,3},{2,0},{3,1},{4,6},{5,7},{6,4},{7,5},{8,10},{9,11},{10,... | collective-permute-start | bytes 196616 | tf_op jit(solution)/shard_map/ppermute | solution.py:72
  108.0 4.3 %collective-permute-start.23 = (bf16[64,512]{1,0:T(8,128)(2,1)S(1)}, bf16[64,512]{1,0:T(8,128)(2,1)S(1)}, u32[]{:S(2)}, u32[]{:S(2)}) collective-permute-start(bf16[64,512]{1,0:T(8,128)(2,1)S(1)} %get-tuple-element.76), channel_id=1, source_target_pairs={{0,4},{1,5},{2,6},{3,7},{4,0},{5,1},{6,2},{7,3},{8,12},{9,13},{10,... | collective-permute-start | bytes 196616 | tf_op jit(solution)/shard_map/ppermute | solution.py:72
  109.6 5.2 %collective-permute-start.24 = (bf16[64,512]{1,0:T(8,128)(2,1)S(1)}, bf16[64,512]{1,0:T(8,128)(2,1)S(1)}, u32[]{:S(2)}, u32[]{:S(2)}) collective-permute-start(bf16[64,512]{1,0:T(8,128)(2,1)S(1)} %get-tuple-element.77), channel_id=1, source_target_pairs={{0,6},{1,7},{2,4},{3,5},{4,2},{5,3},{6,0},{7,1},{8,14},{9,15},{10,... | collective-permute-start | bytes 196616 | tf_op jit(solution)/shard_map/ppermute | solution.py:72
  114.8 9.8 %collective-permute-start.25 = (bf16[64,128]{1,0:T(8,128)(2,1)S(1)}, bf16[64,128]{1,0:T(8,128)(2,1)S(1)}, u32[]{:S(2)}, u32[]{:S(2)}) collective-permute-start(bf16[64,128]{1,0:T(8,128)(2,1)S(1)} %get-tuple-element.80), channel_id=1, source_target_pairs={{0,8},{8,0},{16,24},{24,16},{1,9},{9,1},{17,25},{25,17},{2,10},{10... | collective-permute-start | bytes 49160 | tf_op jit(solution)/shard_map/ppermute | solution.py:76
  117.4 7.1 %collective-permute-start.26 = (bf16[64,128]{1,0:T(8,128)(2,1)S(1)}, bf16[64,128]{1,0:T(8,128)(2,1)S(1)}, u32[]{:S(2)}, u32[]{:S(2)}) collective-permute-start(bf16[64,128]{1,0:T(8,128)(2,1)S(1)} %get-tuple-element.81), channel_id=1, source_target_pairs={{0,16},{8,24},{16,0},{24,8},{1,17},{9,25},{17,1},{25,9},{2,18},{10... | collective-permute-start | bytes 49160 | tf_op jit(solution)/shard_map/ppermute | solution.py:76
  117.9 6.6 %collective-permute-start.27 = (bf16[64,128]{1,0:T(8,128)(2,1)S(1)}, bf16[64,128]{1,0:T(8,128)(2,1)S(1)}, u32[]{:S(2)}, u32[]{:S(2)}) collective-permute-start(bf16[64,128]{1,0:T(8,128)(2,1)S(1)} %get-tuple-element.82), channel_id=1, source_target_pairs={{0,24},{8,16},{16,8},{24,0},{1,25},{9,17},{17,9},{25,1},{2,26},{10... | collective-permute-start | bytes 49160 | tf_op jit(solution)/shard_map/ppermute | solution.py:76
  125.4 2.8 %collective-permute-start.28 = (bf16[272,2048]{1,0:T(8,128)(2,1)S(1)}, bf16[272,2048]{1,0:T(8,128)(2,1)S(1)}, u32[]{:S(2)}, u32[]{:S(2)}) collective-permute-start(bf16[272,2048]{1,0:T(8,128)(2,1)S(1)} %get-tuple-element.88), channel_id=1, source_target_pairs={{0,1},{1,0},{2,3},{3,2},{4,5},{5,4},{6,7},{7,6},{8,9},{9,8},{10,11... | collective-permute-start | bytes 3342344 | tf_op jit(solution)/shard_map/ppermute | solution.py:72
  128.6 9.6 %collective-permute-start.29 = (bf16[272,512]{1,0:T(8,128)(2,1)S(1)}, bf16[272,512]{1,0:T(8,128)(2,1)S(1)}, u32[]{:S(2)}, u32[]{:S(2)}) collective-permute-start(bf16[272,512]{1,0:T(8,128)(2,1)S(1)} %get-tuple-element.91), channel_id=1, source_target_pairs={{0,2},{1,3},{2,0},{3,1},{4,6},{5,7},{6,4},{7,5},{8,10},{9,11},{10,... | collective-permute-start | bytes 835592 | tf_op jit(solution)/shard_map/ppermute | solution.py:72
  130.2 14.4 %collective-permute-start.30 = (bf16[272,512]{1,0:T(8,128)(2,1)S(1)}, bf16[272,512]{1,0:T(8,128)(2,1)S(1)}, u32[]{:S(2)}, u32[]{:S(2)}) collective-permute-start(bf16[272,512]{1,0:T(8,128)(2,1)S(1)} %get-tuple-element.92), channel_id=1, source_target_pairs={{0,4},{1,5},{2,6},{3,7},{4,0},{5,1},{6,2},{7,3},{8,12},{9,13},{10,... | collective-permute-start | bytes 835592 | tf_op jit(solution)/shard_map/ppermute | solution.py:72
  130.7 13.9 %collective-permute-start.31 = (bf16[272,512]{1,0:T(8,128)(2,1)S(1)}, bf16[272,512]{1,0:T(8,128)(2,1)S(1)}, u32[]{:S(2)}, u32[]{:S(2)}) collective-permute-start(bf16[272,512]{1,0:T(8,128)(2,1)S(1)} %get-tuple-element.93), channel_id=1, source_target_pairs={{0,6},{1,7},{2,4},{3,5},{4,2},{5,3},{6,0},{7,1},{8,14},{9,15},{10,... | collective-permute-start | bytes 835592 | tf_op jit(solution)/shard_map/ppermute | solution.py:72
  144.7 4.6 %collective-permute-start.32 = (bf16[272,128]{1,0:T(8,128)(2,1)S(1)}, bf16[272,128]{1,0:T(8,128)(2,1)S(1)}, u32[]{:S(2)}, u32[]{:S(2)}) collective-permute-start(bf16[272,128]{1,0:T(8,128)(2,1)S(1)} %get-tuple-element.96), channel_id=1, source_target_pairs={{0,8},{8,0},{16,24},{24,16},{1,9},{9,1},{17,25},{25,17},{2,10},{10... | collective-permute-start | bytes 208904 | tf_op jit(solution)/shard_map/ppermute | solution.py:76
  145.9 6.7 %collective-permute-start.33 = (bf16[272,128]{1,0:T(8,128)(2,1)S(1)}, bf16[272,128]{1,0:T(8,128)(2,1)S(1)}, u32[]{:S(2)}, u32[]{:S(2)}) collective-permute-start(bf16[272,128]{1,0:T(8,128)(2,1)S(1)} %get-tuple-element.97), channel_id=1, source_target_pairs={{0,16},{8,24},{16,0},{24,8},{1,17},{9,25},{17,1},{25,9},{2,18},{10... | collective-permute-start | bytes 208904 | tf_op jit(solution)/shard_map/ppermute | solution.py:76
  147.3 6.2 %collective-permute-start.34 = (bf16[272,128]{1,0:T(8,128)(2,1)S(1)}, bf16[272,128]{1,0:T(8,128)(2,1)S(1)}, u32[]{:S(2)}, u32[]{:S(2)}) collective-permute-start(bf16[272,128]{1,0:T(8,128)(2,1)S(1)} %get-tuple-element.98), channel_id=1, source_target_pairs={{0,24},{8,16},{16,8},{24,0},{1,25},{9,17},{17,9},{25,1},{2,26},{10... | collective-permute-start | bytes 208904 | tf_op jit(solution)/shard_map/ppermute | solution.py:76
  157.4 9.2 %collective-permute-start.36 = (bf16[256,512]{1,0:T(8,128)(2,1)S(1)}, bf16[256,512]{1,0:T(8,128)(2,1)S(1)}, u32[]{:S(2)}, u32[]{:S(2)}) collective-permute-start(bf16[256,512]{1,0:T(8,128)(2,1)S(1)} %get-tuple-element.103), channel_id=1, source_target_pairs={{0,2},{1,3},{2,0},{3,1},{4,6},{5,7},{6,4},{7,5},{8,10},{9,11},{10,... | collective-permute-start | bytes 786440 | tf_op jit(solution)/shard_map/ppermute | solution.py:72
  158.0 13.7 %collective-permute-start.37 = (bf16[256,512]{1,0:T(8,128)(2,1)S(1)}, bf16[256,512]{1,0:T(8,128)(2,1)S(1)}, u32[]{:S(2)}, u32[]{:S(2)}) collective-permute-start(bf16[256,512]{1,0:T(8,128)(2,1)S(1)} %get-tuple-element.104), channel_id=1, source_target_pairs={{0,4},{1,5},{2,6},{3,7},{4,0},{5,1},{6,2},{7,3},{8,12},{9,13},{10,... | collective-permute-start | bytes 786440 | tf_op jit(solution)/shard_map/ppermute | solution.py:72
  159.3 12.4 %collective-permute-start.38 = (bf16[256,512]{1,0:T(8,128)(2,1)S(1)}, bf16[256,512]{1,0:T(8,128)(2,1)S(1)}, u32[]{:S(2)}, u32[]{:S(2)}) collective-permute-start(bf16[256,512]{1,0:T(8,128)(2,1)S(1)} %get-tuple-element.105), channel_id=1, source_target_pairs={{0,6},{1,7},{2,4},{3,5},{4,2},{5,3},{6,0},{7,1},{8,14},{9,15},{10,... | collective-permute-start | bytes 786440 | tf_op jit(solution)/shard_map/ppermute | solution.py:72
  171.9 4.6 %collective-permute-start.39 = (bf16[256,128]{1,0:T(8,128)(2,1)S(1)}, bf16[256,128]{1,0:T(8,128)(2,1)S(1)}, u32[]{:S(2)}, u32[]{:S(2)}) collective-permute-start(bf16[256,128]{1,0:T(8,128)(2,1)S(1)} %get-tuple-element.107), channel_id=1, source_target_pairs={{0,8},{8,0},{16,24},{24,16},{1,9},{9,1},{17,25},{25,17},{2,10},{10... | collective-permute-start | bytes 196616 | tf_op jit(solution)/shard_map/ppermute | solution.py:76
  173.1 6.5 %collective-permute-start.40 = (bf16[256,128]{1,0:T(8,128)(2,1)S(1)}, bf16[256,128]{1,0:T(8,128)(2,1)S(1)}, u32[]{:S(2)}, u32[]{:S(2)}) collective-permute-start(bf16[256,128]{1,0:T(8,128)(2,1)S(1)} %get-tuple-element.108), channel_id=1, source_target_pairs={{0,16},{8,24},{16,0},{24,8},{1,17},{9,25},{17,1},{25,9},{2,18},{10... | collective-permute-start | bytes 196616 | tf_op jit(solution)/shard_map/ppermute | solution.py:76
  174.4 6.2 %collective-permute-start.41 = (bf16[256,128]{1,0:T(8,128)(2,1)S(1)}, bf16[256,128]{1,0:T(8,128)(2,1)S(1)}, u32[]{:S(2)}, u32[]{:S(2)}) collective-permute-start(bf16[256,128]{1,0:T(8,128)(2,1)S(1)} %get-tuple-element.109), channel_id=1, source_target_pairs={{0,24},{8,16},{16,8},{24,0},{1,25},{9,17},{17,9},{25,1},{2,26},{10... | collective-permute-start | bytes 196616 | tf_op jit(solution)/shard_map/ppermute | solution.py:76
  182.7 4.3 %collective-permute-start.43 = (bf16[128,256]{1,0:T(8,128)(2,1)S(1)}, bf16[128,256]{1,0:T(8,128)(2,1)S(1)}, u32[]{:S(2)}, u32[]{:S(2)}) collective-permute-start(bf16[128,256]{1,0:T(8,128)(2,1)S(1)} %get-tuple-element.115), channel_id=1, source_target_pairs={{0,2},{1,3},{2,0},{3,1},{4,6},{5,7},{6,4},{7,5},{8,10},{9,11},{10,... | collective-permute-start | bytes 196616 | tf_op jit(solution)/shard_map/ppermute | solution.py:72
  184.3 5.0 %collective-permute-start.44 = (bf16[128,256]{1,0:T(8,128)(2,1)S(1)}, bf16[128,256]{1,0:T(8,128)(2,1)S(1)}, u32[]{:S(2)}, u32[]{:S(2)}) collective-permute-start(bf16[128,256]{1,0:T(8,128)(2,1)S(1)} %get-tuple-element.116), channel_id=1, source_target_pairs={{0,4},{1,5},{2,6},{3,7},{4,0},{5,1},{6,2},{7,3},{8,12},{9,13},{10,... | collective-permute-start | bytes 196616 | tf_op jit(solution)/shard_map/ppermute | solution.py:72
  184.8 5.2 %collective-permute-start.45 = (bf16[128,256]{1,0:T(8,128)(2,1)S(1)}, bf16[128,256]{1,0:T(8,128)(2,1)S(1)}, u32[]{:S(2)}, u32[]{:S(2)}) collective-permute-start(bf16[128,256]{1,0:T(8,128)(2,1)S(1)} %get-tuple-element.117), channel_id=1, source_target_pairs={{0,6},{1,7},{2,4},{3,5},{4,2},{5,3},{6,0},{7,1},{8,14},{9,15},{10,... | collective-permute-start | bytes 196616 | tf_op jit(solution)/shard_map/ppermute | solution.py:72
  190.0 4.5 %collective-permute-start.46 = (bf16[128,256]{1,0:T(8,128)(2,1)S(1)}, bf16[128,256]{1,0:T(8,128)(2,1)S(1)}, u32[]{:S(2)}, u32[]{:S(2)}) collective-permute-start(bf16[128,256]{1,0:T(8,128)(2,1)S(1)} %shard_map.338.own_ref), channel_id=1, source_target_pairs={{0,8},{8,0},{16,24},{24,16},{1,9},{9,1},{17,25},{25,17},{2,10},{10... | collective-permute-start | bytes 196616 | tf_op jit(solution)/shard_map/ppermute | solution.py:76
  191.0 6.2 %collective-permute-start.47 = (bf16[128,256]{1,0:T(8,128)(2,1)S(1)}, bf16[128,256]{1,0:T(8,128)(2,1)S(1)}, u32[]{:S(2)}, u32[]{:S(2)}) collective-permute-start(bf16[128,256]{1,0:T(8,128)(2,1)S(1)} %shard_map.338.own_ref), channel_id=1, source_target_pairs={{0,16},{8,24},{16,0},{24,8},{1,17},{9,25},{17,1},{25,9},{2,18},{10... | collective-permute-start | bytes 196616 | tf_op jit(solution)/shard_map/ppermute | solution.py:76
  192.5 6.2 %collective-permute-start.48 = (bf16[128,256]{1,0:T(8,128)(2,1)S(1)}, bf16[128,256]{1,0:T(8,128)(2,1)S(1)}, u32[]{:S(2)}, u32[]{:S(2)}) collective-permute-start(bf16[128,256]{1,0:T(8,128)(2,1)S(1)} %shard_map.338.own_ref), channel_id=1, source_target_pairs={{0,24},{8,16},{16,8},{24,0},{1,25},{9,17},{17,9},{25,1},{2,26},{10... | collective-permute-start | bytes 196616 | tf_op jit(solution)/shard_map/ppermute | solution.py:76
  198.7 4.3 %collective-permute-start.49 = (bf16[128,256]{1,0:T(8,128)(2,1)S(1)}, bf16[128,256]{1,0:T(8,128)(2,1)S(1)}, u32[]{:S(2)}, u32[]{:S(2)}) collective-permute-start(bf16[128,256]{1,0:T(8,128)(2,1)S(1)} %shard_map.339), channel_id=1, source_target_pairs={{0,2},{1,3},{2,0},{3,1},{4,6},{5,7},{6,4},{7,5},{8,10},{9,11},{10,... | collective-permute-start | bytes 196616 | tf_op jit(solution)/shard_map/ppermute | solution.py:72
  200.1 4.3 %collective-permute-start.50 = (bf16[128,256]{1,0:T(8,128)(2,1)S(1)}, bf16[128,256]{1,0:T(8,128)(2,1)S(1)}, u32[]{:S(2)}, u32[]{:S(2)}) collective-permute-start(bf16[128,256]{1,0:T(8,128)(2,1)S(1)} %shard_map.339), channel_id=1, source_target_pairs={{0,4},{1,5},{2,6},{3,7},{4,0},{5,1},{6,2},{7,3},{8,12},{9,13},{10,... | collective-permute-start | bytes 196616 | tf_op jit(solution)/shard_map/ppermute | solution.py:72
  200.8 5.2 %collective-permute-start.51 = (bf16[128,256]{1,0:T(8,128)(2,1)S(1)}, bf16[128,256]{1,0:T(8,128)(2,1)S(1)}, u32[]{:S(2)}, u32[]{:S(2)}) collective-permute-start(bf16[128,256]{1,0:T(8,128)(2,1)S(1)} %shard_map.339), channel_id=1, source_target_pairs={{0,6},{1,7},{2,4},{3,5},{4,2},{5,3},{6,0},{7,1},{8,14},{9,15},{10,... | collective-permute-start | bytes 196616 | tf_op jit(solution)/shard_map/ppermute | solution.py:72
  (32 other events, 344.1 us)

commit v2 on v1

v2 whole, which is shorter than its diff:
```python
import functools
import math

import jax
import jax.numpy as jnp
from jax import lax
from jax.experimental import pallas as pl
from jax.experimental.pallas import tpu as pltpu
from jax.sharding import Mesh
from jax.sharding import PartitionSpec as P

TILE = 128
STEP = 10
EPS_NORM = 1e-05
EPS_ADAM = 1e-08
BETA_ONE = 0.9
BETA_TWO = 0.999
DECAY = 0.01
RATE_MATRIX = 0.03
RATE_SMALL = 0.3

BF = jnp.bfloat16
F32 = jnp.float32
PLANE = ("y", "x", "c")
EVERY = ("z", "y", "x", "c")
LANES = 128
HEAD_ROWS = 48
EXTRA = 16
ROOT = math.sqrt(2.0 / math.pi)
BEND = 0.044715


def adamw(weight, gradient, first, second, rate):
    first_new = BETA_ONE * first + (1.0 - BETA_ONE) * gradient
    second_new = BETA_TWO * second + (1.0 - BETA_TWO) * gradient * gradient
    scaled = (
        first_new
        / (1.0 - BETA_ONE**STEP)
        / (jnp.sqrt(second_new / (1.0 - BETA_TWO**STEP)) + EPS_ADAM)
    )
    return (weight - rate * (scaled + DECAY * weight), first_new, second_new)


def dot(left, right):
    return jnp.dot(left, right, preferred_element_type=F32)


def dot_turned(left, right):
    return lax.dot_general(left, right, (((1,), (1,)), ((), ())), preferred_element_type=F32)


def shape(dims, kind=F32):
    return jax.ShapeDtypeStruct(dims, kind)


def run(body, outs, ins, scratch=(), flops=0, scalars=0):
    held = sum(math.prod(a.shape[:-1]) * max(a.shape[-1], LANES) * a.dtype.itemsize for a in (*ins, *outs))
    limit = min(60 << 20, 2 * held + (8 << 20))
    return pl.pallas_call(
        body,
        out_shape=tuple(outs),
        in_specs=[pl.BlockSpec(memory_space=pltpu.SMEM)] * scalars
        + [pl.BlockSpec(memory_space=pltpu.VMEM)] * (len(ins) - scalars),
        out_specs=tuple(pl.BlockSpec(memory_space=pltpu.VMEM) for unused in outs),
        scratch_shapes=list(scratch),
        compiler_params=pltpu.CompilerParams(vmem_limit_bytes=limit),
        cost_estimate=pl.CostEstimate(flops=flops, bytes_accessed=held, transcendentals=0),
    )(*ins)


def swap(block, mask):
    return lax.ppermute(block, PLANE, [(i, i ^ mask) for i in range(8)])


def pass_line(block, mask):
    return lax.ppermute(block, "z", [(i, i ^ mask) for i in range(4)])


def short_line():
    return lax.axis_size("z") == 4


def after(block, *others):
    return lax.optimization_barrier((block, *others))[0]


def gather_all(block, beside=()):
    if short_line():
        line = jnp.stack([block] + [pass_line(block, k) for k in range(1, 4)])
    else:
        line = lax.all_gather(block, "z", axis=0)
    passed = [pass_line(after(part, line), mask) for part, mask in beside]
    lines = [line] + [swap(line, 2 * k) for k in range(1, 4)]
    if passed:
        held = lax.optimization_barrier((*lines, *passed))
        lines, passed = list(held[:4]), list(held[4:])
    return lines + [swap(line, 1) for line in lines], passed


def arrange_kernel(mask_ref, values_ref, near_ref, far_ref, *level_refs):
    half = near_ref.shape[1] // TILE
    lines = half // 4
    here = 4 * lax.axis_index("y") + 2 * lax.axis_index("x") + lax.axis_index("c")
    level = lax.axis_index("z") if short_line() else 0

    for core, out_ref in ((0, near_ref), (1, far_ref)):
        for place in range(4):

            def one(step, carry, core=core, place=place, out_ref=out_ref):
                source = jnp.bitwise_xor(step, level) * 8 + jnp.bitwise_xor(place * 2 + core, here)
                keep = mask_ref[0, source].astype(F32).astype(BF)
                block = values_ref[:, pl.ds(pl.multiple_of(source * TILE, TILE), TILE)] * keep
                at = pl.multiple_of((place * lines + step) * TILE, TILE)
                out_ref[:, pl.ds(at, TILE)] = block
                cols = slice((core * 4 + place) * TILE, (core * 4 + place + 1) * TILE)
                if len(level_refs) == 1:
                    level_refs[0][step, :, cols] = block
                else:
                    level_refs[step][:, cols] = block
                return carry

            if len(level_refs) == 1:
                lax.fori_loop(0, lines, one, 0)
            else:
                for step in range(lines):
                    one(step, 0)


def centre_into(out_ref, summed):
    rows = summed.shape[0]
    centre = (jnp.sum(summed, axis=0, keepdims=True) / rows).astype(BF).astype(F32)
    out_ref[:rows, :] = (summed - centre).astype(BF)
    out_ref[rows:, :] = jnp.broadcast_to(centre, (EXTRA, summed.shape[1])).astype(BF)


def moments(refs, node_total):
    count, tall, width = refs[0].shape
    rows = tall - EXTRA
    pivot = refs[0][0, rows:, :].astype(F32)[:1]
    zero = jnp.zeros((8, width), F32)
    sums = (zero, zero)
    for ref in refs:

        def one(i, carry, ref=ref):
            total, square = carry
            value = ref[i, :rows, :].astype(F32).reshape(rows // 8, 8, width)
            part = jnp.sum(value, axis=0)
            away = ref[i, rows:, :].astype(F32)[:1] - pivot
            each = away * (rows // 8)
            return (
                total + part + each,
                square + jnp.sum(value * value, axis=0) + away * (2.0 * part + each),
            )

        sums = lax.fori_loop(0, count, one, sums, unroll=4)
    shift = jnp.sum(sums[0], axis=0, keepdims=True) / node_total
    variance = jnp.sum(sums[1], axis=0, keepdims=True) / node_total - shift * shift
    return pivot + shift, lax.rsqrt(jnp.maximum(variance, 0.0) + EPS_NORM)


def gelu_half(value):
    square = value * value
    bend = jnp.tanh(value * (ROOT + (ROOT * BEND) * square))
    return 0.5 + 0.5 * bend, bend, square


def gelu_slope(value, half, bend, square):
    return half + (0.5 * value) * (1.0 - bend * bend) * (ROOT + (3 * ROOT * BEND) * square)


def blocks_of(ref, i, pair, rows):
    parts = [
        (ref[i * pair + j, :rows, :].astype(F32), ref[i * pair + j, rows:, :].astype(F32)[:1])
        for j in range(pair)
    ]
    return parts


def with_columns(refs, near_ref, far_ref, rows, pair, act, total):
    count = refs[0].shape[0]
    for n, ref in enumerate(refs):
        adjacent_ref = far_ref if n >= 4 else near_ref

        def one(i, total, ref=ref, adjacent_ref=adjacent_ref, at=n % 4 * count * rows):
            start = pl.multiple_of(at + i * (pair * rows), pair * rows)
            return act(
                blocks_of(ref, i, pair, rows), adjacent_ref[:, pl.ds(start, pair * rows)], total
            )

        total = lax.fori_loop(0, count // pair, one, total, unroll=2)
    return total


def split_sums(total):
    high = total.astype(BF).astype(F32)
    low = (total - high).astype(BF).astype(F32)
    return jnp.concatenate([high, low])


def joined(parts):
    parts = parts.astype(F32)
    return parts[: EXTRA // 2] + parts[EXTRA // 2 :]


def put_sums(out_ref, width, parts):
    out_ref[width:, :LANES] = parts.astype(BF)
    if out_ref.shape[1] > LANES:
        out_ref[width:, LANES:] = jnp.zeros((EXTRA, out_ref.shape[1] - LANES), BF)


def pack_into(out_ref, turned, parts):
    width = turned.shape[0]
    out_ref[:width, :] = turned.astype(BF)
    if parts is not None:
        put_sums(out_ref, width, parts)


def add_up(values):
    values = list(values)
    while len(values) > 1:
        values = [values[i] + values[i + 1] for i in range(0, len(values), 2)]
    return values[0]


def cross(turned_refs, level_refs, start, stop, width, out):
    if len(level_refs) == 1:
        count = level_refs[0].shape[0]
        turned = [turned_refs[0].at[i] for i in range(count)]
        levels = [level_refs[0].at[i] for i in range(count)]
    else:
        turned, levels = turned_refs, level_refs
    total = None
    for i in range(0, len(levels), 2):
        left = jnp.concatenate([turned[i][:width, :], turned[i + 1][:width, :]], axis=1)
        right = jnp.concatenate([levels[i][:, start:stop], levels[i + 1][:, start:stop]])
        part = dot(left, right)
        total = part if total is None else total + part
    out(total)


def cross_kernel(width, count, *refs):
    turned_refs, level_refs, (send_ref,) = refs[:count], refs[count : 2 * count], refs[2 * count :]
    half = send_ref.shape[1]

    def out(value):
        send_ref[:width, :] = value.astype(BF)

    cross(turned_refs, level_refs, half, 2 * half, width, out)
    if send_ref.shape[0] > width:
        if count == 1:
            parts = [joined(turned_refs[0][i, width:, :]) for i in range(turned_refs[0].shape[0])]
        else:
            parts = [joined(ref[width:, :]) for ref in turned_refs]
        put_sums(send_ref, width, split_sums(add_up(parts)))


def keep_kernel(width, count, *refs):
    turned_refs, level_refs, (out_ref,) = refs[:count], refs[count : 2 * count], refs[2 * count :]

    def out(value):
        out_ref[...] = value

    cross(turned_refs, level_refs, 0, out_ref.shape[1], width, out)


def fold_kernel(kept_ref, send_ref, got_ref, own_ref, *piece_refs):
    width = kept_ref.shape[0]
    for k in range(4):
        cols = slice(k * LANES, (k + 1) * LANES)
        value = kept_ref[:, cols] + got_ref[:width, cols].astype(F32)
        if k == 0:
            own_ref[:width, :] = value
        else:
            piece_refs[k - 1][:width, :] = value.astype(BF)
    if own_ref.shape[0] > width:
        parts = split_sums(joined(send_ref[width:, :LANES]) + joined(got_ref[width:, :LANES]))
        own_ref[width:, :] = parts
        for piece_ref in piece_refs:
            put_sums(piece_ref, width, parts)


def spread_back(packed, levels, width):
    tall = packed.shape[0]
    if short_line():
        turned = [packed] + [pass_line(packed, k) for k in range(1, 4)]
    else:
        turned = [lax.all_gather(packed, "z", axis=0)]
    count = len(levels)
    half = levels[0].shape[-1] // 2
    work = 8 * width * LANES * half
    (send,) = run(
        functools.partial(cross_kernel, width, count),
        [shape((tall, half), BF)],
        [*turned, *levels],
        flops=work,
    )
    got = swap(send, 1)
    (kept,) = run(
        functools.partial(keep_kernel, width, count),
        [shape((width, half))],
        [*turned, *levels],
        flops=work,
    )
    own, *pieces = run(
        fold_kernel, [shape((tall, LANES))] + [shape((tall, LANES), BF)] * 3, [kept, send, got]
    )
    return [own] + [swap(pieces[k - 1], 2 * k) for k in range(1, 4)]


def line_total(refs, width):
    total = add_up(ref[:width, :].astype(F32) for ref in refs)
    if refs[0].shape[0] == width:
        return total, None
    return total, add_up(joined(ref[width:, :]) for ref in refs)


def wide(sums, row):
    return jnp.concatenate([sums[row : row + 1], sums[row + 1 : row + 2]], axis=1)


def put_wide(ref, row, value):
    ref[row : row + 1, :] = value[:, :LANES]
    ref[row + 1 : row + 2, :] = value[:, LANES:]


def layer_kernel(node_total, layer, near_ref, far_ref, weight_ref, norm_ref, *refs):
    refs, (out_ref, stats_ref) = refs[:8], refs[8:]
    count, tall, width = refs[0].shape
    rows = tall - EXTRA
    mean_value, inverse = moments(refs, node_total)
    stats_ref[0:1, :] = mean_value
    stats_ref[1:2, :] = inverse
    scale = norm_ref[2 * layer : 2 * layer + 1, :] * inverse
    start = norm_ref[2 * layer + 1 : 2 * layer + 2, :] - mean_value * scale
    low = weight_ref[...].astype(BF)

    def act(blocks, adjacent, total):
        hidden = []
        for value, centre in blocks:
            value = value * scale + (start + centre * scale)
            hidden.append((value * gelu_half(value)[0]).astype(BF))
        projected = dot(jnp.concatenate(hidden), low).astype(BF)
        return total + dot(adjacent, projected)

    total = jnp.zeros((rows, low.shape[1]), F32)
    centre_into(out_ref, with_columns(refs, near_ref, far_ref, rows, 2, act, total))


def slopes_kernel(layer, near_ref, far_ref, norm_ref, stats_ref, *refs):
    refs, out_ref = refs[:8], refs[8]
    count, tall, width = refs[0].shape
    rows = tall - EXTRA
    mean_value, inverse = stats_ref[0:1, :], stats_ref[1:2, :]
    gain = norm_ref[2 * layer : 2 * layer + 1, :]
    offset = norm_ref[2 * layer + 1 : 2 * layer + 2, :]
    out_ref[...] = jnp.zeros(out_ref.shape, F32)

    def act(blocks, adjacent, carry):
        slopes = []
        for value, centre in blocks:
            normed = value * inverse + (centre - mean_value) * inverse
            value = gain * normed + offset
            slope = gelu_slope(value, *gelu_half(value))
            slopes.append(jnp.concatenate([slope.astype(BF), (slope * normed).astype(BF)], axis=1))
        out_ref[...] += dot(adjacent, jnp.concatenate(slopes))
        return carry

    with_columns(refs, near_ref, far_ref, rows, 2, act, 0)


def head_low_of(weight_ref, tall_ref):
    tall_ref[...] = jnp.zeros(tall_ref.shape, F32)
    tall_ref[: weight_ref.shape[0], :] = weight_ref[...]
    return tall_ref[...].astype(BF)


def head_kernel(
    node_total, near_ref, far_ref, weight_ref, norm_ref, bias_ref, label_ref, mask_ref, *refs
):
    refs, (packed_ref, stats_ref, total_ref, sums_ref, tall_ref) = refs[:8], refs[8:]
    count, tall, width = refs[0].shape
    rows = tall - EXTRA
    classes = weight_ref.shape[0]
    mean_value, inverse = moments(refs, node_total)
    stats_ref[0:1, :] = mean_value
    stats_ref[1:2, :] = inverse
    gain, offset = norm_ref[2:3, :], norm_ref[3:4, :]
    low = head_low_of(weight_ref, tall_ref)
    total_ref[...] = jnp.zeros(total_ref.shape, F32)

    def act(blocks, adjacent, carry):
        hidden, slopes = [], []
        for value, centre in blocks:
            normed = value * inverse + (centre - mean_value) * inverse
            value = gain * normed + offset
            half, bend, square = gelu_half(value)
            slope = gelu_slope(value, half, bend, square)
            hidden.append((value * half).astype(BF))
            slopes.append(jnp.concatenate([slope.astype(BF), (slope * normed).astype(BF)], axis=1))
        headed = dot_turned(jnp.concatenate(hidden), low).astype(BF)
        both = jnp.concatenate([headed, jnp.concatenate(slopes)], axis=1)
        total_ref[...] += dot(adjacent, both)
        return carry

    with_columns(refs, near_ref, far_ref, rows, 2, act, 0)

    lane = lax.broadcasted_iota(jnp.int32, (rows, LANES), 1)
    sums_ref[...] = jnp.zeros(sums_ref.shape, F32)
    sums_ref[:1, :classes] = bias_ref[...]
    logits = jnp.where(lane < classes, total_ref[:, :LANES] + sums_ref[:1, :], -1e30)
    logits = logits - jnp.max(logits, axis=1, keepdims=True)
    raised = jnp.exp(logits)
    whole = jnp.sum(raised, axis=1, keepdims=True)
    label = jnp.broadcast_to(label_ref[...].astype(F32), (LANES, rows)).T
    onehot = jnp.where(lane.astype(F32) == label, 1.0, 0.0)
    weight = jnp.broadcast_to(mask_ref[...].astype(F32), (LANES, rows)).T
    losses = jnp.log(whole) - jnp.sum(onehot * logits, axis=1, keepdims=True)
    d_logits = (raised / whole - onehot) * weight
    d_low = d_logits.astype(BF)
    d_wide = dot(d_low, low)
    put_wide(sums_ref, 0, jnp.sum(d_wide * total_ref[:, LANES : LANES + width], axis=0, keepdims=True))
    put_wide(sums_ref, 2, jnp.sum(d_wide * total_ref[:, LANES + width :], axis=0, keepdims=True))
    sums_ref[4:5, :] = jnp.sum(d_logits, axis=0, keepdims=True)
    sums_ref[5:6, :] = jnp.sum(
        jnp.where(lane == 0, losses * weight, weight), axis=0, keepdims=True
    )
    pack_into(packed_ref, d_logits.T[:HEAD_ROWS], split_sums(sums_ref[...]))


def backward_norm(d_hidden, own_ref, stats_ref, norm_ref, layer, shift_grad, gain_grad, node_total):
    rows = own_ref.shape[0] - EXTRA
    mean_value, inverse = stats_ref[0:1, :], stats_ref[1:2, :]
    gain = norm_ref[2 * layer : 2 * layer + 1, :]
    centre = own_ref[rows:, :].astype(F32)[:1]
    normed = own_ref[:rows, :].astype(F32) * inverse + (centre - mean_value) * inverse
    value = gain * normed + norm_ref[2 * layer + 1 : 2 * layer + 2, :]
    half, bend, square = gelu_half(value)
    d_pre = d_hidden * gelu_slope(value, half, bend, square)
    d_summed = (gain * inverse) * (d_pre - (shift_grad + normed * gain_grad) / node_total)
    return d_summed, value * half


def second_kernel(
    node_total,
    head_ref,
    weight_ref,
    norm_ref,
    summed_ref,
    stats_ref,
    slopes_ref,
    *refs,
):
    refs, (packed_ref, grad_ref, out_ref, sums_ref, tall_ref) = refs[:4], refs[4:]
    headed, sums = line_total(refs, HEAD_ROWS)
    rows = headed.shape[1]
    each = 1.0 / sums[5:6, 1:2]
    headed = headed * each
    put_row = lax.broadcasted_iota(jnp.int32, sums.shape, 0)
    out_ref[...] = jnp.where(put_row == 5, sums, sums * each)
    turned_back = jnp.concatenate([headed, jnp.zeros((LANES - HEAD_ROWS, rows), F32)]).T
    d_hidden = dot(turned_back.astype(BF), head_low_of(head_ref, tall_ref))
    d_summed, hidden = backward_norm(
        d_hidden, summed_ref, stats_ref, norm_ref, 1, wide(sums, 0) * each, wide(sums, 2) * each, node_total
    )
    grad_ref[...] = dot(headed.astype(BF), hidden.astype(BF))
    d_wide = dot_turned(d_summed.astype(BF), weight_ref[...].astype(BF))
    width = d_wide.shape[1]
    put_wide(sums_ref, 0, jnp.sum(d_wide * slopes_ref[:, :width], axis=0, keepdims=True))
    put_wide(sums_ref, 2, jnp.sum(d_wide * slopes_ref[:, width:], axis=0, keepdims=True))
    sums_ref[4:8, :] = jnp.zeros((4, LANES), F32)
    pack_into(packed_ref, d_summed.T, split_sums(sums_ref[...]))


def first_kernel(node_total, weight_ref, norm_ref, summed_ref, stats_ref, *refs):
    refs, (packed_ref, grad_ref, out_ref) = refs[:4], refs[4:]
    d_projected, sums = line_total(refs, weight_ref.shape[1])
    out_ref[...] = sums
    d_projected = d_projected.T.astype(BF)
    d_hidden = dot_turned(d_projected, weight_ref[...].astype(BF))
    d_summed, hidden = backward_norm(
        d_hidden, summed_ref, stats_ref, norm_ref, 0, wide(sums, 0), wide(sums, 2), node_total
    )
    pack_into(packed_ref, d_summed.T, None)
    grad_ref[...] = dot(hidden.T.astype(BF), d_projected)


def pile_kernel(inputs_tall, inputs_ref, second_ref, head_ref, *refs):
    refs, (away_ref, kept_ref, pile_ref) = refs[:4], refs[4:]
    d_projected = line_total(refs, second_ref.shape[0])[0].T.astype(BF)
    pile_ref[...] = jnp.zeros(pile_ref.shape, F32)
    pile_ref[: inputs_ref.shape[0], :] = dot(inputs_ref[...], d_projected)
    at = inputs_tall
    pile_ref[at : at + second_ref.shape[0], :] = second_ref[...]
    at += second_ref.shape[0]
    pile_ref[at : at + HEAD_ROWS, :] = head_ref[...]
    half = away_ref.shape[0]
    core = lax.axis_index("c")
    away_ref[...] = pile_ref[pl.ds(pl.multiple_of((1 - core) * half, half), half), :].astype(BF)
    kept_ref[...] = pile_ref[pl.ds(pl.multiple_of(core * half, half), half), :]


def pile_core_kernel(kept_ref, got_ref, own_ref, *piece_refs):
    size = own_ref.shape[0]
    here = 2 * lax.axis_index("y") + lax.axis_index("x")
    for k in range(4):
        at = pl.ds(pl.multiple_of(jnp.bitwise_xor(here, k) * size, size), size)
        value = kept_ref[at, :] + got_ref[at, :].astype(F32)
        if k == 0:
            own_ref[...] = value
        else:
            piece_refs[k - 1][...] = value.astype(BF)


def pile_sum_kernel(own_ref, *refs):
    parts = [own_ref, *refs[:3]]
    refs[3][...] = add_up(ref[...].astype(F32) for ref in parts).astype(refs[3].dtype)


def update_kernel(inputs_tall, *refs):
    pieces, refs = refs[:8], refs[8:]
    inputs, outs, pile_ref = refs[:9], refs[9:18], refs[18]
    size, width = pieces[0].shape
    here = 2 * lax.axis_index("y") + lax.axis_index("x")
    core = lax.axis_index("c")
    for n, ref in enumerate(pieces):
        at = (jnp.bitwise_xor(core, n // 4) * 4 + jnp.bitwise_xor(here, n % 4)) * size
        pile_ref[pl.ds(pl.multiple_of(at, size), size), :] = ref[...].astype(F32)
    tall = inputs[0].shape[0]
    grads = (
        pile_ref[:tall, :],
        pile_ref[inputs_tall : inputs_tall + width, :],
        pile_ref[inputs_tall + width : inputs_tall + width + inputs[6].shape[0], :],
    )
    for n in range(3):
        weight, first, second = (ref[...] for ref in inputs[3 * n : 3 * n + 3])
        results = adamw(weight, grads[n], first, second, RATE_MATRIX)
        for ref, value in zip(outs[3 * n : 3 * n + 3], results, strict=True):
            ref[...] = value


def sum_pile(away, kept):
    size = away.shape[0] // 4
    width = away.shape[1]
    got = swap(away, 1)
    own, *pieces = run(
        pile_core_kernel, [shape((size, width))] + [shape((size, width), BF)] * 3, [kept, got]
    )
    got = [swap(pieces[k - 1], 2 * k) for k in range(1, 4)]
    if short_line():
        (shard,) = run(pile_sum_kernel, [shape((size, width), BF)], [own, *got])
        got = [pass_line(shard, k) for k in range(1, 4)]
        (shard,) = run(pile_sum_kernel, [shape((size, width), BF)], [shard, *got])
    else:
        (shard,) = run(pile_sum_kernel, [shape((size, width))], [own, *got])
        shard = lax.psum(shard, "z").astype(BF)
    pieces = [shard] + [swap(shard, 2 * k) for k in range(1, 4)]
    return pieces + [swap(piece, 1) for piece in pieces]


def first_sum_kernel(near_ref, far_ref, *refs):
    refs, out_ref = refs[:8], refs[8]
    count, rows, width = refs[0].shape
    total = jnp.zeros((rows, width), F32)
    for n, ref in enumerate(refs):
        adjacent_ref = far_ref if n >= 4 else near_ref
        at = n % 4 * count * rows
        total = total + dot(
            adjacent_ref[:, at : at + count * rows], ref[...].reshape(count * rows, width)
        )
    centre_into(out_ref, total)


def per_device(
    features,
    adjacency,
    tile_mask,
    labels,
    train_mask,
    w_first,
    w_second,
    w_head,
    norm_params,
    head_bias,
    m_first,
    m_second,
    m_head,
    m_norms,
    m_bias,
    v_first,
    v_second,
    v_head,
    v_norms,
    v_bias,
):
    rows, node_total = adjacency.shape
    inputs, hidden = w_first.shape
    classes = w_head.shape[1]
    half = node_total // 2
    length = lax.axis_size("z")
    tall = rows + EXTRA
    inputs_tall = -(-inputs // EXTRA) * EXTRA
    head_turned = w_head.T
    work = 2 * rows * node_total * hidden

    if short_line():
        level_shapes = [shape((rows, 8 * rows), BF)] * 4
    else:
        level_shapes = [shape((length, rows, 8 * rows), BF)]
    near, far, *levels = run(
        arrange_kernel,
        [shape((rows, half), BF)] * 2 + level_shapes,
        [tile_mask, adjacency],
        scalars=1,
    )

    projected = dot(features, w_first.astype(BF)).astype(BF)
    if short_line():
        around, passed = gather_all(projected, [(levels[1], 1), (levels[2], 2)])
        levels[1:3] = passed
    else:
        around, passed = gather_all(projected)
        levels = [lax.all_to_all(levels[0], "z", 0, 0)]
    (summed_one,) = run(
        first_sum_kernel, [shape((tall, hidden), BF)], [near, far, *around], flops=work
    )
    if short_line():
        around, passed = gather_all(summed_one, [(levels[3], 3)])
        levels[3:] = passed
    else:
        around, passed = gather_all(summed_one)
    summed_two, stats_one = run(
        functools.partial(layer_kernel, node_total, 0),
        [shape((tall, hidden), BF), shape((8, hidden))],
        [near, far, w_second, norm_params, *around],
        flops=3 * work,
    )
    (slopes_one,) = run(
        functools.partial(slopes_kernel, 0),
        [shape((rows, 2 * hidden))],
        [near, far, norm_params, stats_one, *around],
        flops=3 * work,
    )
    packed, stats_two = run(
        functools.partial(head_kernel, node_total),
        [shape((HEAD_ROWS + EXTRA, rows), BF), shape((8, hidden))],
        [
            near,
            far,
            head_turned,
            norm_params,
            head_bias[None],
            labels[None],
            train_mask[None],
            *gather_all(summed_two)[0],
        ],
        scratch=[
            pltpu.VMEM((rows, LANES + 2 * hidden), F32),
            pltpu.VMEM((8, LANES), F32),
            pltpu.VMEM((LANES, hidden), F32),
        ],
        flops=4 * work,
    )

    packed, head_grad, sums_two = run(
        functools.partial(second_kernel, node_total),
        [shape((hidden + EXTRA, rows), BF), shape((HEAD_ROWS, hidden)), shape((8, LANES))],
        [
            head_turned,
            w_second,
            norm_params,
            summed_two,
            stats_two,
            slopes_one,
            *spread_back(packed, levels, HEAD_ROWS),
        ],
        scratch=[pltpu.VMEM((8, LANES), F32), pltpu.VMEM((LANES, hidden), F32)],
        flops=work // 4,
    )
    packed, second_grad, sums_one = run(
        functools.partial(first_kernel, node_total),
        [shape((hidden, rows), BF), shape((hidden, hidden)), shape((8, LANES))],
        [w_second, norm_params, summed_one, stats_one, *spread_back(packed, levels, hidden)],
        flops=work // 4,
    )
    size = -(-(inputs_tall + hidden + HEAD_ROWS) // (8 * EXTRA)) * EXTRA
    away, kept = run(
        functools.partial(pile_kernel, inputs_tall),
        [shape((4 * size, hidden), BF), shape((4 * size, hidden))],
        [features.T, second_grad, head_grad, *spread_back(packed, levels, hidden)],
        scratch=[pltpu.VMEM((8 * size, hidden), F32)],
    )
    matrices = (
        *(w_first, m_first, v_first, w_second, m_second, v_second),
        *(head_turned, m_head.T, v_head.T),
    )
    updated = run(
        functools.partial(update_kernel, inputs_tall),
        [shape(block.shape) for block in matrices],
        [*sum_pile(away, kept), *matrices],
        scratch=[pltpu.VMEM((8 * size, hidden), F32)],
    )
    updated = [*updated[:6], *(block.T for block in updated[6:])]

    def pair(sums):
        return sums[2:4].reshape(1, hidden), sums[0:2].reshape(1, hidden)

    norm_grad = jnp.concatenate([*pair(sums_one), *pair(sums_two)])
    norms = adamw(norm_params, norm_grad, m_norms, v_norms, RATE_SMALL)
    bias = adamw(head_bias, sums_two[4, :classes], m_bias, v_bias, RATE_SMALL)
    loss_sum, train_count = sums_two[5, 0], sums_two[5, 1]
    return (
        loss_sum,
        train_count,
        *(
            part
            for n in range(3)
            for part in (updated[n], updated[3 + n], updated[6 + n], norms[n], bias[n])
        ),
    )


def solution(mesh):
    wide_mesh = Mesh(mesh.devices.reshape(-1, 2, 2, 2), EVERY)
    split = (P(EVERY, None),) * 3 + (P(EVERY),) * 2
    return jax.shard_map(
        per_device,
        mesh=wide_mesh,
        in_specs=split + (P(),) * 15,
        out_specs=(P(),) * 17,
        check_vma=False,
    )
```

time: 211 us -> 177 us (0.84)
  waiting for transfers between devices: 104 us -> 83.2 us
  local copies, waits for them, and re-layouts: 13.1 us -> 3.13 us
  starting transfers between devices: 63 us -> 68.9 us
  Pallas kernels: 23.2 us -> 18 us
  other arithmetic: 5.15 us -> 1.28 us
    ppermute x32 -> x44, waiting for transfers between devices: 74.5 us -> 48.2 us  [swap(): return lax.ppermute(block, PLANE, [(i, i ^ mask) for i in range(8)])]
    ppermute x21 -> x24, waiting for transfers between devices: 29.5 us -> 35 us  [pass_line(): return lax.ppermute(block, 'z', [(i, i ^ mask) for i in range(4)])]
    pallas_call x18 -> x21, Pallas kernels: 23.2 us -> 18 us  [run(): pl.pallas_call(body, out_shape=tuple(outs), in_specs=[pl.BlockSpec(memory...]
    ppermute x21 -> x24, starting transfers between devices: 33.6 us -> 37.7 us  [pass_line(): return lax.ppermute(block, 'z', [(i, i ^ mask) for i in range(4)])]
    broadcast_in_dim x3 -> x0, local copies, waits for them, and re-layouts: 3.44 us -> none  [the longest x1 1.39 us: per_device(): labels[:, None]]
    unnamed x71 -> x40, local copies, waits for them, and re-layouts: 5.92 us -> 2.54 us
    sub x5 -> x2, other arithmetic: 4.38 us -> 1.17 us  [adamw(): return (weight - rate * (scaled + DECAY * weight), first_new, second_new)]
    ppermute x32 -> x44, starting transfers between devices: 29.4 us -> 31.3 us  [swap(): return lax.ppermute(block, PLANE, [(i, i ^ mask) for i in range(8)])]
  transfers between devices with their start and end apart: 53 -> 68, of which waited for: 42 -> 49; matrix products, arithmetic and copies ran while one was open for 6% -> 1% of each run, Pallas kernels for 3% -> 3%
where the time goes in v2:
time: 177 us
  waiting for transfers between devices  83.2 us (47%)
  starting transfers between devices  68.9 us (39%)
  Pallas kernels  18 us (10%)
  local copies, waits for them, and re-layouts  3.13 us (2%)
    ppermute x44, waiting for transfers between devices, swap(): return lax.ppermute(block, PLANE, [(i, i ^ mask) for i in range(8)])  48.2 us
    ppermute x24, starting transfers between devices, pass_line(): return lax.ppermute(block, 'z', [(i, i ^ mask) for i in range(4)])  37.7 us
    ppermute x24, waiting for transfers between devices, pass_line(): return lax.ppermute(block, 'z', [(i, i ^ mask) for i in range(4)])  35 us
    ppermute x44, starting transfers between devices, swap(): return lax.ppermute(block, PLANE, [(i, i ^ mask) for i in range(8)])  31.3 us
    pallas_call x21, Pallas kernels, run(): pl.pallas_call(body, out_shape=tuple(outs), in_specs=[pl.BlockSpec(memory...  18 us
  transfers between devices with their start and end apart: 68, of which 49 were waited for; matrix products, arithmetic and copies ran while one was open for 1% of the time, Pallas kernels for 3%

profile of v2, /device:TPU:0, one launch (start us, length us, event | category | flops | bytes accessed | tf_op | source)
XLA Modules:
  0.0 176.9 jit_solution(7471358683436195615)
XLA Ops:
  2.1 5.1 %collective-permute-start.2 = (bf16[128,256]{1,0:T(8,128)(2,1)S(1)}, bf16[128,256]{1,0:T(8,128)(2,1)S(1)}, u32[]{:S(2)}, u32[]{:S(2)}) collective-permute-start(bf16[128,256]{1,0:T(8,128)(2,1)S(1)} %convolution_convert_fusion), channel_id=1, source_target_pairs={{0,24},{8,16},{16,8},{24,0},{1,25},{9,17},{17,9},{25,1},{2,26},{10... | collective-permute-start | bytes 196616 | tf_op jit(solution)/shard_map/ppermute | solution.py:76
  10.0 2.8 %collective-permute-done.1 = bf16[128,256]{1,0:T(8,128)(2,1)S(1)} collective-permute-done((bf16[128,256]{1,0:T(8,128)(2,1)S(1)}, bf16[128,256]{1,0:T(8,128)(2,1)S(1)}, u32[]{:S(2)}, u32[]{:S(2)}) %collective-permute-start.1) | collective-permute-done | bytes 65568 | tf_op jit(solution)/shard_map/ppermute | solution.py:76
  12.8 2.5 %collective-permute-start.5 = (bf16[4,128,256]{2,1,0:T(8,128)(2,1)S(1)}, bf16[4,128,256]{2,1,0:T(8,128)(2,1)S(1)}, u32[]{:S(2)}, u32[]{:S(2)}) collective-permute-start(bf16[4,128,256]{2,1,0:T(8,128)(2,1)S(1)} %pad_maximum_fusion.2.refs_0_), channel_id=1, source_target_pairs={{0,6},{1,7},{2,4},{3,5},{4,2},{5,3},{6,0},{7,1},{8,14},{9,15},{10,... | collective-permute-start | bytes 786440 | tf_op jit(solution)/shard_map/ppermute | solution.py:72
  16.4 1.6 collective-permute-start.7
  18.0 1.7 collective-permute-start.6
  19.7 3.4 %collective-permute-done.5.refs_3_ = bf16[4,128,256]{2,1,0:T(8,128)(2,1)S(1)} collective-permute-done((bf16[4,128,256]{2,1,0:T(8,128)(2,1)S(1)}, bf16[4,128,256]{2,1,0:T(8,128)(2,1)S(1)}, u32[]{:S(2)}, u32[]{:S(2)}) %collective-permute-start.5) | collective-permute-done | bytes 262176 | tf_op jit(solution)/shard_map/ppermute | solution.py:72
  23.1 4.2 %collective-permute-done.4.refs_2_ = bf16[4,128,256]{2,1,0:T(8,128)(2,1)S(1)} collective-permute-done((bf16[4,128,256]{2,1,0:T(8,128)(2,1)S(1)}, bf16[4,128,256]{2,1,0:T(8,128)(2,1)S(1)}, u32[]{:S(2)}, u32[]{:S(2)}) %collective-permute-start.4) | collective-permute-done | bytes 262176 | tf_op jit(solution)/shard_map/ppermute | solution.py:72
  27.6 2.0 %collective-permute-done.7.refs_6_ = bf16[128,1024]{1,0:T(8,128)(2,1)S(1)} collective-permute-done((bf16[128,1024]{1,0:T(8,128)(2,1)S(1)}, bf16[128,1024]{1,0:T(8,128)(2,1)S(1)}, u32[]{:S(2)}, u32[]{:S(2)}) %collective-permute-start.7) | collective-permute-done | bytes 262176 | tf_op jit(solution)/shard_map/ppermute | solution.py:76
  32.7 2.0 %collective-permute-start.14 = (bf16[144,256]{1,0:T(8,128)(2,1)S(1)}, bf16[144,256]{1,0:T(8,128)(2,1)S(1)}, u32[]{:S(2)}, u32[]{:S(2)}) collective-permute-start(bf16[144,256]{1,0:T(8,128)(2,1)S(1)} %shard_map.324.summed_ref), channel_id=1, source_target_pairs={{0,24},{8,16},{16,8},{24,0},{1,25},{9,17},{17,9},{25,1},{2,26},{10... | collective-permute-start | bytes 221192 | tf_op jit(solution)/shard_map/ppermute | solution.py:76
  34.7 2.5 %collective-permute-start.12 = (bf16[144,256]{1,0:T(8,128)(2,1)S(1)}, bf16[144,256]{1,0:T(8,128)(2,1)S(1)}, u32[]{:S(2)}, u32[]{:S(2)}) collective-permute-start(bf16[144,256]{1,0:T(8,128)(2,1)S(1)} %shard_map.324.summed_ref), channel_id=1, source_target_pairs={{0,8},{8,0},{16,24},{24,16},{1,9},{9,1},{17,25},{25,17},{2,10},{10... | collective-permute-start | bytes 221192 | tf_op jit(solution)/shard_map/ppermute | solution.py:76
  37.2 2.6 %collective-permute-done.14 = bf16[144,256]{1,0:T(8,128)(2,1)S(1)} collective-permute-done((bf16[144,256]{1,0:T(8,128)(2,1)S(1)}, bf16[144,256]{1,0:T(8,128)(2,1)S(1)}, u32[]{:S(2)}, u32[]{:S(2)}) %collective-permute-start.14) | collective-permute-done | bytes 73760 | tf_op jit(solution)/shard_map/ppermute | solution.py:76
  39.8 2.3 %collective-permute-done.13 = bf16[144,256]{1,0:T(8,128)(2,1)S(1)} collective-permute-done((bf16[144,256]{1,0:T(8,128)(2,1)S(1)}, bf16[144,256]{1,0:T(8,128)(2,1)S(1)}, u32[]{:S(2)}, u32[]{:S(2)}) %collective-permute-start.13) | collective-permute-done | bytes 73760 | tf_op jit(solution)/shard_map/ppermute | solution.py:76
  42.1 2.5 %collective-permute-start.17 = (bf16[4,144,256]{2,1,0:T(8,128)(2,1)S(1)}, bf16[4,144,256]{2,1,0:T(8,128)(2,1)S(1)}, u32[]{:S(2)}, u32[]{:S(2)}) collective-permute-start(bf16[4,144,256]{2,1,0:T(8,128)(2,1)S(1)} %pad_maximum_fusion.refs_0_), channel_id=1, source_target_pairs={{0,6},{1,7},{2,4},{3,5},{4,2},{5,3},{6,0},{7,1},{8,14},{9,15},{10,... | collective-permute-start | bytes 884744 | tf_op jit(solution)/shard_map/ppermute | solution.py:72
  45.7 1.9 %collective-permute-start.18 = (bf16[128,1024]{1,0:T(8,128)(2,1)S(1)}, bf16[128,1024]{1,0:T(8,128)(2,1)S(1)}, u32[]{:S(2)}, u32[]{:S(2)}) collective-permute-start(bf16[128,1024]{1,0:T(8,128)(2,1)S(1)} %get-tuple-element.85), channel_id=1, source_target_pairs={{0,24},{8,16},{16,8},{24,0},{1,25},{9,17},{17,9},{25,1},{2,26},{10... | collective-permute-start | bytes 786440 | tf_op jit(solution)/shard_map/ppermute | solution.py:76
  47.6 7.4 %collective-permute-done.18.refs_7_ = bf16[128,1024]{1,0:T(8,128)(2,1)S(1)} collective-permute-done((bf16[128,1024]{1,0:T(8,128)(2,1)S(1)}, bf16[128,1024]{1,0:T(8,128)(2,1)S(1)}, u32[]{:S(2)}, u32[]{:S(2)}) %collective-permute-start.18) | collective-permute-done | bytes 262176 | tf_op jit(solution)/shard_map/ppermute | solution.py:76
  55.0 3.4 %collective-permute-done.16.refs_2_ = bf16[4,144,256]{2,1,0:T(8,128)(2,1)S(1)} collective-permute-done((bf16[4,144,256]{2,1,0:T(8,128)(2,1)S(1)}, bf16[4,144,256]{2,1,0:T(8,128)(2,1)S(1)}, u32[]{:S(2)}, u32[]{:S(2)}) %collective-permute-start.16) | collective-permute-done | bytes 294944 | tf_op jit(solution)/shard_map/ppermute | solution.py:72
  61.3 2.6 %shard_map.325 = (bf16[144,256]{1,0:T(8,128)(2,1)S(1)}, f32[8,256]{1,0:T(8,128)S(1)}) custom-call(bf16[128,2048]{1,0:T(8,128)(2,1)S(1)} %get-tuple-element.74.near_ref, bf16[128,2048]{1,0:T(8,128)(2,1)S(1)} %get-tuple-element.75.far_ref, f32[256,256]{1,0:T(8,128)S(1)} %copy-done, f32[4,256]{1,0:T(4,128)S(1)} %copy-done.9, ...), custom_call_target="tpu_custom_call" | custom-call | flops 805306368 | bytes 3756032 | tf_op jit(solution)/shard_map/pallas_call | solution.py:59
  63.9 2.1 %collective-permute-start.25 = (bf16[144,256]{1,0:T(8,128)(2,1)S(1)}, bf16[144,256]{1,0:T(8,128)(2,1)S(1)}, u32[]{:S(2)}, u32[]{:S(2)}) collective-permute-start(bf16[144,256]{1,0:T(8,128)(2,1)S(1)} %get-tuple-element.90.summed_ref), channel_id=1, source_target_pairs={{0,24},{8,16},{16,8},{24,0},{1,25},{9,17},{17,9},{25,1},{2,26},{10... | collective-permute-start | bytes 221192 | tf_op jit(solution)/shard_map/ppermute | solution.py:76
  66.0 2.4 %collective-permute-start.23 = (bf16[144,256]{1,0:T(8,128)(2,1)S(1)}, bf16[144,256]{1,0:T(8,128)(2,1)S(1)}, u32[]{:S(2)}, u32[]{:S(2)}) collective-permute-start(bf16[144,256]{1,0:T(8,128)(2,1)S(1)} %get-tuple-element.90.summed_ref), channel_id=1, source_target_pairs={{0,8},{8,0},{16,24},{24,16},{1,9},{9,1},{17,25},{25,17},{2,10},{10... | collective-permute-start | bytes 221192 | tf_op jit(solution)/shard_map/ppermute | solution.py:76
  68.4 2.6 %collective-permute-done.25 = bf16[144,256]{1,0:T(8,128)(2,1)S(1)} collective-permute-done((bf16[144,256]{1,0:T(8,128)(2,1)S(1)}, bf16[144,256]{1,0:T(8,128)(2,1)S(1)}, u32[]{:S(2)}, u32[]{:S(2)}) %collective-permute-start.25) | collective-permute-done | bytes 73760 | tf_op jit(solution)/shard_map/ppermute | solution.py:76
  71.0 2.3 %collective-permute-done.24 = bf16[144,256]{1,0:T(8,128)(2,1)S(1)} collective-permute-done((bf16[144,256]{1,0:T(8,128)(2,1)S(1)}, bf16[144,256]{1,0:T(8,128)(2,1)S(1)}, u32[]{:S(2)}, u32[]{:S(2)}) %collective-permute-start.24) | collective-permute-done | bytes 73760 | tf_op jit(solution)/shard_map/ppermute | solution.py:76
  73.3 1.7 collective-permute-start.28
  76.9 7.3 %collective-permute-done.28.refs_3_ = bf16[4,144,256]{2,1,0:T(8,128)(2,1)S(1)} collective-permute-done((bf16[4,144,256]{2,1,0:T(8,128)(2,1)S(1)}, bf16[4,144,256]{2,1,0:T(8,128)(2,1)S(1)}, u32[]{:S(2)}, u32[]{:S(2)}) %collective-permute-start.28) | collective-permute-done | bytes 294944 | tf_op jit(solution)/shard_map/ppermute | solution.py:72
  84.2 5.3 %collective-permute-done.27.refs_2_ = bf16[4,144,256]{2,1,0:T(8,128)(2,1)S(1)} collective-permute-done((bf16[4,144,256]{2,1,0:T(8,128)(2,1)S(1)}, bf16[4,144,256]{2,1,0:T(8,128)(2,1)S(1)}, u32[]{:S(2)}, u32[]{:S(2)}) %collective-permute-start.27) | collective-permute-done | bytes 294944 | tf_op jit(solution)/shard_map/ppermute | solution.py:72
  92.2 4.9 %shard_map.326 = (bf16[64,128]{1,0:T(8,128)(2,1)S(1)}, f32[8,256]{1,0:T(8,128)S(1)}) custom-call(bf16[128,2048]{1,0:T(8,128)(2,1)S(1)} %get-tuple-element.74.near_ref, bf16[128,2048]{1,0:T(8,128)(2,1)S(1)} %get-tuple-element.75.far_ref, f32[41,256]{1,0:T(8,128)S(1)} %bitcast.39, f32[4,256]{1,0:T(4,128)S(1)} %copy-done.9, f32[1,41]{1,0:T(1,128)S(1)} %bitcast.44, ...), custom_call_target="tpu_custom_call" | custom-call | flops 1073741824 | bytes 3480064 | tf_op jit(solution)/shard_map/pallas_call | solution.py:59
  97.2 2.1 %collective-permute-start.35 = (bf16[64,128]{1,0:T(8,128)(2,1)S(1)}, bf16[64,128]{1,0:T(8,128)(2,1)S(1)}, u32[]{:S(2)}, u32[]{:S(2)}) collective-permute-start(bf16[64,128]{1,0:T(8,128)(2,1)S(1)} %get-tuple-element.93.refs_0_), channel_id=1, source_target_pairs={{0,24},{8,16},{16,8},{24,0},{1,25},{9,17},{17,9},{25,1},{2,26},{10... | collective-permute-start | bytes 49160 | tf_op jit(solution)/shard_map/ppermute | solution.py:76
  99.3 2.4 %collective-permute-start.33 = (bf16[64,128]{1,0:T(8,128)(2,1)S(1)}, bf16[64,128]{1,0:T(8,128)(2,1)S(1)}, u32[]{:S(2)}, u32[]{:S(2)}) collective-permute-start(bf16[64,128]{1,0:T(8,128)(2,1)S(1)} %get-tuple-element.93.refs_0_), channel_id=1, source_target_pairs={{0,8},{8,0},{16,24},{24,16},{1,9},{9,1},{17,25},{25,17},{2,10},{10... | collective-permute-start | bytes 49160 | tf_op jit(solution)/shard_map/ppermute | solution.py:76
  105.4 1.6 collective-permute-start.37
  109.0 3.5 %shard_map.327.slopes_ref = f32[128,512]{1,0:T(8,128)S(1)} custom-call(bf16[128,2048]{1,0:T(8,128)(2,1)S(1)} %get-tuple-element.74.near_ref, bf16[128,2048]{1,0:T(8,128)(2,1)S(1)} %get-tuple-element.75.far_ref, f32[4,256]{1,0:T(4,128)S(1)} %copy-done.9, f32[8,256]{1,0:T(8,128)S(1)} %get-tuple-element.92.stats_ref, ...), custom_call_target="tpu_custom_call" | custom-call | flops 805306368 | bytes 3682304 | tf_op jit(solution)/shard_map/pallas_call | solution.py:59
  113.0 1.9 %collective-permute-start.42 = (bf16[272,128]{1,0:T(8,128)(2,1)S(1)}, bf16[272,128]{1,0:T(8,128)(2,1)S(1)}, u32[]{:S(2)}, u32[]{:S(2)}) collective-permute-start(bf16[272,128]{1,0:T(8,128)(2,1)S(1)} %get-tuple-element.103.refs_0_), channel_id=1, source_target_pairs={{0,24},{8,16},{16,8},{24,0},{1,25},{9,17},{17,9},{25,1},{2,26},{10... | collective-permute-start | bytes 208904 | tf_op jit(solution)/shard_map/ppermute | solution.py:76
  116.0 1.5 collective-permute-start.40
  117.5 2.4 %collective-permute-done.42.refs_3_ = bf16[272,128]{1,0:T(8,128)(2,1)S(1)} collective-permute-done((bf16[272,128]{1,0:T(8,128)(2,1)S(1)}, bf16[272,128]{1,0:T(8,128)(2,1)S(1)}, u32[]{:S(2)}, u32[]{:S(2)}) %collective-permute-start.42) | collective-permute-done | bytes 69664 | tf_op jit(solution)/shard_map/ppermute | solution.py:76
  119.9 2.2 %collective-permute-done.41.refs_2_ = bf16[272,128]{1,0:T(8,128)(2,1)S(1)} collective-permute-done((bf16[272,128]{1,0:T(8,128)(2,1)S(1)}, bf16[272,128]{1,0:T(8,128)(2,1)S(1)}, u32[]{:S(2)}, u32[]{:S(2)}) %collective-permute-start.41) | collective-permute-done | bytes 69664 | tf_op jit(solution)/shard_map/ppermute | solution.py:76
  124.0 1.6 collective-permute-start.44
  128.4 2.2 %collective-permute-done.45.refs_2_ = bf16[272,128]{1,0:T(8,128)(2,1)S(1)} collective-permute-done((bf16[272,128]{1,0:T(8,128)(2,1)S(1)}, bf16[272,128]{1,0:T(8,128)(2,1)S(1)}, u32[]{:S(2)}, u32[]{:S(2)}) %collective-permute-start.45) | collective-permute-done | bytes 69664 | tf_op jit(solution)/shard_map/ppermute | solution.py:72
  131.7 2.0 %collective-permute-start.49 = (bf16[256,128]{1,0:T(8,128)(2,1)S(1)}, bf16[256,128]{1,0:T(8,128)(2,1)S(1)}, u32[]{:S(2)}, u32[]{:S(2)}) collective-permute-start(bf16[256,128]{1,0:T(8,128)(2,1)S(1)} %get-tuple-element.110.refs_0_), channel_id=1, source_target_pairs={{0,24},{8,16},{16,8},{24,0},{1,25},{9,17},{17,9},{25,1},{2,26},{10... | collective-permute-start | bytes 196616 | tf_op jit(solution)/shard_map/ppermute | solution.py:76
  133.7 2.5 %collective-permute-start.47 = (bf16[256,128]{1,0:T(8,128)(2,1)S(1)}, bf16[256,128]{1,0:T(8,128)(2,1)S(1)}, u32[]{:S(2)}, u32[]{:S(2)}) collective-permute-start(bf16[256,128]{1,0:T(8,128)(2,1)S(1)} %get-tuple-element.110.refs_0_), channel_id=1, source_target_pairs={{0,8},{8,0},{16,24},{24,16},{1,9},{9,1},{17,25},{25,17},{2,10},{10... | collective-permute-start | bytes 196616 | tf_op jit(solution)/shard_map/ppermute | solution.py:76
  136.2 1.9 %collective-permute-done.49.refs_3_ = bf16[256,128]{1,0:T(8,128)(2,1)S(1)} collective-permute-done((bf16[256,128]{1,0:T(8,128)(2,1)S(1)}, bf16[256,128]{1,0:T(8,128)(2,1)S(1)}, u32[]{:S(2)}, u32[]{:S(2)}) %collective-permute-start.49) | collective-permute-done | bytes 65568 | tf_op jit(solution)/shard_map/ppermute | solution.py:76
  143.6 1.5 collective-permute-start.53
  145.9 2.0 %collective-permute-done.52.refs_2_ = bf16[256,128]{1,0:T(8,128)(2,1)S(1)} collective-permute-done((bf16[256,128]{1,0:T(8,128)(2,1)S(1)}, bf16[256,128]{1,0:T(8,128)(2,1)S(1)}, u32[]{:S(2)}, u32[]{:S(2)}) %collective-permute-start.52) | collective-permute-done | bytes 65568 | tf_op jit(solution)/shard_map/ppermute | solution.py:72
  150.9 1.6 collective-permute-start.55
  155.2 2.2 %collective-permute-done.56.refs_1_ = bf16[128,256]{1,0:T(8,128)(2,1)S(1)} collective-permute-done((bf16[128,256]{1,0:T(8,128)(2,1)S(1)}, bf16[128,256]{1,0:T(8,128)(2,1)S(1)}, u32[]{:S(2)}, u32[]{:S(2)}) %collective-permute-start.56) | collective-permute-done | bytes 65568 | tf_op jit(solution)/shard_map/ppermute | solution.py:72
  158.2 2.0 %collective-permute-start.60 = (bf16[128,256]{1,0:T(8,128)(2,1)S(1)}, bf16[128,256]{1,0:T(8,128)(2,1)S(1)}, u32[]{:S(2)}, u32[]{:S(2)}) collective-permute-start(bf16[128,256]{1,0:T(8,128)(2,1)S(1)} %shard_map.341.own_ref), channel_id=1, source_target_pairs={{0,24},{8,16},{16,8},{24,0},{1,25},{9,17},{17,9},{25,1},{2,26},{10... | collective-permute-start | bytes 196616 | tf_op jit(solution)/shard_map/ppermute | solution.py:76
  160.7 2.0 %collective-permute-start.58 = (bf16[128,256]{1,0:T(8,128)(2,1)S(1)}, bf16[128,256]{1,0:T(8,128)(2,1)S(1)}, u32[]{:S(2)}, u32[]{:S(2)}) collective-permute-start(bf16[128,256]{1,0:T(8,128)(2,1)S(1)} %shard_map.341.own_ref), channel_id=1, source_target_pairs={{0,8},{8,0},{16,24},{24,16},{1,9},{9,1},{17,25},{25,17},{2,10},{10... | collective-permute-start | bytes 196616 | tf_op jit(solution)/shard_map/ppermute | solution.py:76
  164.6 1.6 collective-permute-done.59.refs_1_
  166.2 1.5 collective-permute-start.63
  169.8 2.0 %collective-permute-done.63.refs_3_ = bf16[128,256]{1,0:T(8,128)(2,1)S(1)} collective-permute-done((bf16[128,256]{1,0:T(8,128)(2,1)S(1)}, bf16[128,256]{1,0:T(8,128)(2,1)S(1)}, u32[]{:S(2)}, u32[]{:S(2)}) %collective-permute-start.63) | collective-permute-done | bytes 65568 | tf_op jit(solution)/shard_map/ppermute | solution.py:72
  174.5 2.4 %shard_map.343 = (f32[602,256]{1,0:T(8,128)}, f32[602,256]{1,0:T(8,128)}, f32[602,256]{1,0:T(8,128)}, f32[256,256]{1,0:T(8,128)}, f32[256,256]{1,0:T(8,128)}, /*...) custom-call(bf16[128,256]{1,0:T(8,128)(2,1)S(1)} %shard_map.342.refs_0_, ...), custom_call_target="tpu_custom_call" | custom-call | bytes 6047744 | tf_op jit(solution)/shard_map/pallas_call | solution.py:59
  (158 shorter events, 50.5 us)
Async XLA Ops:
  2.1 7.9 %collective-permute-start.2 = (bf16[128,256]{1,0:T(8,128)(2,1)S(1)}, bf16[128,256]{1,0:T(8,128)(2,1)S(1)}, u32[]{:S(2)}, u32[]{:S(2)}) collective-permute-start(bf16[128,256]{1,0:T(8,128)(2,1)S(1)} %convolution_convert_fusion), channel_id=1, source_target_pairs={{0,24},{8,16},{16,8},{24,0},{1,25},{9,17},{17,9},{25,1},{2,26},{10... | collective-permute-start | bytes 196616 | tf_op jit(solution)/shard_map/ppermute | solution.py:76
  7.2 5.6 %collective-permute-start.1 = (bf16[128,256]{1,0:T(8,128)(2,1)S(1)}, bf16[128,256]{1,0:T(8,128)(2,1)S(1)}, u32[]{:S(2)}, u32[]{:S(2)}) collective-permute-start(bf16[128,256]{1,0:T(8,128)(2,1)S(1)} %convolution_convert_fusion), channel_id=1, source_target_pairs={{0,16},{8,24},{16,0},{24,8},{1,17},{9,25},{17,1},{25,9},{2,18},{10... | collective-permute-start | bytes 196616 | tf_op jit(solution)/shard_map/ppermute | solution.py:76
  7.2 5.6 %collective-permute-start = (bf16[128,256]{1,0:T(8,128)(2,1)S(1)}, bf16[128,256]{1,0:T(8,128)(2,1)S(1)}, u32[]{:S(2)}, u32[]{:S(2)}) collective-permute-start(bf16[128,256]{1,0:T(8,128)(2,1)S(1)} %convolution_convert_fusion), channel_id=1, source_target_pairs={{0,8},{8,0},{16,24},{24,16},{1,9},{9,1},{17,25},{25,17},{2,10},{10... | collective-permute-start | bytes 196616 | tf_op jit(solution)/shard_map/ppermute | solution.py:76
  12.8 10.2 %collective-permute-start.5 = (bf16[4,128,256]{2,1,0:T(8,128)(2,1)S(1)}, bf16[4,128,256]{2,1,0:T(8,128)(2,1)S(1)}, u32[]{:S(2)}, u32[]{:S(2)}) collective-permute-start(bf16[4,128,256]{2,1,0:T(8,128)(2,1)S(1)} %pad_maximum_fusion.2.refs_0_), channel_id=1, source_target_pairs={{0,6},{1,7},{2,4},{3,5},{4,2},{5,3},{6,0},{7,1},{8,14},{9,15},{10,... | collective-permute-start | bytes 786440 | tf_op jit(solution)/shard_map/ppermute | solution.py:72
  15.4 11.9 %collective-permute-start.4 = (bf16[4,128,256]{2,1,0:T(8,128)(2,1)S(1)}, bf16[4,128,256]{2,1,0:T(8,128)(2,1)S(1)}, u32[]{:S(2)}, u32[]{:S(2)}) collective-permute-start(bf16[4,128,256]{2,1,0:T(8,128)(2,1)S(1)} %pad_maximum_fusion.2.refs_0_), channel_id=1, source_target_pairs={{0,4},{1,5},{2,6},{3,7},{4,0},{5,1},{6,2},{7,3},{8,12},{9,13},{10,... | collective-permute-start | bytes 786440 | tf_op jit(solution)/shard_map/ppermute | solution.py:72
  15.9 11.7 %collective-permute-start.3 = (bf16[4,128,256]{2,1,0:T(8,128)(2,1)S(1)}, bf16[4,128,256]{2,1,0:T(8,128)(2,1)S(1)}, u32[]{:S(2)}, u32[]{:S(2)}) collective-permute-start(bf16[4,128,256]{2,1,0:T(8,128)(2,1)S(1)} %pad_maximum_fusion.2.refs_0_), channel_id=1, source_target_pairs={{0,2},{1,3},{2,0},{3,1},{4,6},{5,7},{6,4},{7,5},{8,10},{9,11},{10,... | collective-permute-start | bytes 786440 | tf_op jit(solution)/shard_map/ppermute | solution.py:72
  16.4 13.2 %collective-permute-start.7 = (bf16[128,1024]{1,0:T(8,128)(2,1)S(1)}, bf16[128,1024]{1,0:T(8,128)(2,1)S(1)}, u32[]{:S(2)}, u32[]{:S(2)}) collective-permute-start(bf16[128,1024]{1,0:T(8,128)(2,1)S(1)} %get-tuple-element.79), channel_id=1, source_target_pairs={{0,16},{8,24},{16,0},{24,8},{1,17},{9,25},{17,1},{25,9},{2,18},{10... | collective-permute-start | bytes 786440 | tf_op jit(solution)/shard_map/ppermute | solution.py:76
  18.0 11.6 %collective-permute-start.6 = (bf16[128,1024]{1,0:T(8,128)(2,1)S(1)}, bf16[128,1024]{1,0:T(8,128)(2,1)S(1)}, u32[]{:S(2)}, u32[]{:S(2)}) collective-permute-start(bf16[128,1024]{1,0:T(8,128)(2,1)S(1)} %get-tuple-element.77), channel_id=1, source_target_pairs={{0,8},{8,0},{16,24},{24,16},{1,9},{9,1},{17,25},{25,17},{2,10},{10... | collective-permute-start | bytes 786440 | tf_op jit(solution)/shard_map/ppermute | solution.py:76
  32.7 7.1 %collective-permute-start.14 = (bf16[144,256]{1,0:T(8,128)(2,1)S(1)}, bf16[144,256]{1,0:T(8,128)(2,1)S(1)}, u32[]{:S(2)}, u32[]{:S(2)}) collective-permute-start(bf16[144,256]{1,0:T(8,128)(2,1)S(1)} %shard_map.324.summed_ref), channel_id=1, source_target_pairs={{0,24},{8,16},{16,8},{24,0},{1,25},{9,17},{17,9},{25,1},{2,26},{10... | collective-permute-start | bytes 221192 | tf_op jit(solution)/shard_map/ppermute | solution.py:76
  34.7 7.4 %collective-permute-start.13 = (bf16[144,256]{1,0:T(8,128)(2,1)S(1)}, bf16[144,256]{1,0:T(8,128)(2,1)S(1)}, u32[]{:S(2)}, u32[]{:S(2)}) collective-permute-start(bf16[144,256]{1,0:T(8,128)(2,1)S(1)} %shard_map.324.summed_ref), channel_id=1, source_target_pairs={{0,16},{8,24},{16,0},{24,8},{1,17},{9,25},{17,1},{25,9},{2,18},{10... | collective-permute-start | bytes 221192 | tf_op jit(solution)/shard_map/ppermute | solution.py:76
  34.7 7.4 %collective-permute-start.12 = (bf16[144,256]{1,0:T(8,128)(2,1)S(1)}, bf16[144,256]{1,0:T(8,128)(2,1)S(1)}, u32[]{:S(2)}, u32[]{:S(2)}) collective-permute-start(bf16[144,256]{1,0:T(8,128)(2,1)S(1)} %shard_map.324.summed_ref), channel_id=1, source_target_pairs={{0,8},{8,0},{16,24},{24,16},{1,9},{9,1},{17,25},{25,17},{2,10},{10... | collective-permute-start | bytes 221192 | tf_op jit(solution)/shard_map/ppermute | solution.py:76
  42.1 12.9 %collective-permute-start.17 = (bf16[4,144,256]{2,1,0:T(8,128)(2,1)S(1)}, bf16[4,144,256]{2,1,0:T(8,128)(2,1)S(1)}, u32[]{:S(2)}, u32[]{:S(2)}) collective-permute-start(bf16[4,144,256]{2,1,0:T(8,128)(2,1)S(1)} %pad_maximum_fusion.refs_0_), channel_id=1, source_target_pairs={{0,6},{1,7},{2,4},{3,5},{4,2},{5,3},{6,0},{7,1},{8,14},{9,15},{10,... | collective-permute-start | bytes 884744 | tf_op jit(solution)/shard_map/ppermute | solution.py:72
  44.6 13.7 %collective-permute-start.16 = (bf16[4,144,256]{2,1,0:T(8,128)(2,1)S(1)}, bf16[4,144,256]{2,1,0:T(8,128)(2,1)S(1)}, u32[]{:S(2)}, u32[]{:S(2)}) collective-permute-start(bf16[4,144,256]{2,1,0:T(8,128)(2,1)S(1)} %pad_maximum_fusion.refs_0_), channel_id=1, source_target_pairs={{0,4},{1,5},{2,6},{3,7},{4,0},{5,1},{6,2},{7,3},{8,12},{9,13},{10,... | collective-permute-start | bytes 884744 | tf_op jit(solution)/shard_map/ppermute | solution.py:72
  45.1 13.3 %collective-permute-start.15 = (bf16[4,144,256]{2,1,0:T(8,128)(2,1)S(1)}, bf16[4,144,256]{2,1,0:T(8,128)(2,1)S(1)}, u32[]{:S(2)}, u32[]{:S(2)}) collective-permute-start(bf16[4,144,256]{2,1,0:T(8,128)(2,1)S(1)} %pad_maximum_fusion.refs_0_), channel_id=1, source_target_pairs={{0,2},{1,3},{2,0},{3,1},{4,6},{5,7},{6,4},{7,5},{8,10},{9,11},{10,... | collective-permute-start | bytes 884744 | tf_op jit(solution)/shard_map/ppermute | solution.py:72
  45.7 9.3 %collective-permute-start.18 = (bf16[128,1024]{1,0:T(8,128)(2,1)S(1)}, bf16[128,1024]{1,0:T(8,128)(2,1)S(1)}, u32[]{:S(2)}, u32[]{:S(2)}) collective-permute-start(bf16[128,1024]{1,0:T(8,128)(2,1)S(1)} %get-tuple-element.85), channel_id=1, source_target_pairs={{0,24},{8,16},{16,8},{24,0},{1,25},{9,17},{17,9},{25,1},{2,26},{10... | collective-permute-start | bytes 786440 | tf_op jit(solution)/shard_map/ppermute | solution.py:76
  63.9 7.1 %collective-permute-start.25 = (bf16[144,256]{1,0:T(8,128)(2,1)S(1)}, bf16[144,256]{1,0:T(8,128)(2,1)S(1)}, u32[]{:S(2)}, u32[]{:S(2)}) collective-permute-start(bf16[144,256]{1,0:T(8,128)(2,1)S(1)} %get-tuple-element.90.summed_ref), channel_id=1, source_target_pairs={{0,24},{8,16},{16,8},{24,0},{1,25},{9,17},{17,9},{25,1},{2,26},{10... | collective-permute-start | bytes 221192 | tf_op jit(solution)/shard_map/ppermute | solution.py:76
  66.0 7.2 %collective-permute-start.24 = (bf16[144,256]{1,0:T(8,128)(2,1)S(1)}, bf16[144,256]{1,0:T(8,128)(2,1)S(1)}, u32[]{:S(2)}, u32[]{:S(2)}) collective-permute-start(bf16[144,256]{1,0:T(8,128)(2,1)S(1)} %get-tuple-element.90.summed_ref), channel_id=1, source_target_pairs={{0,16},{8,24},{16,0},{24,8},{1,17},{9,25},{17,1},{25,9},{2,18},{10... | collective-permute-start | bytes 221192 | tf_op jit(solution)/shard_map/ppermute | solution.py:76
  66.0 7.2 %collective-permute-start.23 = (bf16[144,256]{1,0:T(8,128)(2,1)S(1)}, bf16[144,256]{1,0:T(8,128)(2,1)S(1)}, u32[]{:S(2)}, u32[]{:S(2)}) collective-permute-start(bf16[144,256]{1,0:T(8,128)(2,1)S(1)} %get-tuple-element.90.summed_ref), channel_id=1, source_target_pairs={{0,8},{8,0},{16,24},{24,16},{1,9},{9,1},{17,25},{25,17},{2,10},{10... | collective-permute-start | bytes 221192 | tf_op jit(solution)/shard_map/ppermute | solution.py:76
  73.3 10.9 %collective-permute-start.28 = (bf16[4,144,256]{2,1,0:T(8,128)(2,1)S(1)}, bf16[4,144,256]{2,1,0:T(8,128)(2,1)S(1)}, u32[]{:S(2)}, u32[]{:S(2)}) collective-permute-start(bf16[4,144,256]{2,1,0:T(8,128)(2,1)S(1)} %pad_maximum_fusion.1.refs_0_), channel_id=1, source_target_pairs={{0,6},{1,7},{2,4},{3,5},{4,2},{5,3},{6,0},{7,1},{8,14},{9,15},{10,... | collective-permute-start | bytes 884744 | tf_op jit(solution)/shard_map/ppermute | solution.py:72
  75.0 14.5 %collective-permute-start.27 = (bf16[4,144,256]{2,1,0:T(8,128)(2,1)S(1)}, bf16[4,144,256]{2,1,0:T(8,128)(2,1)S(1)}, u32[]{:S(2)}, u32[]{:S(2)}) collective-permute-start(bf16[4,144,256]{2,1,0:T(8,128)(2,1)S(1)} %pad_maximum_fusion.1.refs_0_), channel_id=1, source_target_pairs={{0,4},{1,5},{2,6},{3,7},{4,0},{5,1},{6,2},{7,3},{8,12},{9,13},{10,... | collective-permute-start | bytes 884744 | tf_op jit(solution)/shard_map/ppermute | solution.py:72
  76.3 13.2 %collective-permute-start.26 = (bf16[4,144,256]{2,1,0:T(8,128)(2,1)S(1)}, bf16[4,144,256]{2,1,0:T(8,128)(2,1)S(1)}, u32[]{:S(2)}, u32[]{:S(2)}) collective-permute-start(bf16[4,144,256]{2,1,0:T(8,128)(2,1)S(1)} %pad_maximum_fusion.1.refs_0_), channel_id=1, source_target_pairs={{0,2},{1,3},{2,0},{3,1},{4,6},{5,7},{6,4},{7,5},{8,10},{9,11},{10,... | collective-permute-start | bytes 884744 | tf_op jit(solution)/shard_map/ppermute | solution.py:72
  76.8 13.2 %collective-permute-start.29 = (bf16[4,144,256]{2,1,0:T(8,128)(2,1)S(1)}, bf16[4,144,256]{2,1,0:T(8,128)(2,1)S(1)}, u32[]{:S(2)}, u32[]{:S(2)}) collective-permute-start(bf16[4,144,256]{2,1,0:T(8,128)(2,1)S(1)} %pad_maximum_fusion.1.refs_0_), channel_id=1, source_target_pairs={{0,1},{1,0},{2,3},{3,2},{4,5},{5,4},{6,7},{7,6},{8,9},{9,8},{10,11... | collective-permute-start | bytes 884744 | tf_op jit(solution)/shard_map/ppermute | solution.py:72
  84.2 5.9 %collective-permute-start.32 = (bf16[4,144,256]{2,1,0:T(8,128)(2,1)S(1)}, bf16[4,144,256]{2,1,0:T(8,128)(2,1)S(1)}, u32[]{:S(2)}, u32[]{:S(2)}) collective-permute-start(bf16[4,144,256]{2,1,0:T(8,128)(2,1)S(1)} %collective-permute-done.28.refs_3_), channel_id=1, source_target_pairs={{0,1},{1,0},{2,3},{3,2},{4,5},{5,4},{6,7},{7,6},{8,9},{9,8},{10,11... | collective-permute-start | bytes 884744 | tf_op jit(solution)/shard_map/ppermute | solution.py:72
  97.2 5.6 %collective-permute-start.35 = (bf16[64,128]{1,0:T(8,128)(2,1)S(1)}, bf16[64,128]{1,0:T(8,128)(2,1)S(1)}, u32[]{:S(2)}, u32[]{:S(2)}) collective-permute-start(bf16[64,128]{1,0:T(8,128)(2,1)S(1)} %get-tuple-element.93.refs_0_), channel_id=1, source_target_pairs={{0,24},{8,16},{16,8},{24,0},{1,25},{9,17},{17,9},{25,1},{2,26},{10... | collective-permute-start | bytes 49160 | tf_op jit(solution)/shard_map/ppermute | solution.py:76
  99.2 4.6 %collective-permute-start.34 = (bf16[64,128]{1,0:T(8,128)(2,1)S(1)}, bf16[64,128]{1,0:T(8,128)(2,1)S(1)}, u32[]{:S(2)}, u32[]{:S(2)}) collective-permute-start(bf16[64,128]{1,0:T(8,128)(2,1)S(1)} %get-tuple-element.93.refs_0_), channel_id=1, source_target_pairs={{0,16},{8,24},{16,0},{24,8},{1,17},{9,25},{17,1},{25,9},{2,18},{10... | collective-permute-start | bytes 49160 | tf_op jit(solution)/shard_map/ppermute | solution.py:76
  99.3 4.6 %collective-permute-start.33 = (bf16[64,128]{1,0:T(8,128)(2,1)S(1)}, bf16[64,128]{1,0:T(8,128)(2,1)S(1)}, u32[]{:S(2)}, u32[]{:S(2)}) collective-permute-start(bf16[64,128]{1,0:T(8,128)(2,1)S(1)} %get-tuple-element.93.refs_0_), channel_id=1, source_target_pairs={{0,8},{8,0},{16,24},{24,16},{1,9},{9,1},{17,25},{25,17},{2,10},{10... | collective-permute-start | bytes 49160 | tf_op jit(solution)/shard_map/ppermute | solution.py:76
  105.4 7.1 %collective-permute-start.37 = (bf16[64,128]{1,0:T(8,128)(2,1)S(1)}, bf16[64,128]{1,0:T(8,128)(2,1)S(1)}, u32[]{:S(2)}, u32[]{:S(2)}) collective-permute-start(bf16[64,128]{1,0:T(8,128)(2,1)S(1)} %get-tuple-element.99), channel_id=1, source_target_pairs={{0,2},{1,3},{2,0},{3,1},{4,6},{5,7},{6,4},{7,5},{8,10},{9,11},{10,... | collective-permute-start | bytes 49160 | tf_op jit(solution)/shard_map/ppermute | solution.py:72
  107.0 5.5 %collective-permute-start.38 = (bf16[64,128]{1,0:T(8,128)(2,1)S(1)}, bf16[64,128]{1,0:T(8,128)(2,1)S(1)}, u32[]{:S(2)}, u32[]{:S(2)}) collective-permute-start(bf16[64,128]{1,0:T(8,128)(2,1)S(1)} %get-tuple-element.100), channel_id=1, source_target_pairs={{0,4},{1,5},{2,6},{3,7},{4,0},{5,1},{6,2},{7,3},{8,12},{9,13},{10,... | collective-permute-start | bytes 49160 | tf_op jit(solution)/shard_map/ppermute | solution.py:72
  107.6 4.9 %collective-permute-start.39 = (bf16[64,128]{1,0:T(8,128)(2,1)S(1)}, bf16[64,128]{1,0:T(8,128)(2,1)S(1)}, u32[]{:S(2)}, u32[]{:S(2)}) collective-permute-start(bf16[64,128]{1,0:T(8,128)(2,1)S(1)} %get-tuple-element.101), channel_id=1, source_target_pairs={{0,6},{1,7},{2,4},{3,5},{4,2},{5,3},{6,0},{7,1},{8,14},{9,15},{10,... | collective-permute-start | bytes 49160 | tf_op jit(solution)/shard_map/ppermute | solution.py:72
  113.0 6.8 %collective-permute-start.42 = (bf16[272,128]{1,0:T(8,128)(2,1)S(1)}, bf16[272,128]{1,0:T(8,128)(2,1)S(1)}, u32[]{:S(2)}, u32[]{:S(2)}) collective-permute-start(bf16[272,128]{1,0:T(8,128)(2,1)S(1)} %get-tuple-element.103.refs_0_), channel_id=1, source_target_pairs={{0,24},{8,16},{16,8},{24,0},{1,25},{9,17},{17,9},{25,1},{2,26},{10... | collective-permute-start | bytes 208904 | tf_op jit(solution)/shard_map/ppermute | solution.py:76
  114.9 7.1 %collective-permute-start.41 = (bf16[272,128]{1,0:T(8,128)(2,1)S(1)}, bf16[272,128]{1,0:T(8,128)(2,1)S(1)}, u32[]{:S(2)}, u32[]{:S(2)}) collective-permute-start(bf16[272,128]{1,0:T(8,128)(2,1)S(1)} %get-tuple-element.103.refs_0_), channel_id=1, source_target_pairs={{0,16},{8,24},{16,0},{24,8},{1,17},{9,25},{17,1},{25,9},{2,18},{10... | collective-permute-start | bytes 208904 | tf_op jit(solution)/shard_map/ppermute | solution.py:76
  116.0 6.0 %collective-permute-start.40 = (bf16[272,128]{1,0:T(8,128)(2,1)S(1)}, bf16[272,128]{1,0:T(8,128)(2,1)S(1)}, u32[]{:S(2)}, u32[]{:S(2)}) collective-permute-start(bf16[272,128]{1,0:T(8,128)(2,1)S(1)} %get-tuple-element.103.refs_0_), channel_id=1, source_target_pairs={{0,8},{8,0},{16,24},{24,16},{1,9},{9,1},{17,25},{25,17},{2,10},{10... | collective-permute-start | bytes 208904 | tf_op jit(solution)/shard_map/ppermute | solution.py:76
  124.0 4.4 %collective-permute-start.44 = (bf16[272,128]{1,0:T(8,128)(2,1)S(1)}, bf16[272,128]{1,0:T(8,128)(2,1)S(1)}, u32[]{:S(2)}, u32[]{:S(2)}) collective-permute-start(bf16[272,128]{1,0:T(8,128)(2,1)S(1)} %get-tuple-element.105), channel_id=1, source_target_pairs={{0,2},{1,3},{2,0},{3,1},{4,6},{5,7},{6,4},{7,5},{8,10},{9,11},{10,... | collective-permute-start | bytes 208904 | tf_op jit(solution)/shard_map/ppermute | solution.py:72
  125.6 5.1 %collective-permute-start.45 = (bf16[272,128]{1,0:T(8,128)(2,1)S(1)}, bf16[272,128]{1,0:T(8,128)(2,1)S(1)}, u32[]{:S(2)}, u32[]{:S(2)}) collective-permute-start(bf16[272,128]{1,0:T(8,128)(2,1)S(1)} %get-tuple-element.106), channel_id=1, source_target_pairs={{0,4},{1,5},{2,6},{3,7},{4,0},{5,1},{6,2},{7,3},{8,12},{9,13},{10,... | collective-permute-start | bytes 208904 | tf_op jit(solution)/shard_map/ppermute | solution.py:72
  126.2 5.2 %collective-permute-start.46 = (bf16[272,128]{1,0:T(8,128)(2,1)S(1)}, bf16[272,128]{1,0:T(8,128)(2,1)S(1)}, u32[]{:S(2)}, u32[]{:S(2)}) collective-permute-start(bf16[272,128]{1,0:T(8,128)(2,1)S(1)} %get-tuple-element.107), channel_id=1, source_target_pairs={{0,6},{1,7},{2,4},{3,5},{4,2},{5,3},{6,0},{7,1},{8,14},{9,15},{10,... | collective-permute-start | bytes 208904 | tf_op jit(solution)/shard_map/ppermute | solution.py:72
  131.7 6.4 %collective-permute-start.49 = (bf16[256,128]{1,0:T(8,128)(2,1)S(1)}, bf16[256,128]{1,0:T(8,128)(2,1)S(1)}, u32[]{:S(2)}, u32[]{:S(2)}) collective-permute-start(bf16[256,128]{1,0:T(8,128)(2,1)S(1)} %get-tuple-element.110.refs_0_), channel_id=1, source_target_pairs={{0,24},{8,16},{16,8},{24,0},{1,25},{9,17},{17,9},{25,1},{2,26},{10... | collective-permute-start | bytes 196616 | tf_op jit(solution)/shard_map/ppermute | solution.py:76
  133.7 5.8 %collective-permute-start.48 = (bf16[256,128]{1,0:T(8,128)(2,1)S(1)}, bf16[256,128]{1,0:T(8,128)(2,1)S(1)}, u32[]{:S(2)}, u32[]{:S(2)}) collective-permute-start(bf16[256,128]{1,0:T(8,128)(2,1)S(1)} %get-tuple-element.110.refs_0_), channel_id=1, source_target_pairs={{0,16},{8,24},{16,0},{24,8},{1,17},{9,25},{17,1},{25,9},{2,18},{10... | collective-permute-start | bytes 196616 | tf_op jit(solution)/shard_map/ppermute | solution.py:76
  133.7 5.8 %collective-permute-start.47 = (bf16[256,128]{1,0:T(8,128)(2,1)S(1)}, bf16[256,128]{1,0:T(8,128)(2,1)S(1)}, u32[]{:S(2)}, u32[]{:S(2)}) collective-permute-start(bf16[256,128]{1,0:T(8,128)(2,1)S(1)} %get-tuple-element.110.refs_0_), channel_id=1, source_target_pairs={{0,8},{8,0},{16,24},{24,16},{1,9},{9,1},{17,25},{25,17},{2,10},{10... | collective-permute-start | bytes 196616 | tf_op jit(solution)/shard_map/ppermute | solution.py:76
  141.5 4.3 %collective-permute-start.51 = (bf16[256,128]{1,0:T(8,128)(2,1)S(1)}, bf16[256,128]{1,0:T(8,128)(2,1)S(1)}, u32[]{:S(2)}, u32[]{:S(2)}) collective-permute-start(bf16[256,128]{1,0:T(8,128)(2,1)S(1)} %get-tuple-element.112), channel_id=1, source_target_pairs={{0,2},{1,3},{2,0},{3,1},{4,6},{5,7},{6,4},{7,5},{8,10},{9,11},{10,... | collective-permute-start | bytes 196616 | tf_op jit(solution)/shard_map/ppermute | solution.py:72
  142.9 5.0 %collective-permute-start.52 = (bf16[256,128]{1,0:T(8,128)(2,1)S(1)}, bf16[256,128]{1,0:T(8,128)(2,1)S(1)}, u32[]{:S(2)}, u32[]{:S(2)}) collective-permute-start(bf16[256,128]{1,0:T(8,128)(2,1)S(1)} %get-tuple-element.113), channel_id=1, source_target_pairs={{0,4},{1,5},{2,6},{3,7},{4,0},{5,1},{6,2},{7,3},{8,12},{9,13},{10,... | collective-permute-start | bytes 196616 | tf_op jit(solution)/shard_map/ppermute | solution.py:72
  143.6 5.2 %collective-permute-start.53 = (bf16[256,128]{1,0:T(8,128)(2,1)S(1)}, bf16[256,128]{1,0:T(8,128)(2,1)S(1)}, u32[]{:S(2)}, u32[]{:S(2)}) collective-permute-start(bf16[256,128]{1,0:T(8,128)(2,1)S(1)} %get-tuple-element.114), channel_id=1, source_target_pairs={{0,6},{1,7},{2,4},{3,5},{4,2},{5,3},{6,0},{7,1},{8,14},{9,15},{10,... | collective-permute-start | bytes 196616 | tf_op jit(solution)/shard_map/ppermute | solution.py:72
  152.4 5.0 %collective-permute-start.56 = (bf16[128,256]{1,0:T(8,128)(2,1)S(1)}, bf16[128,256]{1,0:T(8,128)(2,1)S(1)}, u32[]{:S(2)}, u32[]{:S(2)}) collective-permute-start(bf16[128,256]{1,0:T(8,128)(2,1)S(1)} %get-tuple-element.119), channel_id=1, source_target_pairs={{0,4},{1,5},{2,6},{3,7},{4,0},{5,1},{6,2},{7,3},{8,12},{9,13},{10,... | collective-permute-start | bytes 196616 | tf_op jit(solution)/shard_map/ppermute | solution.py:72
  153.0 5.2 %collective-permute-start.57 = (bf16[128,256]{1,0:T(8,128)(2,1)S(1)}, bf16[128,256]{1,0:T(8,128)(2,1)S(1)}, u32[]{:S(2)}, u32[]{:S(2)}) collective-permute-start(bf16[128,256]{1,0:T(8,128)(2,1)S(1)} %get-tuple-element.120), channel_id=1, source_target_pairs={{0,6},{1,7},{2,4},{3,5},{4,2},{5,3},{6,0},{7,1},{8,14},{9,15},{10,... | collective-permute-start | bytes 196616 | tf_op jit(solution)/shard_map/ppermute | solution.py:72
  158.2 6.3 %collective-permute-start.60 = (bf16[128,256]{1,0:T(8,128)(2,1)S(1)}, bf16[128,256]{1,0:T(8,128)(2,1)S(1)}, u32[]{:S(2)}, u32[]{:S(2)}) collective-permute-start(bf16[128,256]{1,0:T(8,128)(2,1)S(1)} %shard_map.341.own_ref), channel_id=1, source_target_pairs={{0,24},{8,16},{16,8},{24,0},{1,25},{9,17},{17,9},{25,1},{2,26},{10... | collective-permute-start | bytes 196616 | tf_op jit(solution)/shard_map/ppermute | solution.py:76
  160.2 5.9 %collective-permute-start.59 = (bf16[128,256]{1,0:T(8,128)(2,1)S(1)}, bf16[128,256]{1,0:T(8,128)(2,1)S(1)}, u32[]{:S(2)}, u32[]{:S(2)}) collective-permute-start(bf16[128,256]{1,0:T(8,128)(2,1)S(1)} %shard_map.341.own_ref), channel_id=1, source_target_pairs={{0,16},{8,24},{16,0},{24,8},{1,17},{9,25},{17,1},{25,9},{2,18},{10... | collective-permute-start | bytes 196616 | tf_op jit(solution)/shard_map/ppermute | solution.py:76
  160.7 5.5 %collective-permute-start.58 = (bf16[128,256]{1,0:T(8,128)(2,1)S(1)}, bf16[128,256]{1,0:T(8,128)(2,1)S(1)}, u32[]{:S(2)}, u32[]{:S(2)}) collective-permute-start(bf16[128,256]{1,0:T(8,128)(2,1)S(1)} %shard_map.341.own_ref), channel_id=1, source_target_pairs={{0,8},{8,0},{16,24},{24,16},{1,9},{9,1},{17,25},{25,17},{2,10},{10... | collective-permute-start | bytes 196616 | tf_op jit(solution)/shard_map/ppermute | solution.py:76
  166.2 5.6 %collective-permute-start.63 = (bf16[128,256]{1,0:T(8,128)(2,1)S(1)}, bf16[128,256]{1,0:T(8,128)(2,1)S(1)}, u32[]{:S(2)}, u32[]{:S(2)}) collective-permute-start(bf16[128,256]{1,0:T(8,128)(2,1)S(1)} %shard_map.342.refs_0_), channel_id=1, source_target_pairs={{0,6},{1,7},{2,4},{3,5},{4,2},{5,3},{6,0},{7,1},{8,14},{9,15},{10,... | collective-permute-start | bytes 196616 | tf_op jit(solution)/shard_map/ppermute | solution.py:72
  167.7 4.7 %collective-permute-start.62 = (bf16[128,256]{1,0:T(8,128)(2,1)S(1)}, bf16[128,256]{1,0:T(8,128)(2,1)S(1)}, u32[]{:S(2)}, u32[]{:S(2)}) collective-permute-start(bf16[128,256]{1,0:T(8,128)(2,1)S(1)} %shard_map.342.refs_0_), channel_id=1, source_target_pairs={{0,4},{1,5},{2,6},{3,7},{4,0},{5,1},{6,2},{7,3},{8,12},{9,13},{10,... | collective-permute-start | bytes 196616 | tf_op jit(solution)/shard_map/ppermute | solution.py:72
  (40 other events, 297.2 us)

commit v3 on v2

--- a/solution.py
+++ b/solution.py
@@ -84,17 +84,18 @@
     return lax.optimization_barrier((block, *others))[0]
 
 
-def gather_all(block, beside=()):
+def gather_all(block, beside=(), early=()):
     if short_line():
         line = jnp.stack([block] + [pass_line(block, k) for k in range(1, 4)])
     else:
         line = lax.all_gather(block, "z", axis=0)
+    if early:
+        line, *early = lax.optimization_barrier((line, *early))
     passed = [pass_line(after(part, line), mask) for part, mask in beside]
     lines = [line] + [swap(line, 2 * k) for k in range(1, 4)]
     if passed:
-        held = lax.optimization_barrier((*lines, *passed))
-        lines, passed = list(held[:4]), list(held[4:])
-    return lines + [swap(line, 1) for line in lines], passed
+        lines[3], *passed = lax.optimization_barrier((lines[3], *passed))
+    return lines + [swap(line, 1) for line in lines], passed, early
 
 
 def arrange_kernel(mask_ref, values_ref, near_ref, far_ref, *level_refs):
@@ -471,27 +472,48 @@
     pack_into(packed_ref, d_summed.T, split_sums(sums_ref[...]))
 
 
-def first_kernel(node_total, weight_ref, norm_ref, summed_ref, stats_ref, *refs):
-    refs, (packed_ref, grad_ref, out_ref) = refs[:4], refs[4:]
-    d_projected, sums = line_total(refs, weight_ref.shape[1])
+def mix_kernel(near_ref, far_ref, *refs):
+    outs = 1 if len(refs) == 2 else 4
+    level_refs, out_refs = refs[:outs], refs[outs:]
+
+    def one(level_ref):
+        total = None
+        for n in range(0, 8, 2):
+            ref = far_ref if n >= 4 else near_ref
+            left = jnp.concatenate([ref[n % 4], ref[n % 4 + 1]], axis=1)
+            part = dot_turned(left, level_ref[:, n * TILE : (n + 2) * TILE])
+            total = part if total is None else total + part
+        return total
+
+    if outs == 1:
+
+        def step(i, carry):
+            out_refs[0][i] = one(level_refs[0].at[i])
+            return carry
+
+        lax.fori_loop(0, level_refs[0].shape[0], step, 0)
+        return
+    for level_ref, out_ref in zip(level_refs, out_refs, strict=True):
+        out_ref[...] = one(level_ref).astype(out_ref.dtype)
+
+
+def first_kernel(node_total, inputs_tall, mixes, weight_ref, norm_ref, summed_ref, stats_ref, head_ref, *refs):
+    mix_refs, refs = refs[:mixes], refs[mixes:]
+    refs, (away_ref, kept_ref, out_ref, pile_ref) = refs[:4], refs[4:]
+    width = weight_ref.shape[1]
+    d_projected, sums = line_total(refs, width)
     out_ref[...] = sums
     d_projected = d_projected.T.astype(BF)
     d_hidden = dot_turned(d_projected, weight_ref[...].astype(BF))
     d_summed, hidden = backward_norm(
         d_hidden, summed_ref, stats_ref, norm_ref, 0, wide(sums, 0), wide(sums, 2), node_total
     )
-    pack_into(packed_ref, d_summed.T, None)
-    grad_ref[...] = dot(hidden.T.astype(BF), d_projected)
-
-
-def pile_kernel(inputs_tall, inputs_ref, second_ref, head_ref, *refs):
-    refs, (away_ref, kept_ref, pile_ref) = refs[:4], refs[4:]
-    d_projected = line_total(refs, second_ref.shape[0])[0].T.astype(BF)
+    mixed = add_up(ref[...].astype(F32) for ref in mix_refs).astype(BF)
     pile_ref[...] = jnp.zeros(pile_ref.shape, F32)
-    pile_ref[: inputs_ref.shape[0], :] = dot(inputs_ref[...], d_projected)
+    pile_ref[: mixed.shape[0], :] = dot(mixed, d_summed.astype(BF))
     at = inputs_tall
-    pile_ref[at : at + second_ref.shape[0], :] = second_ref[...]
-    at += second_ref.shape[0]
+    pile_ref[at : at + width, :] = dot(hidden.T.astype(BF), d_projected)
+    at += width
     pile_ref[at : at + HEAD_ROWS, :] = head_ref[...]
     half = away_ref.shape[0]
     core = lax.axis_index("c")
@@ -614,20 +636,23 @@
     )
 
     projected = dot(features, w_first.astype(BF)).astype(BF)
+    turned = features.T
+    turned = jnp.stack([turned] + [swap(turned, 2 * k) for k in range(1, 4)])
     if short_line():
-        around, passed = gather_all(projected, [(levels[1], 1), (levels[2], 2)])
+        around, passed, (turned,) = gather_all(
+            projected, [(levels[1], 1), (levels[2], 2)], [turned]
+        )
         levels[1:3] = passed
     else:
-        around, passed = gather_all(projected)
+        around, *unused = gather_all(projected)
         levels = [lax.all_to_all(levels[0], "z", 0, 0)]
     (summed_one,) = run(
         first_sum_kernel, [shape((tall, hidden), BF)], [near, far, *around], flops=work
     )
     if short_line():
-        around, passed = gather_all(summed_one, [(levels[3], 3)])
-        levels[3:] = passed
-    else:
-        around, passed = gather_all(summed_one)
+        around, levels[3:], unused = gather_all(summed_one, [(levels[3], 3)])
+    else:
+        around, *unused = gather_all(summed_one)
     summed_two, stats_one = run(
         functools.partial(layer_kernel, node_total, 0),
         [shape((tall, hidden), BF), shape((8, hidden))],
@@ -640,6 +665,19 @@
         [near, far, norm_params, stats_one, *around],
         flops=3 * work,
     )
+    if short_line():
+        mixed_shapes = [shape((inputs, rows))] + [shape((inputs, rows), BF)] * 3
+    else:
+        mixed_shapes = [shape((length, inputs, rows))]
+    mixed = run(
+        mix_kernel, mixed_shapes, [turned, swap(turned, 1), *levels], flops=2 * work
+    )
+    if short_line():
+        around, passed, unused = gather_all(summed_two, [(mixed[k], k) for k in range(1, 4)])
+        mixed = [mixed[0], *passed]
+    else:
+        around, *unused = gather_all(summed_two)
+        mixed = [lax.psum_scatter(mixed[0], "z", scatter_dimension=0)]
     packed, stats_two = run(
         functools.partial(head_kernel, node_total),
         [shape((HEAD_ROWS + EXTRA, rows), BF), shape((8, hidden))],
@@ -651,7 +689,7 @@
             head_bias[None],
             labels[None],
             train_mask[None],
-            *gather_all(summed_two)[0],
+            *around,
         ],
         scratch=[
             pltpu.VMEM((rows, LANES + 2 * hidden), F32),
@@ -676,18 +714,21 @@
         scratch=[pltpu.VMEM((8, LANES), F32), pltpu.VMEM((LANES, hidden), F32)],
         flops=work // 4,
     )
-    packed, second_grad, sums_one = run(
-        functools.partial(first_kernel, node_total),
-        [shape((hidden, rows), BF), shape((hidden, hidden)), shape((8, LANES))],
-        [w_second, norm_params, summed_one, stats_one, *spread_back(packed, levels, hidden)],
-        flops=work // 4,
-    )
     size = -(-(inputs_tall + hidden + HEAD_ROWS) // (8 * EXTRA)) * EXTRA
-    away, kept = run(
-        functools.partial(pile_kernel, inputs_tall),
-        [shape((4 * size, hidden), BF), shape((4 * size, hidden))],
-        [features.T, second_grad, head_grad, *spread_back(packed, levels, hidden)],
+    away, kept, sums_one = run(
+        functools.partial(first_kernel, node_total, inputs_tall, len(mixed)),
+        [shape((4 * size, hidden), BF), shape((4 * size, hidden)), shape((8, LANES))],
+        [
+            w_second,
+            norm_params,
+            summed_one,
+            stats_one,
+            head_grad,
+            *mixed,
+            *spread_back(packed, levels, hidden),
+        ],
         scratch=[pltpu.VMEM((8 * size, hidden), F32)],
+        flops=work,
     )
     matrices = (
         *(w_first, m_first, v_first, w_second, m_second, v_second),

time: 177 us -> 164 us (0.927)
  waiting for transfers between devices: 83.2 us -> 66.9 us
  starting transfers between devices: 68.9 us -> 71.2 us
    ppermute x44, waiting for transfers between devices: 48.2 us -> 25.6 us  [swap(): return lax.ppermute(block, PLANE, [(i, i ^ mask) for i in range(8)])]
    ppermute x24, waiting for transfers between devices: 35 us -> 41.3 us  [pass_line(): return lax.ppermute(block, 'z', [(i, i ^ mask) for i in range(4)])]
    pallas_call x21 -> x18, Pallas kernels: 18 us -> 18.7 us  [run(): pl.pallas_call(body, out_shape=tuple(outs), in_specs=[pl.BlockSpec(memory...]
  transfers between devices with their start and end apart: 68 -> 68, of which waited for: 49 -> 43; matrix products, arithmetic and copies ran while one was open for 1% -> 1% of each run, Pallas kernels for 3% -> 5%
where the time goes in v3:
time: 164 us
  starting transfers between devices  71.2 us (43%)
  waiting for transfers between devices  66.9 us (41%)
  Pallas kernels  18.7 us (11%)
  local copies, waits for them, and re-layouts  3.53 us (2%)
    ppermute x24, waiting for transfers between devices, pass_line(): return lax.ppermute(block, 'z', [(i, i ^ mask) for i in range(4)])  41.3 us
    ppermute x24, starting transfers between devices, pass_line(): return lax.ppermute(block, 'z', [(i, i ^ mask) for i in range(4)])  38.2 us
    ppermute x44, starting transfers between devices, swap(): return lax.ppermute(block, PLANE, [(i, i ^ mask) for i in range(8)])  33 us
    ppermute x44, waiting for transfers between devices, swap(): return lax.ppermute(block, PLANE, [(i, i ^ mask) for i in range(8)])  25.6 us
    pallas_call x18, Pallas kernels, run(): pl.pallas_call(body, out_shape=tuple(outs), in_specs=[pl.BlockSpec(memory...  18.7 us
  transfers between devices with their start and end apart: 68, of which 43 were waited for; matrix products, arithmetic and copies ran while one was open for 1% of the time, Pallas kernels for 5%

profile of v3, /device:TPU:0, one launch (start us, length us, event | category | flops | bytes accessed | tf_op | source)
XLA Modules:
  0.0 164.1 jit_solution(15056027108045768618)
XLA Ops:
  0.7 1.4 convolution_convert_fusion
  2.1 5.1 %collective-permute-start.2 = (bf16[128,256]{1,0:T(8,128)(2,1)S(1)}, bf16[128,256]{1,0:T(8,128)(2,1)S(1)}, u32[]{:S(2)}, u32[]{:S(2)}) collective-permute-start(bf16[128,256]{1,0:T(8,128)(2,1)S(1)} %convolution_convert_fusion), channel_id=1, source_target_pairs={{0,24},{8,16},{16,8},{24,0},{1,25},{9,17},{17,9},{25,1},{2,26},{10... | collective-permute-start | bytes 196616 | tf_op jit(solution)/shard_map/ppermute | solution.py:76
  7.9 1.7 %collective-permute-start.4 = (bf16[602,128]{1,0:T(8,128)(2,1)S(1)}, bf16[602,128]{1,0:T(8,128)(2,1)S(1)}, u32[]{:S(2)}, u32[]{:S(2)}) collective-permute-start(bf16[602,128]{1,0:T(8,128)(2,1)S(1)} %bitcast.51), channel_id=1, source_target_pairs={{0,4},{1,5},{2,6},{3,7},{4,0},{5,1},{6,2},{7,3},{8,12},{9,13},{10,... | collective-permute-start | bytes 462344 | tf_op jit(solution)/shard_map/ppermute | solution.py:72
  9.5 1.5 collective-permute-start.3
  11.0 1.6 collective-permute-start.5
  16.0 1.9 %collective-permute-done.5 = bf16[602,128]{1,0:T(8,128)(2,1)S(1)} collective-permute-done((bf16[602,128]{1,0:T(8,128)(2,1)S(1)}, bf16[602,128]{1,0:T(8,128)(2,1)S(1)}, u32[]{:S(2)}, u32[]{:S(2)}) %collective-permute-start.5) | collective-permute-done | bytes 154144 | tf_op jit(solution)/shard_map/ppermute | solution.py:72
  18.0 2.2 %collective-permute-start.8 = (bf16[4,128,256]{2,1,0:T(8,128)(2,1)S(1)}, bf16[4,128,256]{2,1,0:T(8,128)(2,1)S(1)}, u32[]{:S(2)}, u32[]{:S(2)}) collective-permute-start(bf16[4,128,256]{2,1,0:T(8,128)(2,1)S(1)} %pad_maximum_fusion.3.refs_0_), channel_id=1, source_target_pairs={{0,6},{1,7},{2,4},{3,5},{4,2},{5,3},{6,0},{7,1},{8,14},{9,15},{10,... | collective-permute-start | bytes 786440 | tf_op jit(solution)/shard_map/ppermute | solution.py:72
  20.2 2.3 %collective-permute-start.10 = (bf16[128,1024]{1,0:T(8,128)(2,1)S(1)}, bf16[128,1024]{1,0:T(8,128)(2,1)S(1)}, u32[]{:S(2)}, u32[]{:S(2)}) collective-permute-start(bf16[128,1024]{1,0:T(8,128)(2,1)S(1)} %get-tuple-element.81), channel_id=1, source_target_pairs={{0,16},{8,24},{16,0},{24,8},{1,17},{9,25},{17,1},{25,9},{2,18},{10... | collective-permute-start | bytes 786440 | tf_op jit(solution)/shard_map/ppermute | solution.py:76
  22.5 1.7 %collective-permute-start.9 = (bf16[128,1024]{1,0:T(8,128)(2,1)S(1)}, bf16[128,1024]{1,0:T(8,128)(2,1)S(1)}, u32[]{:S(2)}, u32[]{:S(2)}) collective-permute-start(bf16[128,1024]{1,0:T(8,128)(2,1)S(1)} %get-tuple-element.79), channel_id=1, source_target_pairs={{0,8},{8,0},{16,24},{24,16},{1,9},{9,1},{17,25},{25,17},{2,10},{10... | collective-permute-start | bytes 786440 | tf_op jit(solution)/shard_map/ppermute | solution.py:76
  26.9 5.5 %collective-permute-done.10.refs_2_.refs_6_ = bf16[128,1024]{1,0:T(8,128)(2,1)S(1)} collective-permute-done((bf16[128,1024]{1,0:T(8,128)(2,1)S(1)}, bf16[128,1024]{1,0:T(8,128)(2,1)S(1)}, u32[]{:S(2)}, u32[]{:S(2)}) %collective-permute-start.10) | collective-permute-done | bytes 262176 | tf_op jit(solution)/shard_map/ppermute | solution.py:76
  35.3 3.1 %collective-permute-start.17 = (bf16[144,256]{1,0:T(8,128)(2,1)S(1)}, bf16[144,256]{1,0:T(8,128)(2,1)S(1)}, u32[]{:S(2)}, u32[]{:S(2)}) collective-permute-start(bf16[144,256]{1,0:T(8,128)(2,1)S(1)} %shard_map.324.summed_ref), channel_id=1, source_target_pairs={{0,24},{8,16},{16,8},{24,0},{1,25},{9,17},{17,9},{25,1},{2,26},{10... | collective-permute-start | bytes 221192 | tf_op jit(solution)/shard_map/ppermute | solution.py:76
  39.8 2.7 %collective-permute-done.17 = bf16[144,256]{1,0:T(8,128)(2,1)S(1)} collective-permute-done((bf16[144,256]{1,0:T(8,128)(2,1)S(1)}, bf16[144,256]{1,0:T(8,128)(2,1)S(1)}, u32[]{:S(2)}, u32[]{:S(2)}) %collective-permute-start.17) | collective-permute-done | bytes 73760 | tf_op jit(solution)/shard_map/ppermute | solution.py:76
  42.5 2.8 %collective-permute-done.16 = bf16[144,256]{1,0:T(8,128)(2,1)S(1)} collective-permute-done((bf16[144,256]{1,0:T(8,128)(2,1)S(1)}, bf16[144,256]{1,0:T(8,128)(2,1)S(1)}, u32[]{:S(2)}, u32[]{:S(2)}) %collective-permute-start.16) | collective-permute-done | bytes 73760 | tf_op jit(solution)/shard_map/ppermute | solution.py:76
  45.3 1.7 %collective-permute-start.20 = (bf16[4,144,256]{2,1,0:T(8,128)(2,1)S(1)}, bf16[4,144,256]{2,1,0:T(8,128)(2,1)S(1)}, u32[]{:S(2)}, u32[]{:S(2)}) collective-permute-start(bf16[4,144,256]{2,1,0:T(8,128)(2,1)S(1)} %pad_maximum_fusion.1.refs_0_), channel_id=1, source_target_pairs={{0,6},{1,7},{2,4},{3,5},{4,2},{5,3},{6,0},{7,1},{8,14},{9,15},{10,... | collective-permute-start | bytes 884744 | tf_op jit(solution)/shard_map/ppermute | solution.py:72
  47.3 1.5 collective-permute-start.18
  48.8 2.1 %collective-permute-start.21 = (bf16[128,1024]{1,0:T(8,128)(2,1)S(1)}, bf16[128,1024]{1,0:T(8,128)(2,1)S(1)}, u32[]{:S(2)}, u32[]{:S(2)}) collective-permute-start(bf16[128,1024]{1,0:T(8,128)(2,1)S(1)} %get-tuple-element.84), channel_id=1, source_target_pairs={{0,24},{8,16},{16,8},{24,0},{1,25},{9,17},{17,9},{25,1},{2,26},{10... | collective-permute-start | bytes 786440 | tf_op jit(solution)/shard_map/ppermute | solution.py:76
  51.3 6.4 %collective-permute-done.21.refs_3_.refs_7_ = bf16[128,1024]{1,0:T(8,128)(2,1)S(1)} collective-permute-done((bf16[128,1024]{1,0:T(8,128)(2,1)S(1)}, bf16[128,1024]{1,0:T(8,128)(2,1)S(1)}, u32[]{:S(2)}, u32[]{:S(2)}) %collective-permute-start.21) | collective-permute-done | bytes 262176 | tf_op jit(solution)/shard_map/ppermute | solution.py:76
  58.2 2.8 %collective-permute-done.19.refs_2_ = bf16[4,144,256]{2,1,0:T(8,128)(2,1)S(1)} collective-permute-done((bf16[4,144,256]{2,1,0:T(8,128)(2,1)S(1)}, bf16[4,144,256]{2,1,0:T(8,128)(2,1)S(1)}, u32[]{:S(2)}, u32[]{:S(2)}) %collective-permute-start.19) | collective-permute-done | bytes 294944 | tf_op jit(solution)/shard_map/ppermute | solution.py:72
  63.1 2.6 %shard_map.325 = (bf16[144,256]{1,0:T(8,128)(2,1)S(1)}, f32[8,256]{1,0:T(8,128)S(1)}) custom-call(bf16[128,2048]{1,0:T(8,128)(2,1)S(1)} %get-tuple-element.75.near_ref, bf16[128,2048]{1,0:T(8,128)(2,1)S(1)} %get-tuple-element.76.far_ref, f32[256,256]{1,0:T(8,128)S(1)} %copy-done, f32[4,256]{1,0:T(4,128)S(1)} %copy-done.8, ...), custom_call_target="tpu_custom_call" | custom-call | flops 805306368 | bytes 3756032 | tf_op jit(solution)/shard_map/pallas_call | solution.py:59
  65.7 1.8 %collective-permute-start.28 = (bf16[144,256]{1,0:T(8,128)(2,1)S(1)}, bf16[144,256]{1,0:T(8,128)(2,1)S(1)}, u32[]{:S(2)}, u32[]{:S(2)}) collective-permute-start(bf16[144,256]{1,0:T(8,128)(2,1)S(1)} %get-tuple-element.86.summed_ref), channel_id=1, source_target_pairs={{0,24},{8,16},{16,8},{24,0},{1,25},{9,17},{17,9},{25,1},{2,26},{10... | collective-permute-start | bytes 221192 | tf_op jit(solution)/shard_map/ppermute | solution.py:76
  68.6 1.6 collective-permute-start.26
  70.3 1.4 shard_map.326
  72.8 2.9 %collective-permute-done.27 = bf16[144,256]{1,0:T(8,128)(2,1)S(1)} collective-permute-done((bf16[144,256]{1,0:T(8,128)(2,1)S(1)}, bf16[144,256]{1,0:T(8,128)(2,1)S(1)}, u32[]{:S(2)}, u32[]{:S(2)}) %collective-permute-start.27) | collective-permute-done | bytes 73760 | tf_op jit(solution)/shard_map/ppermute | solution.py:76
  75.8 1.6 collective-permute-start.31
  77.8 1.5 collective-permute-start.29
  79.3 1.7 %collective-permute-start.34 = (bf16[602,128]{1,0:T(8,128)(2,1)S(1)}, bf16[602,128]{1,0:T(8,128)(2,1)S(1)}, u32[]{:S(2)}, u32[]{:S(2)}) collective-permute-start(bf16[602,128]{1,0:T(8,128)(2,1)S(1)} %get-tuple-element.95), channel_id=1, source_target_pairs={{0,16},{8,24},{16,0},{24,8},{1,17},{9,25},{17,1},{25,9},{2,18},{10... | collective-permute-start | bytes 462344 | tf_op jit(solution)/shard_map/ppermute | solution.py:76
  81.3 2.3 %collective-permute-start.35 = (bf16[602,128]{1,0:T(8,128)(2,1)S(1)}, bf16[602,128]{1,0:T(8,128)(2,1)S(1)}, u32[]{:S(2)}, u32[]{:S(2)}) collective-permute-start(bf16[602,128]{1,0:T(8,128)(2,1)S(1)} %get-tuple-element.97), channel_id=1, source_target_pairs={{0,24},{8,16},{16,8},{24,0},{1,25},{9,17},{17,9},{25,1},{2,26},{10... | collective-permute-start | bytes 462344 | tf_op jit(solution)/shard_map/ppermute | solution.py:76
  83.7 9.2 %collective-permute-done.34.refs_2_ = bf16[602,128]{1,0:T(8,128)(2,1)S(1)} collective-permute-done((bf16[602,128]{1,0:T(8,128)(2,1)S(1)}, bf16[602,128]{1,0:T(8,128)(2,1)S(1)}, u32[]{:S(2)}, u32[]{:S(2)}) %collective-permute-start.34) | collective-permute-done | bytes 154144 | tf_op jit(solution)/shard_map/ppermute | solution.py:76
  96.4 5.1 %shard_map.327 = (bf16[64,128]{1,0:T(8,128)(2,1)S(1)}, f32[8,256]{1,0:T(8,128)S(1)}) custom-call(bf16[128,2048]{1,0:T(8,128)(2,1)S(1)} %get-tuple-element.75.near_ref, bf16[128,2048]{1,0:T(8,128)(2,1)S(1)} %get-tuple-element.76.far_ref, f32[41,256]{1,0:T(8,128)S(1)} %bitcast.43, f32[4,256]{1,0:T(4,128)S(1)} %copy-done.8, f32[1,41]{1,0:T(1,128)S(1)} %bitcast.48, ...), custom_call_target="tpu_custom_call" | custom-call | flops 1073741824 | bytes 3480064 | tf_op jit(solution)/shard_map/pallas_call | solution.py:59
  101.6 1.7 %collective-permute-start.42 = (bf16[64,128]{1,0:T(8,128)(2,1)S(1)}, bf16[64,128]{1,0:T(8,128)(2,1)S(1)}, u32[]{:S(2)}, u32[]{:S(2)}) collective-permute-start(bf16[64,128]{1,0:T(8,128)(2,1)S(1)} %get-tuple-element.101.refs_0_), channel_id=1, source_target_pairs={{0,24},{8,16},{16,8},{24,0},{1,25},{9,17},{17,9},{25,1},{2,26},{10... | collective-permute-start | bytes 49160 | tf_op jit(solution)/shard_map/ppermute | solution.py:76
  103.2 2.1 %collective-permute-start.41 = (bf16[64,128]{1,0:T(8,128)(2,1)S(1)}, bf16[64,128]{1,0:T(8,128)(2,1)S(1)}, u32[]{:S(2)}, u32[]{:S(2)}) collective-permute-start(bf16[64,128]{1,0:T(8,128)(2,1)S(1)} %get-tuple-element.101.refs_0_), channel_id=1, source_target_pairs={{0,16},{8,24},{16,0},{24,8},{1,17},{9,25},{17,1},{25,9},{2,18},{10... | collective-permute-start | bytes 49160 | tf_op jit(solution)/shard_map/ppermute | solution.py:76
  111.3 1.7 %collective-permute-start.45 = (bf16[64,128]{1,0:T(8,128)(2,1)S(1)}, bf16[64,128]{1,0:T(8,128)(2,1)S(1)}, u32[]{:S(2)}, u32[]{:S(2)}) collective-permute-start(bf16[64,128]{1,0:T(8,128)(2,1)S(1)} %get-tuple-element.104), channel_id=1, source_target_pairs={{0,4},{1,5},{2,6},{3,7},{4,0},{5,1},{6,2},{7,3},{8,12},{9,13},{10,... | collective-permute-start | bytes 49160 | tf_op jit(solution)/shard_map/ppermute | solution.py:72
  114.2 3.3 %shard_map.328.slopes_ref = f32[128,512]{1,0:T(8,128)S(1)} custom-call(bf16[128,2048]{1,0:T(8,128)(2,1)S(1)} %get-tuple-element.75.near_ref, bf16[128,2048]{1,0:T(8,128)(2,1)S(1)} %get-tuple-element.76.far_ref, f32[4,256]{1,0:T(4,128)S(1)} %copy-done.8, f32[8,256]{1,0:T(8,128)S(1)} %get-tuple-element.100.stats_ref, ...), custom_call_target="tpu_custom_call" | custom-call | flops 805306368 | bytes 3682304 | tf_op jit(solution)/shard_map/pallas_call | solution.py:59
  118.1 1.9 %collective-permute-start.49 = (bf16[272,128]{1,0:T(8,128)(2,1)S(1)}, bf16[272,128]{1,0:T(8,128)(2,1)S(1)}, u32[]{:S(2)}, u32[]{:S(2)}) collective-permute-start(bf16[272,128]{1,0:T(8,128)(2,1)S(1)} %get-tuple-element.112.refs_0_), channel_id=1, source_target_pairs={{0,24},{8,16},{16,8},{24,0},{1,25},{9,17},{17,9},{25,1},{2,26},{10... | collective-permute-start | bytes 208904 | tf_op jit(solution)/shard_map/ppermute | solution.py:76
  120.3 2.2 %collective-permute-start.47 = (bf16[272,128]{1,0:T(8,128)(2,1)S(1)}, bf16[272,128]{1,0:T(8,128)(2,1)S(1)}, u32[]{:S(2)}, u32[]{:S(2)}) collective-permute-start(bf16[272,128]{1,0:T(8,128)(2,1)S(1)} %get-tuple-element.112.refs_0_), channel_id=1, source_target_pairs={{0,8},{8,0},{16,24},{24,16},{1,9},{9,1},{17,25},{25,17},{2,10},{10... | collective-permute-start | bytes 208904 | tf_op jit(solution)/shard_map/ppermute | solution.py:76
  122.6 2.3 %collective-permute-done.49.refs_3_ = bf16[272,128]{1,0:T(8,128)(2,1)S(1)} collective-permute-done((bf16[272,128]{1,0:T(8,128)(2,1)S(1)}, bf16[272,128]{1,0:T(8,128)(2,1)S(1)}, u32[]{:S(2)}, u32[]{:S(2)}) %collective-permute-start.49) | collective-permute-done | bytes 69664 | tf_op jit(solution)/shard_map/ppermute | solution.py:76
  124.9 2.1 %collective-permute-done.48.refs_2_ = bf16[272,128]{1,0:T(8,128)(2,1)S(1)} collective-permute-done((bf16[272,128]{1,0:T(8,128)(2,1)S(1)}, bf16[272,128]{1,0:T(8,128)(2,1)S(1)}, u32[]{:S(2)}, u32[]{:S(2)}) %collective-permute-start.48) | collective-permute-done | bytes 69664 | tf_op jit(solution)/shard_map/ppermute | solution.py:76
  129.7 1.7 %collective-permute-start.52 = (bf16[272,128]{1,0:T(8,128)(2,1)S(1)}, bf16[272,128]{1,0:T(8,128)(2,1)S(1)}, u32[]{:S(2)}, u32[]{:S(2)}) collective-permute-start(bf16[272,128]{1,0:T(8,128)(2,1)S(1)} %get-tuple-element.115), channel_id=1, source_target_pairs={{0,4},{1,5},{2,6},{3,7},{4,0},{5,1},{6,2},{7,3},{8,12},{9,13},{10,... | collective-permute-start | bytes 208904 | tf_op jit(solution)/shard_map/ppermute | solution.py:72
  134.0 2.6 %collective-permute-done.53.refs_7_ = bf16[272,128]{1,0:T(8,128)(2,1)S(1)} collective-permute-done((bf16[272,128]{1,0:T(8,128)(2,1)S(1)}, bf16[272,128]{1,0:T(8,128)(2,1)S(1)}, u32[]{:S(2)}, u32[]{:S(2)}) %collective-permute-start.53) | collective-permute-done | bytes 69664 | tf_op jit(solution)/shard_map/ppermute | solution.py:72
  139.4 1.4 collective-permute-start.56
  140.8 1.7 %collective-permute-start.57 = (bf16[128,256]{1,0:T(8,128)(2,1)S(1)}, bf16[128,256]{1,0:T(8,128)(2,1)S(1)}, u32[]{:S(2)}, u32[]{:S(2)}) collective-permute-start(bf16[128,256]{1,0:T(8,128)(2,1)S(1)} %get-tuple-element.122), channel_id=1, source_target_pairs={{0,6},{1,7},{2,4},{3,5},{4,2},{5,3},{6,0},{7,1},{8,14},{9,15},{10,... | collective-permute-start | bytes 196616 | tf_op jit(solution)/shard_map/ppermute | solution.py:72
  143.7 2.3 %collective-permute-done.57.refs_2_ = bf16[128,256]{1,0:T(8,128)(2,1)S(1)} collective-permute-done((bf16[128,256]{1,0:T(8,128)(2,1)S(1)}, bf16[128,256]{1,0:T(8,128)(2,1)S(1)}, u32[]{:S(2)}, u32[]{:S(2)}) %collective-permute-start.57) | collective-permute-done | bytes 65568 | tf_op jit(solution)/shard_map/ppermute | solution.py:72
  146.0 1.7 %collective-permute-start.60 = (bf16[128,256]{1,0:T(8,128)(2,1)S(1)}, bf16[128,256]{1,0:T(8,128)(2,1)S(1)}, u32[]{:S(2)}, u32[]{:S(2)}) collective-permute-start(bf16[128,256]{1,0:T(8,128)(2,1)S(1)} %shard_map.338.own_ref), channel_id=1, source_target_pairs={{0,24},{8,16},{16,8},{24,0},{1,25},{9,17},{17,9},{25,1},{2,26},{10... | collective-permute-start | bytes 196616 | tf_op jit(solution)/shard_map/ppermute | solution.py:76
  147.7 2.8 %collective-permute-start.58 = (bf16[128,256]{1,0:T(8,128)(2,1)S(1)}, bf16[128,256]{1,0:T(8,128)(2,1)S(1)}, u32[]{:S(2)}, u32[]{:S(2)}) collective-permute-start(bf16[128,256]{1,0:T(8,128)(2,1)S(1)} %shard_map.338.own_ref), channel_id=1, source_target_pairs={{0,8},{8,0},{16,24},{24,16},{1,9},{9,1},{17,25},{25,17},{2,10},{10... | collective-permute-start | bytes 196616 | tf_op jit(solution)/shard_map/ppermute | solution.py:76
  152.3 1.5 collective-permute-done.59.refs_1_
  153.9 1.7 %collective-permute-start.63 = (bf16[128,256]{1,0:T(8,128)(2,1)S(1)}, bf16[128,256]{1,0:T(8,128)(2,1)S(1)}, u32[]{:S(2)}, u32[]{:S(2)}) collective-permute-start(bf16[128,256]{1,0:T(8,128)(2,1)S(1)} %shard_map.339.refs_0_), channel_id=1, source_target_pairs={{0,6},{1,7},{2,4},{3,5},{4,2},{5,3},{6,0},{7,1},{8,14},{9,15},{10,... | collective-permute-start | bytes 196616 | tf_op jit(solution)/shard_map/ppermute | solution.py:72
  157.4 2.2 %collective-permute-done.63.refs_3_ = bf16[128,256]{1,0:T(8,128)(2,1)S(1)} collective-permute-done((bf16[128,256]{1,0:T(8,128)(2,1)S(1)}, bf16[128,256]{1,0:T(8,128)(2,1)S(1)}, u32[]{:S(2)}, u32[]{:S(2)}) %collective-permute-start.63) | collective-permute-done | bytes 65568 | tf_op jit(solution)/shard_map/ppermute | solution.py:72
  161.7 2.4 %shard_map.340 = (f32[602,256]{1,0:T(8,128)}, f32[602,256]{1,0:T(8,128)}, f32[602,256]{1,0:T(8,128)}, f32[256,256]{1,0:T(8,128)}, f32[256,256]{1,0:T(8,128)}, /*...) custom-call(bf16[128,256]{1,0:T(8,128)(2,1)S(1)} %shard_map.339.refs_0_, ...), custom_call_target="tpu_custom_call" | custom-call | bytes 6047744 | tf_op jit(solution)/shard_map/pallas_call | solution.py:59
  (158 shorter events, 43.8 us)
Async XLA Ops:
  2.1 8.9 %collective-permute-start.2 = (bf16[128,256]{1,0:T(8,128)(2,1)S(1)}, bf16[128,256]{1,0:T(8,128)(2,1)S(1)}, u32[]{:S(2)}, u32[]{:S(2)}) collective-permute-start(bf16[128,256]{1,0:T(8,128)(2,1)S(1)} %convolution_convert_fusion), channel_id=1, source_target_pairs={{0,24},{8,16},{16,8},{24,0},{1,25},{9,17},{17,9},{25,1},{2,26},{10... | collective-permute-start | bytes 196616 | tf_op jit(solution)/shard_map/ppermute | solution.py:76
  7.2 7.6 %collective-permute-start.1 = (bf16[128,256]{1,0:T(8,128)(2,1)S(1)}, bf16[128,256]{1,0:T(8,128)(2,1)S(1)}, u32[]{:S(2)}, u32[]{:S(2)}) collective-permute-start(bf16[128,256]{1,0:T(8,128)(2,1)S(1)} %convolution_convert_fusion), channel_id=1, source_target_pairs={{0,16},{8,24},{16,0},{24,8},{1,17},{9,25},{17,1},{25,9},{2,18},{10... | collective-permute-start | bytes 196616 | tf_op jit(solution)/shard_map/ppermute | solution.py:76
  7.2 7.6 %collective-permute-start = (bf16[128,256]{1,0:T(8,128)(2,1)S(1)}, bf16[128,256]{1,0:T(8,128)(2,1)S(1)}, u32[]{:S(2)}, u32[]{:S(2)}) collective-permute-start(bf16[128,256]{1,0:T(8,128)(2,1)S(1)} %convolution_convert_fusion), channel_id=1, source_target_pairs={{0,8},{8,0},{16,24},{24,16},{1,9},{9,1},{17,25},{25,17},{2,10},{10... | collective-permute-start | bytes 196616 | tf_op jit(solution)/shard_map/ppermute | solution.py:76
  7.9 7.0 %collective-permute-start.4 = (bf16[602,128]{1,0:T(8,128)(2,1)S(1)}, bf16[602,128]{1,0:T(8,128)(2,1)S(1)}, u32[]{:S(2)}, u32[]{:S(2)}) collective-permute-start(bf16[602,128]{1,0:T(8,128)(2,1)S(1)} %bitcast.51), channel_id=1, source_target_pairs={{0,4},{1,5},{2,6},{3,7},{4,0},{5,1},{6,2},{7,3},{8,12},{9,13},{10,... | collective-permute-start | bytes 462344 | tf_op jit(solution)/shard_map/ppermute | solution.py:72
  9.5 6.4 %collective-permute-start.3 = (bf16[602,128]{1,0:T(8,128)(2,1)S(1)}, bf16[602,128]{1,0:T(8,128)(2,1)S(1)}, u32[]{:S(2)}, u32[]{:S(2)}) collective-permute-start(bf16[602,128]{1,0:T(8,128)(2,1)S(1)} %bitcast.52), channel_id=1, source_target_pairs={{0,2},{1,3},{2,0},{3,1},{4,6},{5,7},{6,4},{7,5},{8,10},{9,11},{10,... | collective-permute-start | bytes 462344 | tf_op jit(solution)/shard_map/ppermute | solution.py:72
  11.0 6.9 %collective-permute-start.5 = (bf16[602,128]{1,0:T(8,128)(2,1)S(1)}, bf16[602,128]{1,0:T(8,128)(2,1)S(1)}, u32[]{:S(2)}, u32[]{:S(2)}) collective-permute-start(bf16[602,128]{1,0:T(8,128)(2,1)S(1)} %bitcast.53), channel_id=1, source_target_pairs={{0,6},{1,7},{2,4},{3,5},{4,2},{5,3},{6,0},{7,1},{8,14},{9,15},{10,... | collective-permute-start | bytes 462344 | tf_op jit(solution)/shard_map/ppermute | solution.py:72
  18.0 8.9 %collective-permute-start.8 = (bf16[4,128,256]{2,1,0:T(8,128)(2,1)S(1)}, bf16[4,128,256]{2,1,0:T(8,128)(2,1)S(1)}, u32[]{:S(2)}, u32[]{:S(2)}) collective-permute-start(bf16[4,128,256]{2,1,0:T(8,128)(2,1)S(1)} %pad_maximum_fusion.3.refs_0_), channel_id=1, source_target_pairs={{0,6},{1,7},{2,4},{3,5},{4,2},{5,3},{6,0},{7,1},{8,14},{9,15},{10,... | collective-permute-start | bytes 786440 | tf_op jit(solution)/shard_map/ppermute | solution.py:72
  20.2 12.2 %collective-permute-start.10 = (bf16[128,1024]{1,0:T(8,128)(2,1)S(1)}, bf16[128,1024]{1,0:T(8,128)(2,1)S(1)}, u32[]{:S(2)}, u32[]{:S(2)}) collective-permute-start(bf16[128,1024]{1,0:T(8,128)(2,1)S(1)} %get-tuple-element.81), channel_id=1, source_target_pairs={{0,16},{8,24},{16,0},{24,8},{1,17},{9,25},{17,1},{25,9},{2,18},{10... | collective-permute-start | bytes 786440 | tf_op jit(solution)/shard_map/ppermute | solution.py:76
  22.5 10.0 %collective-permute-start.9 = (bf16[128,1024]{1,0:T(8,128)(2,1)S(1)}, bf16[128,1024]{1,0:T(8,128)(2,1)S(1)}, u32[]{:S(2)}, u32[]{:S(2)}) collective-permute-start(bf16[128,1024]{1,0:T(8,128)(2,1)S(1)} %get-tuple-element.79), channel_id=1, source_target_pairs={{0,8},{8,0},{16,24},{24,16},{1,9},{9,1},{17,25},{25,17},{2,10},{10... | collective-permute-start | bytes 786440 | tf_op jit(solution)/shard_map/ppermute | solution.py:76
  24.2 8.3 %collective-permute-start.7 = (bf16[4,128,256]{2,1,0:T(8,128)(2,1)S(1)}, bf16[4,128,256]{2,1,0:T(8,128)(2,1)S(1)}, u32[]{:S(2)}, u32[]{:S(2)}) collective-permute-start(bf16[4,128,256]{2,1,0:T(8,128)(2,1)S(1)} %pad_maximum_fusion.3.refs_0_), channel_id=1, source_target_pairs={{0,4},{1,5},{2,6},{3,7},{4,0},{5,1},{6,2},{7,3},{8,12},{9,13},{10,... | collective-permute-start | bytes 786440 | tf_op jit(solution)/shard_map/ppermute | solution.py:72
  24.7 7.8 %collective-permute-start.6 = (bf16[4,128,256]{2,1,0:T(8,128)(2,1)S(1)}, bf16[4,128,256]{2,1,0:T(8,128)(2,1)S(1)}, u32[]{:S(2)}, u32[]{:S(2)}) collective-permute-start(bf16[4,128,256]{2,1,0:T(8,128)(2,1)S(1)} %pad_maximum_fusion.3.refs_0_), channel_id=1, source_target_pairs={{0,2},{1,3},{2,0},{3,1},{4,6},{5,7},{6,4},{7,5},{8,10},{9,11},{10,... | collective-permute-start | bytes 786440 | tf_op jit(solution)/shard_map/ppermute | solution.py:72
  26.9 6.2 %collective-permute-start.11 = (bf16[4,128,256]{2,1,0:T(8,128)(2,1)S(1)}, bf16[4,128,256]{2,1,0:T(8,128)(2,1)S(1)}, u32[]{:S(2)}, u32[]{:S(2)}) collective-permute-start(bf16[4,128,256]{2,1,0:T(8,128)(2,1)S(1)} %pad_maximum_fusion.3.refs_0_), channel_id=1, source_target_pairs={{0,1},{1,0},{2,3},{3,2},{4,5},{5,4},{6,7},{7,6},{8,9},{9,8},{10,11... | collective-permute-start | bytes 786440 | tf_op jit(solution)/shard_map/ppermute | solution.py:72
  35.3 7.2 %collective-permute-start.17 = (bf16[144,256]{1,0:T(8,128)(2,1)S(1)}, bf16[144,256]{1,0:T(8,128)(2,1)S(1)}, u32[]{:S(2)}, u32[]{:S(2)}) collective-permute-start(bf16[144,256]{1,0:T(8,128)(2,1)S(1)} %shard_map.324.summed_ref), channel_id=1, source_target_pairs={{0,24},{8,16},{16,8},{24,0},{1,25},{9,17},{17,9},{25,1},{2,26},{10... | collective-permute-start | bytes 221192 | tf_op jit(solution)/shard_map/ppermute | solution.py:76
  38.5 6.8 %collective-permute-start.16 = (bf16[144,256]{1,0:T(8,128)(2,1)S(1)}, bf16[144,256]{1,0:T(8,128)(2,1)S(1)}, u32[]{:S(2)}, u32[]{:S(2)}) collective-permute-start(bf16[144,256]{1,0:T(8,128)(2,1)S(1)} %shard_map.324.summed_ref), channel_id=1, source_target_pairs={{0,16},{8,24},{16,0},{24,8},{1,17},{9,25},{17,1},{25,9},{2,18},{10... | collective-permute-start | bytes 221192 | tf_op jit(solution)/shard_map/ppermute | solution.py:76
  38.5 6.8 %collective-permute-start.15 = (bf16[144,256]{1,0:T(8,128)(2,1)S(1)}, bf16[144,256]{1,0:T(8,128)(2,1)S(1)}, u32[]{:S(2)}, u32[]{:S(2)}) collective-permute-start(bf16[144,256]{1,0:T(8,128)(2,1)S(1)} %shard_map.324.summed_ref), channel_id=1, source_target_pairs={{0,8},{8,0},{16,24},{24,16},{1,9},{9,1},{17,25},{25,17},{2,10},{10... | collective-permute-start | bytes 221192 | tf_op jit(solution)/shard_map/ppermute | solution.py:76
  45.3 12.5 %collective-permute-start.20 = (bf16[4,144,256]{2,1,0:T(8,128)(2,1)S(1)}, bf16[4,144,256]{2,1,0:T(8,128)(2,1)S(1)}, u32[]{:S(2)}, u32[]{:S(2)}) collective-permute-start(bf16[4,144,256]{2,1,0:T(8,128)(2,1)S(1)} %pad_maximum_fusion.1.refs_0_), channel_id=1, source_target_pairs={{0,6},{1,7},{2,4},{3,5},{4,2},{5,3},{6,0},{7,1},{8,14},{9,15},{10,... | collective-permute-start | bytes 884744 | tf_op jit(solution)/shard_map/ppermute | solution.py:72
  47.0 14.1 %collective-permute-start.19 = (bf16[4,144,256]{2,1,0:T(8,128)(2,1)S(1)}, bf16[4,144,256]{2,1,0:T(8,128)(2,1)S(1)}, u32[]{:S(2)}, u32[]{:S(2)}) collective-permute-start(bf16[4,144,256]{2,1,0:T(8,128)(2,1)S(1)} %pad_maximum_fusion.1.refs_0_), channel_id=1, source_target_pairs={{0,4},{1,5},{2,6},{3,7},{4,0},{5,1},{6,2},{7,3},{8,12},{9,13},{10,... | collective-permute-start | bytes 884744 | tf_op jit(solution)/shard_map/ppermute | solution.py:72
  47.3 13.8 %collective-permute-start.18 = (bf16[4,144,256]{2,1,0:T(8,128)(2,1)S(1)}, bf16[4,144,256]{2,1,0:T(8,128)(2,1)S(1)}, u32[]{:S(2)}, u32[]{:S(2)}) collective-permute-start(bf16[4,144,256]{2,1,0:T(8,128)(2,1)S(1)} %pad_maximum_fusion.1.refs_0_), channel_id=1, source_target_pairs={{0,2},{1,3},{2,0},{3,1},{4,6},{5,7},{6,4},{7,5},{8,10},{9,11},{10,... | collective-permute-start | bytes 884744 | tf_op jit(solution)/shard_map/ppermute | solution.py:72
  48.8 8.9 %collective-permute-start.21 = (bf16[128,1024]{1,0:T(8,128)(2,1)S(1)}, bf16[128,1024]{1,0:T(8,128)(2,1)S(1)}, u32[]{:S(2)}, u32[]{:S(2)}) collective-permute-start(bf16[128,1024]{1,0:T(8,128)(2,1)S(1)} %get-tuple-element.84), channel_id=1, source_target_pairs={{0,24},{8,16},{16,8},{24,0},{1,25},{9,17},{17,9},{25,1},{2,26},{10... | collective-permute-start | bytes 786440 | tf_op jit(solution)/shard_map/ppermute | solution.py:76
  51.2 19.0 %collective-permute-start.32 = (bf16[4,602,128]{2,0,1:T(4,128)(2,1)S(1)}, bf16[4,602,128]{2,0,1:T(4,128)(2,1)S(1)}, u32[]{:S(2)}, u32[]{:S(2)}) collective-permute-start(bf16[4,602,128]{2,0,1:T(4,128)(2,1)S(1)} %copy.37), channel_id=1, source_target_pairs={{0,1},{1,0},{2,3},{3,2},{4,5},{5,4},{6,7},{7,6},{8,9},{9,8},{10,11... | collective-permute-start | bytes 1849352 | tf_op jit(solution)/shard_map/ppermute | solution.py:72
  65.7 7.1 %collective-permute-start.28 = (bf16[144,256]{1,0:T(8,128)(2,1)S(1)}, bf16[144,256]{1,0:T(8,128)(2,1)S(1)}, u32[]{:S(2)}, u32[]{:S(2)}) collective-permute-start(bf16[144,256]{1,0:T(8,128)(2,1)S(1)} %get-tuple-element.86.summed_ref), channel_id=1, source_target_pairs={{0,24},{8,16},{16,8},{24,0},{1,25},{9,17},{17,9},{25,1},{2,26},{10... | collective-permute-start | bytes 221192 | tf_op jit(solution)/shard_map/ppermute | solution.py:76
  67.5 8.1 %collective-permute-start.27 = (bf16[144,256]{1,0:T(8,128)(2,1)S(1)}, bf16[144,256]{1,0:T(8,128)(2,1)S(1)}, u32[]{:S(2)}, u32[]{:S(2)}) collective-permute-start(bf16[144,256]{1,0:T(8,128)(2,1)S(1)} %get-tuple-element.86.summed_ref), channel_id=1, source_target_pairs={{0,16},{8,24},{16,0},{24,8},{1,17},{9,25},{17,1},{25,9},{2,18},{10... | collective-permute-start | bytes 221192 | tf_op jit(solution)/shard_map/ppermute | solution.py:76
  68.6 7.1 %collective-permute-start.26 = (bf16[144,256]{1,0:T(8,128)(2,1)S(1)}, bf16[144,256]{1,0:T(8,128)(2,1)S(1)}, u32[]{:S(2)}, u32[]{:S(2)}) collective-permute-start(bf16[144,256]{1,0:T(8,128)(2,1)S(1)} %get-tuple-element.86.summed_ref), channel_id=1, source_target_pairs={{0,8},{8,0},{16,24},{24,16},{1,9},{9,1},{17,25},{25,17},{2,10},{10... | collective-permute-start | bytes 221192 | tf_op jit(solution)/shard_map/ppermute | solution.py:76
  75.7 5.6 %collective-permute-start.33 = (bf16[602,128]{1,0:T(8,128)(2,1)S(1)}, bf16[602,128]{1,0:T(8,128)(2,1)S(1)}, u32[]{:S(2)}, u32[]{:S(2)}) collective-permute-start(bf16[602,128]{1,0:T(8,128)(2,1)S(1)} %get-tuple-element.93), channel_id=1, source_target_pairs={{0,8},{8,0},{16,24},{24,16},{1,9},{9,1},{17,25},{25,17},{2,10},{10... | collective-permute-start | bytes 462344 | tf_op jit(solution)/shard_map/ppermute | solution.py:76
  75.8 17.1 %collective-permute-start.31 = (bf16[4,144,256]{2,1,0:T(8,128)(2,1)S(1)}, bf16[4,144,256]{2,1,0:T(8,128)(2,1)S(1)}, u32[]{:S(2)}, u32[]{:S(2)}) collective-permute-start(bf16[4,144,256]{2,1,0:T(8,128)(2,1)S(1)} %pad_maximum_fusion.2.refs_0_), channel_id=1, source_target_pairs={{0,6},{1,7},{2,4},{3,5},{4,2},{5,3},{6,0},{7,1},{8,14},{9,15},{10,... | collective-permute-start | bytes 884744 | tf_op jit(solution)/shard_map/ppermute | solution.py:72
  77.4 16.0 %collective-permute-start.30 = (bf16[4,144,256]{2,1,0:T(8,128)(2,1)S(1)}, bf16[4,144,256]{2,1,0:T(8,128)(2,1)S(1)}, u32[]{:S(2)}, u32[]{:S(2)}) collective-permute-start(bf16[4,144,256]{2,1,0:T(8,128)(2,1)S(1)} %pad_maximum_fusion.2.refs_0_), channel_id=1, source_target_pairs={{0,4},{1,5},{2,6},{3,7},{4,0},{5,1},{6,2},{7,3},{8,12},{9,13},{10,... | collective-permute-start | bytes 884744 | tf_op jit(solution)/shard_map/ppermute | solution.py:72
  77.8 15.6 %collective-permute-start.29 = (bf16[4,144,256]{2,1,0:T(8,128)(2,1)S(1)}, bf16[4,144,256]{2,1,0:T(8,128)(2,1)S(1)}, u32[]{:S(2)}, u32[]{:S(2)}) collective-permute-start(bf16[4,144,256]{2,1,0:T(8,128)(2,1)S(1)} %pad_maximum_fusion.2.refs_0_), channel_id=1, source_target_pairs={{0,2},{1,3},{2,0},{3,1},{4,6},{5,7},{6,4},{7,5},{8,10},{9,11},{10,... | collective-permute-start | bytes 884744 | tf_op jit(solution)/shard_map/ppermute | solution.py:72
  79.3 13.5 %collective-permute-start.34 = (bf16[602,128]{1,0:T(8,128)(2,1)S(1)}, bf16[602,128]{1,0:T(8,128)(2,1)S(1)}, u32[]{:S(2)}, u32[]{:S(2)}) collective-permute-start(bf16[602,128]{1,0:T(8,128)(2,1)S(1)} %get-tuple-element.95), channel_id=1, source_target_pairs={{0,16},{8,24},{16,0},{24,8},{1,17},{9,25},{17,1},{25,9},{2,18},{10... | collective-permute-start | bytes 462344 | tf_op jit(solution)/shard_map/ppermute | solution.py:76
  81.3 11.6 %collective-permute-start.35 = (bf16[602,128]{1,0:T(8,128)(2,1)S(1)}, bf16[602,128]{1,0:T(8,128)(2,1)S(1)}, u32[]{:S(2)}, u32[]{:S(2)}) collective-permute-start(bf16[602,128]{1,0:T(8,128)(2,1)S(1)} %get-tuple-element.97), channel_id=1, source_target_pairs={{0,24},{8,16},{16,8},{24,0},{1,25},{9,17},{17,9},{25,1},{2,26},{10... | collective-permute-start | bytes 462344 | tf_op jit(solution)/shard_map/ppermute | solution.py:76
  101.6 5.6 %collective-permute-start.42 = (bf16[64,128]{1,0:T(8,128)(2,1)S(1)}, bf16[64,128]{1,0:T(8,128)(2,1)S(1)}, u32[]{:S(2)}, u32[]{:S(2)}) collective-permute-start(bf16[64,128]{1,0:T(8,128)(2,1)S(1)} %get-tuple-element.101.refs_0_), channel_id=1, source_target_pairs={{0,24},{8,16},{16,8},{24,0},{1,25},{9,17},{17,9},{25,1},{2,26},{10... | collective-permute-start | bytes 49160 | tf_op jit(solution)/shard_map/ppermute | solution.py:76
  103.2 4.6 %collective-permute-start.41 = (bf16[64,128]{1,0:T(8,128)(2,1)S(1)}, bf16[64,128]{1,0:T(8,128)(2,1)S(1)}, u32[]{:S(2)}, u32[]{:S(2)}) collective-permute-start(bf16[64,128]{1,0:T(8,128)(2,1)S(1)} %get-tuple-element.101.refs_0_), channel_id=1, source_target_pairs={{0,16},{8,24},{16,0},{24,8},{1,17},{9,25},{17,1},{25,9},{2,18},{10... | collective-permute-start | bytes 49160 | tf_op jit(solution)/shard_map/ppermute | solution.py:76
  110.6 6.9 %collective-permute-start.44 = (bf16[64,128]{1,0:T(8,128)(2,1)S(1)}, bf16[64,128]{1,0:T(8,128)(2,1)S(1)}, u32[]{:S(2)}, u32[]{:S(2)}) collective-permute-start(bf16[64,128]{1,0:T(8,128)(2,1)S(1)} %get-tuple-element.103), channel_id=1, source_target_pairs={{0,2},{1,3},{2,0},{3,1},{4,6},{5,7},{6,4},{7,5},{8,10},{9,11},{10,... | collective-permute-start | bytes 49160 | tf_op jit(solution)/shard_map/ppermute | solution.py:72
  111.3 6.2 %collective-permute-start.45 = (bf16[64,128]{1,0:T(8,128)(2,1)S(1)}, bf16[64,128]{1,0:T(8,128)(2,1)S(1)}, u32[]{:S(2)}, u32[]{:S(2)}) collective-permute-start(bf16[64,128]{1,0:T(8,128)(2,1)S(1)} %get-tuple-element.104), channel_id=1, source_target_pairs={{0,4},{1,5},{2,6},{3,7},{4,0},{5,1},{6,2},{7,3},{8,12},{9,13},{10,... | collective-permute-start | bytes 49160 | tf_op jit(solution)/shard_map/ppermute | solution.py:72
  113.0 4.6 %collective-permute-start.46 = (bf16[64,128]{1,0:T(8,128)(2,1)S(1)}, bf16[64,128]{1,0:T(8,128)(2,1)S(1)}, u32[]{:S(2)}, u32[]{:S(2)}) collective-permute-start(bf16[64,128]{1,0:T(8,128)(2,1)S(1)} %get-tuple-element.105), channel_id=1, source_target_pairs={{0,6},{1,7},{2,4},{3,5},{4,2},{5,3},{6,0},{7,1},{8,14},{9,15},{10,... | collective-permute-start | bytes 49160 | tf_op jit(solution)/shard_map/ppermute | solution.py:72
  118.1 6.8 %collective-permute-start.49 = (bf16[272,128]{1,0:T(8,128)(2,1)S(1)}, bf16[272,128]{1,0:T(8,128)(2,1)S(1)}, u32[]{:S(2)}, u32[]{:S(2)}) collective-permute-start(bf16[272,128]{1,0:T(8,128)(2,1)S(1)} %get-tuple-element.112.refs_0_), channel_id=1, source_target_pairs={{0,24},{8,16},{16,8},{24,0},{1,25},{9,17},{17,9},{25,1},{2,26},{10... | collective-permute-start | bytes 208904 | tf_op jit(solution)/shard_map/ppermute | solution.py:76
  120.0 7.0 %collective-permute-start.48 = (bf16[272,128]{1,0:T(8,128)(2,1)S(1)}, bf16[272,128]{1,0:T(8,128)(2,1)S(1)}, u32[]{:S(2)}, u32[]{:S(2)}) collective-permute-start(bf16[272,128]{1,0:T(8,128)(2,1)S(1)} %get-tuple-element.112.refs_0_), channel_id=1, source_target_pairs={{0,16},{8,24},{16,0},{24,8},{1,17},{9,25},{17,1},{25,9},{2,18},{10... | collective-permute-start | bytes 208904 | tf_op jit(solution)/shard_map/ppermute | solution.py:76
  120.3 6.7 %collective-permute-start.47 = (bf16[272,128]{1,0:T(8,128)(2,1)S(1)}, bf16[272,128]{1,0:T(8,128)(2,1)S(1)}, u32[]{:S(2)}, u32[]{:S(2)}) collective-permute-start(bf16[272,128]{1,0:T(8,128)(2,1)S(1)} %get-tuple-element.112.refs_0_), channel_id=1, source_target_pairs={{0,8},{8,0},{16,24},{24,16},{1,9},{9,1},{17,25},{25,17},{2,10},{10... | collective-permute-start | bytes 208904 | tf_op jit(solution)/shard_map/ppermute | solution.py:76
  129.0 4.5 %collective-permute-start.51 = (bf16[272,128]{1,0:T(8,128)(2,1)S(1)}, bf16[272,128]{1,0:T(8,128)(2,1)S(1)}, u32[]{:S(2)}, u32[]{:S(2)}) collective-permute-start(bf16[272,128]{1,0:T(8,128)(2,1)S(1)} %get-tuple-element.114), channel_id=1, source_target_pairs={{0,2},{1,3},{2,0},{3,1},{4,6},{5,7},{6,4},{7,5},{8,10},{9,11},{10,... | collective-permute-start | bytes 208904 | tf_op jit(solution)/shard_map/ppermute | solution.py:72
  129.7 4.3 %collective-permute-start.52 = (bf16[272,128]{1,0:T(8,128)(2,1)S(1)}, bf16[272,128]{1,0:T(8,128)(2,1)S(1)}, u32[]{:S(2)}, u32[]{:S(2)}) collective-permute-start(bf16[272,128]{1,0:T(8,128)(2,1)S(1)} %get-tuple-element.115), channel_id=1, source_target_pairs={{0,4},{1,5},{2,6},{3,7},{4,0},{5,1},{6,2},{7,3},{8,12},{9,13},{10,... | collective-permute-start | bytes 208904 | tf_op jit(solution)/shard_map/ppermute | solution.py:72
  131.4 5.2 %collective-permute-start.53 = (bf16[272,128]{1,0:T(8,128)(2,1)S(1)}, bf16[272,128]{1,0:T(8,128)(2,1)S(1)}, u32[]{:S(2)}, u32[]{:S(2)}) collective-permute-start(bf16[272,128]{1,0:T(8,128)(2,1)S(1)} %get-tuple-element.116), channel_id=1, source_target_pairs={{0,6},{1,7},{2,4},{3,5},{4,2},{5,3},{6,0},{7,1},{8,14},{9,15},{10,... | collective-permute-start | bytes 208904 | tf_op jit(solution)/shard_map/ppermute | solution.py:72
  139.0 4.7 %collective-permute-start.55 = (bf16[128,256]{1,0:T(8,128)(2,1)S(1)}, bf16[128,256]{1,0:T(8,128)(2,1)S(1)}, u32[]{:S(2)}, u32[]{:S(2)}) collective-permute-start(bf16[128,256]{1,0:T(8,128)(2,1)S(1)} %get-tuple-element.120), channel_id=1, source_target_pairs={{0,2},{1,3},{2,0},{3,1},{4,6},{5,7},{6,4},{7,5},{8,10},{9,11},{10,... | collective-permute-start | bytes 196616 | tf_op jit(solution)/shard_map/ppermute | solution.py:72
  139.4 4.3 %collective-permute-start.56 = (bf16[128,256]{1,0:T(8,128)(2,1)S(1)}, bf16[128,256]{1,0:T(8,128)(2,1)S(1)}, u32[]{:S(2)}, u32[]{:S(2)}) collective-permute-start(bf16[128,256]{1,0:T(8,128)(2,1)S(1)} %get-tuple-element.121), channel_id=1, source_target_pairs={{0,4},{1,5},{2,6},{3,7},{4,0},{5,1},{6,2},{7,3},{8,12},{9,13},{10,... | collective-permute-start | bytes 196616 | tf_op jit(solution)/shard_map/ppermute | solution.py:72
  140.8 5.2 %collective-permute-start.57 = (bf16[128,256]{1,0:T(8,128)(2,1)S(1)}, bf16[128,256]{1,0:T(8,128)(2,1)S(1)}, u32[]{:S(2)}, u32[]{:S(2)}) collective-permute-start(bf16[128,256]{1,0:T(8,128)(2,1)S(1)} %get-tuple-element.122), channel_id=1, source_target_pairs={{0,6},{1,7},{2,4},{3,5},{4,2},{5,3},{6,0},{7,1},{8,14},{9,15},{10,... | collective-permute-start | bytes 196616 | tf_op jit(solution)/shard_map/ppermute | solution.py:72
  146.0 6.3 %collective-permute-start.60 = (bf16[128,256]{1,0:T(8,128)(2,1)S(1)}, bf16[128,256]{1,0:T(8,128)(2,1)S(1)}, u32[]{:S(2)}, u32[]{:S(2)}) collective-permute-start(bf16[128,256]{1,0:T(8,128)(2,1)S(1)} %shard_map.338.own_ref), channel_id=1, source_target_pairs={{0,24},{8,16},{16,8},{24,0},{1,25},{9,17},{17,9},{25,1},{2,26},{10... | collective-permute-start | bytes 196616 | tf_op jit(solution)/shard_map/ppermute | solution.py:76
  147.7 6.1 %collective-permute-start.59 = (bf16[128,256]{1,0:T(8,128)(2,1)S(1)}, bf16[128,256]{1,0:T(8,128)(2,1)S(1)}, u32[]{:S(2)}, u32[]{:S(2)}) collective-permute-start(bf16[128,256]{1,0:T(8,128)(2,1)S(1)} %shard_map.338.own_ref), channel_id=1, source_target_pairs={{0,16},{8,24},{16,0},{24,8},{1,17},{9,25},{17,1},{25,9},{2,18},{10... | collective-permute-start | bytes 196616 | tf_op jit(solution)/shard_map/ppermute | solution.py:76
  147.7 6.1 %collective-permute-start.58 = (bf16[128,256]{1,0:T(8,128)(2,1)S(1)}, bf16[128,256]{1,0:T(8,128)(2,1)S(1)}, u32[]{:S(2)}, u32[]{:S(2)}) collective-permute-start(bf16[128,256]{1,0:T(8,128)(2,1)S(1)} %shard_map.338.own_ref), channel_id=1, source_target_pairs={{0,8},{8,0},{16,24},{24,16},{1,9},{9,1},{17,25},{25,17},{2,10},{10... | collective-permute-start | bytes 196616 | tf_op jit(solution)/shard_map/ppermute | solution.py:76
  153.9 5.8 %collective-permute-start.63 = (bf16[128,256]{1,0:T(8,128)(2,1)S(1)}, bf16[128,256]{1,0:T(8,128)(2,1)S(1)}, u32[]{:S(2)}, u32[]{:S(2)}) collective-permute-start(bf16[128,256]{1,0:T(8,128)(2,1)S(1)} %shard_map.339.refs_0_), channel_id=1, source_target_pairs={{0,6},{1,7},{2,4},{3,5},{4,2},{5,3},{6,0},{7,1},{8,14},{9,15},{10,... | collective-permute-start | bytes 196616 | tf_op jit(solution)/shard_map/ppermute | solution.py:72
  155.6 4.5 %collective-permute-start.62 = (bf16[128,256]{1,0:T(8,128)(2,1)S(1)}, bf16[128,256]{1,0:T(8,128)(2,1)S(1)}, u32[]{:S(2)}, u32[]{:S(2)}) collective-permute-start(bf16[128,256]{1,0:T(8,128)(2,1)S(1)} %shard_map.339.refs_0_), channel_id=1, source_target_pairs={{0,4},{1,5},{2,6},{3,7},{4,0},{5,1},{6,2},{7,3},{8,12},{9,13},{10,... | collective-permute-start | bytes 196616 | tf_op jit(solution)/shard_map/ppermute | solution.py:72
  (40 other events, 289.2 us)

commit v4 on v3

--- a/solution.py
+++ b/solution.py
@@ -84,21 +84,27 @@
     return lax.optimization_barrier((block, *others))[0]
 
 
-def gather_all(block, beside=(), early=()):
+def gather_all(block, beside=(), within=()):
     if short_line():
-        line = jnp.stack([block] + [pass_line(block, k) for k in range(1, 4)])
+        line = [block] + [pass_line(block, k) for k in range(1, 4)]
+        line = jnp.stack(line)
     else:
         line = lax.all_gather(block, "z", axis=0)
-    if early:
-        line, *early = lax.optimization_barrier((line, *early))
     passed = [pass_line(after(part, line), mask) for part, mask in beside]
     lines = [line] + [swap(line, 2 * k) for k in range(1, 4)]
-    if passed:
-        lines[3], *passed = lax.optimization_barrier((lines[3], *passed))
-    return lines + [swap(line, 1) for line in lines], passed, early
-
-
-def arrange_kernel(mask_ref, values_ref, near_ref, far_ref, *level_refs):
+    if passed or within:
+        lines[3], *rest = lax.optimization_barrier((lines[3], *passed, *within))
+        passed, within = rest[: len(passed)], rest[len(passed) :]
+    return lines + [swap(line, 1) for line in lines], passed, within
+
+
+def arrange_kernel(
+    mask_ref, values_ref, label_ref, train_ref, bias_ref, near_ref, far_ref, notes_ref, *level_refs
+):
+    notes_ref[...] = jnp.zeros(notes_ref.shape, F32)
+    notes_ref[0:1, :] = label_ref[...].astype(F32)
+    notes_ref[1:2, :] = train_ref[...].astype(F32)
+    notes_ref[2:3, : bias_ref.shape[1]] = bias_ref[...]
     half = near_ref.shape[1] // TILE
     lines = half // 4
     here = 4 * lax.axis_index("y") + 2 * lax.axis_index("x") + lax.axis_index("c")
@@ -134,26 +140,40 @@
     out_ref[rows:, :] = jnp.broadcast_to(centre, (EXTRA, summed.shape[1])).astype(BF)
 
 
-def moments(refs, node_total):
-    count, tall, width = refs[0].shape
-    rows = tall - EXTRA
-    pivot = refs[0][0, rows:, :].astype(F32)[:1]
+def block_at(ref, i, rows):
+    return ref[i, :rows, :].astype(F32), ref[i, rows:, :].astype(F32)[:1]
+
+
+def block_loop(ref, pair, body, carry):
+    if ref.shape[0] > 4:
+        return lax.fori_loop(
+            0, ref.shape[0] // pair, lambda i, carry: body(i * pair, carry), carry
+        )
+    for i in range(0, 4, pair):
+        carry = body(i, carry)
+    return carry
+
+
+def moments(refs, rows, node_total):
+    width = refs[0].shape[-1]
+    pivot = block_at(refs[0], 0, rows)[1]
     zero = jnp.zeros((8, width), F32)
     sums = (zero, zero)
     for ref in refs:
 
         def one(i, carry, ref=ref):
             total, square = carry
-            value = ref[i, :rows, :].astype(F32).reshape(rows // 8, 8, width)
+            value, centre = block_at(ref, i, rows)
+            value = value.reshape(rows // 8, 8, width)
             part = jnp.sum(value, axis=0)
-            away = ref[i, rows:, :].astype(F32)[:1] - pivot
+            away = centre - pivot
             each = away * (rows // 8)
             return (
                 total + part + each,
                 square + jnp.sum(value * value, axis=0) + away * (2.0 * part + each),
             )
 
-        sums = lax.fori_loop(0, count, one, sums, unroll=4)
+        sums = block_loop(ref, 1, one, sums)
     shift = jnp.sum(sums[0], axis=0, keepdims=True) / node_total
     variance = jnp.sum(sums[1], axis=0, keepdims=True) / node_total - shift * shift
     return pivot + shift, lax.rsqrt(jnp.maximum(variance, 0.0) + EPS_NORM)
@@ -162,33 +182,26 @@
 def gelu_half(value):
     square = value * value
     bend = jnp.tanh(value * (ROOT + (ROOT * BEND) * square))
-    return 0.5 + 0.5 * bend, bend, square
-
-
-def gelu_slope(value, half, bend, square):
-    return half + (0.5 * value) * (1.0 - bend * bend) * (ROOT + (3 * ROOT * BEND) * square)
-
-
-def blocks_of(ref, i, pair, rows):
-    parts = [
-        (ref[i * pair + j, :rows, :].astype(F32), ref[i * pair + j, rows:, :].astype(F32)[:1])
-        for j in range(pair)
-    ]
-    return parts
-
-
-def with_columns(refs, near_ref, far_ref, rows, pair, act, total):
-    count = refs[0].shape[0]
+    return 0.5 + 0.5 * bend, square
+
+
+def gelu_slope(value, half, square):
+    return half + (value * half) * (1.0 - half) * (2 * ROOT + (6 * ROOT * BEND) * square)
+
+
+def with_columns(refs, near_ref, far_ref, act, total):
+    rows, columns = near_ref.shape
     for n, ref in enumerate(refs):
         adjacent_ref = far_ref if n >= 4 else near_ref
 
-        def one(i, total, ref=ref, adjacent_ref=adjacent_ref, at=n % 4 * count * rows):
-            start = pl.multiple_of(at + i * (pair * rows), pair * rows)
-            return act(
-                blocks_of(ref, i, pair, rows), adjacent_ref[:, pl.ds(start, pair * rows)], total
-            )
-
-        total = lax.fori_loop(0, count // pair, one, total, unroll=2)
+        def one(i, total, ref=ref, adjacent_ref=adjacent_ref, at=n % 4 * (columns // 4)):
+            start = at + i * rows
+            if not isinstance(start, int):
+                start = pl.multiple_of(start, 4 * rows)
+            blocks = [block_at(ref, i + j, rows) for j in range(4)]
+            return act(blocks, adjacent_ref[:, pl.ds(start, 4 * rows)], total)
+
+        total = block_loop(ref, 4, one, total)
     return total
 
 
@@ -326,9 +339,8 @@
 
 def layer_kernel(node_total, layer, near_ref, far_ref, weight_ref, norm_ref, *refs):
     refs, (out_ref, stats_ref) = refs[:8], refs[8:]
-    count, tall, width = refs[0].shape
-    rows = tall - EXTRA
-    mean_value, inverse = moments(refs, node_total)
+    rows, width = near_ref.shape[0], refs[0].shape[-1]
+    mean_value, inverse = moments(refs, rows, node_total)
     stats_ref[0:1, :] = mean_value
     stats_ref[1:2, :] = inverse
     scale = norm_ref[2 * layer : 2 * layer + 1, :] * inverse
@@ -344,13 +356,11 @@
         return total + dot(adjacent, projected)
 
     total = jnp.zeros((rows, low.shape[1]), F32)
-    centre_into(out_ref, with_columns(refs, near_ref, far_ref, rows, 2, act, total))
+    centre_into(out_ref, with_columns(refs, near_ref, far_ref, act, total))
 
 
 def slopes_kernel(layer, near_ref, far_ref, norm_ref, stats_ref, *refs):
     refs, out_ref = refs[:8], refs[8]
-    count, tall, width = refs[0].shape
-    rows = tall - EXTRA
     mean_value, inverse = stats_ref[0:1, :], stats_ref[1:2, :]
     gain = norm_ref[2 * layer : 2 * layer + 1, :]
     offset = norm_ref[2 * layer + 1 : 2 * layer + 2, :]
@@ -366,7 +376,7 @@
         out_ref[...] += dot(adjacent, jnp.concatenate(slopes))
         return carry
 
-    with_columns(refs, near_ref, far_ref, rows, 2, act, 0)
+    with_columns(refs, near_ref, far_ref, act, 0)
 
 
 def head_low_of(weight_ref, tall_ref):
@@ -375,14 +385,11 @@
     return tall_ref[...].astype(BF)
 
 
-def head_kernel(
-    node_total, near_ref, far_ref, weight_ref, norm_ref, bias_ref, label_ref, mask_ref, *refs
-):
+def head_kernel(node_total, near_ref, far_ref, weight_ref, norm_ref, notes_ref, *refs):
     refs, (packed_ref, stats_ref, total_ref, sums_ref, tall_ref) = refs[:8], refs[8:]
-    count, tall, width = refs[0].shape
-    rows = tall - EXTRA
+    rows, width = near_ref.shape[0], refs[0].shape[-1]
     classes = weight_ref.shape[0]
-    mean_value, inverse = moments(refs, node_total)
+    mean_value, inverse = moments(refs, rows, node_total)
     stats_ref[0:1, :] = mean_value
     stats_ref[1:2, :] = inverse
     gain, offset = norm_ref[2:3, :], norm_ref[3:4, :]
@@ -394,8 +401,8 @@
         for value, centre in blocks:
             normed = value * inverse + (centre - mean_value) * inverse
             value = gain * normed + offset
-            half, bend, square = gelu_half(value)
-            slope = gelu_slope(value, half, bend, square)
+            half, square = gelu_half(value)
+            slope = gelu_slope(value, half, square)
             hidden.append((value * half).astype(BF))
             slopes.append(jnp.concatenate([slope.astype(BF), (slope * normed).astype(BF)], axis=1))
         headed = dot_turned(jnp.concatenate(hidden), low).astype(BF)
@@ -403,18 +410,17 @@
         total_ref[...] += dot(adjacent, both)
         return carry
 
-    with_columns(refs, near_ref, far_ref, rows, 2, act, 0)
+    with_columns(refs, near_ref, far_ref, act, 0)
 
     lane = lax.broadcasted_iota(jnp.int32, (rows, LANES), 1)
     sums_ref[...] = jnp.zeros(sums_ref.shape, F32)
-    sums_ref[:1, :classes] = bias_ref[...]
-    logits = jnp.where(lane < classes, total_ref[:, :LANES] + sums_ref[:1, :], -1e30)
+    logits = jnp.where(lane < classes, total_ref[:, :LANES] + notes_ref[2:3, :], -1e30)
     logits = logits - jnp.max(logits, axis=1, keepdims=True)
     raised = jnp.exp(logits)
     whole = jnp.sum(raised, axis=1, keepdims=True)
-    label = jnp.broadcast_to(label_ref[...].astype(F32), (LANES, rows)).T
+    label = jnp.broadcast_to(notes_ref[0:1, :], (LANES, rows)).T
     onehot = jnp.where(lane.astype(F32) == label, 1.0, 0.0)
-    weight = jnp.broadcast_to(mask_ref[...].astype(F32), (LANES, rows)).T
+    weight = jnp.broadcast_to(notes_ref[1:2, :], (LANES, rows)).T
     losses = jnp.log(whole) - jnp.sum(onehot * logits, axis=1, keepdims=True)
     d_logits = (raised / whole - onehot) * weight
     d_low = d_logits.astype(BF)
@@ -435,8 +441,8 @@
     centre = own_ref[rows:, :].astype(F32)[:1]
     normed = own_ref[:rows, :].astype(F32) * inverse + (centre - mean_value) * inverse
     value = gain * normed + norm_ref[2 * layer + 1 : 2 * layer + 2, :]
-    half, bend, square = gelu_half(value)
-    d_pre = d_hidden * gelu_slope(value, half, bend, square)
+    half, square = gelu_half(value)
+    d_pre = d_hidden * gelu_slope(value, half, square)
     d_summed = (gain * inverse) * (d_pre - (shift_grad + normed * gain_grad) / node_total)
     return d_summed, value * half
 
@@ -628,31 +634,30 @@
         level_shapes = [shape((rows, 8 * rows), BF)] * 4
     else:
         level_shapes = [shape((length, rows, 8 * rows), BF)]
-    near, far, *levels = run(
+    near, far, notes, *levels = run(
         arrange_kernel,
-        [shape((rows, half), BF)] * 2 + level_shapes,
-        [tile_mask, adjacency],
+        [shape((rows, half), BF)] * 2 + [shape((8, LANES))] + level_shapes,
+        [tile_mask, adjacency, labels[None], train_mask[None], head_bias[None]],
         scalars=1,
     )
 
     projected = dot(features, w_first.astype(BF)).astype(BF)
     turned = features.T
     turned = jnp.stack([turned] + [swap(turned, 2 * k) for k in range(1, 4)])
-    if short_line():
-        around, passed, (turned,) = gather_all(
-            projected, [(levels[1], 1), (levels[2], 2)], [turned]
-        )
+    short = short_line()
+    if not short:
+        levels = [lax.all_to_all(levels[0], "z", 0, 0)]
+    around, passed, unused = gather_all(
+        projected, [(levels[1], 1), (levels[2], 2)] if short else ()
+    )
+    if short:
         levels[1:3] = passed
-    else:
-        around, *unused = gather_all(projected)
-        levels = [lax.all_to_all(levels[0], "z", 0, 0)]
     (summed_one,) = run(
         first_sum_kernel, [shape((tall, hidden), BF)], [near, far, *around], flops=work
     )
-    if short_line():
-        around, levels[3:], unused = gather_all(summed_one, [(levels[3], 3)])
-    else:
-        around, *unused = gather_all(summed_one)
+    around, passed, unused = gather_all(summed_one, [(levels[3], 3)] if short else ())
+    if short:
+        levels[3:] = passed
     summed_two, stats_one = run(
         functools.partial(layer_kernel, node_total, 0),
         [shape((tall, hidden), BF), shape((8, hidden))],
@@ -665,18 +670,19 @@
         [near, far, norm_params, stats_one, *around],
         flops=3 * work,
     )
-    if short_line():
+    if short:
         mixed_shapes = [shape((inputs, rows))] + [shape((inputs, rows), BF)] * 3
     else:
         mixed_shapes = [shape((length, inputs, rows))]
     mixed = run(
         mix_kernel, mixed_shapes, [turned, swap(turned, 1), *levels], flops=2 * work
     )
-    if short_line():
-        around, passed, unused = gather_all(summed_two, [(mixed[k], k) for k in range(1, 4)])
-        mixed = [mixed[0], *passed]
+    around, passed, (slopes_one,) = gather_all(
+        summed_two, [(mixed[k], k) for k in (3, 2, 1)] if short else (), [slopes_one]
+    )
+    if short:
+        mixed = [mixed[0], *passed[::-1]]
     else:
-        around, *unused = gather_all(summed_two)
         mixed = [lax.psum_scatter(mixed[0], "z", scatter_dimension=0)]
     packed, stats_two = run(
         functools.partial(head_kernel, node_total),
@@ -686,9 +692,7 @@
             far,
             head_turned,
             norm_params,
-            head_bias[None],
-            labels[None],
-            train_mask[None],
+            notes,
             *around,
         ],
         scratch=[

time: 164 us -> 158 us (0.963)
  starting transfers between devices: 71.2 us -> 67.2 us
    ppermute x24, waiting for transfers between devices: 41.3 us -> 34.6 us  [pass_line(): return lax.ppermute(block, 'z', [(i, i ^ mask) for i in range(4)])]
    ppermute x44, waiting for transfers between devices: 25.6 us -> 30.7 us  [swap(): return lax.ppermute(block, PLANE, [(i, i ^ mask) for i in range(8)])]
    ppermute x44, starting transfers between devices: 33 us -> 29.7 us  [swap(): return lax.ppermute(block, PLANE, [(i, i ^ mask) for i in range(8)])]
where the time goes in v4:
time: 158 us
  starting transfers between devices  67.2 us (43%)
  waiting for transfers between devices  65.3 us (41%)
  Pallas kernels  18 us (11%)
  local copies, waits for them, and re-layouts  3.54 us (2%)
    ppermute x24, starting transfers between devices, pass_line(): return lax.ppermute(block, 'z', [(i, i ^ mask) for i in range(4)])  37.5 us
    ppermute x24, waiting for transfers between devices, pass_line(): return lax.ppermute(block, 'z', [(i, i ^ mask) for i in range(4)])  34.6 us
    ppermute x44, waiting for transfers between devices, swap(): return lax.ppermute(block, PLANE, [(i, i ^ mask) for i in range(8)])  30.7 us
    ppermute x44, starting transfers between devices, swap(): return lax.ppermute(block, PLANE, [(i, i ^ mask) for i in range(8)])  29.7 us
    pallas_call x18, Pallas kernels, run(): pl.pallas_call(body, out_shape=tuple(outs), in_specs=[pl.BlockSpec(memory...  18 us
  transfers between devices with their start and end apart: 68, of which 43 were waited for; matrix products, arithmetic and copies ran while one was open for 1% of the time, Pallas kernels for 5%

profile of v4, /device:TPU:0, one launch (start us, length us, event | category | flops | bytes accessed | tf_op | source)
XLA Modules:
  0.0 157.8 jit_solution(18322905897591849084)
XLA Ops:
  0.7 1.4 convolution_convert_fusion
  2.1 5.1 %collective-permute-start.2 = (bf16[128,256]{1,0:T(8,128)(2,1)S(1)}, bf16[128,256]{1,0:T(8,128)(2,1)S(1)}, u32[]{:S(2)}, u32[]{:S(2)}) collective-permute-start(bf16[128,256]{1,0:T(8,128)(2,1)S(1)} %convolution_convert_fusion), channel_id=1, source_target_pairs={{0,24},{8,16},{16,8},{24,0},{1,25},{9,17},{17,9},{25,1},{2,26},{10... | collective-permute-start | bytes 196616 | tf_op jit(solution)/shard_map/ppermute | solution.py:76
  10.7 2.1 %collective-permute-done.1 = bf16[128,256]{1,0:T(8,128)(2,1)S(1)} collective-permute-done((bf16[128,256]{1,0:T(8,128)(2,1)S(1)}, bf16[128,256]{1,0:T(8,128)(2,1)S(1)}, u32[]{:S(2)}, u32[]{:S(2)}) %collective-permute-start.1) | collective-permute-done | bytes 65568 | tf_op jit(solution)/shard_map/ppermute | solution.py:76
  12.8 2.5 %collective-permute-start.5 = (bf16[4,128,256]{2,1,0:T(8,128)(2,1)S(1)}, bf16[4,128,256]{2,1,0:T(8,128)(2,1)S(1)}, u32[]{:S(2)}, u32[]{:S(2)}) collective-permute-start(bf16[4,128,256]{2,1,0:T(8,128)(2,1)S(1)} %pad_maximum_fusion.3.refs_0_), channel_id=1, source_target_pairs={{0,6},{1,7},{2,4},{3,5},{4,2},{5,3},{6,0},{7,1},{8,14},{9,15},{10,... | collective-permute-start | bytes 786440 | tf_op jit(solution)/shard_map/ppermute | solution.py:72
  15.4 1.6 %collective-permute-start.7 = (bf16[128,1024]{1,0:T(8,128)(2,1)S(1)}, bf16[128,1024]{1,0:T(8,128)(2,1)S(1)}, u32[]{:S(2)}, u32[]{:S(2)}) collective-permute-start(bf16[128,1024]{1,0:T(8,128)(2,1)S(1)} %get-tuple-element.80), channel_id=1, source_target_pairs={{0,16},{8,24},{16,0},{24,8},{1,17},{9,25},{17,1},{25,9},{2,18},{10... | collective-permute-start | bytes 786440 | tf_op jit(solution)/shard_map/ppermute | solution.py:76
  16.9 1.7 %collective-permute-start.6 = (bf16[128,1024]{1,0:T(8,128)(2,1)S(1)}, bf16[128,1024]{1,0:T(8,128)(2,1)S(1)}, u32[]{:S(2)}, u32[]{:S(2)}) collective-permute-start(bf16[128,1024]{1,0:T(8,128)(2,1)S(1)} %get-tuple-element.78), channel_id=1, source_target_pairs={{0,8},{8,0},{16,24},{24,16},{1,9},{9,1},{17,25},{25,17},{2,10},{10... | collective-permute-start | bytes 786440 | tf_op jit(solution)/shard_map/ppermute | solution.py:76
  19.7 3.3 %collective-permute-done.5.refs_3_ = bf16[4,128,256]{2,1,0:T(8,128)(2,1)S(1)} collective-permute-done((bf16[4,128,256]{2,1,0:T(8,128)(2,1)S(1)}, bf16[4,128,256]{2,1,0:T(8,128)(2,1)S(1)}, u32[]{:S(2)}, u32[]{:S(2)}) %collective-permute-start.5) | collective-permute-done | bytes 262176 | tf_op jit(solution)/shard_map/ppermute | solution.py:72
  23.0 6.0 %collective-permute-done.7.refs_2_.refs_6_ = bf16[128,1024]{1,0:T(8,128)(2,1)S(1)} collective-permute-done((bf16[128,1024]{1,0:T(8,128)(2,1)S(1)}, bf16[128,1024]{1,0:T(8,128)(2,1)S(1)}, u32[]{:S(2)}, u32[]{:S(2)}) %collective-permute-start.7) | collective-permute-done | bytes 262176 | tf_op jit(solution)/shard_map/ppermute | solution.py:76
  31.8 2.1 %collective-permute-start.14 = (bf16[144,256]{1,0:T(8,128)(2,1)S(1)}, bf16[144,256]{1,0:T(8,128)(2,1)S(1)}, u32[]{:S(2)}, u32[]{:S(2)}) collective-permute-start(bf16[144,256]{1,0:T(8,128)(2,1)S(1)} %shard_map.324.summed_ref), channel_id=1, source_target_pairs={{0,24},{8,16},{16,8},{24,0},{1,25},{9,17},{17,9},{25,1},{2,26},{10... | collective-permute-start | bytes 221192 | tf_op jit(solution)/shard_map/ppermute | solution.py:76
  34.0 2.3 %collective-permute-start.12 = (bf16[144,256]{1,0:T(8,128)(2,1)S(1)}, bf16[144,256]{1,0:T(8,128)(2,1)S(1)}, u32[]{:S(2)}, u32[]{:S(2)}) collective-permute-start(bf16[144,256]{1,0:T(8,128)(2,1)S(1)} %shard_map.324.summed_ref), channel_id=1, source_target_pairs={{0,8},{8,0},{16,24},{24,16},{1,9},{9,1},{17,25},{25,17},{2,10},{10... | collective-permute-start | bytes 221192 | tf_op jit(solution)/shard_map/ppermute | solution.py:76
  39.8 1.4 collective-permute-done.13
  43.3 1.5 collective-permute-start.15
  44.8 2.1 %collective-permute-start.18 = (bf16[128,1024]{1,0:T(8,128)(2,1)S(1)}, bf16[128,1024]{1,0:T(8,128)(2,1)S(1)}, u32[]{:S(2)}, u32[]{:S(2)}) collective-permute-start(bf16[128,1024]{1,0:T(8,128)(2,1)S(1)} %get-tuple-element.83), channel_id=1, source_target_pairs={{0,24},{8,16},{16,8},{24,0},{1,25},{9,17},{17,9},{25,1},{2,26},{10... | collective-permute-start | bytes 786440 | tf_op jit(solution)/shard_map/ppermute | solution.py:76
  47.8 6.3 %collective-permute-done.18.refs_3_.refs_7_ = bf16[128,1024]{1,0:T(8,128)(2,1)S(1)} collective-permute-done((bf16[128,1024]{1,0:T(8,128)(2,1)S(1)}, bf16[128,1024]{1,0:T(8,128)(2,1)S(1)}, u32[]{:S(2)}, u32[]{:S(2)}) %collective-permute-start.18) | collective-permute-done | bytes 262176 | tf_op jit(solution)/shard_map/ppermute | solution.py:76
  54.6 4.1 %collective-permute-done.16.refs_2_ = bf16[4,144,256]{2,1,0:T(8,128)(2,1)S(1)} collective-permute-done((bf16[4,144,256]{2,1,0:T(8,128)(2,1)S(1)}, bf16[4,144,256]{2,1,0:T(8,128)(2,1)S(1)}, u32[]{:S(2)}, u32[]{:S(2)}) %collective-permute-start.16) | collective-permute-done | bytes 294944 | tf_op jit(solution)/shard_map/ppermute | solution.py:72
  60.7 2.6 %shard_map.325 = (bf16[144,256]{1,0:T(8,128)(2,1)S(1)}, f32[8,256]{1,0:T(8,128)S(1)}) custom-call(bf16[128,2048]{1,0:T(8,128)(2,1)S(1)} %get-tuple-element.75.near_ref, bf16[128,2048]{1,0:T(8,128)(2,1)S(1)} %get-tuple-element.76.far_ref, f32[256,256]{1,0:T(8,128)S(1)} %copy-done, f32[4,256]{1,0:T(4,128)S(1)} %copy-done.8, ...), custom_call_target="tpu_custom_call" | custom-call | flops 805306368 | bytes 3756032 | tf_op jit(solution)/shard_map/pallas_call | solution.py:59
  63.2 1.8 %collective-permute-start.25 = (bf16[144,256]{1,0:T(8,128)(2,1)S(1)}, bf16[144,256]{1,0:T(8,128)(2,1)S(1)}, u32[]{:S(2)}, u32[]{:S(2)}) collective-permute-start(bf16[144,256]{1,0:T(8,128)(2,1)S(1)} %get-tuple-element.85.summed_ref), channel_id=1, source_target_pairs={{0,24},{8,16},{16,8},{24,0},{1,25},{9,17},{17,9},{25,1},{2,26},{10... | collective-permute-start | bytes 221192 | tf_op jit(solution)/shard_map/ppermute | solution.py:76
  65.0 2.7 %collective-permute-start.23 = (bf16[144,256]{1,0:T(8,128)(2,1)S(1)}, bf16[144,256]{1,0:T(8,128)(2,1)S(1)}, u32[]{:S(2)}, u32[]{:S(2)}) collective-permute-start(bf16[144,256]{1,0:T(8,128)(2,1)S(1)} %get-tuple-element.85.summed_ref), channel_id=1, source_target_pairs={{0,8},{8,0},{16,24},{24,16},{1,9},{9,1},{17,25},{25,17},{2,10},{10... | collective-permute-start | bytes 221192 | tf_op jit(solution)/shard_map/ppermute | solution.py:76
  67.8 1.4 shard_map.326
  70.3 2.3 %collective-permute-done.24 = bf16[144,256]{1,0:T(8,128)(2,1)S(1)} collective-permute-done((bf16[144,256]{1,0:T(8,128)(2,1)S(1)}, bf16[144,256]{1,0:T(8,128)(2,1)S(1)}, u32[]{:S(2)}, u32[]{:S(2)}) %collective-permute-start.24) | collective-permute-done | bytes 73760 | tf_op jit(solution)/shard_map/ppermute | solution.py:76
  72.6 1.8 %collective-permute-start.33 = (bf16[602,128]{1,0:T(8,128)(2,1)S(1)}, bf16[602,128]{1,0:T(8,128)(2,1)S(1)}, u32[]{:S(2)}, u32[]{:S(2)}) collective-permute-start(bf16[602,128]{1,0:T(8,128)(2,1)S(1)} %get-tuple-element.92), channel_id=1, source_target_pairs={{0,24},{8,16},{16,8},{24,0},{1,25},{9,17},{17,9},{25,1},{2,26},{10... | collective-permute-start | bytes 462344 | tf_op jit(solution)/shard_map/ppermute | solution.py:76
  75.4 1.4 collective-permute-start.27
  77.9 3.3 %collective-permute-done.33.refs_3_ = bf16[602,128]{1,0:T(8,128)(2,1)S(1)} collective-permute-done((bf16[602,128]{1,0:T(8,128)(2,1)S(1)}, bf16[602,128]{1,0:T(8,128)(2,1)S(1)}, u32[]{:S(2)}, u32[]{:S(2)}) %collective-permute-start.33) | collective-permute-done | bytes 154144 | tf_op jit(solution)/shard_map/ppermute | solution.py:76
  81.2 2.3 %collective-permute-start.35 = (bf16[602,128]{1,0:T(8,128)(2,1)S(1)}, bf16[602,128]{1,0:T(8,128)(2,1)S(1)}, u32[]{:S(2)}, u32[]{:S(2)}) collective-permute-start(bf16[602,128]{1,0:T(8,128)(2,1)S(1)} %get-tuple-element.96), channel_id=1, source_target_pairs={{0,8},{8,0},{16,24},{24,16},{1,9},{9,1},{17,25},{25,17},{2,10},{10... | collective-permute-start | bytes 462344 | tf_op jit(solution)/shard_map/ppermute | solution.py:76
  83.5 3.2 %shard_map.327.slopes_ref = f32[128,512]{1,0:T(8,128)S(1)} custom-call(bf16[128,2048]{1,0:T(8,128)(2,1)S(1)} %get-tuple-element.75.near_ref, bf16[128,2048]{1,0:T(8,128)(2,1)S(1)} %get-tuple-element.76.far_ref, f32[4,256]{1,0:T(4,128)S(1)} %copy-done.8, f32[8,256]{1,0:T(8,128)S(1)} %get-tuple-element.97.stats_ref, ...), custom_call_target="tpu_custom_call" | custom-call | flops 805306368 | bytes 3682304 | tf_op jit(solution)/shard_map/pallas_call | solution.py:59
  87.4 1.5 collective-permute-done.35.refs_1_
  92.1 4.7 %shard_map.328 = (bf16[64,128]{1,0:T(8,128)(2,1)S(1)}, f32[8,256]{1,0:T(8,128)S(1)}) custom-call(bf16[128,2048]{1,0:T(8,128)(2,1)S(1)} %get-tuple-element.75.near_ref, bf16[128,2048]{1,0:T(8,128)(2,1)S(1)} %get-tuple-element.76.far_ref, f32[41,256]{1,0:T(8,128)S(1)} %bitcast.43, f32[4,256]{1,0:T(4,128)S(1)} %copy-done.8, ...), custom_call_target="tpu_custom_call" | custom-call | flops 1073741824 | bytes 3482624 | tf_op jit(solution)/shard_map/pallas_call | solution.py:59
  96.8 2.1 %collective-permute-start.42 = (bf16[64,128]{1,0:T(8,128)(2,1)S(1)}, bf16[64,128]{1,0:T(8,128)(2,1)S(1)}, u32[]{:S(2)}, u32[]{:S(2)}) collective-permute-start(bf16[64,128]{1,0:T(8,128)(2,1)S(1)} %get-tuple-element.101.refs_0_), channel_id=1, source_target_pairs={{0,24},{8,16},{16,8},{24,0},{1,25},{9,17},{17,9},{25,1},{2,26},{10... | collective-permute-start | bytes 49160 | tf_op jit(solution)/shard_map/ppermute | solution.py:76
  98.9 2.3 %collective-permute-start.40 = (bf16[64,128]{1,0:T(8,128)(2,1)S(1)}, bf16[64,128]{1,0:T(8,128)(2,1)S(1)}, u32[]{:S(2)}, u32[]{:S(2)}) collective-permute-start(bf16[64,128]{1,0:T(8,128)(2,1)S(1)} %get-tuple-element.101.refs_0_), channel_id=1, source_target_pairs={{0,8},{8,0},{16,24},{24,16},{1,9},{9,1},{17,25},{25,17},{2,10},{10... | collective-permute-start | bytes 49160 | tf_op jit(solution)/shard_map/ppermute | solution.py:76
  106.9 1.7 %collective-permute-start.46 = (bf16[64,128]{1,0:T(8,128)(2,1)S(1)}, bf16[64,128]{1,0:T(8,128)(2,1)S(1)}, u32[]{:S(2)}, u32[]{:S(2)}) collective-permute-start(bf16[64,128]{1,0:T(8,128)(2,1)S(1)} %get-tuple-element.105), channel_id=1, source_target_pairs={{0,6},{1,7},{2,4},{3,5},{4,2},{5,3},{6,0},{7,1},{8,14},{9,15},{10,... | collective-permute-start | bytes 49160 | tf_op jit(solution)/shard_map/ppermute | solution.py:72
  109.6 1.9 %collective-permute-done.46.refs_3_ = bf16[64,128]{1,0:T(8,128)(2,1)S(1)} collective-permute-done((bf16[64,128]{1,0:T(8,128)(2,1)S(1)}, bf16[64,128]{1,0:T(8,128)(2,1)S(1)}, u32[]{:S(2)}, u32[]{:S(2)}) %collective-permute-start.46) | collective-permute-done | bytes 16416 | tf_op jit(solution)/shard_map/ppermute | solution.py:72
  112.0 1.8 %collective-permute-start.49 = (bf16[272,128]{1,0:T(8,128)(2,1)S(1)}, bf16[272,128]{1,0:T(8,128)(2,1)S(1)}, u32[]{:S(2)}, u32[]{:S(2)}) collective-permute-start(bf16[272,128]{1,0:T(8,128)(2,1)S(1)} %get-tuple-element.112.refs_0_), channel_id=1, source_target_pairs={{0,24},{8,16},{16,8},{24,0},{1,25},{9,17},{17,9},{25,1},{2,26},{10... | collective-permute-start | bytes 208904 | tf_op jit(solution)/shard_map/ppermute | solution.py:76
  115.0 1.5 collective-permute-start.47
  116.5 1.8 %collective-permute-done.49.refs_3_ = bf16[272,128]{1,0:T(8,128)(2,1)S(1)} collective-permute-done((bf16[272,128]{1,0:T(8,128)(2,1)S(1)}, bf16[272,128]{1,0:T(8,128)(2,1)S(1)}, u32[]{:S(2)}, u32[]{:S(2)}) %collective-permute-start.49) | collective-permute-done | bytes 69664 | tf_op jit(solution)/shard_map/ppermute | solution.py:76
  118.3 1.9 %collective-permute-done.48.refs_2_ = bf16[272,128]{1,0:T(8,128)(2,1)S(1)} collective-permute-done((bf16[272,128]{1,0:T(8,128)(2,1)S(1)}, bf16[272,128]{1,0:T(8,128)(2,1)S(1)}, u32[]{:S(2)}, u32[]{:S(2)}) %collective-permute-start.48) | collective-permute-done | bytes 69664 | tf_op jit(solution)/shard_map/ppermute | solution.py:76
  120.9 1.2 collective-permute-done.50.got_ref
  122.2 1.3 collective-permute-start.51
  126.5 1.9 %collective-permute-done.52.refs_6_ = bf16[272,128]{1,0:T(8,128)(2,1)S(1)} collective-permute-done((bf16[272,128]{1,0:T(8,128)(2,1)S(1)}, bf16[272,128]{1,0:T(8,128)(2,1)S(1)}, u32[]{:S(2)}, u32[]{:S(2)}) %collective-permute-start.52) | collective-permute-done | bytes 69664 | tf_op jit(solution)/shard_map/ppermute | solution.py:72
  128.5 1.3 collective-permute-done.53.refs_7_
  133.9 1.7 %collective-permute-start.57 = (bf16[128,256]{1,0:T(8,128)(2,1)S(1)}, bf16[128,256]{1,0:T(8,128)(2,1)S(1)}, u32[]{:S(2)}, u32[]{:S(2)}) collective-permute-start(bf16[128,256]{1,0:T(8,128)(2,1)S(1)} %get-tuple-element.122), channel_id=1, source_target_pairs={{0,6},{1,7},{2,4},{3,5},{4,2},{5,3},{6,0},{7,1},{8,14},{9,15},{10,... | collective-permute-start | bytes 196616 | tf_op jit(solution)/shard_map/ppermute | solution.py:72
  136.5 1.6 %collective-permute-done.56.refs_1_ = bf16[128,256]{1,0:T(8,128)(2,1)S(1)} collective-permute-done((bf16[128,256]{1,0:T(8,128)(2,1)S(1)}, bf16[128,256]{1,0:T(8,128)(2,1)S(1)}, u32[]{:S(2)}, u32[]{:S(2)}) %collective-permute-start.56) | collective-permute-done | bytes 65568 | tf_op jit(solution)/shard_map/ppermute | solution.py:72
  139.2 2.0 %collective-permute-start.60 = (bf16[128,256]{1,0:T(8,128)(2,1)S(1)}, bf16[128,256]{1,0:T(8,128)(2,1)S(1)}, u32[]{:S(2)}, u32[]{:S(2)}) collective-permute-start(bf16[128,256]{1,0:T(8,128)(2,1)S(1)} %shard_map.338.own_ref), channel_id=1, source_target_pairs={{0,24},{8,16},{16,8},{24,0},{1,25},{9,17},{17,9},{25,1},{2,26},{10... | collective-permute-start | bytes 196616 | tf_op jit(solution)/shard_map/ppermute | solution.py:76
  141.3 2.3 %collective-permute-start.58 = (bf16[128,256]{1,0:T(8,128)(2,1)S(1)}, bf16[128,256]{1,0:T(8,128)(2,1)S(1)}, u32[]{:S(2)}, u32[]{:S(2)}) collective-permute-start(bf16[128,256]{1,0:T(8,128)(2,1)S(1)} %shard_map.338.own_ref), channel_id=1, source_target_pairs={{0,8},{8,0},{16,24},{24,16},{1,9},{9,1},{17,25},{25,17},{2,10},{10... | collective-permute-start | bytes 196616 | tf_op jit(solution)/shard_map/ppermute | solution.py:76
  144.2 1.3 collective-permute-done.60.refs_2_
  145.5 1.5 collective-permute-done.59.refs_1_
  147.1 1.8 %collective-permute-start.63 = (bf16[128,256]{1,0:T(8,128)(2,1)S(1)}, bf16[128,256]{1,0:T(8,128)(2,1)S(1)}, u32[]{:S(2)}, u32[]{:S(2)}) collective-permute-start(bf16[128,256]{1,0:T(8,128)(2,1)S(1)} %shard_map.339.refs_0_), channel_id=1, source_target_pairs={{0,6},{1,7},{2,4},{3,5},{4,2},{5,3},{6,0},{7,1},{8,14},{9,15},{10,... | collective-permute-start | bytes 196616 | tf_op jit(solution)/shard_map/ppermute | solution.py:72
  150.7 2.3 %collective-permute-done.63.refs_3_ = bf16[128,256]{1,0:T(8,128)(2,1)S(1)} collective-permute-done((bf16[128,256]{1,0:T(8,128)(2,1)S(1)}, bf16[128,256]{1,0:T(8,128)(2,1)S(1)}, u32[]{:S(2)}, u32[]{:S(2)}) %collective-permute-start.63) | collective-permute-done | bytes 65568 | tf_op jit(solution)/shard_map/ppermute | solution.py:72
  155.4 2.4 %shard_map.340 = (f32[602,256]{1,0:T(8,128)}, f32[602,256]{1,0:T(8,128)}, f32[602,256]{1,0:T(8,128)}, f32[256,256]{1,0:T(8,128)}, f32[256,256]{1,0:T(8,128)}, /*...) custom-call(bf16[128,256]{1,0:T(8,128)(2,1)S(1)} %shard_map.339.refs_0_, ...), custom_call_target="tpu_custom_call" | custom-call | bytes 6047744 | tf_op jit(solution)/shard_map/pallas_call | solution.py:59
  (158 shorter events, 46.5 us)
Async XLA Ops:
  2.1 8.6 %collective-permute-start.2 = (bf16[128,256]{1,0:T(8,128)(2,1)S(1)}, bf16[128,256]{1,0:T(8,128)(2,1)S(1)}, u32[]{:S(2)}, u32[]{:S(2)}) collective-permute-start(bf16[128,256]{1,0:T(8,128)(2,1)S(1)} %convolution_convert_fusion), channel_id=1, source_target_pairs={{0,24},{8,16},{16,8},{24,0},{1,25},{9,17},{17,9},{25,1},{2,26},{10... | collective-permute-start | bytes 196616 | tf_op jit(solution)/shard_map/ppermute | solution.py:76
  7.2 5.6 %collective-permute-start.1 = (bf16[128,256]{1,0:T(8,128)(2,1)S(1)}, bf16[128,256]{1,0:T(8,128)(2,1)S(1)}, u32[]{:S(2)}, u32[]{:S(2)}) collective-permute-start(bf16[128,256]{1,0:T(8,128)(2,1)S(1)} %convolution_convert_fusion), channel_id=1, source_target_pairs={{0,16},{8,24},{16,0},{24,8},{1,17},{9,25},{17,1},{25,9},{2,18},{10... | collective-permute-start | bytes 196616 | tf_op jit(solution)/shard_map/ppermute | solution.py:76
  7.2 5.6 %collective-permute-start = (bf16[128,256]{1,0:T(8,128)(2,1)S(1)}, bf16[128,256]{1,0:T(8,128)(2,1)S(1)}, u32[]{:S(2)}, u32[]{:S(2)}) collective-permute-start(bf16[128,256]{1,0:T(8,128)(2,1)S(1)} %convolution_convert_fusion), channel_id=1, source_target_pairs={{0,8},{8,0},{16,24},{24,16},{1,9},{9,1},{17,25},{25,17},{2,10},{10... | collective-permute-start | bytes 196616 | tf_op jit(solution)/shard_map/ppermute | solution.py:76
  12.8 10.2 %collective-permute-start.5 = (bf16[4,128,256]{2,1,0:T(8,128)(2,1)S(1)}, bf16[4,128,256]{2,1,0:T(8,128)(2,1)S(1)}, u32[]{:S(2)}, u32[]{:S(2)}) collective-permute-start(bf16[4,128,256]{2,1,0:T(8,128)(2,1)S(1)} %pad_maximum_fusion.3.refs_0_), channel_id=1, source_target_pairs={{0,6},{1,7},{2,4},{3,5},{4,2},{5,3},{6,0},{7,1},{8,14},{9,15},{10,... | collective-permute-start | bytes 786440 | tf_op jit(solution)/shard_map/ppermute | solution.py:72
  15.4 13.7 %collective-permute-start.7 = (bf16[128,1024]{1,0:T(8,128)(2,1)S(1)}, bf16[128,1024]{1,0:T(8,128)(2,1)S(1)}, u32[]{:S(2)}, u32[]{:S(2)}) collective-permute-start(bf16[128,1024]{1,0:T(8,128)(2,1)S(1)} %get-tuple-element.80), channel_id=1, source_target_pairs={{0,16},{8,24},{16,0},{24,8},{1,17},{9,25},{17,1},{25,9},{2,18},{10... | collective-permute-start | bytes 786440 | tf_op jit(solution)/shard_map/ppermute | solution.py:76
  16.9 12.1 %collective-permute-start.6 = (bf16[128,1024]{1,0:T(8,128)(2,1)S(1)}, bf16[128,1024]{1,0:T(8,128)(2,1)S(1)}, u32[]{:S(2)}, u32[]{:S(2)}) collective-permute-start(bf16[128,1024]{1,0:T(8,128)(2,1)S(1)} %get-tuple-element.78), channel_id=1, source_target_pairs={{0,8},{8,0},{16,24},{24,16},{1,9},{9,1},{17,25},{25,17},{2,10},{10... | collective-permute-start | bytes 786440 | tf_op jit(solution)/shard_map/ppermute | solution.py:76
  18.6 10.4 %collective-permute-start.4 = (bf16[4,128,256]{2,1,0:T(8,128)(2,1)S(1)}, bf16[4,128,256]{2,1,0:T(8,128)(2,1)S(1)}, u32[]{:S(2)}, u32[]{:S(2)}) collective-permute-start(bf16[4,128,256]{2,1,0:T(8,128)(2,1)S(1)} %pad_maximum_fusion.3.refs_0_), channel_id=1, source_target_pairs={{0,4},{1,5},{2,6},{3,7},{4,0},{5,1},{6,2},{7,3},{8,12},{9,13},{10,... | collective-permute-start | bytes 786440 | tf_op jit(solution)/shard_map/ppermute | solution.py:72
  19.1 9.9 %collective-permute-start.3 = (bf16[4,128,256]{2,1,0:T(8,128)(2,1)S(1)}, bf16[4,128,256]{2,1,0:T(8,128)(2,1)S(1)}, u32[]{:S(2)}, u32[]{:S(2)}) collective-permute-start(bf16[4,128,256]{2,1,0:T(8,128)(2,1)S(1)} %pad_maximum_fusion.3.refs_0_), channel_id=1, source_target_pairs={{0,2},{1,3},{2,0},{3,1},{4,6},{5,7},{6,4},{7,5},{8,10},{9,11},{10,... | collective-permute-start | bytes 786440 | tf_op jit(solution)/shard_map/ppermute | solution.py:72
  23.0 6.6 %collective-permute-start.8 = (bf16[4,128,256]{2,1,0:T(8,128)(2,1)S(1)}, bf16[4,128,256]{2,1,0:T(8,128)(2,1)S(1)}, u32[]{:S(2)}, u32[]{:S(2)}) collective-permute-start(bf16[4,128,256]{2,1,0:T(8,128)(2,1)S(1)} %pad_maximum_fusion.3.refs_0_), channel_id=1, source_target_pairs={{0,1},{1,0},{2,3},{3,2},{4,5},{5,4},{6,7},{7,6},{8,9},{9,8},{10,11... | collective-permute-start | bytes 786440 | tf_op jit(solution)/shard_map/ppermute | solution.py:72
  31.8 7.1 %collective-permute-start.14 = (bf16[144,256]{1,0:T(8,128)(2,1)S(1)}, bf16[144,256]{1,0:T(8,128)(2,1)S(1)}, u32[]{:S(2)}, u32[]{:S(2)}) collective-permute-start(bf16[144,256]{1,0:T(8,128)(2,1)S(1)} %shard_map.324.summed_ref), channel_id=1, source_target_pairs={{0,24},{8,16},{16,8},{24,0},{1,25},{9,17},{17,9},{25,1},{2,26},{10... | collective-permute-start | bytes 221192 | tf_op jit(solution)/shard_map/ppermute | solution.py:76
  34.0 7.2 %collective-permute-start.13 = (bf16[144,256]{1,0:T(8,128)(2,1)S(1)}, bf16[144,256]{1,0:T(8,128)(2,1)S(1)}, u32[]{:S(2)}, u32[]{:S(2)}) collective-permute-start(bf16[144,256]{1,0:T(8,128)(2,1)S(1)} %shard_map.324.summed_ref), channel_id=1, source_target_pairs={{0,16},{8,24},{16,0},{24,8},{1,17},{9,25},{17,1},{25,9},{2,18},{10... | collective-permute-start | bytes 221192 | tf_op jit(solution)/shard_map/ppermute | solution.py:76
  34.0 7.2 %collective-permute-start.12 = (bf16[144,256]{1,0:T(8,128)(2,1)S(1)}, bf16[144,256]{1,0:T(8,128)(2,1)S(1)}, u32[]{:S(2)}, u32[]{:S(2)}) collective-permute-start(bf16[144,256]{1,0:T(8,128)(2,1)S(1)} %shard_map.324.summed_ref), channel_id=1, source_target_pairs={{0,8},{8,0},{16,24},{24,16},{1,9},{9,1},{17,25},{25,17},{2,10},{10... | collective-permute-start | bytes 221192 | tf_op jit(solution)/shard_map/ppermute | solution.py:76
  36.3 7.0 %collective-permute-start.30 = (bf16[602,128]{1,0:T(8,128)(2,1)S(1)}, bf16[602,128]{1,0:T(8,128)(2,1)S(1)}, u32[]{:S(2)}, u32[]{:S(2)}) collective-permute-start(bf16[602,128]{1,0:T(8,128)(2,1)S(1)} %bitcast.51), channel_id=1, source_target_pairs={{0,4},{1,5},{2,6},{3,7},{4,0},{5,1},{6,2},{7,3},{8,12},{9,13},{10,... | collective-permute-start | bytes 462344 | tf_op jit(solution)/shard_map/ppermute | solution.py:72
  36.8 8.0 %collective-permute-start.29 = (bf16[602,128]{1,0:T(8,128)(2,1)S(1)}, bf16[602,128]{1,0:T(8,128)(2,1)S(1)}, u32[]{:S(2)}, u32[]{:S(2)}) collective-permute-start(bf16[602,128]{1,0:T(8,128)(2,1)S(1)} %bitcast.52), channel_id=1, source_target_pairs={{0,2},{1,3},{2,0},{3,1},{4,6},{5,7},{6,4},{7,5},{8,10},{9,11},{10,... | collective-permute-start | bytes 462344 | tf_op jit(solution)/shard_map/ppermute | solution.py:72
  38.9 8.4 %collective-permute-start.31 = (bf16[602,128]{1,0:T(8,128)(2,1)S(1)}, bf16[602,128]{1,0:T(8,128)(2,1)S(1)}, u32[]{:S(2)}, u32[]{:S(2)}) collective-permute-start(bf16[602,128]{1,0:T(8,128)(2,1)S(1)} %bitcast.53), channel_id=1, source_target_pairs={{0,6},{1,7},{2,4},{3,5},{4,2},{5,3},{6,0},{7,1},{8,14},{9,15},{10,... | collective-permute-start | bytes 462344 | tf_op jit(solution)/shard_map/ppermute | solution.py:72
  41.2 12.9 %collective-permute-start.17 = (bf16[4,144,256]{2,1,0:T(8,128)(2,1)S(1)}, bf16[4,144,256]{2,1,0:T(8,128)(2,1)S(1)}, u32[]{:S(2)}, u32[]{:S(2)}) collective-permute-start(bf16[4,144,256]{2,1,0:T(8,128)(2,1)S(1)} %pad_maximum_fusion.1.refs_0_), channel_id=1, source_target_pairs={{0,6},{1,7},{2,4},{3,5},{4,2},{5,3},{6,0},{7,1},{8,14},{9,15},{10,... | collective-permute-start | bytes 884744 | tf_op jit(solution)/shard_map/ppermute | solution.py:72
  42.2 16.5 %collective-permute-start.16 = (bf16[4,144,256]{2,1,0:T(8,128)(2,1)S(1)}, bf16[4,144,256]{2,1,0:T(8,128)(2,1)S(1)}, u32[]{:S(2)}, u32[]{:S(2)}) collective-permute-start(bf16[4,144,256]{2,1,0:T(8,128)(2,1)S(1)} %pad_maximum_fusion.1.refs_0_), channel_id=1, source_target_pairs={{0,4},{1,5},{2,6},{3,7},{4,0},{5,1},{6,2},{7,3},{8,12},{9,13},{10,... | collective-permute-start | bytes 884744 | tf_op jit(solution)/shard_map/ppermute | solution.py:72
  43.3 15.5 %collective-permute-start.15 = (bf16[4,144,256]{2,1,0:T(8,128)(2,1)S(1)}, bf16[4,144,256]{2,1,0:T(8,128)(2,1)S(1)}, u32[]{:S(2)}, u32[]{:S(2)}) collective-permute-start(bf16[4,144,256]{2,1,0:T(8,128)(2,1)S(1)} %pad_maximum_fusion.1.refs_0_), channel_id=1, source_target_pairs={{0,2},{1,3},{2,0},{3,1},{4,6},{5,7},{6,4},{7,5},{8,10},{9,11},{10,... | collective-permute-start | bytes 884744 | tf_op jit(solution)/shard_map/ppermute | solution.py:72
  44.8 9.3 %collective-permute-start.18 = (bf16[128,1024]{1,0:T(8,128)(2,1)S(1)}, bf16[128,1024]{1,0:T(8,128)(2,1)S(1)}, u32[]{:S(2)}, u32[]{:S(2)}) collective-permute-start(bf16[128,1024]{1,0:T(8,128)(2,1)S(1)} %get-tuple-element.83), channel_id=1, source_target_pairs={{0,24},{8,16},{16,8},{24,0},{1,25},{9,17},{17,9},{25,1},{2,26},{10... | collective-permute-start | bytes 786440 | tf_op jit(solution)/shard_map/ppermute | solution.py:76
  47.7 20.0 %collective-permute-start.32 = (bf16[4,602,128]{2,0,1:T(4,128)(2,1)S(1)}, bf16[4,602,128]{2,0,1:T(4,128)(2,1)S(1)}, u32[]{:S(2)}, u32[]{:S(2)}) collective-permute-start(bf16[4,602,128]{2,0,1:T(4,128)(2,1)S(1)} %copy.37), channel_id=1, source_target_pairs={{0,1},{1,0},{2,3},{3,2},{4,5},{5,4},{6,7},{7,6},{8,9},{9,8},{10,11... | collective-permute-start | bytes 1849352 | tf_op jit(solution)/shard_map/ppermute | solution.py:72
  54.1 5.1 %collective-permute-start.19 = (bf16[4,144,256]{2,1,0:T(8,128)(2,1)S(1)}, bf16[4,144,256]{2,1,0:T(8,128)(2,1)S(1)}, u32[]{:S(2)}, u32[]{:S(2)}) collective-permute-start(bf16[4,144,256]{2,1,0:T(8,128)(2,1)S(1)} %pad_maximum_fusion.1.refs_0_), channel_id=1, source_target_pairs={{0,1},{1,0},{2,3},{3,2},{4,5},{5,4},{6,7},{7,6},{8,9},{9,8},{10,11... | collective-permute-start | bytes 884744 | tf_op jit(solution)/shard_map/ppermute | solution.py:72
  54.1 5.1 %collective-permute-start.22 = (bf16[4,144,256]{2,1,0:T(8,128)(2,1)S(1)}, bf16[4,144,256]{2,1,0:T(8,128)(2,1)S(1)}, u32[]{:S(2)}, u32[]{:S(2)}) collective-permute-start(bf16[4,144,256]{2,1,0:T(8,128)(2,1)S(1)} %collective-permute-done.17.refs_3_), channel_id=1, source_target_pairs={{0,1},{1,0},{2,3},{3,2},{4,5},{5,4},{6,7},{7,6},{8,9},{9,8},{10,11... | collective-permute-start | bytes 884744 | tf_op jit(solution)/shard_map/ppermute | solution.py:72
  63.2 7.1 %collective-permute-start.25 = (bf16[144,256]{1,0:T(8,128)(2,1)S(1)}, bf16[144,256]{1,0:T(8,128)(2,1)S(1)}, u32[]{:S(2)}, u32[]{:S(2)}) collective-permute-start(bf16[144,256]{1,0:T(8,128)(2,1)S(1)} %get-tuple-element.85.summed_ref), channel_id=1, source_target_pairs={{0,24},{8,16},{16,8},{24,0},{1,25},{9,17},{17,9},{25,1},{2,26},{10... | collective-permute-start | bytes 221192 | tf_op jit(solution)/shard_map/ppermute | solution.py:76
  65.0 7.6 %collective-permute-start.24 = (bf16[144,256]{1,0:T(8,128)(2,1)S(1)}, bf16[144,256]{1,0:T(8,128)(2,1)S(1)}, u32[]{:S(2)}, u32[]{:S(2)}) collective-permute-start(bf16[144,256]{1,0:T(8,128)(2,1)S(1)} %get-tuple-element.85.summed_ref), channel_id=1, source_target_pairs={{0,16},{8,24},{16,0},{24,8},{1,17},{9,25},{17,1},{25,9},{2,18},{10... | collective-permute-start | bytes 221192 | tf_op jit(solution)/shard_map/ppermute | solution.py:76
  65.0 7.6 %collective-permute-start.23 = (bf16[144,256]{1,0:T(8,128)(2,1)S(1)}, bf16[144,256]{1,0:T(8,128)(2,1)S(1)}, u32[]{:S(2)}, u32[]{:S(2)}) collective-permute-start(bf16[144,256]{1,0:T(8,128)(2,1)S(1)} %get-tuple-element.85.summed_ref), channel_id=1, source_target_pairs={{0,8},{8,0},{16,24},{24,16},{1,9},{9,1},{17,25},{25,17},{2,10},{10... | collective-permute-start | bytes 221192 | tf_op jit(solution)/shard_map/ppermute | solution.py:76
  72.6 8.6 %collective-permute-start.33 = (bf16[602,128]{1,0:T(8,128)(2,1)S(1)}, bf16[602,128]{1,0:T(8,128)(2,1)S(1)}, u32[]{:S(2)}, u32[]{:S(2)}) collective-permute-start(bf16[602,128]{1,0:T(8,128)(2,1)S(1)} %get-tuple-element.92), channel_id=1, source_target_pairs={{0,24},{8,16},{16,8},{24,0},{1,25},{9,17},{17,9},{25,1},{2,26},{10... | collective-permute-start | bytes 462344 | tf_op jit(solution)/shard_map/ppermute | solution.py:76
  74.4 14.5 %collective-permute-start.28 = (bf16[4,144,256]{2,1,0:T(8,128)(2,1)S(1)}, bf16[4,144,256]{2,1,0:T(8,128)(2,1)S(1)}, u32[]{:S(2)}, u32[]{:S(2)}) collective-permute-start(bf16[4,144,256]{2,1,0:T(8,128)(2,1)S(1)} %pad_maximum_fusion.2.refs_0_), channel_id=1, source_target_pairs={{0,6},{1,7},{2,4},{3,5},{4,2},{5,3},{6,0},{7,1},{8,14},{9,15},{10,... | collective-permute-start | bytes 884744 | tf_op jit(solution)/shard_map/ppermute | solution.py:72
  75.4 14.7 %collective-permute-start.27 = (bf16[4,144,256]{2,1,0:T(8,128)(2,1)S(1)}, bf16[4,144,256]{2,1,0:T(8,128)(2,1)S(1)}, u32[]{:S(2)}, u32[]{:S(2)}) collective-permute-start(bf16[4,144,256]{2,1,0:T(8,128)(2,1)S(1)} %pad_maximum_fusion.2.refs_0_), channel_id=1, source_target_pairs={{0,4},{1,5},{2,6},{3,7},{4,0},{5,1},{6,2},{7,3},{8,12},{9,13},{10,... | collective-permute-start | bytes 884744 | tf_op jit(solution)/shard_map/ppermute | solution.py:72
  76.8 13.3 %collective-permute-start.26 = (bf16[4,144,256]{2,1,0:T(8,128)(2,1)S(1)}, bf16[4,144,256]{2,1,0:T(8,128)(2,1)S(1)}, u32[]{:S(2)}, u32[]{:S(2)}) collective-permute-start(bf16[4,144,256]{2,1,0:T(8,128)(2,1)S(1)} %pad_maximum_fusion.2.refs_0_), channel_id=1, source_target_pairs={{0,2},{1,3},{2,0},{3,1},{4,6},{5,7},{6,4},{7,5},{8,10},{9,11},{10,... | collective-permute-start | bytes 884744 | tf_op jit(solution)/shard_map/ppermute | solution.py:72
  77.9 9.5 %collective-permute-start.34 = (bf16[602,128]{1,0:T(8,128)(2,1)S(1)}, bf16[602,128]{1,0:T(8,128)(2,1)S(1)}, u32[]{:S(2)}, u32[]{:S(2)}) collective-permute-start(bf16[602,128]{1,0:T(8,128)(2,1)S(1)} %get-tuple-element.94), channel_id=1, source_target_pairs={{0,16},{8,24},{16,0},{24,8},{1,17},{9,25},{17,1},{25,9},{2,18},{10... | collective-permute-start | bytes 462344 | tf_op jit(solution)/shard_map/ppermute | solution.py:76
  81.2 7.8 %collective-permute-start.35 = (bf16[602,128]{1,0:T(8,128)(2,1)S(1)}, bf16[602,128]{1,0:T(8,128)(2,1)S(1)}, u32[]{:S(2)}, u32[]{:S(2)}) collective-permute-start(bf16[602,128]{1,0:T(8,128)(2,1)S(1)} %get-tuple-element.96), channel_id=1, source_target_pairs={{0,8},{8,0},{16,24},{24,16},{1,9},{9,1},{17,25},{25,17},{2,10},{10... | collective-permute-start | bytes 462344 | tf_op jit(solution)/shard_map/ppermute | solution.py:76
  96.8 5.6 %collective-permute-start.42 = (bf16[64,128]{1,0:T(8,128)(2,1)S(1)}, bf16[64,128]{1,0:T(8,128)(2,1)S(1)}, u32[]{:S(2)}, u32[]{:S(2)}) collective-permute-start(bf16[64,128]{1,0:T(8,128)(2,1)S(1)} %get-tuple-element.101.refs_0_), channel_id=1, source_target_pairs={{0,24},{8,16},{16,8},{24,0},{1,25},{9,17},{17,9},{25,1},{2,26},{10... | collective-permute-start | bytes 49160 | tf_op jit(solution)/shard_map/ppermute | solution.py:76
  98.9 4.6 %collective-permute-start.41 = (bf16[64,128]{1,0:T(8,128)(2,1)S(1)}, bf16[64,128]{1,0:T(8,128)(2,1)S(1)}, u32[]{:S(2)}, u32[]{:S(2)}) collective-permute-start(bf16[64,128]{1,0:T(8,128)(2,1)S(1)} %get-tuple-element.101.refs_0_), channel_id=1, source_target_pairs={{0,16},{8,24},{16,0},{24,8},{1,17},{9,25},{17,1},{25,9},{2,18},{10... | collective-permute-start | bytes 49160 | tf_op jit(solution)/shard_map/ppermute | solution.py:76
  98.9 4.6 %collective-permute-start.40 = (bf16[64,128]{1,0:T(8,128)(2,1)S(1)}, bf16[64,128]{1,0:T(8,128)(2,1)S(1)}, u32[]{:S(2)}, u32[]{:S(2)}) collective-permute-start(bf16[64,128]{1,0:T(8,128)(2,1)S(1)} %get-tuple-element.101.refs_0_), channel_id=1, source_target_pairs={{0,8},{8,0},{16,24},{24,16},{1,9},{9,1},{17,25},{25,17},{2,10},{10... | collective-permute-start | bytes 49160 | tf_op jit(solution)/shard_map/ppermute | solution.py:76
  106.9 4.6 %collective-permute-start.46 = (bf16[64,128]{1,0:T(8,128)(2,1)S(1)}, bf16[64,128]{1,0:T(8,128)(2,1)S(1)}, u32[]{:S(2)}, u32[]{:S(2)}) collective-permute-start(bf16[64,128]{1,0:T(8,128)(2,1)S(1)} %get-tuple-element.105), channel_id=1, source_target_pairs={{0,6},{1,7},{2,4},{3,5},{4,2},{5,3},{6,0},{7,1},{8,14},{9,15},{10,... | collective-permute-start | bytes 49160 | tf_op jit(solution)/shard_map/ppermute | solution.py:72
  112.0 6.3 %collective-permute-start.49 = (bf16[272,128]{1,0:T(8,128)(2,1)S(1)}, bf16[272,128]{1,0:T(8,128)(2,1)S(1)}, u32[]{:S(2)}, u32[]{:S(2)}) collective-permute-start(bf16[272,128]{1,0:T(8,128)(2,1)S(1)} %get-tuple-element.112.refs_0_), channel_id=1, source_target_pairs={{0,24},{8,16},{16,8},{24,0},{1,25},{9,17},{17,9},{25,1},{2,26},{10... | collective-permute-start | bytes 208904 | tf_op jit(solution)/shard_map/ppermute | solution.py:76
  113.8 6.3 %collective-permute-start.48 = (bf16[272,128]{1,0:T(8,128)(2,1)S(1)}, bf16[272,128]{1,0:T(8,128)(2,1)S(1)}, u32[]{:S(2)}, u32[]{:S(2)}) collective-permute-start(bf16[272,128]{1,0:T(8,128)(2,1)S(1)} %get-tuple-element.112.refs_0_), channel_id=1, source_target_pairs={{0,16},{8,24},{16,0},{24,8},{1,17},{9,25},{17,1},{25,9},{2,18},{10... | collective-permute-start | bytes 208904 | tf_op jit(solution)/shard_map/ppermute | solution.py:76
  115.0 5.2 %collective-permute-start.47 = (bf16[272,128]{1,0:T(8,128)(2,1)S(1)}, bf16[272,128]{1,0:T(8,128)(2,1)S(1)}, u32[]{:S(2)}, u32[]{:S(2)}) collective-permute-start(bf16[272,128]{1,0:T(8,128)(2,1)S(1)} %get-tuple-element.112.refs_0_), channel_id=1, source_target_pairs={{0,8},{8,0},{16,24},{24,16},{1,9},{9,1},{17,25},{25,17},{2,10},{10... | collective-permute-start | bytes 208904 | tf_op jit(solution)/shard_map/ppermute | solution.py:76
  122.2 4.4 %collective-permute-start.51 = (bf16[272,128]{1,0:T(8,128)(2,1)S(1)}, bf16[272,128]{1,0:T(8,128)(2,1)S(1)}, u32[]{:S(2)}, u32[]{:S(2)}) collective-permute-start(bf16[272,128]{1,0:T(8,128)(2,1)S(1)} %get-tuple-element.114), channel_id=1, source_target_pairs={{0,2},{1,3},{2,0},{3,1},{4,6},{5,7},{6,4},{7,5},{8,10},{9,11},{10,... | collective-permute-start | bytes 208904 | tf_op jit(solution)/shard_map/ppermute | solution.py:72
  123.4 5.1 %collective-permute-start.52 = (bf16[272,128]{1,0:T(8,128)(2,1)S(1)}, bf16[272,128]{1,0:T(8,128)(2,1)S(1)}, u32[]{:S(2)}, u32[]{:S(2)}) collective-permute-start(bf16[272,128]{1,0:T(8,128)(2,1)S(1)} %get-tuple-element.115), channel_id=1, source_target_pairs={{0,4},{1,5},{2,6},{3,7},{4,0},{5,1},{6,2},{7,3},{8,12},{9,13},{10,... | collective-permute-start | bytes 208904 | tf_op jit(solution)/shard_map/ppermute | solution.py:72
  124.5 5.2 %collective-permute-start.53 = (bf16[272,128]{1,0:T(8,128)(2,1)S(1)}, bf16[272,128]{1,0:T(8,128)(2,1)S(1)}, u32[]{:S(2)}, u32[]{:S(2)}) collective-permute-start(bf16[272,128]{1,0:T(8,128)(2,1)S(1)} %get-tuple-element.116), channel_id=1, source_target_pairs={{0,6},{1,7},{2,4},{3,5},{4,2},{5,3},{6,0},{7,1},{8,14},{9,15},{10,... | collective-permute-start | bytes 208904 | tf_op jit(solution)/shard_map/ppermute | solution.py:72
  133.1 5.0 %collective-permute-start.56 = (bf16[128,256]{1,0:T(8,128)(2,1)S(1)}, bf16[128,256]{1,0:T(8,128)(2,1)S(1)}, u32[]{:S(2)}, u32[]{:S(2)}) collective-permute-start(bf16[128,256]{1,0:T(8,128)(2,1)S(1)} %get-tuple-element.121), channel_id=1, source_target_pairs={{0,4},{1,5},{2,6},{3,7},{4,0},{5,1},{6,2},{7,3},{8,12},{9,13},{10,... | collective-permute-start | bytes 196616 | tf_op jit(solution)/shard_map/ppermute | solution.py:72
  133.9 5.2 %collective-permute-start.57 = (bf16[128,256]{1,0:T(8,128)(2,1)S(1)}, bf16[128,256]{1,0:T(8,128)(2,1)S(1)}, u32[]{:S(2)}, u32[]{:S(2)}) collective-permute-start(bf16[128,256]{1,0:T(8,128)(2,1)S(1)} %get-tuple-element.122), channel_id=1, source_target_pairs={{0,6},{1,7},{2,4},{3,5},{4,2},{5,3},{6,0},{7,1},{8,14},{9,15},{10,... | collective-permute-start | bytes 196616 | tf_op jit(solution)/shard_map/ppermute | solution.py:72
  139.2 6.4 %collective-permute-start.60 = (bf16[128,256]{1,0:T(8,128)(2,1)S(1)}, bf16[128,256]{1,0:T(8,128)(2,1)S(1)}, u32[]{:S(2)}, u32[]{:S(2)}) collective-permute-start(bf16[128,256]{1,0:T(8,128)(2,1)S(1)} %shard_map.338.own_ref), channel_id=1, source_target_pairs={{0,24},{8,16},{16,8},{24,0},{1,25},{9,17},{17,9},{25,1},{2,26},{10... | collective-permute-start | bytes 196616 | tf_op jit(solution)/shard_map/ppermute | solution.py:76
  141.2 5.9 %collective-permute-start.59 = (bf16[128,256]{1,0:T(8,128)(2,1)S(1)}, bf16[128,256]{1,0:T(8,128)(2,1)S(1)}, u32[]{:S(2)}, u32[]{:S(2)}) collective-permute-start(bf16[128,256]{1,0:T(8,128)(2,1)S(1)} %shard_map.338.own_ref), channel_id=1, source_target_pairs={{0,16},{8,24},{16,0},{24,8},{1,17},{9,25},{17,1},{25,9},{2,18},{10... | collective-permute-start | bytes 196616 | tf_op jit(solution)/shard_map/ppermute | solution.py:76
  141.3 5.7 %collective-permute-start.58 = (bf16[128,256]{1,0:T(8,128)(2,1)S(1)}, bf16[128,256]{1,0:T(8,128)(2,1)S(1)}, u32[]{:S(2)}, u32[]{:S(2)}) collective-permute-start(bf16[128,256]{1,0:T(8,128)(2,1)S(1)} %shard_map.338.own_ref), channel_id=1, source_target_pairs={{0,8},{8,0},{16,24},{24,16},{1,9},{9,1},{17,25},{25,17},{2,10},{10... | collective-permute-start | bytes 196616 | tf_op jit(solution)/shard_map/ppermute | solution.py:76
  147.1 5.9 %collective-permute-start.63 = (bf16[128,256]{1,0:T(8,128)(2,1)S(1)}, bf16[128,256]{1,0:T(8,128)(2,1)S(1)}, u32[]{:S(2)}, u32[]{:S(2)}) collective-permute-start(bf16[128,256]{1,0:T(8,128)(2,1)S(1)} %shard_map.339.refs_0_), channel_id=1, source_target_pairs={{0,6},{1,7},{2,4},{3,5},{4,2},{5,3},{6,0},{7,1},{8,14},{9,15},{10,... | collective-permute-start | bytes 196616 | tf_op jit(solution)/shard_map/ppermute | solution.py:72
  148.9 4.6 %collective-permute-start.62 = (bf16[128,256]{1,0:T(8,128)(2,1)S(1)}, bf16[128,256]{1,0:T(8,128)(2,1)S(1)}, u32[]{:S(2)}, u32[]{:S(2)}) collective-permute-start(bf16[128,256]{1,0:T(8,128)(2,1)S(1)} %shard_map.339.refs_0_), channel_id=1, source_target_pairs={{0,4},{1,5},{2,6},{3,7},{4,0},{5,1},{6,2},{7,3},{8,12},{9,13},{10,... | collective-permute-start | bytes 196616 | tf_op jit(solution)/shard_map/ppermute | solution.py:72
  (40 other events, 276.2 us)

commit v5 on v4

--- a/solution.py
+++ b/solution.py
@@ -84,18 +84,45 @@
     return lax.optimization_barrier((block, *others))[0]
 
 
-def gather_all(block, beside=(), within=()):
+def stack_kernel(*refs):
+    refs, out_ref = refs[3::-1], refs[4]
+    for k, ref in enumerate(refs):
+        out_ref[k] = ref[...]
+
+
+def line_kernel(*refs):
+    refs, (out_ref, centres_ref) = refs[3::-1], refs[4:]
+    rows = refs[0].shape[0] - EXTRA
+    centres_ref[...] = jnp.zeros(centres_ref.shape, F32)
+    for k, ref in enumerate(refs):
+        out_ref[k * rows : (k + 1) * rows, :] = ref[:rows, :]
+        centres_ref[k : k + 1, :] = ref[rows:, :].astype(F32)[:1]
+    out_ref[4 * rows :, :] = centres_ref[...].astype(BF)
+
+
+def gather_all(block, beside=(), within=(), centred=True, early=()):
     if short_line():
         line = [block] + [pass_line(block, k) for k in range(1, 4)]
-        line = jnp.stack(line)
+        if centred:
+            tall, width = block.shape
+            (line,) = run(
+                line_kernel,
+                [shape((4 * tall - 3 * EXTRA, width), BF)],
+                line[::-1],
+                scratch=[pltpu.VMEM((EXTRA, width), F32)],
+            )
+        else:
+            (line,) = run(stack_kernel, [shape((4, *block.shape), BF)], line[::-1])
     else:
         line = lax.all_gather(block, "z", axis=0)
+    if early:
+        line, *early = lax.optimization_barrier((line, *early))
     passed = [pass_line(after(part, line), mask) for part, mask in beside]
     lines = [line] + [swap(line, 2 * k) for k in range(1, 4)]
     if passed or within:
         lines[3], *rest = lax.optimization_barrier((lines[3], *passed, *within))
         passed, within = rest[: len(passed)], rest[len(passed) :]
-    return lines + [swap(line, 1) for line in lines], passed, within
+    return lines + [swap(line, 1) for line in lines], passed, within, early
 
 
 def arrange_kernel(
@@ -141,11 +168,16 @@
 
 
 def block_at(ref, i, rows):
-    return ref[i, :rows, :].astype(F32), ref[i, rows:, :].astype(F32)[:1]
+    if len(ref.shape) == 3:
+        return ref[i, :rows, :].astype(F32), ref[i, rows:, :].astype(F32)[:1]
+    return (
+        ref[i * rows : (i + 1) * rows, :].astype(F32),
+        ref[4 * rows :, :].astype(F32)[i : i + 1],
+    )
 
 
 def block_loop(ref, pair, body, carry):
-    if ref.shape[0] > 4:
+    if len(ref.shape) == 3:
         return lax.fori_loop(
             0, ref.shape[0] // pair, lambda i, carry: body(i * pair, carry), carry
         )
@@ -253,7 +285,7 @@
 
 
 def cross_kernel(width, count, *refs):
-    turned_refs, level_refs, (send_ref,) = refs[:count], refs[count : 2 * count], refs[2 * count :]
+    turned_refs, level_refs, (send_ref,) = refs[:count][::-1], refs[count : 2 * count], refs[2 * count :]
     half = send_ref.shape[1]
 
     def out(value):
@@ -269,7 +301,7 @@
 
 
 def keep_kernel(width, count, *refs):
-    turned_refs, level_refs, (out_ref,) = refs[:count], refs[count : 2 * count], refs[2 * count :]
+    turned_refs, level_refs, (out_ref,) = refs[:count][::-1], refs[count : 2 * count], refs[2 * count :]
 
     def out(value):
         out_ref[...] = value
@@ -305,20 +337,20 @@
     (send,) = run(
         functools.partial(cross_kernel, width, count),
         [shape((tall, half), BF)],
-        [*turned, *levels],
+        [*turned[::-1], *levels],
         flops=work,
     )
     got = swap(send, 1)
     (kept,) = run(
         functools.partial(keep_kernel, width, count),
         [shape((width, half))],
-        [*turned, *levels],
+        [*turned[::-1], *levels],
         flops=work,
     )
     own, *pieces = run(
         fold_kernel, [shape((tall, LANES))] + [shape((tall, LANES), BF)] * 3, [kept, send, got]
     )
-    return [own] + [swap(pieces[k - 1], 2 * k) for k in range(1, 4)]
+    return [swap(pieces[k - 1], 2 * k) for k in (3, 2, 1)] + [own]
 
 
 def line_total(refs, width):
@@ -577,7 +609,7 @@
     if short_line():
         (shard,) = run(pile_sum_kernel, [shape((size, width), BF)], [own, *got])
         got = [pass_line(shard, k) for k in range(1, 4)]
-        (shard,) = run(pile_sum_kernel, [shape((size, width), BF)], [shard, *got])
+        (shard,) = run(pile_sum_kernel, [shape((size, width), BF)], [*got[::-1], shard])
     else:
         (shard,) = run(pile_sum_kernel, [shape((size, width))], [own, *got])
         shard = lax.psum(shard, "z").astype(BF)
@@ -643,19 +675,23 @@
 
     projected = dot(features, w_first.astype(BF)).astype(BF)
     turned = features.T
-    turned = jnp.stack([turned] + [swap(turned, 2 * k) for k in range(1, 4)])
     short = short_line()
     if not short:
         levels = [lax.all_to_all(levels[0], "z", 0, 0)]
-    around, passed, unused = gather_all(
-        projected, [(levels[1], 1), (levels[2], 2)] if short else ()
-    )
+    around, passed, unused, (turned_x,) = gather_all(
+        projected,
+        [(levels[1], 1), (levels[2], 2)] if short else (),
+        centred=False,
+        early=[swap(turned, 2)],
+    )
+    turned = jnp.stack([turned, turned_x])
+    turned = jnp.concatenate([turned, swap(turned, 4)])
     if short:
         levels[1:3] = passed
     (summed_one,) = run(
         first_sum_kernel, [shape((tall, hidden), BF)], [near, far, *around], flops=work
     )
-    around, passed, unused = gather_all(summed_one, [(levels[3], 3)] if short else ())
+    around, passed, *unused = gather_all(summed_one, [(levels[3], 3)] if short else ())
     if short:
         levels[3:] = passed
     summed_two, stats_one = run(
@@ -677,11 +713,11 @@
     mixed = run(
         mix_kernel, mixed_shapes, [turned, swap(turned, 1), *levels], flops=2 * work
     )
-    around, passed, (slopes_one,) = gather_all(
-        summed_two, [(mixed[k], k) for k in (3, 2, 1)] if short else (), [slopes_one]
+    around, passed, (slopes_one,), unused = gather_all(
+        summed_two, [(mixed[k], k) for k in (1, 2, 3)] if short else (), [slopes_one]
     )
     if short:
-        mixed = [mixed[0], *passed[::-1]]
+        mixed = [mixed[0], *passed]
     else:
         mixed = [lax.psum_scatter(mixed[0], "z", scatter_dimension=0)]
     packed, stats_two = run(

time: 158 us -> 155 us (0.981)
  waiting for transfers between devices: 65.3 us -> 63.4 us
    ppermute x44 -> x43, waiting for transfers between devices: 30.7 us -> 22.9 us  [swap(): return lax.ppermute(block, PLANE, [(i, i ^ mask) for i in range(8)])]
    ppermute x24, waiting for transfers between devices: 34.6 us -> 40.6 us  [pass_line(): return lax.ppermute(block, 'z', [(i, i ^ mask) for i in range(4)])]
    ppermute x24, starting transfers between devices: 37.5 us -> 35.8 us  [pass_line(): return lax.ppermute(block, 'z', [(i, i ^ mask) for i in range(4)])]
    ppermute x44 -> x43, starting transfers between devices: 29.7 us -> 30.8 us  [swap(): return lax.ppermute(block, PLANE, [(i, i ^ mask) for i in range(8)])]
    pallas_call x18 -> x21, Pallas kernels: 18 us -> 18 us  [run(): pl.pallas_call(body, out_shape=tuple(outs), in_specs=[pl.BlockSpec(memory...]
  transfers between devices with their start and end apart: 68 -> 67, of which waited for: 43 -> 43; matrix products, arithmetic and copies ran while one was open for 1% -> 2% of each run, Pallas kernels for 5% -> 6%
where the time goes in v5:
time: 155 us
  starting transfers between devices  66.6 us (43%)
  waiting for transfers between devices  63.4 us (41%)
  Pallas kernels  18 us (12%)
  local copies, waits for them, and re-layouts  3.54 us (2%)
    ppermute x24, waiting for transfers between devices, pass_line(): return lax.ppermute(block, 'z', [(i, i ^ mask) for i in range(4)])  40.6 us
    ppermute x24, starting transfers between devices, pass_line(): return lax.ppermute(block, 'z', [(i, i ^ mask) for i in range(4)])  35.8 us
    ppermute x43, starting transfers between devices, swap(): return lax.ppermute(block, PLANE, [(i, i ^ mask) for i in range(8)])  30.8 us
    ppermute x43, waiting for transfers between devices, swap(): return lax.ppermute(block, PLANE, [(i, i ^ mask) for i in range(8)])  22.9 us
    pallas_call x21, Pallas kernels, run(): pl.pallas_call(body, out_shape=tuple(outs), in_specs=[pl.BlockSpec(memory...  18 us
  transfers between devices with their start and end apart: 67, of which 43 were waited for; matrix products, arithmetic and copies ran while one was open for 2% of the time, Pallas kernels for 6%

profile of v5, /device:TPU:0, one launch (start us, length us, event | category | flops | bytes accessed | tf_op | source)
XLA Modules:
  0.0 155.2 jit_solution(2154807580490452609)
XLA Ops:
  0.7 3.0 %collective-permute-start.3 = (bf16[602,128]{1,0:T(8,128)(2,1)}, bf16[602,128]{1,0:T(8,128)(2,1)S(1)}, u32[]{:S(2)}, u32[]{:S(2)}) collective-permute-start(bf16[602,128]{1,0:T(8,128)(2,1)} %bitcast.35), channel_id=1, source_target_pairs={{0,2},{1,3},{2,0},{3,1},{4,6},{5,7},{6,4},{7,5},{8,10},{9,11},{10,... | collective-permute-start | bytes 462344 | tf_op jit(solution)/shard_map/ppermute | solution.py:72
  3.7 1.4 convolution_convert_fusion.refs_3_
  5.1 3.7 %collective-permute-start = (bf16[128,256]{1,0:T(8,128)(2,1)S(1)}, bf16[128,256]{1,0:T(8,128)(2,1)S(1)}, u32[]{:S(2)}, u32[]{:S(2)}) collective-permute-start(bf16[128,256]{1,0:T(8,128)(2,1)S(1)} %convolution_convert_fusion.refs_3_), channel_id=1, source_target_pairs={{0,24},{8,16},{16,8},{24,0},{1,25},{9,17},{17,9},{25,1},{2,26},{10... | collective-permute-start | bytes 196616 | tf_op jit(solution)/shard_map/ppermute | solution.py:76
  12.4 1.7 %collective-permute-done.1.refs_1_ = bf16[128,256]{1,0:T(8,128)(2,1)S(1)} collective-permute-done((bf16[128,256]{1,0:T(8,128)(2,1)S(1)}, bf16[128,256]{1,0:T(8,128)(2,1)S(1)}, u32[]{:S(2)}, u32[]{:S(2)}) %collective-permute-start.1) | collective-permute-done | bytes 65568 | tf_op jit(solution)/shard_map/ppermute | solution.py:76
  15.3 2.2 %collective-permute-start.8 = (bf16[128,1024]{1,0:T(8,128)(2,1)S(1)}, bf16[128,1024]{1,0:T(8,128)(2,1)S(1)}, u32[]{:S(2)}, u32[]{:S(2)}) collective-permute-start(bf16[128,1024]{1,0:T(8,128)(2,1)S(1)} %get-tuple-element.83), channel_id=1, source_target_pairs={{0,16},{8,24},{16,0},{24,8},{1,17},{9,25},{17,1},{25,9},{2,18},{10... | collective-permute-start | bytes 786440 | tf_op jit(solution)/shard_map/ppermute | solution.py:76
  17.5 1.5 collective-permute-start.6
  18.9 1.5 collective-permute-start.4
  20.9 5.8 %collective-permute-done.7.refs_1_.refs_5_ = bf16[128,1024]{1,0:T(8,128)(2,1)S(1)} collective-permute-done((bf16[128,1024]{1,0:T(8,128)(2,1)S(1)}, bf16[128,1024]{1,0:T(8,128)(2,1)S(1)}, u32[]{:S(2)}, u32[]{:S(2)}) %collective-permute-start.7) | collective-permute-done | bytes 262176 | tf_op jit(solution)/shard_map/ppermute | solution.py:76
  26.7 1.8 %collective-permute-done.8.refs_2_.refs_6_ = bf16[128,1024]{1,0:T(8,128)(2,1)S(1)} collective-permute-done((bf16[128,1024]{1,0:T(8,128)(2,1)S(1)}, bf16[128,1024]{1,0:T(8,128)(2,1)S(1)}, u32[]{:S(2)}, u32[]{:S(2)}) %collective-permute-start.8) | collective-permute-done | bytes 262176 | tf_op jit(solution)/shard_map/ppermute | solution.py:76
  32.1 2.7 %collective-permute-start.13 = (bf16[144,256]{1,0:T(8,128)(2,1)S(1)}, bf16[144,256]{1,0:T(8,128)(2,1)S(1)}, u32[]{:S(2)}, u32[]{:S(2)}) collective-permute-start(bf16[144,256]{1,0:T(8,128)(2,1)S(1)} %shard_map.325.refs_3_.summed_ref), channel_id=1, source_target_pairs={{0,24},{8,16},{16,8},{24,0},{1,25},{9,17},{17,9},{25,1},{2,26},{10... | collective-permute-start | bytes 221192 | tf_op jit(solution)/shard_map/ppermute | solution.py:76
  34.8 1.7 %collective-permute-start.15 = (bf16[144,256]{1,0:T(8,128)(2,1)S(1)}, bf16[144,256]{1,0:T(8,128)(2,1)S(1)}, u32[]{:S(2)}, u32[]{:S(2)}) collective-permute-start(bf16[144,256]{1,0:T(8,128)(2,1)S(1)} %shard_map.325.refs_3_.summed_ref), channel_id=1, source_target_pairs={{0,8},{8,0},{16,24},{24,16},{1,9},{9,1},{17,25},{25,17},{2,10},{10... | collective-permute-start | bytes 221192 | tf_op jit(solution)/shard_map/ppermute | solution.py:76
  36.5 2.6 %collective-permute-done.13.refs_0_ = bf16[144,256]{1,0:T(8,128)(2,1)S(1)} collective-permute-done((bf16[144,256]{1,0:T(8,128)(2,1)S(1)}, bf16[144,256]{1,0:T(8,128)(2,1)S(1)}, u32[]{:S(2)}, u32[]{:S(2)}) %collective-permute-start.13) | collective-permute-done | bytes 73760 | tf_op jit(solution)/shard_map/ppermute | solution.py:76
  39.1 2.5 %collective-permute-done.14.refs_1_ = bf16[144,256]{1,0:T(8,128)(2,1)S(1)} collective-permute-done((bf16[144,256]{1,0:T(8,128)(2,1)S(1)}, bf16[144,256]{1,0:T(8,128)(2,1)S(1)}, u32[]{:S(2)}, u32[]{:S(2)}) %collective-permute-start.14) | collective-permute-done | bytes 73760 | tf_op jit(solution)/shard_map/ppermute | solution.py:76
  42.8 1.5 collective-permute-start.16
  45.3 2.4 %collective-permute-start.19 = (bf16[128,1024]{1,0:T(8,128)(2,1)S(1)}, bf16[128,1024]{1,0:T(8,128)(2,1)S(1)}, u32[]{:S(2)}, u32[]{:S(2)}) collective-permute-start(bf16[128,1024]{1,0:T(8,128)(2,1)S(1)} %get-tuple-element.86), channel_id=1, source_target_pairs={{0,24},{8,16},{16,8},{24,0},{1,25},{9,17},{17,9},{25,1},{2,26},{10... | collective-permute-start | bytes 786440 | tf_op jit(solution)/shard_map/ppermute | solution.py:76
  48.1 6.4 %collective-permute-done.19.refs_3_.refs_7_ = bf16[128,1024]{1,0:T(8,128)(2,1)S(1)} collective-permute-done((bf16[128,1024]{1,0:T(8,128)(2,1)S(1)}, bf16[128,1024]{1,0:T(8,128)(2,1)S(1)}, u32[]{:S(2)}, u32[]{:S(2)}) %collective-permute-start.19) | collective-permute-done | bytes 262176 | tf_op jit(solution)/shard_map/ppermute | solution.py:76
  55.1 1.4 collective-permute-done.16.refs_1_
  58.4 2.5 %shard_map.327 = (bf16[144,256]{1,0:T(8,128)(2,1)S(1)}, f32[8,256]{1,0:T(8,128)S(1)}) custom-call(bf16[128,2048]{1,0:T(8,128)(2,1)S(1)} %get-tuple-element.77.near_ref, bf16[128,2048]{1,0:T(8,128)(2,1)S(1)} %get-tuple-element.78.far_ref, f32[256,256]{1,0:T(8,128)S(1)} %copy-done, f32[4,256]{1,0:T(4,128)S(1)} %copy-done.8, ...), custom_call_target="tpu_custom_call" | custom-call | flops 805306368 | bytes 3559424 | tf_op jit(solution)/shard_map/pallas_call | solution.py:59
  60.9 2.4 %collective-permute-start.24 = (bf16[144,256]{1,0:T(8,128)(2,1)S(1)}, bf16[144,256]{1,0:T(8,128)(2,1)S(1)}, u32[]{:S(2)}, u32[]{:S(2)}) collective-permute-start(bf16[144,256]{1,0:T(8,128)(2,1)S(1)} %get-tuple-element.88.refs_3_.summed_ref), channel_id=1, source_target_pairs={{0,24},{8,16},{16,8},{24,0},{1,25},{9,17},{17,9},{25,1},{2,26},{10... | collective-permute-start | bytes 221192 | tf_op jit(solution)/shard_map/ppermute | solution.py:76
  65.5 1.4 shard_map.329
  67.7 4.0 %collective-permute-done.25.refs_1_ = bf16[144,256]{1,0:T(8,128)(2,1)S(1)} collective-permute-done((bf16[144,256]{1,0:T(8,128)(2,1)S(1)}, bf16[144,256]{1,0:T(8,128)(2,1)S(1)}, u32[]{:S(2)}, u32[]{:S(2)}) %collective-permute-start.25) | collective-permute-done | bytes 73760 | tf_op jit(solution)/shard_map/ppermute | solution.py:76
  71.7 1.7 %collective-permute-start.34 = (bf16[602,128]{1,0:T(8,128)(2,1)S(1)}, bf16[602,128]{1,0:T(8,128)(2,1)S(1)}, u32[]{:S(2)}, u32[]{:S(2)}) collective-permute-start(bf16[602,128]{1,0:T(8,128)(2,1)S(1)} %get-tuple-element.100), channel_id=1, source_target_pairs={{0,24},{8,16},{16,8},{24,0},{1,25},{9,17},{17,9},{25,1},{2,26},{10... | collective-permute-start | bytes 462344 | tf_op jit(solution)/shard_map/ppermute | solution.py:76
  74.4 1.5 collective-permute-start.27
  76.9 3.2 %collective-permute-done.34.refs_3_ = bf16[602,128]{1,0:T(8,128)(2,1)S(1)} collective-permute-done((bf16[602,128]{1,0:T(8,128)(2,1)S(1)}, bf16[602,128]{1,0:T(8,128)(2,1)S(1)}, u32[]{:S(2)}, u32[]{:S(2)}) %collective-permute-start.34) | collective-permute-done | bytes 154144 | tf_op jit(solution)/shard_map/ppermute | solution.py:76
  80.1 1.8 %collective-permute-start.32 = (bf16[602,128]{1,0:T(8,128)(2,1)S(1)}, bf16[602,128]{1,0:T(8,128)(2,1)S(1)}, u32[]{:S(2)}, u32[]{:S(2)}) collective-permute-start(bf16[602,128]{1,0:T(8,128)(2,1)S(1)} %get-tuple-element.96), channel_id=1, source_target_pairs={{0,8},{8,0},{16,24},{24,16},{1,9},{9,1},{17,25},{25,17},{2,10},{10... | collective-permute-start | bytes 462344 | tf_op jit(solution)/shard_map/ppermute | solution.py:76
  81.9 3.2 %shard_map.330.slopes_ref = f32[128,512]{1,0:T(8,128)S(1)} custom-call(bf16[128,2048]{1,0:T(8,128)(2,1)S(1)} %get-tuple-element.77.near_ref, bf16[128,2048]{1,0:T(8,128)(2,1)S(1)} %get-tuple-element.78.far_ref, f32[4,256]{1,0:T(4,128)S(1)} %copy-done.8, f32[8,256]{1,0:T(8,128)S(1)} %get-tuple-element.101.stats_ref, bf16[528,256]{1,0:T(8,128)(2,1)S(1)} %shard_map.326.refs_0_, ...), custom_call_target="tpu_custom_call" | custom-call | flops 805306368 | bytes 3485696 | tf_op jit(solution)/shard_map/pallas_call | solution.py:59
  86.1 1.4 collective-permute-done.32.refs_1_
  89.8 4.6 %shard_map.331 = (bf16[64,128]{1,0:T(8,128)(2,1)S(1)}, f32[8,256]{1,0:T(8,128)S(1)}) custom-call(bf16[128,2048]{1,0:T(8,128)(2,1)S(1)} %get-tuple-element.77.near_ref, bf16[128,2048]{1,0:T(8,128)(2,1)S(1)} %get-tuple-element.78.far_ref, f32[41,256]{1,0:T(8,128)S(1)} %bitcast.27, f32[4,256]{1,0:T(4,128)S(1)} %copy-done.8, ...), custom_call_target="tpu_custom_call" | custom-call | flops 1073741824 | bytes 3286016 | tf_op jit(solution)/shard_map/pallas_call | solution.py:59
  94.5 2.2 %collective-permute-start.39 = (bf16[64,128]{1,0:T(8,128)(2,1)S(1)}, bf16[64,128]{1,0:T(8,128)(2,1)S(1)}, u32[]{:S(2)}, u32[]{:S(2)}) collective-permute-start(bf16[64,128]{1,0:T(8,128)(2,1)S(1)} %get-tuple-element.105.refs_3_), channel_id=1, source_target_pairs={{0,24},{8,16},{16,8},{24,0},{1,25},{9,17},{17,9},{25,1},{2,26},{10... | collective-permute-start | bytes 49160 | tf_op jit(solution)/shard_map/ppermute | solution.py:76
  96.7 2.2 %collective-permute-start.41 = (bf16[64,128]{1,0:T(8,128)(2,1)S(1)}, bf16[64,128]{1,0:T(8,128)(2,1)S(1)}, u32[]{:S(2)}, u32[]{:S(2)}) collective-permute-start(bf16[64,128]{1,0:T(8,128)(2,1)S(1)} %get-tuple-element.105.refs_3_), channel_id=1, source_target_pairs={{0,8},{8,0},{16,24},{24,16},{1,9},{9,1},{17,25},{25,17},{2,10},{10... | collective-permute-start | bytes 49160 | tf_op jit(solution)/shard_map/ppermute | solution.py:76
  98.9 1.3 collective-permute-done.39.refs_0_
  105.0 1.5 collective-permute-start.45
  109.2 1.9 %collective-permute-start.46 = (bf16[272,128]{1,0:T(8,128)(2,1)S(1)}, bf16[272,128]{1,0:T(8,128)(2,1)S(1)}, u32[]{:S(2)}, u32[]{:S(2)}) collective-permute-start(bf16[272,128]{1,0:T(8,128)(2,1)S(1)} %get-tuple-element.116.refs_3_), channel_id=1, source_target_pairs={{0,24},{8,16},{16,8},{24,0},{1,25},{9,17},{17,9},{25,1},{2,26},{10... | collective-permute-start | bytes 208904 | tf_op jit(solution)/shard_map/ppermute | solution.py:76
  112.0 1.6 %collective-permute-start.48 = (bf16[272,128]{1,0:T(8,128)(2,1)S(1)}, bf16[272,128]{1,0:T(8,128)(2,1)S(1)}, u32[]{:S(2)}, u32[]{:S(2)}) collective-permute-start(bf16[272,128]{1,0:T(8,128)(2,1)S(1)} %get-tuple-element.116.refs_3_), channel_id=1, source_target_pairs={{0,8},{8,0},{16,24},{24,16},{1,9},{9,1},{17,25},{25,17},{2,10},{10... | collective-permute-start | bytes 208904 | tf_op jit(solution)/shard_map/ppermute | solution.py:76
  113.6 2.3 %collective-permute-done.46.refs_0_ = bf16[272,128]{1,0:T(8,128)(2,1)S(1)} collective-permute-done((bf16[272,128]{1,0:T(8,128)(2,1)S(1)}, bf16[272,128]{1,0:T(8,128)(2,1)S(1)}, u32[]{:S(2)}, u32[]{:S(2)}) %collective-permute-start.46) | collective-permute-done | bytes 69664 | tf_op jit(solution)/shard_map/ppermute | solution.py:76
  115.9 1.7 %collective-permute-done.47.refs_1_ = bf16[272,128]{1,0:T(8,128)(2,1)S(1)} collective-permute-done((bf16[272,128]{1,0:T(8,128)(2,1)S(1)}, bf16[272,128]{1,0:T(8,128)(2,1)S(1)}, u32[]{:S(2)}, u32[]{:S(2)}) %collective-permute-start.47) | collective-permute-done | bytes 69664 | tf_op jit(solution)/shard_map/ppermute | solution.py:76
  119.7 1.7 %collective-permute-start.50 = (bf16[272,128]{1,0:T(8,128)(2,1)S(1)}, bf16[272,128]{1,0:T(8,128)(2,1)S(1)}, u32[]{:S(2)}, u32[]{:S(2)}) collective-permute-start(bf16[272,128]{1,0:T(8,128)(2,1)S(1)} %get-tuple-element.117), channel_id=1, source_target_pairs={{0,6},{1,7},{2,4},{3,5},{4,2},{5,3},{6,0},{7,1},{8,14},{9,15},{10,... | collective-permute-start | bytes 208904 | tf_op jit(solution)/shard_map/ppermute | solution.py:72
  123.2 1.8 %collective-permute-done.50.refs_4_ = bf16[272,128]{1,0:T(8,128)(2,1)S(1)} collective-permute-done((bf16[272,128]{1,0:T(8,128)(2,1)S(1)}, bf16[272,128]{1,0:T(8,128)(2,1)S(1)}, u32[]{:S(2)}, u32[]{:S(2)}) %collective-permute-start.50) | collective-permute-done | bytes 69664 | tf_op jit(solution)/shard_map/ppermute | solution.py:72
  125.0 1.3 collective-permute-done.51.refs_5_
  131.0 1.6 %collective-permute-start.56 = (bf16[128,256]{1,0:T(8,128)(2,1)S(1)}, bf16[128,256]{1,0:T(8,128)(2,1)S(1)}, u32[]{:S(2)}, u32[]{:S(2)}) collective-permute-start(bf16[128,256]{1,0:T(8,128)(2,1)S(1)} %get-tuple-element.126), channel_id=1, source_target_pairs={{0,6},{1,7},{2,4},{3,5},{4,2},{5,3},{6,0},{7,1},{8,14},{9,15},{10,... | collective-permute-start | bytes 196616 | tf_op jit(solution)/shard_map/ppermute | solution.py:72
  133.4 1.6 %collective-permute-done.55.refs_1_ = bf16[128,256]{1,0:T(8,128)(2,1)S(1)} collective-permute-done((bf16[128,256]{1,0:T(8,128)(2,1)S(1)}, bf16[128,256]{1,0:T(8,128)(2,1)S(1)}, u32[]{:S(2)}, u32[]{:S(2)}) %collective-permute-start.55) | collective-permute-done | bytes 65568 | tf_op jit(solution)/shard_map/ppermute | solution.py:72
  136.2 2.0 %collective-permute-start.57 = (bf16[128,256]{1,0:T(8,128)(2,1)S(1)}, bf16[128,256]{1,0:T(8,128)(2,1)S(1)}, u32[]{:S(2)}, u32[]{:S(2)}) collective-permute-start(bf16[128,256]{1,0:T(8,128)(2,1)S(1)} %shard_map.341.refs_2_), channel_id=1, source_target_pairs={{0,24},{8,16},{16,8},{24,0},{1,25},{9,17},{17,9},{25,1},{2,26},{10... | collective-permute-start | bytes 196616 | tf_op jit(solution)/shard_map/ppermute | solution.py:76
  138.2 2.5 %collective-permute-start.59 = (bf16[128,256]{1,0:T(8,128)(2,1)S(1)}, bf16[128,256]{1,0:T(8,128)(2,1)S(1)}, u32[]{:S(2)}, u32[]{:S(2)}) collective-permute-start(bf16[128,256]{1,0:T(8,128)(2,1)S(1)} %shard_map.341.refs_2_), channel_id=1, source_target_pairs={{0,8},{8,0},{16,24},{24,16},{1,9},{9,1},{17,25},{25,17},{2,10},{10... | collective-permute-start | bytes 196616 | tf_op jit(solution)/shard_map/ppermute | solution.py:76
  141.3 1.3 collective-permute-done.57.own_ref
  142.6 1.5 collective-permute-done.58.refs_0_
  146.4 1.4 collective-permute-start.62
  150.1 1.4 collective-permute-done.62.refs_3_
  152.9 2.4 %shard_map.343 = (f32[602,256]{1,0:T(8,128)}, f32[602,256]{1,0:T(8,128)}, f32[602,256]{1,0:T(8,128)}, f32[256,256]{1,0:T(8,128)}, f32[256,256]{1,0:T(8,128)}, /*...) custom-call(bf16[128,256]{1,0:T(8,128)(2,1)S(1)} %shard_map.342.refs_0_, ...), custom_call_target="tpu_custom_call" | custom-call | bytes 6047744 | tf_op jit(solution)/shard_map/pallas_call | solution.py:59
  (157 shorter events, 47.4 us)
Async XLA Ops:
  0.7 13.6 %collective-permute-start.3 = (bf16[602,128]{1,0:T(8,128)(2,1)}, bf16[602,128]{1,0:T(8,128)(2,1)S(1)}, u32[]{:S(2)}, u32[]{:S(2)}) collective-permute-start(bf16[602,128]{1,0:T(8,128)(2,1)} %bitcast.35), channel_id=1, source_target_pairs={{0,2},{1,3},{2,0},{3,1},{4,6},{5,7},{6,4},{7,5},{8,10},{9,11},{10,... | collective-permute-start | bytes 462344 | tf_op jit(solution)/shard_map/ppermute | solution.py:72
  5.1 7.3 %collective-permute-start = (bf16[128,256]{1,0:T(8,128)(2,1)S(1)}, bf16[128,256]{1,0:T(8,128)(2,1)S(1)}, u32[]{:S(2)}, u32[]{:S(2)}) collective-permute-start(bf16[128,256]{1,0:T(8,128)(2,1)S(1)} %convolution_convert_fusion.refs_3_), channel_id=1, source_target_pairs={{0,24},{8,16},{16,8},{24,0},{1,25},{9,17},{17,9},{25,1},{2,26},{10... | collective-permute-start | bytes 196616 | tf_op jit(solution)/shard_map/ppermute | solution.py:76
  8.7 5.4 %collective-permute-start.1 = (bf16[128,256]{1,0:T(8,128)(2,1)S(1)}, bf16[128,256]{1,0:T(8,128)(2,1)S(1)}, u32[]{:S(2)}, u32[]{:S(2)}) collective-permute-start(bf16[128,256]{1,0:T(8,128)(2,1)S(1)} %convolution_convert_fusion.refs_3_), channel_id=1, source_target_pairs={{0,16},{8,24},{16,0},{24,8},{1,17},{9,25},{17,1},{25,9},{2,18},{10... | collective-permute-start | bytes 196616 | tf_op jit(solution)/shard_map/ppermute | solution.py:76
  8.8 5.4 %collective-permute-start.2 = (bf16[128,256]{1,0:T(8,128)(2,1)S(1)}, bf16[128,256]{1,0:T(8,128)(2,1)S(1)}, u32[]{:S(2)}, u32[]{:S(2)}) collective-permute-start(bf16[128,256]{1,0:T(8,128)(2,1)S(1)} %convolution_convert_fusion.refs_3_), channel_id=1, source_target_pairs={{0,8},{8,0},{16,24},{24,16},{1,9},{9,1},{17,25},{25,17},{2,10},{10... | collective-permute-start | bytes 196616 | tf_op jit(solution)/shard_map/ppermute | solution.py:76
  14.2 12.5 %collective-permute-start.7 = (bf16[128,1024]{1,0:T(8,128)(2,1)S(1)}, bf16[128,1024]{1,0:T(8,128)(2,1)S(1)}, u32[]{:S(2)}, u32[]{:S(2)}) collective-permute-start(bf16[128,1024]{1,0:T(8,128)(2,1)S(1)} %get-tuple-element.81), channel_id=1, source_target_pairs={{0,8},{8,0},{16,24},{24,16},{1,9},{9,1},{17,25},{25,17},{2,10},{10... | collective-permute-start | bytes 786440 | tf_op jit(solution)/shard_map/ppermute | solution.py:76
  15.3 13.3 %collective-permute-start.8 = (bf16[128,1024]{1,0:T(8,128)(2,1)S(1)}, bf16[128,1024]{1,0:T(8,128)(2,1)S(1)}, u32[]{:S(2)}, u32[]{:S(2)}) collective-permute-start(bf16[128,1024]{1,0:T(8,128)(2,1)S(1)} %get-tuple-element.83), channel_id=1, source_target_pairs={{0,16},{8,24},{16,0},{24,8},{1,17},{9,25},{17,1},{25,9},{2,18},{10... | collective-permute-start | bytes 786440 | tf_op jit(solution)/shard_map/ppermute | solution.py:76
  17.5 11.1 %collective-permute-start.6 = (bf16[4,128,256]{2,1,0:T(8,128)(2,1)S(1)}, bf16[4,128,256]{2,1,0:T(8,128)(2,1)S(1)}, u32[]{:S(2)}, u32[]{:S(2)}) collective-permute-start(bf16[4,128,256]{2,1,0:T(8,128)(2,1)S(1)} %shard_map.324.refs_0_), channel_id=1, source_target_pairs={{0,6},{1,7},{2,4},{3,5},{4,2},{5,3},{6,0},{7,1},{8,14},{9,15},{10,... | collective-permute-start | bytes 786440 | tf_op jit(solution)/shard_map/ppermute | solution.py:72
  18.9 10.7 %collective-permute-start.4 = (bf16[4,128,256]{2,1,0:T(8,128)(2,1)S(1)}, bf16[4,128,256]{2,1,0:T(8,128)(2,1)S(1)}, u32[]{:S(2)}, u32[]{:S(2)}) collective-permute-start(bf16[4,128,256]{2,1,0:T(8,128)(2,1)S(1)} %shard_map.324.refs_0_), channel_id=1, source_target_pairs={{0,2},{1,3},{2,0},{3,1},{4,6},{5,7},{6,4},{7,5},{8,10},{9,11},{10,... | collective-permute-start | bytes 786440 | tf_op jit(solution)/shard_map/ppermute | solution.py:72
  20.4 9.2 %collective-permute-start.5 = (bf16[4,128,256]{2,1,0:T(8,128)(2,1)S(1)}, bf16[4,128,256]{2,1,0:T(8,128)(2,1)S(1)}, u32[]{:S(2)}, u32[]{:S(2)}) collective-permute-start(bf16[4,128,256]{2,1,0:T(8,128)(2,1)S(1)} %shard_map.324.refs_0_), channel_id=1, source_target_pairs={{0,4},{1,5},{2,6},{3,7},{4,0},{5,1},{6,2},{7,3},{8,12},{9,13},{10,... | collective-permute-start | bytes 786440 | tf_op jit(solution)/shard_map/ppermute | solution.py:72
  26.7 4.5 %collective-permute-start.9 = (bf16[4,128,256]{2,1,0:T(8,128)(2,1)S(1)}, bf16[4,128,256]{2,1,0:T(8,128)(2,1)S(1)}, u32[]{:S(2)}, u32[]{:S(2)}) collective-permute-start(bf16[4,128,256]{2,1,0:T(8,128)(2,1)S(1)} %shard_map.324.refs_0_), channel_id=1, source_target_pairs={{0,1},{1,0},{2,3},{3,2},{4,5},{5,4},{6,7},{7,6},{8,9},{9,8},{10,11... | collective-permute-start | bytes 786440 | tf_op jit(solution)/shard_map/ppermute | solution.py:72
  30.2 17.4 %collective-permute-start.30 = (bf16[2,602,128]{2,1,0:T(8,128)(2,1)S(1)}, bf16[2,602,128]{2,1,0:T(8,128)(2,1)S(1)}, u32[]{:S(2)}, u32[]{:S(2)}) collective-permute-start(bf16[2,602,128]{2,1,0:T(8,128)(2,1)S(1)} %pad_maximum_fusion.1), channel_id=1, source_target_pairs={{0,4},{1,5},{2,6},{3,7},{4,0},{5,1},{6,2},{7,3},{8,12},{9,13},{10,... | collective-permute-start | bytes 924680 | tf_op jit(solution)/shard_map/ppermute | solution.py:72
  32.1 7.1 %collective-permute-start.13 = (bf16[144,256]{1,0:T(8,128)(2,1)S(1)}, bf16[144,256]{1,0:T(8,128)(2,1)S(1)}, u32[]{:S(2)}, u32[]{:S(2)}) collective-permute-start(bf16[144,256]{1,0:T(8,128)(2,1)S(1)} %shard_map.325.refs_3_.summed_ref), channel_id=1, source_target_pairs={{0,24},{8,16},{16,8},{24,0},{1,25},{9,17},{17,9},{25,1},{2,26},{10... | collective-permute-start | bytes 221192 | tf_op jit(solution)/shard_map/ppermute | solution.py:76
  34.8 6.9 %collective-permute-start.14 = (bf16[144,256]{1,0:T(8,128)(2,1)S(1)}, bf16[144,256]{1,0:T(8,128)(2,1)S(1)}, u32[]{:S(2)}, u32[]{:S(2)}) collective-permute-start(bf16[144,256]{1,0:T(8,128)(2,1)S(1)} %shard_map.325.refs_3_.summed_ref), channel_id=1, source_target_pairs={{0,16},{8,24},{16,0},{24,8},{1,17},{9,25},{17,1},{25,9},{2,18},{10... | collective-permute-start | bytes 221192 | tf_op jit(solution)/shard_map/ppermute | solution.py:76
  34.8 6.9 %collective-permute-start.15 = (bf16[144,256]{1,0:T(8,128)(2,1)S(1)}, bf16[144,256]{1,0:T(8,128)(2,1)S(1)}, u32[]{:S(2)}, u32[]{:S(2)}) collective-permute-start(bf16[144,256]{1,0:T(8,128)(2,1)S(1)} %shard_map.325.refs_3_.summed_ref), channel_id=1, source_target_pairs={{0,8},{8,0},{16,24},{24,16},{1,9},{9,1},{17,25},{25,17},{2,10},{10... | collective-permute-start | bytes 221192 | tf_op jit(solution)/shard_map/ppermute | solution.py:76
  41.7 12.9 %collective-permute-start.18 = (bf16[528,256]{1,0:T(8,128)(2,1)S(1)}, bf16[528,256]{1,0:T(8,128)(2,1)S(1)}, u32[]{:S(2)}, u32[]{:S(2)}) collective-permute-start(bf16[528,256]{1,0:T(8,128)(2,1)S(1)} %shard_map.326.refs_0_), channel_id=1, source_target_pairs={{0,6},{1,7},{2,4},{3,5},{4,2},{5,3},{6,0},{7,1},{8,14},{9,15},{10,... | collective-permute-start | bytes 811016 | tf_op jit(solution)/shard_map/ppermute | solution.py:72
  42.8 13.7 %collective-permute-start.16 = (bf16[528,256]{1,0:T(8,128)(2,1)S(1)}, bf16[528,256]{1,0:T(8,128)(2,1)S(1)}, u32[]{:S(2)}, u32[]{:S(2)}) collective-permute-start(bf16[528,256]{1,0:T(8,128)(2,1)S(1)} %shard_map.326.refs_0_), channel_id=1, source_target_pairs={{0,2},{1,3},{2,0},{3,1},{4,6},{5,7},{6,4},{7,5},{8,10},{9,11},{10,... | collective-permute-start | bytes 811016 | tf_op jit(solution)/shard_map/ppermute | solution.py:72
  44.3 12.6 %collective-permute-start.17 = (bf16[528,256]{1,0:T(8,128)(2,1)S(1)}, bf16[528,256]{1,0:T(8,128)(2,1)S(1)}, u32[]{:S(2)}, u32[]{:S(2)}) collective-permute-start(bf16[528,256]{1,0:T(8,128)(2,1)S(1)} %shard_map.326.refs_0_), channel_id=1, source_target_pairs={{0,4},{1,5},{2,6},{3,7},{4,0},{5,1},{6,2},{7,3},{8,12},{9,13},{10,... | collective-permute-start | bytes 811016 | tf_op jit(solution)/shard_map/ppermute | solution.py:72
  45.3 9.3 %collective-permute-start.19 = (bf16[128,1024]{1,0:T(8,128)(2,1)S(1)}, bf16[128,1024]{1,0:T(8,128)(2,1)S(1)}, u32[]{:S(2)}, u32[]{:S(2)}) collective-permute-start(bf16[128,1024]{1,0:T(8,128)(2,1)S(1)} %get-tuple-element.86), channel_id=1, source_target_pairs={{0,24},{8,16},{16,8},{24,0},{1,25},{9,17},{17,9},{25,1},{2,26},{10... | collective-permute-start | bytes 786440 | tf_op jit(solution)/shard_map/ppermute | solution.py:76
  48.1 17.3 %collective-permute-start.31 = (bf16[4,602,128]{2,0,1:T(4,128)(2,1)S(1)}, bf16[4,602,128]{2,0,1:T(4,128)(2,1)S(1)}, u32[]{:S(2)}, u32[]{:S(2)}) collective-permute-start(bf16[4,602,128]{2,0,1:T(4,128)(2,1)S(1)} %copy.37), channel_id=1, source_target_pairs={{0,1},{1,0},{2,3},{3,2},{4,5},{5,4},{6,7},{7,6},{8,9},{9,8},{10,11... | collective-permute-start | bytes 1849352 | tf_op jit(solution)/shard_map/ppermute | solution.py:72
  60.9 6.8 %collective-permute-start.24 = (bf16[144,256]{1,0:T(8,128)(2,1)S(1)}, bf16[144,256]{1,0:T(8,128)(2,1)S(1)}, u32[]{:S(2)}, u32[]{:S(2)}) collective-permute-start(bf16[144,256]{1,0:T(8,128)(2,1)S(1)} %get-tuple-element.88.refs_3_.summed_ref), channel_id=1, source_target_pairs={{0,24},{8,16},{16,8},{24,0},{1,25},{9,17},{17,9},{25,1},{2,26},{10... | collective-permute-start | bytes 221192 | tf_op jit(solution)/shard_map/ppermute | solution.py:76
  63.4 8.3 %collective-permute-start.25 = (bf16[144,256]{1,0:T(8,128)(2,1)S(1)}, bf16[144,256]{1,0:T(8,128)(2,1)S(1)}, u32[]{:S(2)}, u32[]{:S(2)}) collective-permute-start(bf16[144,256]{1,0:T(8,128)(2,1)S(1)} %get-tuple-element.88.refs_3_.summed_ref), channel_id=1, source_target_pairs={{0,16},{8,24},{16,0},{24,8},{1,17},{9,25},{17,1},{25,9},{2,18},{10... | collective-permute-start | bytes 221192 | tf_op jit(solution)/shard_map/ppermute | solution.py:76
  64.7 7.0 %collective-permute-start.26 = (bf16[144,256]{1,0:T(8,128)(2,1)S(1)}, bf16[144,256]{1,0:T(8,128)(2,1)S(1)}, u32[]{:S(2)}, u32[]{:S(2)}) collective-permute-start(bf16[144,256]{1,0:T(8,128)(2,1)S(1)} %get-tuple-element.88.refs_3_.summed_ref), channel_id=1, source_target_pairs={{0,8},{8,0},{16,24},{24,16},{1,9},{9,1},{17,25},{25,17},{2,10},{10... | collective-permute-start | bytes 221192 | tf_op jit(solution)/shard_map/ppermute | solution.py:76
  71.7 8.3 %collective-permute-start.34 = (bf16[602,128]{1,0:T(8,128)(2,1)S(1)}, bf16[602,128]{1,0:T(8,128)(2,1)S(1)}, u32[]{:S(2)}, u32[]{:S(2)}) collective-permute-start(bf16[602,128]{1,0:T(8,128)(2,1)S(1)} %get-tuple-element.100), channel_id=1, source_target_pairs={{0,24},{8,16},{16,8},{24,0},{1,25},{9,17},{17,9},{25,1},{2,26},{10... | collective-permute-start | bytes 462344 | tf_op jit(solution)/shard_map/ppermute | solution.py:76
  73.4 14.1 %collective-permute-start.29 = (bf16[528,256]{1,0:T(8,128)(2,1)S(1)}, bf16[528,256]{1,0:T(8,128)(2,1)S(1)}, u32[]{:S(2)}, u32[]{:S(2)}) collective-permute-start(bf16[528,256]{1,0:T(8,128)(2,1)S(1)} %shard_map.328.refs_0_), channel_id=1, source_target_pairs={{0,6},{1,7},{2,4},{3,5},{4,2},{5,3},{6,0},{7,1},{8,14},{9,15},{10,... | collective-permute-start | bytes 811016 | tf_op jit(solution)/shard_map/ppermute | solution.py:72
  74.4 13.1 %collective-permute-start.27 = (bf16[528,256]{1,0:T(8,128)(2,1)S(1)}, bf16[528,256]{1,0:T(8,128)(2,1)S(1)}, u32[]{:S(2)}, u32[]{:S(2)}) collective-permute-start(bf16[528,256]{1,0:T(8,128)(2,1)S(1)} %shard_map.328.refs_0_), channel_id=1, source_target_pairs={{0,2},{1,3},{2,0},{3,1},{4,6},{5,7},{6,4},{7,5},{8,10},{9,11},{10,... | collective-permute-start | bytes 811016 | tf_op jit(solution)/shard_map/ppermute | solution.py:72
  75.9 12.1 %collective-permute-start.28 = (bf16[528,256]{1,0:T(8,128)(2,1)S(1)}, bf16[528,256]{1,0:T(8,128)(2,1)S(1)}, u32[]{:S(2)}, u32[]{:S(2)}) collective-permute-start(bf16[528,256]{1,0:T(8,128)(2,1)S(1)} %shard_map.328.refs_0_), channel_id=1, source_target_pairs={{0,4},{1,5},{2,6},{3,7},{4,0},{5,1},{6,2},{7,3},{8,12},{9,13},{10,... | collective-permute-start | bytes 811016 | tf_op jit(solution)/shard_map/ppermute | solution.py:72
  76.9 9.3 %collective-permute-start.33 = (bf16[602,128]{1,0:T(8,128)(2,1)S(1)}, bf16[602,128]{1,0:T(8,128)(2,1)S(1)}, u32[]{:S(2)}, u32[]{:S(2)}) collective-permute-start(bf16[602,128]{1,0:T(8,128)(2,1)S(1)} %get-tuple-element.98), channel_id=1, source_target_pairs={{0,16},{8,24},{16,0},{24,8},{1,17},{9,25},{17,1},{25,9},{2,18},{10... | collective-permute-start | bytes 462344 | tf_op jit(solution)/shard_map/ppermute | solution.py:76
  80.1 7.4 %collective-permute-start.32 = (bf16[602,128]{1,0:T(8,128)(2,1)S(1)}, bf16[602,128]{1,0:T(8,128)(2,1)S(1)}, u32[]{:S(2)}, u32[]{:S(2)}) collective-permute-start(bf16[602,128]{1,0:T(8,128)(2,1)S(1)} %get-tuple-element.96), channel_id=1, source_target_pairs={{0,8},{8,0},{16,24},{24,16},{1,9},{9,1},{17,25},{25,17},{2,10},{10... | collective-permute-start | bytes 462344 | tf_op jit(solution)/shard_map/ppermute | solution.py:76
  94.5 5.8 %collective-permute-start.39 = (bf16[64,128]{1,0:T(8,128)(2,1)S(1)}, bf16[64,128]{1,0:T(8,128)(2,1)S(1)}, u32[]{:S(2)}, u32[]{:S(2)}) collective-permute-start(bf16[64,128]{1,0:T(8,128)(2,1)S(1)} %get-tuple-element.105.refs_3_), channel_id=1, source_target_pairs={{0,24},{8,16},{16,8},{24,0},{1,25},{9,17},{17,9},{25,1},{2,26},{10... | collective-permute-start | bytes 49160 | tf_op jit(solution)/shard_map/ppermute | solution.py:76
  96.7 4.6 %collective-permute-start.40 = (bf16[64,128]{1,0:T(8,128)(2,1)S(1)}, bf16[64,128]{1,0:T(8,128)(2,1)S(1)}, u32[]{:S(2)}, u32[]{:S(2)}) collective-permute-start(bf16[64,128]{1,0:T(8,128)(2,1)S(1)} %get-tuple-element.105.refs_3_), channel_id=1, source_target_pairs={{0,16},{8,24},{16,0},{24,8},{1,17},{9,25},{17,1},{25,9},{2,18},{10... | collective-permute-start | bytes 49160 | tf_op jit(solution)/shard_map/ppermute | solution.py:76
  96.7 4.6 %collective-permute-start.41 = (bf16[64,128]{1,0:T(8,128)(2,1)S(1)}, bf16[64,128]{1,0:T(8,128)(2,1)S(1)}, u32[]{:S(2)}, u32[]{:S(2)}) collective-permute-start(bf16[64,128]{1,0:T(8,128)(2,1)S(1)} %get-tuple-element.105.refs_3_), channel_id=1, source_target_pairs={{0,8},{8,0},{16,24},{24,16},{1,9},{9,1},{17,25},{25,17},{2,10},{10... | collective-permute-start | bytes 49160 | tf_op jit(solution)/shard_map/ppermute | solution.py:76
  102.9 4.7 %collective-permute-start.43 = (bf16[64,128]{1,0:T(8,128)(2,1)S(1)}, bf16[64,128]{1,0:T(8,128)(2,1)S(1)}, u32[]{:S(2)}, u32[]{:S(2)}) collective-permute-start(bf16[64,128]{1,0:T(8,128)(2,1)S(1)} %get-tuple-element.106), channel_id=1, source_target_pairs={{0,6},{1,7},{2,4},{3,5},{4,2},{5,3},{6,0},{7,1},{8,14},{9,15},{10,... | collective-permute-start | bytes 49160 | tf_op jit(solution)/shard_map/ppermute | solution.py:72
  109.2 6.7 %collective-permute-start.46 = (bf16[272,128]{1,0:T(8,128)(2,1)S(1)}, bf16[272,128]{1,0:T(8,128)(2,1)S(1)}, u32[]{:S(2)}, u32[]{:S(2)}) collective-permute-start(bf16[272,128]{1,0:T(8,128)(2,1)S(1)} %get-tuple-element.116.refs_3_), channel_id=1, source_target_pairs={{0,24},{8,16},{16,8},{24,0},{1,25},{9,17},{17,9},{25,1},{2,26},{10... | collective-permute-start | bytes 208904 | tf_op jit(solution)/shard_map/ppermute | solution.py:76
  111.1 6.6 %collective-permute-start.47 = (bf16[272,128]{1,0:T(8,128)(2,1)S(1)}, bf16[272,128]{1,0:T(8,128)(2,1)S(1)}, u32[]{:S(2)}, u32[]{:S(2)}) collective-permute-start(bf16[272,128]{1,0:T(8,128)(2,1)S(1)} %get-tuple-element.116.refs_3_), channel_id=1, source_target_pairs={{0,16},{8,24},{16,0},{24,8},{1,17},{9,25},{17,1},{25,9},{2,18},{10... | collective-permute-start | bytes 208904 | tf_op jit(solution)/shard_map/ppermute | solution.py:76
  112.0 5.6 %collective-permute-start.48 = (bf16[272,128]{1,0:T(8,128)(2,1)S(1)}, bf16[272,128]{1,0:T(8,128)(2,1)S(1)}, u32[]{:S(2)}, u32[]{:S(2)}) collective-permute-start(bf16[272,128]{1,0:T(8,128)(2,1)S(1)} %get-tuple-element.116.refs_3_), channel_id=1, source_target_pairs={{0,8},{8,0},{16,24},{24,16},{1,9},{9,1},{17,25},{25,17},{2,10},{10... | collective-permute-start | bytes 208904 | tf_op jit(solution)/shard_map/ppermute | solution.py:76
  119.7 5.3 %collective-permute-start.50 = (bf16[272,128]{1,0:T(8,128)(2,1)S(1)}, bf16[272,128]{1,0:T(8,128)(2,1)S(1)}, u32[]{:S(2)}, u32[]{:S(2)}) collective-permute-start(bf16[272,128]{1,0:T(8,128)(2,1)S(1)} %get-tuple-element.117), channel_id=1, source_target_pairs={{0,6},{1,7},{2,4},{3,5},{4,2},{5,3},{6,0},{7,1},{8,14},{9,15},{10,... | collective-permute-start | bytes 208904 | tf_op jit(solution)/shard_map/ppermute | solution.py:72
  121.4 5.0 %collective-permute-start.51 = (bf16[272,128]{1,0:T(8,128)(2,1)S(1)}, bf16[272,128]{1,0:T(8,128)(2,1)S(1)}, u32[]{:S(2)}, u32[]{:S(2)}) collective-permute-start(bf16[272,128]{1,0:T(8,128)(2,1)S(1)} %get-tuple-element.118), channel_id=1, source_target_pairs={{0,4},{1,5},{2,6},{3,7},{4,0},{5,1},{6,2},{7,3},{8,12},{9,13},{10,... | collective-permute-start | bytes 208904 | tf_op jit(solution)/shard_map/ppermute | solution.py:72
  122.3 4.3 %collective-permute-start.52 = (bf16[272,128]{1,0:T(8,128)(2,1)S(1)}, bf16[272,128]{1,0:T(8,128)(2,1)S(1)}, u32[]{:S(2)}, u32[]{:S(2)}) collective-permute-start(bf16[272,128]{1,0:T(8,128)(2,1)S(1)} %get-tuple-element.119), channel_id=1, source_target_pairs={{0,2},{1,3},{2,0},{3,1},{4,6},{5,7},{6,4},{7,5},{8,10},{9,11},{10,... | collective-permute-start | bytes 208904 | tf_op jit(solution)/shard_map/ppermute | solution.py:72
  129.0 4.3 %collective-permute-start.54 = (bf16[128,256]{1,0:T(8,128)(2,1)S(1)}, bf16[128,256]{1,0:T(8,128)(2,1)S(1)}, u32[]{:S(2)}, u32[]{:S(2)}) collective-permute-start(bf16[128,256]{1,0:T(8,128)(2,1)S(1)} %get-tuple-element.124), channel_id=1, source_target_pairs={{0,2},{1,3},{2,0},{3,1},{4,6},{5,7},{6,4},{7,5},{8,10},{9,11},{10,... | collective-permute-start | bytes 196616 | tf_op jit(solution)/shard_map/ppermute | solution.py:72
  130.0 5.0 %collective-permute-start.55 = (bf16[128,256]{1,0:T(8,128)(2,1)S(1)}, bf16[128,256]{1,0:T(8,128)(2,1)S(1)}, u32[]{:S(2)}, u32[]{:S(2)}) collective-permute-start(bf16[128,256]{1,0:T(8,128)(2,1)S(1)} %get-tuple-element.125), channel_id=1, source_target_pairs={{0,4},{1,5},{2,6},{3,7},{4,0},{5,1},{6,2},{7,3},{8,12},{9,13},{10,... | collective-permute-start | bytes 196616 | tf_op jit(solution)/shard_map/ppermute | solution.py:72
  131.0 5.2 %collective-permute-start.56 = (bf16[128,256]{1,0:T(8,128)(2,1)S(1)}, bf16[128,256]{1,0:T(8,128)(2,1)S(1)}, u32[]{:S(2)}, u32[]{:S(2)}) collective-permute-start(bf16[128,256]{1,0:T(8,128)(2,1)S(1)} %get-tuple-element.126), channel_id=1, source_target_pairs={{0,6},{1,7},{2,4},{3,5},{4,2},{5,3},{6,0},{7,1},{8,14},{9,15},{10,... | collective-permute-start | bytes 196616 | tf_op jit(solution)/shard_map/ppermute | solution.py:72
  136.2 6.4 %collective-permute-start.57 = (bf16[128,256]{1,0:T(8,128)(2,1)S(1)}, bf16[128,256]{1,0:T(8,128)(2,1)S(1)}, u32[]{:S(2)}, u32[]{:S(2)}) collective-permute-start(bf16[128,256]{1,0:T(8,128)(2,1)S(1)} %shard_map.341.refs_2_), channel_id=1, source_target_pairs={{0,24},{8,16},{16,8},{24,0},{1,25},{9,17},{17,9},{25,1},{2,26},{10... | collective-permute-start | bytes 196616 | tf_op jit(solution)/shard_map/ppermute | solution.py:76
  138.2 5.9 %collective-permute-start.58 = (bf16[128,256]{1,0:T(8,128)(2,1)S(1)}, bf16[128,256]{1,0:T(8,128)(2,1)S(1)}, u32[]{:S(2)}, u32[]{:S(2)}) collective-permute-start(bf16[128,256]{1,0:T(8,128)(2,1)S(1)} %shard_map.341.refs_2_), channel_id=1, source_target_pairs={{0,16},{8,24},{16,0},{24,8},{1,17},{9,25},{17,1},{25,9},{2,18},{10... | collective-permute-start | bytes 196616 | tf_op jit(solution)/shard_map/ppermute | solution.py:76
  138.2 5.9 %collective-permute-start.59 = (bf16[128,256]{1,0:T(8,128)(2,1)S(1)}, bf16[128,256]{1,0:T(8,128)(2,1)S(1)}, u32[]{:S(2)}, u32[]{:S(2)}) collective-permute-start(bf16[128,256]{1,0:T(8,128)(2,1)S(1)} %shard_map.341.refs_2_), channel_id=1, source_target_pairs={{0,8},{8,0},{16,24},{24,16},{1,9},{9,1},{17,25},{25,17},{2,10},{10... | collective-permute-start | bytes 196616 | tf_op jit(solution)/shard_map/ppermute | solution.py:76
  144.2 4.8 %collective-permute-start.60 = (bf16[128,256]{1,0:T(8,128)(2,1)S(1)}, bf16[128,256]{1,0:T(8,128)(2,1)S(1)}, u32[]{:S(2)}, u32[]{:S(2)}) collective-permute-start(bf16[128,256]{1,0:T(8,128)(2,1)S(1)} %shard_map.342.refs_0_), channel_id=1, source_target_pairs={{0,2},{1,3},{2,0},{3,1},{4,6},{5,7},{6,4},{7,5},{8,10},{9,11},{10,... | collective-permute-start | bytes 196616 | tf_op jit(solution)/shard_map/ppermute | solution.py:72
  145.4 4.7 %collective-permute-start.61 = (bf16[128,256]{1,0:T(8,128)(2,1)S(1)}, bf16[128,256]{1,0:T(8,128)(2,1)S(1)}, u32[]{:S(2)}, u32[]{:S(2)}) collective-permute-start(bf16[128,256]{1,0:T(8,128)(2,1)S(1)} %shard_map.342.refs_0_), channel_id=1, source_target_pairs={{0,4},{1,5},{2,6},{3,7},{4,0},{5,1},{6,2},{7,3},{8,12},{9,13},{10,... | collective-permute-start | bytes 196616 | tf_op jit(solution)/shard_map/ppermute | solution.py:72
  146.4 5.2 %collective-permute-start.62 = (bf16[128,256]{1,0:T(8,128)(2,1)S(1)}, bf16[128,256]{1,0:T(8,128)(2,1)S(1)}, u32[]{:S(2)}, u32[]{:S(2)}) collective-permute-start(bf16[128,256]{1,0:T(8,128)(2,1)S(1)} %shard_map.342.refs_0_), channel_id=1, source_target_pairs={{0,6},{1,7},{2,4},{3,5},{4,2},{5,3},{6,0},{7,1},{8,14},{9,15},{10,... | collective-permute-start | bytes 196616 | tf_op jit(solution)/shard_map/ppermute | solution.py:72
  147.7 4.4 %collective-permute-start.63 = (bf16[128,256]{1,0:T(8,128)(2,1)S(1)}, bf16[128,256]{1,0:T(8,128)(2,1)S(1)}, u32[]{:S(2)}, u32[]{:S(2)}) collective-permute-start(bf16[128,256]{1,0:T(8,128)(2,1)S(1)} %shard_map.342.refs_0_), channel_id=1, source_target_pairs={{0,1},{1,0},{2,3},{3,2},{4,5},{5,4},{6,7},{7,6},{8,9},{9,8},{10,11... | collective-permute-start | bytes 196616 | tf_op jit(solution)/shard_map/ppermute | solution.py:72
  (39 other events, 279.8 us)

commit v6 on v5

--- a/solution.py
+++ b/solution.py
@@ -100,7 +100,7 @@
     out_ref[4 * rows :, :] = centres_ref[...].astype(BF)
 
 
-def gather_all(block, beside=(), within=(), centred=True, early=()):
+def gather_all(block, beside=(), within=(), centred=True, early=(), tied=True):
     if short_line():
         line = [block] + [pass_line(block, k) for k in range(1, 4)]
         if centred:
@@ -117,7 +117,7 @@
         line = lax.all_gather(block, "z", axis=0)
     if early:
         line, *early = lax.optimization_barrier((line, *early))
-    passed = [pass_line(after(part, line), mask) for part, mask in beside]
+    passed = [pass_line(after(part, line) if tied else part, mask) for part, mask in beside]
     lines = [line] + [swap(line, 2 * k) for k in range(1, 4)]
     if passed or within:
         lines[3], *rest = lax.optimization_barrier((lines[3], *passed, *within))
@@ -186,11 +186,8 @@
     return carry
 
 
-def moments(refs, rows, node_total):
+def moments_of(refs, rows, pivot, sums):
     width = refs[0].shape[-1]
-    pivot = block_at(refs[0], 0, rows)[1]
-    zero = jnp.zeros((8, width), F32)
-    sums = (zero, zero)
     for ref in refs:
 
         def one(i, carry, ref=ref):
@@ -206,6 +203,27 @@
             )
 
         sums = block_loop(ref, 1, one, sums)
+    return sums
+
+
+def moments_kernel(rows, *refs):
+    refs, out_ref = refs[:4], refs[4]
+    zero = jnp.zeros((8, refs[0].shape[-1]), F32)
+    out_ref[:8, :], out_ref[8:, :] = moments_of(
+        refs, rows, block_at(refs[0], 0, rows)[1], (zero, zero)
+    )
+
+
+def near_moments(lines, rows):
+    (sums,) = run(
+        functools.partial(moments_kernel, rows), [shape((16, lines[0].shape[-1]))], lines[:4]
+    )
+    return sums
+
+
+def moments(refs, sums_ref, rows, node_total):
+    pivot = block_at(refs[0], 0, rows)[1]
+    sums = moments_of(refs[4:], rows, pivot, (sums_ref[:8, :], sums_ref[8:, :]))
     shift = jnp.sum(sums[0], axis=0, keepdims=True) / node_total
     variance = jnp.sum(sums[1], axis=0, keepdims=True) / node_total - shift * shift
     return pivot + shift, lax.rsqrt(jnp.maximum(variance, 0.0) + EPS_NORM)
@@ -370,9 +388,9 @@
 
 
 def layer_kernel(node_total, layer, near_ref, far_ref, weight_ref, norm_ref, *refs):
-    refs, (out_ref, stats_ref) = refs[:8], refs[8:]
+    near_sums_ref, refs, (out_ref, stats_ref) = refs[0], refs[1:9], refs[9:]
     rows, width = near_ref.shape[0], refs[0].shape[-1]
-    mean_value, inverse = moments(refs, rows, node_total)
+    mean_value, inverse = moments(refs, near_sums_ref, rows, node_total)
     stats_ref[0:1, :] = mean_value
     stats_ref[1:2, :] = inverse
     scale = norm_ref[2 * layer : 2 * layer + 1, :] * inverse
@@ -418,10 +436,11 @@
 
 
 def head_kernel(node_total, near_ref, far_ref, weight_ref, norm_ref, notes_ref, *refs):
-    refs, (packed_ref, stats_ref, total_ref, sums_ref, tall_ref) = refs[:8], refs[8:]
+    near_sums_ref, refs, rest = refs[0], refs[1:9], refs[9:]
+    packed_ref, stats_ref, total_ref, sums_ref, tall_ref = rest
     rows, width = near_ref.shape[0], refs[0].shape[-1]
     classes = weight_ref.shape[0]
-    mean_value, inverse = moments(refs, rows, node_total)
+    mean_value, inverse = moments(refs, near_sums_ref, rows, node_total)
     stats_ref[0:1, :] = mean_value
     stats_ref[1:2, :] = inverse
     gain, offset = norm_ref[2:3, :], norm_ref[3:4, :]
@@ -583,7 +602,7 @@
     here = 2 * lax.axis_index("y") + lax.axis_index("x")
     core = lax.axis_index("c")
     for n, ref in enumerate(pieces):
-        at = (jnp.bitwise_xor(core, n // 4) * 4 + jnp.bitwise_xor(here, n % 4)) * size
+        at = (jnp.bitwise_xor(core, n // 4) * 4 + jnp.bitwise_xor(here, 3 - n % 4)) * size
         pile_ref[pl.ds(pl.multiple_of(at, size), size), :] = ref[...].astype(F32)
     tall = inputs[0].shape[0]
     grads = (
@@ -614,7 +633,8 @@
         (shard,) = run(pile_sum_kernel, [shape((size, width))], [own, *got])
         shard = lax.psum(shard, "z").astype(BF)
     pieces = [shard] + [swap(shard, 2 * k) for k in range(1, 4)]
-    return pieces + [swap(piece, 1) for piece in pieces]
+    others = [swap(piece, 1) for piece in pieces]
+    return pieces[::-1] + others[::-1]
 
 
 def first_sum_kernel(near_ref, far_ref, *refs):
@@ -683,6 +703,7 @@
         [(levels[1], 1), (levels[2], 2)] if short else (),
         centred=False,
         early=[swap(turned, 2)],
+        tied=False,
     )
     turned = jnp.stack([turned, turned_x])
     turned = jnp.concatenate([turned, swap(turned, 4)])
@@ -697,7 +718,7 @@
     summed_two, stats_one = run(
         functools.partial(layer_kernel, node_total, 0),
         [shape((tall, hidden), BF), shape((8, hidden))],
-        [near, far, w_second, norm_params, *around],
+        [near, far, w_second, norm_params, near_moments(around, rows), *around],
         flops=3 * work,
     )
     (slopes_one,) = run(
@@ -729,6 +750,7 @@
             head_turned,
             norm_params,
             notes,
+            near_moments(around, rows),
             *around,
         ],
         scratch=[

time: 155 us -> 154 us (level)
  waiting for transfers between devices: 63.4 us -> 58.8 us
  starting transfers between devices: 66.6 us -> 69.6 us
    ppermute x24, waiting for transfers between devices: 40.6 us -> 35.4 us  [pass_line(): return lax.ppermute(block, 'z', [(i, i ^ mask) for i in range(4)])]
    ppermute x24, starting transfers between devices: 35.8 us -> 38.7 us  [pass_line(): return lax.ppermute(block, 'z', [(i, i ^ mask) for i in range(4)])]
    pallas_call x21 -> x23, Pallas kernels: 18 us -> 18 us  [run(): pl.pallas_call(body, out_shape=tuple(outs), in_specs=[pl.BlockSpec(memory...]
  transfers between devices with their start and end apart: 67 -> 67, of which waited for: 43 -> 42; matrix products, arithmetic and copies ran while one was open for 2% -> 2% of each run, Pallas kernels for 6% -> 6%
where the time goes in v6:
time: 154 us
  starting transfers between devices  69.6 us (45%)
  waiting for transfers between devices  58.8 us (38%)
  Pallas kernels  18 us (12%)
  local copies, waits for them, and re-layouts  3.54 us (2%)
    ppermute x24, starting transfers between devices, pass_line(): return lax.ppermute(block, 'z', [(i, i ^ mask) for i in range(4)])  38.7 us
    ppermute x24, waiting for transfers between devices, pass_line(): return lax.ppermute(block, 'z', [(i, i ^ mask) for i in range(4)])  35.4 us
    ppermute x43, starting transfers between devices, swap(): return lax.ppermute(block, PLANE, [(i, i ^ mask) for i in range(8)])  30.8 us
    ppermute x43, waiting for transfers between devices, swap(): return lax.ppermute(block, PLANE, [(i, i ^ mask) for i in range(8)])  23.4 us
    pallas_call x23, Pallas kernels, run(): pl.pallas_call(body, out_shape=tuple(outs), in_specs=[pl.BlockSpec(memory...  18 us
  transfers between devices with their start and end apart: 67, of which 42 were waited for; matrix products, arithmetic and copies ran while one was open for 2% of the time, Pallas kernels for 6%

profile of v6, /device:TPU:0, one launch (start us, length us, event | category | flops | bytes accessed | tf_op | source)
XLA Modules:
  0.0 153.7 jit_solution(16297122705995306129)
XLA Ops:
  0.7 3.0 %collective-permute-start.3 = (bf16[602,128]{1,0:T(8,128)(2,1)}, bf16[602,128]{1,0:T(8,128)(2,1)S(1)}, u32[]{:S(2)}, u32[]{:S(2)}) collective-permute-start(bf16[602,128]{1,0:T(8,128)(2,1)} %bitcast.35), channel_id=1, source_target_pairs={{0,2},{1,3},{2,0},{3,1},{4,6},{5,7},{6,4},{7,5},{8,10},{9,11},{10,... | collective-permute-start | bytes 462344 | tf_op jit(solution)/shard_map/ppermute | solution.py:72
  3.7 1.4 convolution_convert_fusion.refs_3_
  5.1 3.7 %collective-permute-start = (bf16[128,256]{1,0:T(8,128)(2,1)S(1)}, bf16[128,256]{1,0:T(8,128)(2,1)S(1)}, u32[]{:S(2)}, u32[]{:S(2)}) collective-permute-start(bf16[128,256]{1,0:T(8,128)(2,1)S(1)} %convolution_convert_fusion.refs_3_), channel_id=1, source_target_pairs={{0,24},{8,16},{16,8},{24,0},{1,25},{9,17},{17,9},{25,1},{2,26},{10... | collective-permute-start | bytes 196616 | tf_op jit(solution)/shard_map/ppermute | solution.py:76
  12.4 1.3 collective-permute-start.7
  13.7 2.9 %collective-permute-start.8 = (bf16[128,1024]{1,0:T(8,128)(2,1)S(1)}, bf16[128,1024]{1,0:T(8,128)(2,1)S(1)}, u32[]{:S(2)}, u32[]{:S(2)}) collective-permute-start(bf16[128,1024]{1,0:T(8,128)(2,1)S(1)} %get-tuple-element.79), channel_id=1, source_target_pairs={{0,16},{8,24},{16,0},{24,8},{1,17},{9,25},{17,1},{25,9},{2,18},{10... | collective-permute-start | bytes 786440 | tf_op jit(solution)/shard_map/ppermute | solution.py:76
  16.7 1.6 %collective-permute-start.6 = (bf16[4,128,256]{2,1,0:T(8,128)(2,1)S(1)}, bf16[4,128,256]{2,1,0:T(8,128)(2,1)S(1)}, u32[]{:S(2)}, u32[]{:S(2)}) collective-permute-start(bf16[4,128,256]{2,1,0:T(8,128)(2,1)S(1)} %shard_map.324.refs_0_), channel_id=1, source_target_pairs={{0,6},{1,7},{2,4},{3,5},{4,2},{5,3},{6,0},{7,1},{8,14},{9,15},{10,... | collective-permute-start | bytes 786440 | tf_op jit(solution)/shard_map/ppermute | solution.py:72
  18.2 1.5 collective-permute-start.4
  20.2 5.0 %collective-permute-done.7.refs_1_.refs_5_ = bf16[128,1024]{1,0:T(8,128)(2,1)S(1)} collective-permute-done((bf16[128,1024]{1,0:T(8,128)(2,1)S(1)}, bf16[128,1024]{1,0:T(8,128)(2,1)S(1)}, u32[]{:S(2)}, u32[]{:S(2)}) %collective-permute-start.7) | collective-permute-done | bytes 262176 | tf_op jit(solution)/shard_map/ppermute | solution.py:76
  25.2 2.0 %collective-permute-done.8.refs_2_.refs_6_ = bf16[128,1024]{1,0:T(8,128)(2,1)S(1)} collective-permute-done((bf16[128,1024]{1,0:T(8,128)(2,1)S(1)}, bf16[128,1024]{1,0:T(8,128)(2,1)S(1)}, u32[]{:S(2)}, u32[]{:S(2)}) %collective-permute-start.8) | collective-permute-done | bytes 262176 | tf_op jit(solution)/shard_map/ppermute | solution.py:76
  27.2 2.5 %collective-permute-done.4.refs_1_ = bf16[4,128,256]{2,1,0:T(8,128)(2,1)S(1)} collective-permute-done((bf16[4,128,256]{2,1,0:T(8,128)(2,1)S(1)}, bf16[4,128,256]{2,1,0:T(8,128)(2,1)S(1)}, u32[]{:S(2)}, u32[]{:S(2)}) %collective-permute-start.4) | collective-permute-done | bytes 262176 | tf_op jit(solution)/shard_map/ppermute | solution.py:72
  32.5 1.5 collective-permute-start.14
  34.0 2.6 %collective-permute-start.15 = (bf16[144,256]{1,0:T(8,128)(2,1)S(1)}, bf16[144,256]{1,0:T(8,128)(2,1)S(1)}, u32[]{:S(2)}, u32[]{:S(2)}) collective-permute-start(bf16[144,256]{1,0:T(8,128)(2,1)S(1)} %shard_map.325.refs_3_.summed_ref), channel_id=1, source_target_pairs={{0,8},{8,0},{16,24},{24,16},{1,9},{9,1},{17,25},{25,17},{2,10},{10... | collective-permute-start | bytes 221192 | tf_op jit(solution)/shard_map/ppermute | solution.py:76
  36.6 2.6 %collective-permute-done.13.refs_0_ = bf16[144,256]{1,0:T(8,128)(2,1)S(1)} collective-permute-done((bf16[144,256]{1,0:T(8,128)(2,1)S(1)}, bf16[144,256]{1,0:T(8,128)(2,1)S(1)}, u32[]{:S(2)}, u32[]{:S(2)}) %collective-permute-start.13) | collective-permute-done | bytes 73760 | tf_op jit(solution)/shard_map/ppermute | solution.py:76
  39.2 1.9 %collective-permute-done.14.refs_1_ = bf16[144,256]{1,0:T(8,128)(2,1)S(1)} collective-permute-done((bf16[144,256]{1,0:T(8,128)(2,1)S(1)}, bf16[144,256]{1,0:T(8,128)(2,1)S(1)}, u32[]{:S(2)}, u32[]{:S(2)}) %collective-permute-start.14) | collective-permute-done | bytes 73760 | tf_op jit(solution)/shard_map/ppermute | solution.py:76
  42.2 1.5 collective-permute-start.16
  44.7 1.4 collective-permute-start.19
  46.5 6.9 %collective-permute-done.19.refs_3_.refs_7_ = bf16[128,1024]{1,0:T(8,128)(2,1)S(1)} collective-permute-done((bf16[128,1024]{1,0:T(8,128)(2,1)S(1)}, bf16[128,1024]{1,0:T(8,128)(2,1)S(1)}, u32[]{:S(2)}, u32[]{:S(2)}) %collective-permute-start.19) | collective-permute-done | bytes 262176 | tf_op jit(solution)/shard_map/ppermute | solution.py:76
  54.0 1.4 collective-permute-done.16.refs_1_.refs_2_
  57.4 2.3 %shard_map.328 = (bf16[144,256]{1,0:T(8,128)(2,1)S(1)}, f32[8,256]{1,0:T(8,128)S(1)}) custom-call(bf16[128,2048]{1,0:T(8,128)(2,1)S(1)} %get-tuple-element.75.near_ref, bf16[128,2048]{1,0:T(8,128)(2,1)S(1)} %get-tuple-element.76.far_ref, f32[256,256]{1,0:T(8,128)S(1)} %copy-done, f32[4,256]{1,0:T(4,128)S(1)} %copy-done.8, f32[16,256]{1,0:T(8,128)S(1)} %shard_map.327.refs_0_, ...), custom_call_target="tpu_custom_call" | custom-call | flops 805306368 | bytes 3575808 | tf_op jit(solution)/shard_map/pallas_call | solution.py:59
  59.6 2.0 %collective-permute-start.24 = (bf16[144,256]{1,0:T(8,128)(2,1)S(1)}, bf16[144,256]{1,0:T(8,128)(2,1)S(1)}, u32[]{:S(2)}, u32[]{:S(2)}) collective-permute-start(bf16[144,256]{1,0:T(8,128)(2,1)S(1)} %get-tuple-element.84.refs_3_.summed_ref), channel_id=1, source_target_pairs={{0,24},{8,16},{16,8},{24,0},{1,25},{9,17},{17,9},{25,1},{2,26},{10... | collective-permute-start | bytes 221192 | tf_op jit(solution)/shard_map/ppermute | solution.py:76
  61.6 1.7 %collective-permute-start.25 = (bf16[144,256]{1,0:T(8,128)(2,1)S(1)}, bf16[144,256]{1,0:T(8,128)(2,1)S(1)}, u32[]{:S(2)}, u32[]{:S(2)}) collective-permute-start(bf16[144,256]{1,0:T(8,128)(2,1)S(1)} %get-tuple-element.84.refs_3_.summed_ref), channel_id=1, source_target_pairs={{0,16},{8,24},{16,0},{24,8},{1,17},{9,25},{17,1},{25,9},{2,18},{10... | collective-permute-start | bytes 221192 | tf_op jit(solution)/shard_map/ppermute | solution.py:76
  64.2 1.4 shard_map.330
  66.0 4.3 %collective-permute-done.25.refs_1_ = bf16[144,256]{1,0:T(8,128)(2,1)S(1)} collective-permute-done((bf16[144,256]{1,0:T(8,128)(2,1)S(1)}, bf16[144,256]{1,0:T(8,128)(2,1)S(1)}, u32[]{:S(2)}, u32[]{:S(2)}) %collective-permute-start.25) | collective-permute-done | bytes 73760 | tf_op jit(solution)/shard_map/ppermute | solution.py:76
  70.3 2.2 %collective-permute-start.34 = (bf16[602,128]{1,0:T(8,128)(2,1)S(1)}, bf16[602,128]{1,0:T(8,128)(2,1)S(1)}, u32[]{:S(2)}, u32[]{:S(2)}) collective-permute-start(bf16[602,128]{1,0:T(8,128)(2,1)S(1)} %get-tuple-element.96), channel_id=1, source_target_pairs={{0,24},{8,16},{16,8},{24,0},{1,25},{9,17},{17,9},{25,1},{2,26},{10... | collective-permute-start | bytes 462344 | tf_op jit(solution)/shard_map/ppermute | solution.py:76
  73.5 1.5 collective-permute-start.27
  76.0 2.6 %collective-permute-done.34.refs_3_ = bf16[602,128]{1,0:T(8,128)(2,1)S(1)} collective-permute-done((bf16[602,128]{1,0:T(8,128)(2,1)S(1)}, bf16[602,128]{1,0:T(8,128)(2,1)S(1)}, u32[]{:S(2)}, u32[]{:S(2)}) %collective-permute-start.34) | collective-permute-done | bytes 154144 | tf_op jit(solution)/shard_map/ppermute | solution.py:76
  78.6 4.2 %collective-permute-start.32 = (bf16[602,128]{1,0:T(8,128)(2,1)S(1)}, bf16[602,128]{1,0:T(8,128)(2,1)S(1)}, u32[]{:S(2)}, u32[]{:S(2)}) collective-permute-start(bf16[602,128]{1,0:T(8,128)(2,1)S(1)} %get-tuple-element.92), channel_id=1, source_target_pairs={{0,8},{8,0},{16,24},{24,16},{1,9},{9,1},{17,25},{25,17},{2,10},{10... | collective-permute-start | bytes 462344 | tf_op jit(solution)/shard_map/ppermute | solution.py:76
  82.8 3.2 %shard_map.331.slopes_ref = f32[128,512]{1,0:T(8,128)S(1)} custom-call(bf16[128,2048]{1,0:T(8,128)(2,1)S(1)} %get-tuple-element.75.near_ref, bf16[128,2048]{1,0:T(8,128)(2,1)S(1)} %get-tuple-element.76.far_ref, f32[4,256]{1,0:T(4,128)S(1)} %copy-done.8, f32[8,256]{1,0:T(8,128)S(1)} %get-tuple-element.97.stats_ref, ...), custom_call_target="tpu_custom_call" | custom-call | flops 805306368 | bytes 3485696 | tf_op jit(solution)/shard_map/pallas_call | solution.py:59
  89.1 4.4 %shard_map.333 = (bf16[64,128]{1,0:T(8,128)(2,1)S(1)}, f32[8,256]{1,0:T(8,128)S(1)}) custom-call(bf16[128,2048]{1,0:T(8,128)(2,1)S(1)} %get-tuple-element.75.near_ref, bf16[128,2048]{1,0:T(8,128)(2,1)S(1)} %get-tuple-element.76.far_ref, f32[41,256]{1,0:T(8,128)S(1)} %bitcast.27, f32[4,256]{1,0:T(4,128)S(1)} %copy-done.8, ...), custom_call_target="tpu_custom_call" | custom-call | flops 1073741824 | bytes 3302400 | tf_op jit(solution)/shard_map/pallas_call | solution.py:59
  93.5 1.9 %collective-permute-start.39 = (bf16[64,128]{1,0:T(8,128)(2,1)S(1)}, bf16[64,128]{1,0:T(8,128)(2,1)S(1)}, u32[]{:S(2)}, u32[]{:S(2)}) collective-permute-start(bf16[64,128]{1,0:T(8,128)(2,1)S(1)} %get-tuple-element.101.refs_3_), channel_id=1, source_target_pairs={{0,24},{8,16},{16,8},{24,0},{1,25},{9,17},{17,9},{25,1},{2,26},{10... | collective-permute-start | bytes 49160 | tf_op jit(solution)/shard_map/ppermute | solution.py:76
  96.3 1.7 %collective-permute-start.41 = (bf16[64,128]{1,0:T(8,128)(2,1)S(1)}, bf16[64,128]{1,0:T(8,128)(2,1)S(1)}, u32[]{:S(2)}, u32[]{:S(2)}) collective-permute-start(bf16[64,128]{1,0:T(8,128)(2,1)S(1)} %get-tuple-element.101.refs_3_), channel_id=1, source_target_pairs={{0,8},{8,0},{16,24},{24,16},{1,9},{9,1},{17,25},{25,17},{2,10},{10... | collective-permute-start | bytes 49160 | tf_op jit(solution)/shard_map/ppermute | solution.py:76
  103.8 1.5 collective-permute-start.45
  108.0 1.9 %collective-permute-start.46 = (bf16[272,128]{1,0:T(8,128)(2,1)S(1)}, bf16[272,128]{1,0:T(8,128)(2,1)S(1)}, u32[]{:S(2)}, u32[]{:S(2)}) collective-permute-start(bf16[272,128]{1,0:T(8,128)(2,1)S(1)} %get-tuple-element.112.refs_3_), channel_id=1, source_target_pairs={{0,24},{8,16},{16,8},{24,0},{1,25},{9,17},{17,9},{25,1},{2,26},{10... | collective-permute-start | bytes 208904 | tf_op jit(solution)/shard_map/ppermute | solution.py:76
  111.1 1.4 collective-permute-start.48
  112.5 2.1 %collective-permute-done.46.refs_0_ = bf16[272,128]{1,0:T(8,128)(2,1)S(1)} collective-permute-done((bf16[272,128]{1,0:T(8,128)(2,1)S(1)}, bf16[272,128]{1,0:T(8,128)(2,1)S(1)}, u32[]{:S(2)}, u32[]{:S(2)}) %collective-permute-start.46) | collective-permute-done | bytes 69664 | tf_op jit(solution)/shard_map/ppermute | solution.py:76
  114.6 1.8 %collective-permute-done.47.refs_1_ = bf16[272,128]{1,0:T(8,128)(2,1)S(1)} collective-permute-done((bf16[272,128]{1,0:T(8,128)(2,1)S(1)}, bf16[272,128]{1,0:T(8,128)(2,1)S(1)}, u32[]{:S(2)}, u32[]{:S(2)}) %collective-permute-start.47) | collective-permute-done | bytes 69664 | tf_op jit(solution)/shard_map/ppermute | solution.py:76
  118.5 1.7 %collective-permute-start.50 = (bf16[272,128]{1,0:T(8,128)(2,1)S(1)}, bf16[272,128]{1,0:T(8,128)(2,1)S(1)}, u32[]{:S(2)}, u32[]{:S(2)}) collective-permute-start(bf16[272,128]{1,0:T(8,128)(2,1)S(1)} %get-tuple-element.113), channel_id=1, source_target_pairs={{0,6},{1,7},{2,4},{3,5},{4,2},{5,3},{6,0},{7,1},{8,14},{9,15},{10,... | collective-permute-start | bytes 208904 | tf_op jit(solution)/shard_map/ppermute | solution.py:72
  122.0 1.8 %collective-permute-done.50.refs_4_ = bf16[272,128]{1,0:T(8,128)(2,1)S(1)} collective-permute-done((bf16[272,128]{1,0:T(8,128)(2,1)S(1)}, bf16[272,128]{1,0:T(8,128)(2,1)S(1)}, u32[]{:S(2)}, u32[]{:S(2)}) %collective-permute-start.50) | collective-permute-done | bytes 69664 | tf_op jit(solution)/shard_map/ppermute | solution.py:72
  123.8 1.3 collective-permute-done.51.refs_5_
  129.8 1.6 %collective-permute-start.56 = (bf16[128,256]{1,0:T(8,128)(2,1)S(1)}, bf16[128,256]{1,0:T(8,128)(2,1)S(1)}, u32[]{:S(2)}, u32[]{:S(2)}) collective-permute-start(bf16[128,256]{1,0:T(8,128)(2,1)S(1)} %get-tuple-element.122), channel_id=1, source_target_pairs={{0,6},{1,7},{2,4},{3,5},{4,2},{5,3},{6,0},{7,1},{8,14},{9,15},{10,... | collective-permute-start | bytes 196616 | tf_op jit(solution)/shard_map/ppermute | solution.py:72
  132.2 1.6 %collective-permute-done.55.refs_1_ = bf16[128,256]{1,0:T(8,128)(2,1)S(1)} collective-permute-done((bf16[128,256]{1,0:T(8,128)(2,1)S(1)}, bf16[128,256]{1,0:T(8,128)(2,1)S(1)}, u32[]{:S(2)}, u32[]{:S(2)}) %collective-permute-start.55) | collective-permute-done | bytes 65568 | tf_op jit(solution)/shard_map/ppermute | solution.py:72
  135.0 1.9 %collective-permute-start.57 = (bf16[128,256]{1,0:T(8,128)(2,1)S(1)}, bf16[128,256]{1,0:T(8,128)(2,1)S(1)}, u32[]{:S(2)}, u32[]{:S(2)}) collective-permute-start(bf16[128,256]{1,0:T(8,128)(2,1)S(1)} %shard_map.343.refs_2_), channel_id=1, source_target_pairs={{0,24},{8,16},{16,8},{24,0},{1,25},{9,17},{17,9},{25,1},{2,26},{10... | collective-permute-start | bytes 196616 | tf_op jit(solution)/shard_map/ppermute | solution.py:76
  137.0 2.5 %collective-permute-start.59 = (bf16[128,256]{1,0:T(8,128)(2,1)S(1)}, bf16[128,256]{1,0:T(8,128)(2,1)S(1)}, u32[]{:S(2)}, u32[]{:S(2)}) collective-permute-start(bf16[128,256]{1,0:T(8,128)(2,1)S(1)} %shard_map.343.refs_2_), channel_id=1, source_target_pairs={{0,8},{8,0},{16,24},{24,16},{1,9},{9,1},{17,25},{25,17},{2,10},{10... | collective-permute-start | bytes 196616 | tf_op jit(solution)/shard_map/ppermute | solution.py:76
  140.1 1.3 collective-permute-done.57.own_ref
  141.4 1.6 %collective-permute-done.58.refs_0_ = bf16[128,256]{1,0:T(8,128)(2,1)S(1)} collective-permute-done((bf16[128,256]{1,0:T(8,128)(2,1)S(1)}, bf16[128,256]{1,0:T(8,128)(2,1)S(1)}, u32[]{:S(2)}, u32[]{:S(2)}) %collective-permute-start.58) | collective-permute-done | bytes 65568 | tf_op jit(solution)/shard_map/ppermute | solution.py:76
  143.0 1.7 %collective-permute-start.60 = (bf16[128,256]{1,0:T(8,128)(2,1)S(1)}, bf16[128,256]{1,0:T(8,128)(2,1)S(1)}, u32[]{:S(2)}, u32[]{:S(2)}) collective-permute-start(bf16[128,256]{1,0:T(8,128)(2,1)S(1)} %shard_map.344.refs_3_), channel_id=1, source_target_pairs={{0,6},{1,7},{2,4},{3,5},{4,2},{5,3},{6,0},{7,1},{8,14},{9,15},{10,... | collective-permute-start | bytes 196616 | tf_op jit(solution)/shard_map/ppermute | solution.py:72
  146.6 2.2 %collective-permute-done.60.refs_0_ = bf16[128,256]{1,0:T(8,128)(2,1)S(1)} collective-permute-done((bf16[128,256]{1,0:T(8,128)(2,1)S(1)}, bf16[128,256]{1,0:T(8,128)(2,1)S(1)}, u32[]{:S(2)}, u32[]{:S(2)}) %collective-permute-start.60) | collective-permute-done | bytes 65568 | tf_op jit(solution)/shard_map/ppermute | solution.py:72
  151.3 2.4 %shard_map.345 = (f32[602,256]{1,0:T(8,128)}, f32[602,256]{1,0:T(8,128)}, f32[602,256]{1,0:T(8,128)}, f32[256,256]{1,0:T(8,128)}, f32[256,256]{1,0:T(8,128)}, /*...) custom-call(bf16[128,256]{1,0:T(8,128)(2,1)S(1)} %collective-permute-done.60.refs_0_, ...), custom_call_target="tpu_custom_call" | custom-call | bytes 6047744 | tf_op jit(solution)/shard_map/pallas_call | solution.py:59
  (159 shorter events, 44.3 us)
Async XLA Ops:
  0.7 16.0 %collective-permute-start.3 = (bf16[602,128]{1,0:T(8,128)(2,1)}, bf16[602,128]{1,0:T(8,128)(2,1)S(1)}, u32[]{:S(2)}, u32[]{:S(2)}) collective-permute-start(bf16[602,128]{1,0:T(8,128)(2,1)} %bitcast.35), channel_id=1, source_target_pairs={{0,2},{1,3},{2,0},{3,1},{4,6},{5,7},{6,4},{7,5},{8,10},{9,11},{10,... | collective-permute-start | bytes 462344 | tf_op jit(solution)/shard_map/ppermute | solution.py:72
  5.1 8.6 %collective-permute-start = (bf16[128,256]{1,0:T(8,128)(2,1)S(1)}, bf16[128,256]{1,0:T(8,128)(2,1)S(1)}, u32[]{:S(2)}, u32[]{:S(2)}) collective-permute-start(bf16[128,256]{1,0:T(8,128)(2,1)S(1)} %convolution_convert_fusion.refs_3_), channel_id=1, source_target_pairs={{0,24},{8,16},{16,8},{24,0},{1,25},{9,17},{17,9},{25,1},{2,26},{10... | collective-permute-start | bytes 196616 | tf_op jit(solution)/shard_map/ppermute | solution.py:76
  8.7 7.9 %collective-permute-start.1 = (bf16[128,256]{1,0:T(8,128)(2,1)S(1)}, bf16[128,256]{1,0:T(8,128)(2,1)S(1)}, u32[]{:S(2)}, u32[]{:S(2)}) collective-permute-start(bf16[128,256]{1,0:T(8,128)(2,1)S(1)} %convolution_convert_fusion.refs_3_), channel_id=1, source_target_pairs={{0,16},{8,24},{16,0},{24,8},{1,17},{9,25},{17,1},{25,9},{2,18},{10... | collective-permute-start | bytes 196616 | tf_op jit(solution)/shard_map/ppermute | solution.py:76
  8.8 7.9 %collective-permute-start.2 = (bf16[128,256]{1,0:T(8,128)(2,1)S(1)}, bf16[128,256]{1,0:T(8,128)(2,1)S(1)}, u32[]{:S(2)}, u32[]{:S(2)}) collective-permute-start(bf16[128,256]{1,0:T(8,128)(2,1)S(1)} %convolution_convert_fusion.refs_3_), channel_id=1, source_target_pairs={{0,8},{8,0},{16,24},{24,16},{1,9},{9,1},{17,25},{25,17},{2,10},{10... | collective-permute-start | bytes 196616 | tf_op jit(solution)/shard_map/ppermute | solution.py:76
  12.4 12.8 %collective-permute-start.7 = (bf16[128,1024]{1,0:T(8,128)(2,1)S(1)}, bf16[128,1024]{1,0:T(8,128)(2,1)S(1)}, u32[]{:S(2)}, u32[]{:S(2)}) collective-permute-start(bf16[128,1024]{1,0:T(8,128)(2,1)S(1)} %get-tuple-element.78), channel_id=1, source_target_pairs={{0,8},{8,0},{16,24},{24,16},{1,9},{9,1},{17,25},{25,17},{2,10},{10... | collective-permute-start | bytes 786440 | tf_op jit(solution)/shard_map/ppermute | solution.py:76
  13.7 13.5 %collective-permute-start.8 = (bf16[128,1024]{1,0:T(8,128)(2,1)S(1)}, bf16[128,1024]{1,0:T(8,128)(2,1)S(1)}, u32[]{:S(2)}, u32[]{:S(2)}) collective-permute-start(bf16[128,1024]{1,0:T(8,128)(2,1)S(1)} %get-tuple-element.79), channel_id=1, source_target_pairs={{0,16},{8,24},{16,0},{24,8},{1,17},{9,25},{17,1},{25,9},{2,18},{10... | collective-permute-start | bytes 786440 | tf_op jit(solution)/shard_map/ppermute | solution.py:76
  16.7 10.5 %collective-permute-start.6 = (bf16[4,128,256]{2,1,0:T(8,128)(2,1)S(1)}, bf16[4,128,256]{2,1,0:T(8,128)(2,1)S(1)}, u32[]{:S(2)}, u32[]{:S(2)}) collective-permute-start(bf16[4,128,256]{2,1,0:T(8,128)(2,1)S(1)} %shard_map.324.refs_0_), channel_id=1, source_target_pairs={{0,6},{1,7},{2,4},{3,5},{4,2},{5,3},{6,0},{7,1},{8,14},{9,15},{10,... | collective-permute-start | bytes 786440 | tf_op jit(solution)/shard_map/ppermute | solution.py:72
  18.2 11.5 %collective-permute-start.4 = (bf16[4,128,256]{2,1,0:T(8,128)(2,1)S(1)}, bf16[4,128,256]{2,1,0:T(8,128)(2,1)S(1)}, u32[]{:S(2)}, u32[]{:S(2)}) collective-permute-start(bf16[4,128,256]{2,1,0:T(8,128)(2,1)S(1)} %shard_map.324.refs_0_), channel_id=1, source_target_pairs={{0,2},{1,3},{2,0},{3,1},{4,6},{5,7},{6,4},{7,5},{8,10},{9,11},{10,... | collective-permute-start | bytes 786440 | tf_op jit(solution)/shard_map/ppermute | solution.py:72
  19.7 10.0 %collective-permute-start.5 = (bf16[4,128,256]{2,1,0:T(8,128)(2,1)S(1)}, bf16[4,128,256]{2,1,0:T(8,128)(2,1)S(1)}, u32[]{:S(2)}, u32[]{:S(2)}) collective-permute-start(bf16[4,128,256]{2,1,0:T(8,128)(2,1)S(1)} %shard_map.324.refs_0_), channel_id=1, source_target_pairs={{0,4},{1,5},{2,6},{3,7},{4,0},{5,1},{6,2},{7,3},{8,12},{9,13},{10,... | collective-permute-start | bytes 786440 | tf_op jit(solution)/shard_map/ppermute | solution.py:72
  25.2 6.0 %collective-permute-start.9 = (bf16[4,128,256]{2,1,0:T(8,128)(2,1)S(1)}, bf16[4,128,256]{2,1,0:T(8,128)(2,1)S(1)}, u32[]{:S(2)}, u32[]{:S(2)}) collective-permute-start(bf16[4,128,256]{2,1,0:T(8,128)(2,1)S(1)} %shard_map.324.refs_0_), channel_id=1, source_target_pairs={{0,1},{1,0},{2,3},{3,2},{4,5},{5,4},{6,7},{7,6},{8,9},{9,8},{10,11... | collective-permute-start | bytes 786440 | tf_op jit(solution)/shard_map/ppermute | solution.py:72
  27.2 4.0 %collective-permute-start.12 = (bf16[4,128,256]{2,1,0:T(8,128)(2,1)S(1)}, bf16[4,128,256]{2,1,0:T(8,128)(2,1)S(1)}, u32[]{:S(2)}, u32[]{:S(2)}) collective-permute-start(bf16[4,128,256]{2,1,0:T(8,128)(2,1)S(1)} %collective-permute-done.6.refs_3_), channel_id=1, source_target_pairs={{0,1},{1,0},{2,3},{3,2},{4,5},{5,4},{6,7},{7,6},{8,9},{9,8},{10,11... | collective-permute-start | bytes 786440 | tf_op jit(solution)/shard_map/ppermute | solution.py:72
  30.3 15.8 %collective-permute-start.30 = (bf16[2,602,128]{2,1,0:T(8,128)(2,1)S(1)}, bf16[2,602,128]{2,1,0:T(8,128)(2,1)S(1)}, u32[]{:S(2)}, u32[]{:S(2)}) collective-permute-start(bf16[2,602,128]{2,1,0:T(8,128)(2,1)S(1)} %pad_maximum_fusion.1), channel_id=1, source_target_pairs={{0,4},{1,5},{2,6},{3,7},{4,0},{5,1},{6,2},{7,3},{8,12},{9,13},{10,... | collective-permute-start | bytes 924680 | tf_op jit(solution)/shard_map/ppermute | solution.py:72
  32.1 7.1 %collective-permute-start.13 = (bf16[144,256]{1,0:T(8,128)(2,1)S(1)}, bf16[144,256]{1,0:T(8,128)(2,1)S(1)}, u32[]{:S(2)}, u32[]{:S(2)}) collective-permute-start(bf16[144,256]{1,0:T(8,128)(2,1)S(1)} %shard_map.325.refs_3_.summed_ref), channel_id=1, source_target_pairs={{0,24},{8,16},{16,8},{24,0},{1,25},{9,17},{17,9},{25,1},{2,26},{10... | collective-permute-start | bytes 221192 | tf_op jit(solution)/shard_map/ppermute | solution.py:76
  32.5 8.5 %collective-permute-start.14 = (bf16[144,256]{1,0:T(8,128)(2,1)S(1)}, bf16[144,256]{1,0:T(8,128)(2,1)S(1)}, u32[]{:S(2)}, u32[]{:S(2)}) collective-permute-start(bf16[144,256]{1,0:T(8,128)(2,1)S(1)} %shard_map.325.refs_3_.summed_ref), channel_id=1, source_target_pairs={{0,16},{8,24},{16,0},{24,8},{1,17},{9,25},{17,1},{25,9},{2,18},{10... | collective-permute-start | bytes 221192 | tf_op jit(solution)/shard_map/ppermute | solution.py:76
  34.0 7.1 %collective-permute-start.15 = (bf16[144,256]{1,0:T(8,128)(2,1)S(1)}, bf16[144,256]{1,0:T(8,128)(2,1)S(1)}, u32[]{:S(2)}, u32[]{:S(2)}) collective-permute-start(bf16[144,256]{1,0:T(8,128)(2,1)S(1)} %shard_map.325.refs_3_.summed_ref), channel_id=1, source_target_pairs={{0,8},{8,0},{16,24},{24,16},{1,9},{9,1},{17,25},{25,17},{2,10},{10... | collective-permute-start | bytes 221192 | tf_op jit(solution)/shard_map/ppermute | solution.py:76
  41.1 12.4 %collective-permute-start.18 = (bf16[528,256]{1,0:T(8,128)(2,1)S(1)}, bf16[528,256]{1,0:T(8,128)(2,1)S(1)}, u32[]{:S(2)}, u32[]{:S(2)}) collective-permute-start(bf16[528,256]{1,0:T(8,128)(2,1)S(1)} %shard_map.326.refs_0_.refs_1_), channel_id=1, source_target_pairs={{0,6},{1,7},{2,4},{3,5},{4,2},{5,3},{6,0},{7,1},{8,14},{9,15},{10,... | collective-permute-start | bytes 811016 | tf_op jit(solution)/shard_map/ppermute | solution.py:72
  42.2 13.2 %collective-permute-start.16 = (bf16[528,256]{1,0:T(8,128)(2,1)S(1)}, bf16[528,256]{1,0:T(8,128)(2,1)S(1)}, u32[]{:S(2)}, u32[]{:S(2)}) collective-permute-start(bf16[528,256]{1,0:T(8,128)(2,1)S(1)} %shard_map.326.refs_0_.refs_1_), channel_id=1, source_target_pairs={{0,2},{1,3},{2,0},{3,1},{4,6},{5,7},{6,4},{7,5},{8,10},{9,11},{10,... | collective-permute-start | bytes 811016 | tf_op jit(solution)/shard_map/ppermute | solution.py:72
  43.7 12.1 %collective-permute-start.17 = (bf16[528,256]{1,0:T(8,128)(2,1)S(1)}, bf16[528,256]{1,0:T(8,128)(2,1)S(1)}, u32[]{:S(2)}, u32[]{:S(2)}) collective-permute-start(bf16[528,256]{1,0:T(8,128)(2,1)S(1)} %shard_map.326.refs_0_.refs_1_), channel_id=1, source_target_pairs={{0,4},{1,5},{2,6},{3,7},{4,0},{5,1},{6,2},{7,3},{8,12},{9,13},{10,... | collective-permute-start | bytes 811016 | tf_op jit(solution)/shard_map/ppermute | solution.py:72
  44.7 8.8 %collective-permute-start.19 = (bf16[128,1024]{1,0:T(8,128)(2,1)S(1)}, bf16[128,1024]{1,0:T(8,128)(2,1)S(1)}, u32[]{:S(2)}, u32[]{:S(2)}) collective-permute-start(bf16[128,1024]{1,0:T(8,128)(2,1)S(1)} %get-tuple-element.82), channel_id=1, source_target_pairs={{0,24},{8,16},{16,8},{24,0},{1,25},{9,17},{17,9},{25,1},{2,26},{10... | collective-permute-start | bytes 786440 | tf_op jit(solution)/shard_map/ppermute | solution.py:76
  46.5 17.6 %collective-permute-start.31 = (bf16[4,602,128]{2,0,1:T(4,128)(2,1)S(1)}, bf16[4,602,128]{2,0,1:T(4,128)(2,1)S(1)}, u32[]{:S(2)}, u32[]{:S(2)}) collective-permute-start(bf16[4,602,128]{2,0,1:T(4,128)(2,1)S(1)} %copy.37), channel_id=1, source_target_pairs={{0,1},{1,0},{2,3},{3,2},{4,5},{5,4},{6,7},{7,6},{8,9},{9,8},{10,11... | collective-permute-start | bytes 1849352 | tf_op jit(solution)/shard_map/ppermute | solution.py:72
  59.6 6.3 %collective-permute-start.24 = (bf16[144,256]{1,0:T(8,128)(2,1)S(1)}, bf16[144,256]{1,0:T(8,128)(2,1)S(1)}, u32[]{:S(2)}, u32[]{:S(2)}) collective-permute-start(bf16[144,256]{1,0:T(8,128)(2,1)S(1)} %get-tuple-element.84.refs_3_.summed_ref), channel_id=1, source_target_pairs={{0,24},{8,16},{16,8},{24,0},{1,25},{9,17},{17,9},{25,1},{2,26},{10... | collective-permute-start | bytes 221192 | tf_op jit(solution)/shard_map/ppermute | solution.py:76
  61.6 8.7 %collective-permute-start.25 = (bf16[144,256]{1,0:T(8,128)(2,1)S(1)}, bf16[144,256]{1,0:T(8,128)(2,1)S(1)}, u32[]{:S(2)}, u32[]{:S(2)}) collective-permute-start(bf16[144,256]{1,0:T(8,128)(2,1)S(1)} %get-tuple-element.84.refs_3_.summed_ref), channel_id=1, source_target_pairs={{0,16},{8,24},{16,0},{24,8},{1,17},{9,25},{17,1},{25,9},{2,18},{10... | collective-permute-start | bytes 221192 | tf_op jit(solution)/shard_map/ppermute | solution.py:76
  63.2 7.0 %collective-permute-start.26 = (bf16[144,256]{1,0:T(8,128)(2,1)S(1)}, bf16[144,256]{1,0:T(8,128)(2,1)S(1)}, u32[]{:S(2)}, u32[]{:S(2)}) collective-permute-start(bf16[144,256]{1,0:T(8,128)(2,1)S(1)} %get-tuple-element.84.refs_3_.summed_ref), channel_id=1, source_target_pairs={{0,8},{8,0},{16,24},{24,16},{1,9},{9,1},{17,25},{25,17},{2,10},{10... | collective-permute-start | bytes 221192 | tf_op jit(solution)/shard_map/ppermute | solution.py:76
  70.3 8.3 %collective-permute-start.34 = (bf16[602,128]{1,0:T(8,128)(2,1)S(1)}, bf16[602,128]{1,0:T(8,128)(2,1)S(1)}, u32[]{:S(2)}, u32[]{:S(2)}) collective-permute-start(bf16[602,128]{1,0:T(8,128)(2,1)S(1)} %get-tuple-element.96), channel_id=1, source_target_pairs={{0,24},{8,16},{16,8},{24,0},{1,25},{9,17},{17,9},{25,1},{2,26},{10... | collective-permute-start | bytes 462344 | tf_op jit(solution)/shard_map/ppermute | solution.py:76
  72.5 14.3 %collective-permute-start.29 = (bf16[528,256]{1,0:T(8,128)(2,1)S(1)}, bf16[528,256]{1,0:T(8,128)(2,1)S(1)}, u32[]{:S(2)}, u32[]{:S(2)}) collective-permute-start(bf16[528,256]{1,0:T(8,128)(2,1)S(1)} %shard_map.329.refs_0_.refs_1_), channel_id=1, source_target_pairs={{0,6},{1,7},{2,4},{3,5},{4,2},{5,3},{6,0},{7,1},{8,14},{9,15},{10,... | collective-permute-start | bytes 811016 | tf_op jit(solution)/shard_map/ppermute | solution.py:72
  73.5 13.4 %collective-permute-start.27 = (bf16[528,256]{1,0:T(8,128)(2,1)S(1)}, bf16[528,256]{1,0:T(8,128)(2,1)S(1)}, u32[]{:S(2)}, u32[]{:S(2)}) collective-permute-start(bf16[528,256]{1,0:T(8,128)(2,1)S(1)} %shard_map.329.refs_0_.refs_1_), channel_id=1, source_target_pairs={{0,2},{1,3},{2,0},{3,1},{4,6},{5,7},{6,4},{7,5},{8,10},{9,11},{10,... | collective-permute-start | bytes 811016 | tf_op jit(solution)/shard_map/ppermute | solution.py:72
  75.0 12.3 %collective-permute-start.28 = (bf16[528,256]{1,0:T(8,128)(2,1)S(1)}, bf16[528,256]{1,0:T(8,128)(2,1)S(1)}, u32[]{:S(2)}, u32[]{:S(2)}) collective-permute-start(bf16[528,256]{1,0:T(8,128)(2,1)S(1)} %shard_map.329.refs_0_.refs_1_), channel_id=1, source_target_pairs={{0,4},{1,5},{2,6},{3,7},{4,0},{5,1},{6,2},{7,3},{8,12},{9,13},{10,... | collective-permute-start | bytes 811016 | tf_op jit(solution)/shard_map/ppermute | solution.py:72
  76.0 10.0 %collective-permute-start.33 = (bf16[602,128]{1,0:T(8,128)(2,1)S(1)}, bf16[602,128]{1,0:T(8,128)(2,1)S(1)}, u32[]{:S(2)}, u32[]{:S(2)}) collective-permute-start(bf16[602,128]{1,0:T(8,128)(2,1)S(1)} %get-tuple-element.94), channel_id=1, source_target_pairs={{0,16},{8,24},{16,0},{24,8},{1,17},{9,25},{17,1},{25,9},{2,18},{10... | collective-permute-start | bytes 462344 | tf_op jit(solution)/shard_map/ppermute | solution.py:76
  78.6 8.2 %collective-permute-start.32 = (bf16[602,128]{1,0:T(8,128)(2,1)S(1)}, bf16[602,128]{1,0:T(8,128)(2,1)S(1)}, u32[]{:S(2)}, u32[]{:S(2)}) collective-permute-start(bf16[602,128]{1,0:T(8,128)(2,1)S(1)} %get-tuple-element.92), channel_id=1, source_target_pairs={{0,8},{8,0},{16,24},{24,16},{1,9},{9,1},{17,25},{25,17},{2,10},{10... | collective-permute-start | bytes 462344 | tf_op jit(solution)/shard_map/ppermute | solution.py:76
  93.5 5.6 %collective-permute-start.39 = (bf16[64,128]{1,0:T(8,128)(2,1)S(1)}, bf16[64,128]{1,0:T(8,128)(2,1)S(1)}, u32[]{:S(2)}, u32[]{:S(2)}) collective-permute-start(bf16[64,128]{1,0:T(8,128)(2,1)S(1)} %get-tuple-element.101.refs_3_), channel_id=1, source_target_pairs={{0,24},{8,16},{16,8},{24,0},{1,25},{9,17},{17,9},{25,1},{2,26},{10... | collective-permute-start | bytes 49160 | tf_op jit(solution)/shard_map/ppermute | solution.py:76
  95.4 4.7 %collective-permute-start.40 = (bf16[64,128]{1,0:T(8,128)(2,1)S(1)}, bf16[64,128]{1,0:T(8,128)(2,1)S(1)}, u32[]{:S(2)}, u32[]{:S(2)}) collective-permute-start(bf16[64,128]{1,0:T(8,128)(2,1)S(1)} %get-tuple-element.101.refs_3_), channel_id=1, source_target_pairs={{0,16},{8,24},{16,0},{24,8},{1,17},{9,25},{17,1},{25,9},{2,18},{10... | collective-permute-start | bytes 49160 | tf_op jit(solution)/shard_map/ppermute | solution.py:76
  101.7 4.8 %collective-permute-start.43 = (bf16[64,128]{1,0:T(8,128)(2,1)S(1)}, bf16[64,128]{1,0:T(8,128)(2,1)S(1)}, u32[]{:S(2)}, u32[]{:S(2)}) collective-permute-start(bf16[64,128]{1,0:T(8,128)(2,1)S(1)} %get-tuple-element.102), channel_id=1, source_target_pairs={{0,6},{1,7},{2,4},{3,5},{4,2},{5,3},{6,0},{7,1},{8,14},{9,15},{10,... | collective-permute-start | bytes 49160 | tf_op jit(solution)/shard_map/ppermute | solution.py:72
  108.0 6.6 %collective-permute-start.46 = (bf16[272,128]{1,0:T(8,128)(2,1)S(1)}, bf16[272,128]{1,0:T(8,128)(2,1)S(1)}, u32[]{:S(2)}, u32[]{:S(2)}) collective-permute-start(bf16[272,128]{1,0:T(8,128)(2,1)S(1)} %get-tuple-element.112.refs_3_), channel_id=1, source_target_pairs={{0,24},{8,16},{16,8},{24,0},{1,25},{9,17},{17,9},{25,1},{2,26},{10... | collective-permute-start | bytes 208904 | tf_op jit(solution)/shard_map/ppermute | solution.py:76
  110.0 6.5 %collective-permute-start.47 = (bf16[272,128]{1,0:T(8,128)(2,1)S(1)}, bf16[272,128]{1,0:T(8,128)(2,1)S(1)}, u32[]{:S(2)}, u32[]{:S(2)}) collective-permute-start(bf16[272,128]{1,0:T(8,128)(2,1)S(1)} %get-tuple-element.112.refs_3_), channel_id=1, source_target_pairs={{0,16},{8,24},{16,0},{24,8},{1,17},{9,25},{17,1},{25,9},{2,18},{10... | collective-permute-start | bytes 208904 | tf_op jit(solution)/shard_map/ppermute | solution.py:76
  111.1 5.4 %collective-permute-start.48 = (bf16[272,128]{1,0:T(8,128)(2,1)S(1)}, bf16[272,128]{1,0:T(8,128)(2,1)S(1)}, u32[]{:S(2)}, u32[]{:S(2)}) collective-permute-start(bf16[272,128]{1,0:T(8,128)(2,1)S(1)} %get-tuple-element.112.refs_3_), channel_id=1, source_target_pairs={{0,8},{8,0},{16,24},{24,16},{1,9},{9,1},{17,25},{25,17},{2,10},{10... | collective-permute-start | bytes 208904 | tf_op jit(solution)/shard_map/ppermute | solution.py:76
  118.5 5.3 %collective-permute-start.50 = (bf16[272,128]{1,0:T(8,128)(2,1)S(1)}, bf16[272,128]{1,0:T(8,128)(2,1)S(1)}, u32[]{:S(2)}, u32[]{:S(2)}) collective-permute-start(bf16[272,128]{1,0:T(8,128)(2,1)S(1)} %get-tuple-element.113), channel_id=1, source_target_pairs={{0,6},{1,7},{2,4},{3,5},{4,2},{5,3},{6,0},{7,1},{8,14},{9,15},{10,... | collective-permute-start | bytes 208904 | tf_op jit(solution)/shard_map/ppermute | solution.py:72
  120.2 5.0 %collective-permute-start.51 = (bf16[272,128]{1,0:T(8,128)(2,1)S(1)}, bf16[272,128]{1,0:T(8,128)(2,1)S(1)}, u32[]{:S(2)}, u32[]{:S(2)}) collective-permute-start(bf16[272,128]{1,0:T(8,128)(2,1)S(1)} %get-tuple-element.114), channel_id=1, source_target_pairs={{0,4},{1,5},{2,6},{3,7},{4,0},{5,1},{6,2},{7,3},{8,12},{9,13},{10,... | collective-permute-start | bytes 208904 | tf_op jit(solution)/shard_map/ppermute | solution.py:72
  121.2 4.3 %collective-permute-start.52 = (bf16[272,128]{1,0:T(8,128)(2,1)S(1)}, bf16[272,128]{1,0:T(8,128)(2,1)S(1)}, u32[]{:S(2)}, u32[]{:S(2)}) collective-permute-start(bf16[272,128]{1,0:T(8,128)(2,1)S(1)} %get-tuple-element.115), channel_id=1, source_target_pairs={{0,2},{1,3},{2,0},{3,1},{4,6},{5,7},{6,4},{7,5},{8,10},{9,11},{10,... | collective-permute-start | bytes 208904 | tf_op jit(solution)/shard_map/ppermute | solution.py:72
  127.9 4.3 %collective-permute-start.54 = (bf16[128,256]{1,0:T(8,128)(2,1)S(1)}, bf16[128,256]{1,0:T(8,128)(2,1)S(1)}, u32[]{:S(2)}, u32[]{:S(2)}) collective-permute-start(bf16[128,256]{1,0:T(8,128)(2,1)S(1)} %get-tuple-element.120), channel_id=1, source_target_pairs={{0,2},{1,3},{2,0},{3,1},{4,6},{5,7},{6,4},{7,5},{8,10},{9,11},{10,... | collective-permute-start | bytes 196616 | tf_op jit(solution)/shard_map/ppermute | solution.py:72
  128.8 5.0 %collective-permute-start.55 = (bf16[128,256]{1,0:T(8,128)(2,1)S(1)}, bf16[128,256]{1,0:T(8,128)(2,1)S(1)}, u32[]{:S(2)}, u32[]{:S(2)}) collective-permute-start(bf16[128,256]{1,0:T(8,128)(2,1)S(1)} %get-tuple-element.121), channel_id=1, source_target_pairs={{0,4},{1,5},{2,6},{3,7},{4,0},{5,1},{6,2},{7,3},{8,12},{9,13},{10,... | collective-permute-start | bytes 196616 | tf_op jit(solution)/shard_map/ppermute | solution.py:72
  129.8 5.2 %collective-permute-start.56 = (bf16[128,256]{1,0:T(8,128)(2,1)S(1)}, bf16[128,256]{1,0:T(8,128)(2,1)S(1)}, u32[]{:S(2)}, u32[]{:S(2)}) collective-permute-start(bf16[128,256]{1,0:T(8,128)(2,1)S(1)} %get-tuple-element.122), channel_id=1, source_target_pairs={{0,6},{1,7},{2,4},{3,5},{4,2},{5,3},{6,0},{7,1},{8,14},{9,15},{10,... | collective-permute-start | bytes 196616 | tf_op jit(solution)/shard_map/ppermute | solution.py:72
  135.0 6.3 %collective-permute-start.57 = (bf16[128,256]{1,0:T(8,128)(2,1)S(1)}, bf16[128,256]{1,0:T(8,128)(2,1)S(1)}, u32[]{:S(2)}, u32[]{:S(2)}) collective-permute-start(bf16[128,256]{1,0:T(8,128)(2,1)S(1)} %shard_map.343.refs_2_), channel_id=1, source_target_pairs={{0,24},{8,16},{16,8},{24,0},{1,25},{9,17},{17,9},{25,1},{2,26},{10... | collective-permute-start | bytes 196616 | tf_op jit(solution)/shard_map/ppermute | solution.py:76
  137.0 6.0 %collective-permute-start.58 = (bf16[128,256]{1,0:T(8,128)(2,1)S(1)}, bf16[128,256]{1,0:T(8,128)(2,1)S(1)}, u32[]{:S(2)}, u32[]{:S(2)}) collective-permute-start(bf16[128,256]{1,0:T(8,128)(2,1)S(1)} %shard_map.343.refs_2_), channel_id=1, source_target_pairs={{0,16},{8,24},{16,0},{24,8},{1,17},{9,25},{17,1},{25,9},{2,18},{10... | collective-permute-start | bytes 196616 | tf_op jit(solution)/shard_map/ppermute | solution.py:76
  137.0 5.9 %collective-permute-start.59 = (bf16[128,256]{1,0:T(8,128)(2,1)S(1)}, bf16[128,256]{1,0:T(8,128)(2,1)S(1)}, u32[]{:S(2)}, u32[]{:S(2)}) collective-permute-start(bf16[128,256]{1,0:T(8,128)(2,1)S(1)} %shard_map.343.refs_2_), channel_id=1, source_target_pairs={{0,8},{8,0},{16,24},{24,16},{1,9},{9,1},{17,25},{25,17},{2,10},{10... | collective-permute-start | bytes 196616 | tf_op jit(solution)/shard_map/ppermute | solution.py:76
  143.0 5.8 %collective-permute-start.60 = (bf16[128,256]{1,0:T(8,128)(2,1)S(1)}, bf16[128,256]{1,0:T(8,128)(2,1)S(1)}, u32[]{:S(2)}, u32[]{:S(2)}) collective-permute-start(bf16[128,256]{1,0:T(8,128)(2,1)S(1)} %shard_map.344.refs_3_), channel_id=1, source_target_pairs={{0,6},{1,7},{2,4},{3,5},{4,2},{5,3},{6,0},{7,1},{8,14},{9,15},{10,... | collective-permute-start | bytes 196616 | tf_op jit(solution)/shard_map/ppermute | solution.py:72
  144.7 4.6 %collective-permute-start.61 = (bf16[128,256]{1,0:T(8,128)(2,1)S(1)}, bf16[128,256]{1,0:T(8,128)(2,1)S(1)}, u32[]{:S(2)}, u32[]{:S(2)}) collective-permute-start(bf16[128,256]{1,0:T(8,128)(2,1)S(1)} %shard_map.344.refs_3_), channel_id=1, source_target_pairs={{0,4},{1,5},{2,6},{3,7},{4,0},{5,1},{6,2},{7,3},{8,12},{9,13},{10,... | collective-permute-start | bytes 196616 | tf_op jit(solution)/shard_map/ppermute | solution.py:72
  145.7 4.3 %collective-permute-start.62 = (bf16[128,256]{1,0:T(8,128)(2,1)S(1)}, bf16[128,256]{1,0:T(8,128)(2,1)S(1)}, u32[]{:S(2)}, u32[]{:S(2)}) collective-permute-start(bf16[128,256]{1,0:T(8,128)(2,1)S(1)} %shard_map.344.refs_3_), channel_id=1, source_target_pairs={{0,2},{1,3},{2,0},{3,1},{4,6},{5,7},{6,4},{7,5},{8,10},{9,11},{10,... | collective-permute-start | bytes 196616 | tf_op jit(solution)/shard_map/ppermute | solution.py:72
  146.6 4.1 %collective-permute-start.66 = (bf16[128,256]{1,0:T(8,128)(2,1)S(1)}, bf16[128,256]{1,0:T(8,128)(2,1)S(1)}, u32[]{:S(2)}, u32[]{:S(2)}) collective-permute-start(bf16[128,256]{1,0:T(8,128)(2,1)S(1)} %shard_map.344.refs_3_), channel_id=1, source_target_pairs={{0,1},{1,0},{2,3},{3,2},{4,5},{5,4},{6,7},{7,6},{8,9},{9,8},{10,11... | collective-permute-start | bytes 196616 | tf_op jit(solution)/shard_map/ppermute | solution.py:72
  (39 other events, 269.6 us)
